TPU v7x, 128 devices: a whole 4x4x4 slice. The times are simulated.
128 devices in a mesh: ctx: 64 (over z, x_lo, y, core), head: 2 (over x_hi).
Axes of the slice: x: 4 (x_hi: 2, x_lo: 2; x = x_hi * 2 + x_lo), y: 4, z: 4, core: 2. Of those that a mesh axis runs over, the one named last changes fastest.
Arguments:
- queries: bfloat16 [32768, 2048], P('ctx', 'head'), may hold values from -6 to 6
- keys: bfloat16 [32768, 2048], P('ctx', 'head'), may hold values from -6 to 6
- values: bfloat16 [32768, 2048], P('ctx', 'head'), may hold values from -6 to 6
- rates: float32 [32768, 2], P('ctx', 'head'), may hold values from 0.0002762136 to 0.0027621358
- w_up: bfloat16 [2, 1024, 512], P('head'), may hold values from -0.1875 to 0.1875
- w_gate: bfloat16 [2, 1024, 512], P('head'), may hold values from -0.1875 to 0.1875
- w_down: bfloat16 [2, 512, 1024], P('head'), may hold values from -0.25 to 0.25
- w_out: bfloat16 [2048, 5120], P('head'), may hold values from -0.125 to 0.125
Outputs:
- mixed: bfloat16 [32768, 5120], P('ctx', 'head')
All inputs are finite; a program needn't handle non-finite values.
Results may differ from a plain program's by a relative error of at most 0.018.
Values may be sent and summed in bfloat16 or wider, within the bound.
No kernel may reach another device: no remote copies, remote signals or barrier semaphores. Data moves between devices by JAX's collectives and lax.ppermute only.
A program may use at most 128 MiB of HBM per device.

v0:
```python
import jax
import jax.numpy as jnp
from jax import lax
from jax.sharding import Mesh
from jax.sharding import PartitionSpec as P

STEPS = 2
CTX = ("ctx_0", "ctx_1", "ctx_2", "ctx_3")


def split_up(x, dim, peers):
    before, after = (x.shape[:dim], x.shape[dim + 1 :])
    return jnp.moveaxis(x.reshape(*before, peers, -1, *after), dim, 0)


def summed_on_arrival(x, axis, dim):
    pieces = split_up(x, dim, lax.axis_size(axis))
    arrived = lax.all_to_all(pieces, axis, split_axis=0, concat_axis=0, tiled=True)
    return arrived.sum(axis=0)


def summed_rows(x, axes, dim):
    far, near = axes
    own = summed_on_arrival(split_up(x, dim, lax.axis_size(far)), near, dim + 1)
    return jnp.sum(lax.all_to_all(own, far, 0, 0, tiled=True), axis=0)


def from_everyone(x, axis):
    copies = jnp.broadcast_to(x, (lax.axis_size(axis), *x.shape))
    return lax.all_to_all(copies, axis, split_axis=0, concat_axis=0, tiled=True)


def over_copies(x, axis):
    return from_everyone(x, axis).sum(axis=0)


def together(arrays, axis):
    vector, at, gathered = (jnp.concatenate([a.reshape(-1) for a in arrays]), 0, [])
    running = over_copies(vector, axis)
    for a in arrays:
        gathered.append(running[at : at + a.size].reshape(a.shape))
        at += a.size
    return tuple(gathered)


def in_order(pieces, dim):
    pieces = jnp.moveaxis(pieces, 0, dim)
    dims = pieces.shape
    return pieces.reshape(*dims[:dim], dims[dim] * dims[dim + 1], *dims[dim + 2 :])


def whole_of(x, axes, dim):
    far, near = axes
    first = from_everyone(x, far)
    pieces = jnp.swapaxes(from_everyone(first, near), 0, 1)
    return in_order(pieces.reshape(-1, *x.shape), dim)


def sent_together(arrays, axis, dim, along):
    widths = [a.shape[along] for a in arrays]
    both = jnp.concatenate(arrays, axis=along)
    filled = whole_of(both, axis, dim)
    return tuple(jnp.split(filled, [sum(widths[:k]) for k in range(1, len(widths))], axis=along))


def summed_on_arrival_2(x, axis, dim):
    peers = lax.axis_size(axis)
    pieces = lax.all_to_all(split_up(x, dim, peers), axis, 0, 0, tiled=True)
    return jnp.sum(pieces.astype(jnp.float32), axis=0)


def frob(matrix):
    return jnp.sqrt(jnp.sum(matrix * matrix))


def tdot(left, right):
    return lax.dot_general(
        left, right, (((0,), (0,)), ((), ())), preferred_element_type=jnp.float32
    )


def local_grads(keys_h, targets, blocks):
    b_one, b_three, b_two = blocks
    act = jnp.dot(keys_h, b_one, preferred_element_type=jnp.float32)
    lin = jnp.dot(keys_h, b_three, preferred_element_type=jnp.float32)
    sig = jax.nn.sigmoid(act)
    hidden = (act * sig * lin).astype(jnp.bfloat16)
    err = jnp.dot(targets, b_two, preferred_element_type=jnp.float32)
    pgrad = (err * lin * sig * (1.0 + act * (1.0 - sig))).astype(jnp.bfloat16)
    qgrad = (err * act * sig).astype(jnp.bfloat16)
    return (tdot(keys_h, pgrad), tdot(keys_h, qgrad), tdot(targets, hidden))


def blocks_of(weights):
    return tuple((weight.astype(jnp.bfloat16) for weight in weights))


def shards(queries, keys, values, rates, w_up, w_gate, w_down, w_out):
    width = w_up.shape[1]
    targets = (rates[:, 0][:, None] * values.astype(jnp.float32)).astype(jnp.bfloat16)
    weights = [
        w_up[0].astype(jnp.float32),
        w_gate[0].astype(jnp.float32),
        w_down[0].astype(jnp.float32).T,
    ]
    sizes = [frob(weights[0]), frob(weights[1]), frob(weights[2])]
    blocks = blocks_of(weights)
    count = width // lax.axis_size(CTX)
    start = lax.axis_index(CTX) * count
    own_rows = [lax.dynamic_slice_in_dim(weight, start, count, 0) for weight in weights]
    for step in range(STEPS):
        shares = jax.tree.map(
            lambda part: summed_rows(part, (("ctx_0", "ctx_1", "ctx_2"), "ctx_3"), 0),
            local_grads(keys, targets, blocks),
        )
        moved = [rows + share for rows, share in zip(own_rows, shares)]
        squares = together(
            (
                jnp.sum(moved[0] * moved[0]),
                jnp.sum(moved[1] * moved[1]),
                jnp.sum(moved[2] * moved[2]),
            ),
            CTX,
        )
        own_rows = [
            rows * size / jnp.sqrt(total + 1e-06)
            for rows, size, total in zip(moved, sizes, squares)
        ]
        rounded = blocks_of(own_rows)
        blocks = tuple(
            sent_together(
                (rounded[0], rounded[1], rounded[2]), (("ctx_0", "ctx_1", "ctx_2"), "ctx_3"), 0, 1
            )
        )
    b_one, b_three, b_two = blocks
    act = jnp.dot(queries, b_one, preferred_element_type=jnp.float32)
    lin = jnp.dot(queries, b_three, preferred_element_type=jnp.float32)
    hidq = (jax.nn.silu(act) * lin).astype(jnp.bfloat16)
    pieces = lax.dot_general(
        hidq, b_two, (((1,), (1,)), ((), ())), preferred_element_type=jnp.float32
    ).astype(jnp.bfloat16)
    partial_out = jnp.dot(pieces, w_out, preferred_element_type=jnp.float32)
    return summed_on_arrival_2(partial_out.astype(jnp.bfloat16), "head", 1).astype(jnp.bfloat16)


def solution(mesh):
    finer = Mesh(
        mesh.devices.reshape(4, 2, 4, 2, mesh.shape["head"]),
        ("ctx_0", "ctx_1", "ctx_2", "ctx_3", "head"),
    )
    return jax.shard_map(
        shards,
        mesh=finer,
        in_specs=(
            P(CTX, "head"),
            P(CTX, "head"),
            P(CTX, "head"),
            P(CTX, "head"),
            P("head", None, None),
            P("head", None, None),
            P("head", None, None),
            P("head", None),
        ),
        out_specs=P(CTX, "head"),
        check_vma=False,
    )
```

profile of v0, /device:TPU:1, one launch (start us, length us, event | category | flops | bytes accessed | tf_op | source)
XLA Modules:
  0.0 415.3 jit_solution(10489062392422047144)
XLA Ops:
  1.2 1.9 fusion.14
  7.2 2.4 convolution_bitcast_fusion.3
  9.6 1.9 copy.76
  11.5 1.5 copy.77
  13.1 5.2 %all-to-all-start = ((f32[2,32,16,512]{3,2,1,0:T(8,128)}), f32[2,32,16,512]{3,2,1,0:T(8,128)S(1)}, u32[]{:S(2)}, u32[]{:S(2)}) async-start(f32[2,32,16,512]{3,2,1,0:T(8,128)} %copy.77), calls=%async_computation | async-start | bytes 4194304 | tf_op jit(solution)/shard_map/all_to_all | solution.py:18
  18.2 2.9 fusion.21
  21.2 2.1 convolution_bitcast_fusion.2
  23.3 1.6 copy.114
  24.9 2.9 copy.78
  27.8 3.2 copy.79
  31.0 4.9 %all-to-all-start.4 = ((f32[2,32,16,512]{3,2,1,0:T(8,128)}), f32[2,32,16,512]{3,2,1,0:T(8,128)}, u32[]{:S(2)}, u32[]{:S(2)}) async-start(f32[2,32,16,512]{3,2,1,0:T(8,128)} %bitcast.106), calls=%async_computation.4 | async-start | bytes 4194304 | tf_op jit(solution)/shard_map/all_to_all | solution.py:18
  35.9 1.3 reduce_sum.219
  37.2 1.3 all-to-all-done.4
  38.5 6.6 %all_to_all.97 = f32[2,32,16,512]{3,2,1,0:T(8,128)S(1)} all-to-all(f32[2,32,16,512]{3,2,1,0:T(8,128)} %copy.79), channel_id=1, replica_groups=mesh['ctx_0'=4,'ctx_1'=2,'ctx_2'=4,'ctx_3'=2,'head'=2] {'ctx_3'}, dimensions={0} | all-to-all | bytes 4194304 | tf_op jit(solution)/shard_map/all_to_all | solution.py:18
  45.1 9.2 %all-to-all-start.1 = ((f32[32,16,512]{2,1,0:T(8,128)}), f32[32,16,512]{2,1,0:T(8,128)}, u32[]{:S(2)}, u32[]{:S(2)}) async-start(f32[32,16,512]{2,1,0:T(8,128)} %reduce_sum.219), calls=%async_computation.1 | async-start | bytes 2097152 | tf_op jit(solution)/shard_map/all_to_all | solution.py:25
  54.3 2.9 reduce_sum.226
  57.2 12.7 %all-to-all-done.1 = f32[32,16,512]{2,1,0:T(8,128)} async-done(((f32[32,16,512]{2,1,0:T(8,128)}), f32[32,16,512]{2,1,0:T(8,128)}, u32[]{:S(2)}, u32[]{:S(2)}) %all-to-all-start.1) | async-done | bytes 1048608 | tf_op jit(solution)/shard_map/all_to_all | solution.py:25
  69.9 6.0 %all-to-all-start.5 = ((f32[32,16,512]{2,1,0:T(8,128)}), f32[32,16,512]{2,1,0:T(8,128)}, u32[]{:S(2)}, u32[]{:S(2)}) async-start(f32[32,16,512]{2,1,0:T(8,128)} %reduce_sum.226), calls=%async_computation.5 | async-start | bytes 2097152 | tf_op jit(solution)/shard_map/all_to_all | solution.py:25
  77.2 13.7 %all-to-all-done.5 = f32[32,16,512]{2,1,0:T(8,128)} async-done(((f32[32,16,512]{2,1,0:T(8,128)}), f32[32,16,512]{2,1,0:T(8,128)}, u32[]{:S(2)}, u32[]{:S(2)}) %all-to-all-start.5) | async-done | bytes 1048608 | tf_op jit(solution)/shard_map/all_to_all | solution.py:25
  90.9 6.5 %all-to-all-start.3 = ((f32[32,16,512]{2,1,0:T(8,128)}), f32[32,16,512]{2,1,0:T(8,128)}, u32[]{:S(2)}, u32[]{:S(2)}) async-start(f32[32,16,512]{2,1,0:T(8,128)} %reduce_sum.223), calls=%async_computation.3 | async-start | bytes 2097152 | tf_op jit(solution)/shard_map/all_to_all | solution.py:25
  98.6 1.5 copy.80
  100.1 1.6 convert_element_type.77
  101.7 2.5 multiply_reduce_fusion.1
  104.2 1.6 bitcast_convert_fusion.1
  105.8 1.6 bitcast_convert_fusion
  108.7 1.3 reduce_sum.227
  110.0 1.4 multiply_reduce_fusion.8
  111.4 1.4 multiply_reduce_fusion.6
  112.8 1.3 reduce_sum.224
  114.1 1.5 multiply_reduce_fusion.7
  115.5 2.0 pad_maximum_fusion.2
  118.1 9.9 %all-to-all-start.6 = ((f32[64,1,3]{2,1,0:T(1,128)}), f32[64,1,3]{2,1,0:T(1,128)S(1)}, u32[]{:S(2)}, u32[]{:S(2)}) async-start(f32[64,1,3]{2,1,0:T(1,128)} %broadcast_in_dim.18), calls=%async_computation.6 | async-start | bytes 65536 | tf_op jit(solution)/shard_map/all_to_all | solution.py:30
  131.3 4.5 %all-to-all-done.6 = f32[64,1,3]{2,1,0:T(1,128)S(1)} async-done(((f32[64,1,3]{2,1,0:T(1,128)}), f32[64,1,3]{2,1,0:T(1,128)S(1)}, u32[]{:S(2)}, u32[]{:S(2)}) %all-to-all-start.6) | async-done | bytes 800 | tf_op jit(solution)/shard_map/all_to_all | solution.py:30
  140.4 24.4 %all_to_all.98 = bf16[32,16,1536]{2,1,0:T(8,128)(2,1)S(1)} all-to-all(bf16[32,16,1536]{2,1,0:T(8,128)(2,1)S(1)} %broadcast_in_dim.19), channel_id=1, replica_groups=mesh['ctx_0'=4,'ctx_1'=2,'ctx_2'=4,'ctx_3'=2,'head'=2] {'ctx_0','ctx_1',..., dimensions={0} | all-to-all | bytes 3145728 | tf_op jit(solution)/shard_map/all_to_all | solution.py:30
  165.2 8.6 %all_to_all.99 = bf16[2,32,16,1536]{3,2,1,0:T(8,128)(2,1)S(1)} all-to-all(bf16[2,32,16,1536]{3,2,1,0:T(8,128)(2,1)S(1)} %broadcast_in_dim.20), channel_id=1, replica_groups=mesh['ctx_0'=4,'ctx_1'=2,'ctx_2'=4,'ctx_3'=2,'head'=2] {'ctx_3'}, dimensions={0} | all-to-all | bytes 6291456 | tf_op jit(solution)/shard_map/all_to_all | solution.py:30
  176.8 2.2 convolution_bitcast_fusion
  179.0 2.3 convolution_bitcast_fusion.1
  181.3 2.3 fusion.22
  183.6 1.9 copy.86
  185.5 1.5 copy.87
  187.0 4.0 all-to-all-start.9
  191.0 2.9 copy.88
  193.9 3.4 copy.89
  197.3 1.6 copy.113
  198.9 4.8 %all-to-all-start.11 = ((f32[2,32,16,512]{3,2,1,0:T(8,128)}), f32[2,32,16,512]{3,2,1,0:T(8,128)}, u32[]{:S(2)}, u32[]{:S(2)}) async-start(f32[2,32,16,512]{3,2,1,0:T(8,128)} %copy.89), calls=%async_computation.11 | async-start | bytes 4194304 | tf_op jit(solution)/shard_map/all_to_all | solution.py:18
  205.0 1.4 all-to-all-done.11
  206.4 6.6 %all_to_all.100 = f32[2,32,16,512]{3,2,1,0:T(8,128)S(1)} all-to-all(f32[2,32,16,512]{3,2,1,0:T(8,128)} %bitcast.105), channel_id=1, replica_groups=mesh['ctx_0'=4,'ctx_1'=2,'ctx_2'=4,'ctx_3'=2,'head'=2] {'ctx_3'}, dimensions={0} | all-to-all | bytes 4194304 | tf_op jit(solution)/shard_map/all_to_all | solution.py:18
  213.0 4.1 all-to-all-start.10
  217.1 2.9 reduce_sum.235
  220.0 12.7 %all-to-all-done.10 = f32[32,16,512]{2,1,0:T(8,128)S(1)} async-done(((f32[32,16,512]{2,1,0:T(8,128)}), f32[32,16,512]{2,1,0:T(8,128)S(1)}, u32[]{:S(2)}, u32[]{:S(2)}) %all-to-all-start.10) | async-done | bytes 1048608 | tf_op jit(solution)/shard_map/all_to_all | solution.py:25
  232.7 6.0 %all-to-all-start.12 = ((f32[32,16,512]{2,1,0:T(8,128)}), f32[32,16,512]{2,1,0:T(8,128)}, u32[]{:S(2)}, u32[]{:S(2)}) async-start(f32[32,16,512]{2,1,0:T(8,128)} %reduce_sum.235), calls=%async_computation.12 | async-start | bytes 2097152 | tf_op jit(solution)/shard_map/all_to_all | solution.py:25
  239.9 13.8 %all-to-all-done.12 = f32[32,16,512]{2,1,0:T(8,128)} async-done(((f32[32,16,512]{2,1,0:T(8,128)}), f32[32,16,512]{2,1,0:T(8,128)}, u32[]{:S(2)}, u32[]{:S(2)}) %all-to-all-start.12) | async-done | bytes 1048608 | tf_op jit(solution)/shard_map/all_to_all | solution.py:25
  253.7 6.4 %all-to-all-start.14 = ((f32[32,16,512]{2,1,0:T(8,128)}), f32[32,16,512]{2,1,0:T(8,128)S(1)}, u32[]{:S(2)}, u32[]{:S(2)}) async-start(f32[32,16,512]{2,1,0:T(8,128)} %reduce_sum.238), calls=%async_computation.14 | async-start | bytes 2097152 | tf_op jit(solution)/shard_map/all_to_all | solution.py:25
  260.2 1.3 reduce_sum.236
  262.8 12.3 %all-to-all-done.14 = f32[32,16,512]{2,1,0:T(8,128)S(1)} async-done(((f32[32,16,512]{2,1,0:T(8,128)}), f32[32,16,512]{2,1,0:T(8,128)S(1)}, u32[]{:S(2)}, u32[]{:S(2)}) %all-to-all-start.14) | async-done | bytes 1048608 | tf_op jit(solution)/shard_map/all_to_all | solution.py:25
  275.7 2.0 pad_maximum_fusion.3
  277.7 15.9 %all_to_all.101 = f32[64,1,3]{2,1,0:T(1,128)S(1)} all-to-all(f32[64,1,3]{2,1,0:T(1,128)S(1)} %broadcast_in_dim.21), channel_id=1, replica_groups=mesh['ctx_0'=4,'ctx_1'=2,'ctx_2'=4,'ctx_3'=2,'head'=2] {'ctx_0','ctx_1',..., dimensions={0} | all-to-all | bytes 1536 | tf_op jit(solution)/shard_map/all_to_all | solution.py:30
  296.6 24.2 %all_to_all.102 = bf16[32,16,1536]{2,1,0:T(8,128)(2,1)S(1)} all-to-all(bf16[32,16,1536]{2,1,0:T(8,128)(2,1)S(1)} %broadcast_in_dim.22), channel_id=1, replica_groups=mesh['ctx_0'=4,'ctx_1'=2,'ctx_2'=4,'ctx_3'=2,'head'=2] {'ctx_0','ctx_1',..., dimensions={0} | all-to-all | bytes 3145728 | tf_op jit(solution)/shard_map/all_to_all | solution.py:30
  321.2 8.7 %all_to_all.103 = bf16[2,32,16,1536]{3,2,1,0:T(8,128)(2,1)S(1)} all-to-all(bf16[2,32,16,1536]{3,2,1,0:T(8,128)(2,1)S(1)} %broadcast_in_dim.23), channel_id=1, replica_groups=mesh['ctx_0'=4,'ctx_1'=2,'ctx_2'=4,'ctx_3'=2,'head'=2] {'ctx_3'}, dimensions={0} | all-to-all | bytes 6291456 | tf_op jit(solution)/shard_map/all_to_all | solution.py:30
  330.2 1.7 copy-done.5
  332.6 2.9 convolution_convert_fusion.1
  335.4 9.8 %convolution_convert_fusion = bf16[512,5120]{1,0:T(8,128)(2,1)S(1)} fusion(bf16[512,1024]{1,0:T(8,128)(2,1)S(1)} %convolution_convert_fusion.1, bf16[1024,5120]{1,0:T(8,128)(2,1)} %param.15), kind=kOutput, calls=%fused_computation | convolution fusion | flops 5371330560 | bytes 16777216 | tf_op jit(solution)/shard_map/dot_general | solution.py:142
  345.6 64.0 %all_to_all.104 = bf16[2,512,2560]{2,1,0:T(8,128)(2,1)} all-to-all(bf16[2,512,2560]{2,1,0:T(8,128)(2,1)S(1)} %bitcast.104), channel_id=1, replica_groups=mesh['ctx_0'=4,'ctx_1'=2,'ctx_2'=4,'ctx_3'=2,'head'=2] {'head'}, dimensions={0} | all-to-all | bytes 10485760 | tf_op jit(solution)/shard_map/all_to_all | solution.py:68
  409.6 5.7 %reduce_sum.242 = bf16[512,2560]{1,0:T(8,128)(2,1)} reduce(bf16[2,512,2560]{2,1,0:T(8,128)(2,1)} %all_to_all.104, bf16[]{:T(256)} %constant.43.clone.1), dimensions={0}, to_apply=%region_23.24 | reduce | flops 1310720 | bytes 7864322 | tf_op jit(solution)/shard_map/reduce_sum | solution.py:69
  (73 shorter events, 23.9 us)
Async XLA Ops:
  0.0 1.2 copy-start
  0.0 3.2 copy-start.3
  3.2 3.1 copy-start.12
  3.2 1.6 copy-start.7
  3.2 2.3 copy-start.8
  3.2 2.3 copy-start.11
  3.9 2.3 copy-start.14
  6.3 1.0 copy-start.15
  13.1 17.9 %all-to-all-start = ((f32[2,32,16,512]{3,2,1,0:T(8,128)}), f32[2,32,16,512]{3,2,1,0:T(8,128)S(1)}, u32[]{:S(2)}, u32[]{:S(2)}) async-start(f32[2,32,16,512]{3,2,1,0:T(8,128)} %copy.77), calls=%async_computation | async-start | bytes 4194304 | tf_op jit(solution)/shard_map/all_to_all | solution.py:18
  18.2 2.9 copy-start.13
  18.2 2.9 copy-start.16
  31.0 7.5 %all-to-all-start.4 = ((f32[2,32,16,512]{3,2,1,0:T(8,128)}), f32[2,32,16,512]{3,2,1,0:T(8,128)}, u32[]{:S(2)}, u32[]{:S(2)}) async-start(f32[2,32,16,512]{3,2,1,0:T(8,128)} %bitcast.106), calls=%async_computation.4 | async-start | bytes 4194304 | tf_op jit(solution)/shard_map/all_to_all | solution.py:18
  45.1 24.8 %all-to-all-start.1 = ((f32[32,16,512]{2,1,0:T(8,128)}), f32[32,16,512]{2,1,0:T(8,128)}, u32[]{:S(2)}, u32[]{:S(2)}) async-start(f32[32,16,512]{2,1,0:T(8,128)} %reduce_sum.219), calls=%async_computation.1 | async-start | bytes 2097152 | tf_op jit(solution)/shard_map/all_to_all | solution.py:25
  69.9 21.1 %all-to-all-start.5 = ((f32[32,16,512]{2,1,0:T(8,128)}), f32[32,16,512]{2,1,0:T(8,128)}, u32[]{:S(2)}, u32[]{:S(2)}) async-start(f32[32,16,512]{2,1,0:T(8,128)} %reduce_sum.226), calls=%async_computation.5 | async-start | bytes 2097152 | tf_op jit(solution)/shard_map/all_to_all | solution.py:25
  77.2 20.3 %copy-start.2 = (bf16[1,1024,512]{2,1,0:T(8,128)(2,1)S(1)}, bf16[1,1024,512]{2,1,0:T(8,128)(2,1)}, u32[]{:S(2)}) copy-start(bf16[1,1024,512]{2,1,0:T(8,128)(2,1)} %param.12) | copy-start | bytes 3145732
  90.9 21.9 %all-to-all-start.3 = ((f32[32,16,512]{2,1,0:T(8,128)}), f32[32,16,512]{2,1,0:T(8,128)}, u32[]{:S(2)}, u32[]{:S(2)}) async-start(f32[32,16,512]{2,1,0:T(8,128)} %reduce_sum.223), calls=%async_computation.3 | async-start | bytes 2097152 | tf_op jit(solution)/shard_map/all_to_all | solution.py:25
  101.7 4.1 copy-start.4
  118.1 17.7 %all-to-all-start.6 = ((f32[64,1,3]{2,1,0:T(1,128)}), f32[64,1,3]{2,1,0:T(1,128)S(1)}, u32[]{:S(2)}, u32[]{:S(2)}) async-start(f32[64,1,3]{2,1,0:T(1,128)} %broadcast_in_dim.18), calls=%async_computation.6 | async-start | bytes 65536 | tf_op jit(solution)/shard_map/all_to_all | solution.py:30
  174.8 1.2 copy-start.9
  187.0 12.0 %all-to-all-start.9 = ((f32[2,32,16,512]{3,2,1,0:T(8,128)}), f32[2,32,16,512]{3,2,1,0:T(8,128)S(1)}, u32[]{:S(2)}, u32[]{:S(2)}) async-start(f32[2,32,16,512]{3,2,1,0:T(8,128)} %copy.87), calls=%async_computation.9 | async-start | bytes 4194304 | tf_op jit(solution)/shard_map/all_to_all | solution.py:18
  193.9 3.4 copy-start.6
  198.9 7.5 %all-to-all-start.11 = ((f32[2,32,16,512]{3,2,1,0:T(8,128)}), f32[2,32,16,512]{3,2,1,0:T(8,128)}, u32[]{:S(2)}, u32[]{:S(2)}) async-start(f32[2,32,16,512]{3,2,1,0:T(8,128)} %copy.89), calls=%async_computation.11 | async-start | bytes 4194304 | tf_op jit(solution)/shard_map/all_to_all | solution.py:18
  213.0 19.7 %all-to-all-start.10 = ((f32[32,16,512]{2,1,0:T(8,128)}), f32[32,16,512]{2,1,0:T(8,128)S(1)}, u32[]{:S(2)}, u32[]{:S(2)}) async-start(f32[32,16,512]{2,1,0:T(8,128)} %reduce_sum.232), calls=%async_computation.10 | async-start | bytes 2097152 | tf_op jit(solution)/shard_map/all_to_all | solution.py:25
  232.7 21.1 %all-to-all-start.12 = ((f32[32,16,512]{2,1,0:T(8,128)}), f32[32,16,512]{2,1,0:T(8,128)}, u32[]{:S(2)}, u32[]{:S(2)}) async-start(f32[32,16,512]{2,1,0:T(8,128)} %reduce_sum.235), calls=%async_computation.12 | async-start | bytes 2097152 | tf_op jit(solution)/shard_map/all_to_all | solution.py:25
  253.7 21.3 %all-to-all-start.14 = ((f32[32,16,512]{2,1,0:T(8,128)}), f32[32,16,512]{2,1,0:T(8,128)S(1)}, u32[]{:S(2)}, u32[]{:S(2)}) async-start(f32[32,16,512]{2,1,0:T(8,128)} %reduce_sum.238), calls=%async_computation.14 | async-start | bytes 2097152 | tf_op jit(solution)/shard_map/all_to_all | solution.py:25
  329.9 2.0 copy-start.10
  330.2 1.7 copy-start.5
  345.6 69.7 %copy-start.1 = (bf16[512,1024]{1,0:T(8,128)(2,1)S(1)}, bf16[512,1024]{1,0:T(8,128)(2,1)}, u32[]{:S(2)}) copy-start(bf16[512,1024]{1,0:T(8,128)(2,1)} %param.9) | copy-start | bytes 3145732
where the time goes:
time: 418 us; the launch traced here: 415 us
  blocking collectives  159 us (38%)
  waiting for transfers between devices  72.4 us (17%)
  starting transfers between devices  67 us (16%)
  other arithmetic  43.4 us (10%)
  local copies, waits for them, and re-layouts  33.9 us (8%)
  matrix products  33.1 us (8%)
  between operations  6.5 us (2%)
    all_to_all x5, blocking collectives, from_everyone(): return lax.all_to_all(copies, axis, split_axis=0, concat_axis=0, tiled=True)  81.8 us
    all_to_all x6, waiting for transfers between devices, summed_rows(): return jnp.sum(lax.all_to_all(own, far, 0, 0, tiled=True), axis=0)  65.2 us
    all_to_all x1, blocking collectives, summed_on_arrival_2(): pieces = lax.all_to_all(split_up(x, dim, peers), axis, 0, 0, tiled=True)  64 us
    all_to_all x6, starting transfers between devices, summed_rows(): return jnp.sum(lax.all_to_all(own, far, 0, 0, tiled=True), axis=0)  38.2 us
    all_to_all x4, starting transfers between devices, summed_on_arrival(): lax.all_to_all(pieces, axis, split_axis=0, concat_axis=0, tiled=True)  18.9 us
    dot_general x6, matrix products, tdot(): lax.dot_general(left, right, (((0,), (0,)), ((), ())), preferred_element_...  14.2 us
    all_to_all x2, blocking collectives, summed_on_arrival(): lax.all_to_all(pieces, axis, split_axis=0, concat_axis=0, tiled=True)  13.2 us
    reduce_sum x6, other arithmetic, summed_on_arrival(): return arrived.sum(axis=0)  10.9 us
  transfers between devices with their start and end apart: 11, of which 8 were waited for; matrix products, arithmetic and copies ran while one was open for 12% of the time, Pallas kernels for 0%

commit v1 on v0

v1 whole, which is shorter than its diff:
```python
import functools

import jax
import jax.numpy as jnp
from jax import lax
from jax.experimental import pallas as pl
from jax.experimental.pallas import tpu as pltpu
from jax.sharding import Mesh
from jax.sharding import PartitionSpec as P

STEPS = 2
CTX = ("z", "xl", "y", "c")
CHIPS = ("z", "xl", "y")
SWAP = [(0, 1), (1, 0)]
ACROSS = [(0, 3), (3, 0), (1, 2), (2, 1)]
BF = jnp.bfloat16
F32 = jnp.float32
NT = (((1,), (1,)), ((), ()))
TN = (((0,), (0,)), ((), ()))
VMEM = pl.BlockSpec(memory_space=pltpu.VMEM)
SMEM = pl.BlockSpec(memory_space=pltpu.SMEM)
LIMIT = 48 * 1024 * 1024


def dot(x, y):
    return jnp.dot(x, y, preferred_element_type=F32)


def nt(x, y):
    return lax.dot_general(x, y, NT, preferred_element_type=F32)


def tn(x, y):
    return lax.dot_general(x, y, TN, preferred_element_type=F32)


def call(kernel, outs, n_in, flops, nbytes, smem=0, scratch=()):
    return pl.pallas_call(
        kernel,
        out_shape=outs,
        in_specs=[SMEM] * smem + [VMEM] * (n_in - smem),
        out_specs=jax.tree.map(lambda _: VMEM, outs),
        scratch_shapes=list(scratch),
        compiler_params=pltpu.CompilerParams(vmem_limit_bytes=LIMIT),
        cost_estimate=pl.CostEstimate(flops=flops, bytes_accessed=nbytes, transcendentals=0),
    )


def shape(dims, dtype=BF):
    return jax.ShapeDtypeStruct(dims, dtype)


def prepare_kernel(core, up, gate, down, w0, norm):
    width, hid = up.shape
    half = hid // 2
    total = []
    for w in (up, gate, down):
        full = w[...].astype(F32)
        total.append(jnp.sum(full * full))
    for i, value in enumerate(total):
        norm[i : i + 1, :] = jnp.full((1, 128), value, F32)
    norm[3:8, :] = jnp.zeros((5, 128), F32)
    for c in range(2):

        @pl.when(core[0] == c)
        def _():
            w0[0:half, :] = up[:, c * half : (c + 1) * half].T
            w0[half : 2 * half, :] = gate[:, c * half : (c + 1) * half].T
            w0[2 * half :, :] = down[c * half : (c + 1) * half, :]


def act_grads(wb, keys, targets, half):
    act = nt(wb[0:half, :], keys)
    lin = nt(wb[half : 2 * half, :], keys)
    err = nt(wb[2 * half :, :], targets)
    sig = jax.nn.sigmoid(act)
    silu = act * sig
    hidden = (silu * lin).astype(BF)
    pgrad = (err * lin * sig * (1.0 + act * (1.0 - sig))).astype(BF)
    qgrad = (err * silu).astype(BF)
    return pgrad, qgrad, hidden


def grads_into(out, wb, k_own, k_oth, u_own, u_oth):
    half = wb.shape[0] // 3
    width = wb.shape[1]
    cols = width // 2
    own = act_grads(wb, k_own[...], u_own[...], half)
    oth = act_grads(wb, k_oth[...], u_oth[...], half)
    for i in range(3):
        x, y = (k_own, k_oth) if i < 2 else (u_own, u_oth)
        for j in range(2):
            at = slice(j * cols, (j + 1) * cols)
            g = dot(own[i], x[:, at]) + dot(oth[i], y[:, at])
            out[j, i * half : (i + 1) * half, :] = g.astype(BF)


def first_kernel(w0, k_own, k_oth, u_own, u_oth, out):
    grads_into(out, w0, k_own, k_oth, u_own, u_oth)


def update_kernel(w, gathered, moved, squares):
    third = w.shape[0] // 3
    cols = w.shape[1] // 2
    for i in range(3):
        rows = slice(i * third, (i + 1) * third)
        total = jnp.zeros((), F32)
        for j in range(2):
            at = slice(j * cols, (j + 1) * cols)
            m = w[rows, at].astype(F32) + gathered[j, rows, :].astype(F32)
            moved[rows, at] = m
            total = total + jnp.sum(m * m)
        squares[i : i + 1, :] = jnp.full((1, 128), total, F32)
    squares[3:8, :] = jnp.zeros((5, 128), F32)


def scaled(i, moved, norm, own, oth):
    third = moved.shape[0] // 3
    size = jnp.sqrt(norm[i : i + 1, 0:1])
    total = own[i : i + 1, 0:1] + oth[i : i + 1, 0:1]
    return moved[i * third : (i + 1) * third, :] * size / jnp.sqrt(total + 1e-06)


def next_kernel(moved, norm, sq_own, sq_oth, k_own, k_oth, u_own, u_oth, out, w, wb):
    third = moved.shape[0] // 3
    for i in range(3):
        new = scaled(i, moved, norm, sq_own, sq_oth)
        w[i * third : (i + 1) * third, :] = new
        wb[i * third : (i + 1) * third, :] = new.astype(BF)
    grads_into(out, wb, k_own, k_oth, u_own, u_oth)


def hidden_kernel(moved, norm, sq_own, sq_oth, q_own, q_oth, w2, hq_own, hq_oth):
    b1 = scaled(0, moved, norm, sq_own, sq_oth).astype(BF)
    b3 = scaled(1, moved, norm, sq_own, sq_oth).astype(BF)
    w2[...] = scaled(2, moved, norm, sq_own, sq_oth).astype(BF)
    for q, out in ((q_oth, hq_oth), (q_own, hq_own)):
        act = nt(b1, q[...])
        lin = nt(b3, q[...])
        out[...] = (jax.nn.silu(act) * lin).astype(BF)


def piece_kernel(hq_own, hq_got, w2_own, w2_got, o):
    o[...] = (tn(hq_own[...], w2_own[...]) + tn(hq_got[...], w2_got[...])).astype(BF)


def spread_kernel(arrived, out):
    total = arrived[0].astype(F32)
    for i in range(1, arrived.shape[0]):
        total = total + arrived[i].astype(F32)
    rounded = total.astype(BF)
    for i in range(arrived.shape[0]):
        out[i] = rounded


def out_kernel(place, o, w_own, o_first, o_second, w_first, w_second, out):
    total = dot(o[...], w_own[...]) + dot(o_first[...], w_first[...])
    out[...] = (total + dot(o_second[...], w_second[...])).astype(BF)


def last_product(place, o, w_out, o_got, w_first, w_second):
    tokens, width = o.shape
    n = w_first.shape[1]
    tile = 512
    steps = n // tile
    return pl.pallas_call(
        out_kernel,
        out_shape=shape((tokens, n)),
        grid_spec=pltpu.PrefetchScalarGridSpec(
            num_scalar_prefetch=1,
            grid=(steps,),
            in_specs=[
                pl.BlockSpec((tokens, width), lambda i, s: (0, 0)),
                pl.BlockSpec((width, tile), lambda i, s: (0, s[0] * steps + i)),
                pl.BlockSpec((tokens, width // 2), lambda i, s: (0, s[1])),
                pl.BlockSpec((tokens, width // 2), lambda i, s: (0, 1 - s[1])),
                pl.BlockSpec((width // 2, tile), lambda i, s: (0, i)),
                pl.BlockSpec((width // 2, tile), lambda i, s: (0, i)),
            ],
            out_specs=pl.BlockSpec((tokens, tile), lambda i, s: (0, i)),
        ),
        compiler_params=pltpu.CompilerParams(vmem_limit_bytes=LIMIT),
        cost_estimate=pl.CostEstimate(
            flops=4 * tokens * width * n, bytes_accessed=16 << 20, transcendentals=0
        ),
    )(place, o, w_out, o_got, o_got, w_first, w_second)


def all_reduced(grads):
    peers = lax.axis_size(CHIPS)
    pieces = grads.reshape(peers, -1, grads.shape[2])
    arrived = lax.all_to_all(pieces, CHIPS, 0, 0, tiled=True)
    copies = call(spread_kernel, shape(pieces.shape), 1, pieces.size, 4 * pieces.size)(arrived)
    gathered = lax.all_to_all(copies, CHIPS, 0, 0, tiled=True)
    return gathered.reshape(grads.shape)


def swap(x):
    return lax.ppermute(x, "c", SWAP)


def shards(queries, keys, values, rates, w_up, w_gate, w_down, w_out):
    width, hid = w_up.shape[1:]
    tokens = keys.shape[0]
    half, third = hid // 2, 3 * hid // 2
    core, head = lax.axis_index("c"), lax.axis_index("h")
    n = w_out.shape[1] // 2

    k_oth = swap(keys)
    targets = (rates * values.astype(F32)).astype(BF)
    u_oth = swap(targets)
    kus = (keys, k_oth, targets, u_oth)

    place = jnp.stack([head, core]).astype(jnp.int32)
    sent = lax.dynamic_slice(w_out, (core * (width // 2), (1 - head) * n), (width // 2, n))
    w_first = lax.ppermute(sent, ("xl", "h"), ACROSS)
    w_second = swap(w_first)
    q_oth = swap(queries)

    w0, norm = call(
        prepare_kernel, (shape((third, width)), shape((8, 128), F32)), 4, 1 << 21, 5 << 20, smem=1
    )(core.reshape(1).astype(jnp.int32), w_up[0], w_gate[0], w_down[0])
    flops = 12 * 2 * tokens * width * half
    gshape = shape((2, third, width // 2))
    grads = call(first_kernel, gshape, 5, flops, 8 << 20)(w0, *kus)
    w = w0
    for step in range(STEPS):
        gathered = all_reduced(grads)
        moved, squares = call(
            update_kernel, (shape((third, width), F32), shape((8, 128), F32)), 2, 1 << 22, 8 << 20
        )(w, gathered)
        state = (moved, norm, squares, swap(squares))
        if step < STEPS - 1:
            grads, w = call(
                next_kernel,
                (gshape, shape((third, width), F32)),
                8,
                flops,
                14 << 20,
                scratch=[pltpu.VMEM((third, width), BF)],
            )(*state, *kus)
    w2, hq_own, hq_oth = call(
        hidden_kernel,
        (shape((half, width)), shape((half, tokens)), shape((half, tokens))),
        6,
        flops // 3,
        8 << 20,
    )(*state, queries, q_oth)
    o = call(piece_kernel, shape((tokens, width)), 4, 2 * tokens * hid * width, 4 << 20)(
        hq_own, swap(hq_oth), w2, swap(w2)
    )
    o_got = lax.ppermute(o, "h", SWAP)
    return last_product(place, o, w_out, o_got, w_first, w_second)


def solution(mesh):
    finer = Mesh(
        mesh.devices.reshape(4, 2, 4, 2, mesh.shape["head"]),
        ("z", "xl", "y", "c", "h"),
    )
    return jax.shard_map(
        shards,
        mesh=finer,
        in_specs=(
            P(CTX, "h"),
            P(CTX, "h"),
            P(CTX, "h"),
            P(CTX, "h"),
            P("h", None, None),
            P("h", None, None),
            P("h", None, None),
            P("h", None),
        ),
        out_specs=P(CTX, "h"),
        check_vma=False,
    )
```

time: 418 us -> 192 us (0.46)
  blocking collectives: 159 us -> 57.3 us
  starting transfers between devices: 67 us -> 25.1 us
  other arithmetic: 43.4 us -> 1.68 us
  Pallas kernels: 0 us -> 37.4 us
  matrix products: 33.1 us -> 0 us
  local copies, waits for them, and re-layouts: 33.9 us -> 7.61 us
  waiting for transfers between devices: 72.4 us -> 61.8 us
  between operations: 6.5 us -> 0.14 us
    all_to_all x8 -> x2, blocking collectives: 159 us -> 57.3 us  [all_reduced(): arrived = lax.all_to_all(pieces, CHIPS, 0, 0, tiled=True)]
    all_to_all x11 -> x2, starting transfers between devices: 67 us -> 11.7 us  [all_reduced(): gathered = lax.all_to_all(copies, CHIPS, 0, 0, tiled=True)]
    all_to_all x11 -> x2, waiting for transfers between devices: 72.4 us -> 34.5 us  [all_reduced(): gathered = lax.all_to_all(copies, CHIPS, 0, 0, tiled=True)]
    pallas_call x0 -> x10, Pallas kernels: none -> 37.4 us  [the longest x1 10.2 us: last_product(): pl.pallas_call(out_kernel, out_shape=shape((tokens, n)), grid_spec=pltpu....]
    dot_general x15 -> x0, matrix products: 33.1 us -> none  [the longest x6 14.2 us: tdot(): lax.dot_general(left, right, (((0,), (0,)), ((), ())), preferred_element_...]
    reduce_sum x24 -> x0, other arithmetic: 33 us -> none  [the longest x6 10.9 us: summed_on_arrival(): return arrived.sum(axis=0)]
    ppermute x0 -> x10, waiting for transfers between devices: none -> 27.3 us  [the longest x1 23.4 us: shards(): o_got = lax.ppermute(o, 'h', SWAP)]
    ppermute x0 -> x10, starting transfers between devices: none -> 13.4 us  [the longest x8 8.4 us: swap(): return lax.ppermute(x, 'c', SWAP)]
  transfers between devices with their start and end apart: 11 -> 12, of which waited for: 8 -> 7; matrix products, arithmetic and copies ran while one was open for 12% -> 2% of each run, Pallas kernels for 0% -> 10%
where the time goes in v1:
time: 192 us; the launch traced here: 191 us
  waiting for transfers between devices  61.8 us (32%)
  blocking collectives  57.3 us (30%)
  Pallas kernels  37.4 us (19%)
  starting transfers between devices  25.1 us (13%)
  local copies, waits for them, and re-layouts  7.61 us (4%)
    all_to_all x2, blocking collectives, all_reduced(): arrived = lax.all_to_all(pieces, CHIPS, 0, 0, tiled=True)  57.3 us
    all_to_all x2, waiting for transfers between devices, all_reduced(): gathered = lax.all_to_all(copies, CHIPS, 0, 0, tiled=True)  34.5 us
    ppermute x1, waiting for transfers between devices, shards(): o_got = lax.ppermute(o, 'h', SWAP)  23.4 us
    all_to_all x2, starting transfers between devices, all_reduced(): gathered = lax.all_to_all(copies, CHIPS, 0, 0, tiled=True)  11.7 us
    pallas_call x1, Pallas kernels, last_product(): pl.pallas_call(out_kernel, out_shape=shape((tokens, n)), grid_spec=pltpu....  10.2 us
    ppermute x8, starting transfers between devices, swap(): return lax.ppermute(x, 'c', SWAP)  8.4 us
    pallas_call x1, Pallas kernels, shards(): call(next_kernel, (gshape, shape((third, width), F32)), 8, flops, 14 << 2...  7.87 us
    pallas_call x1, Pallas kernels, shards(): grads = call(first_kernel, gshape, 5, flops, 8 << 20)(w0, *kus)  5.78 us
  transfers between devices with their start and end apart: 12, of which 7 were waited for; matrix products, arithmetic and copies ran while one was open for 2% of the time, Pallas kernels for 10%

profile of v1, /device:TPU:1, one launch (start us, length us, event | category | flops | bytes accessed | tf_op | source)
XLA Modules:
  0.0 191.0 jit_solution(3998668945462531393)
XLA Ops:
  0.0 0.0 copy-start.5
  0.0 0.0 copy-start.6
  0.0 1.6 multiply_convert_fusion.u_own
  1.6 0.0 copy-start.3
  1.6 1.5 collective-permute-start.1
  3.1 0.1 collective-permute-start
  3.2 0.0 copy-done.5
  3.2 0.0 copy-done.6
  3.2 0.0 copy-start.7
  3.2 1.2 copy-done.7
  4.5 0.0 copy-start.9
  4.5 1.2 shard_map.82
  5.6 0.0 copy-start.1
  5.7 1.1 copy-done.1
  6.8 0.0 collective-permute-done.1.u_oth
  6.8 0.5 collective-permute-done.k_oth
  7.3 0.0 copy-done.9
  7.3 5.8 %shard_map.83 = bf16[2,768,512]{2,1,0:T(8,128)(2,1)S(1)} custom-call(bf16[768,1024]{1,0:T(8,128)(2,1)} %copy-done.1, bf16[512,1024]{1,0:T(8,128)(2,1)S(1)} %copy-done.9, bf16[512,1024]{1,0:T(8,128)(2,1)} %collective-permute-done.k_oth, bf16[512,1024]{1,0:T(8,128)(2,1)S(1)} %multiply_convert_fusion.u_own, bf16[512,1024]{1,0:T(8,128)(2,1)} %collective-permute-done.1.u_oth), custom_call_target="tpu_custom_call" | custom-call | flops 3221225472 | bytes 8388608 | tf_op jit(solution)/shard_map/pallas_call | solution.py:225
  13.1 0.0 copy-done.3
  13.1 30.3 %all_to_all.20.arrived = bf16[32,48,512]{2,1,0:T(8,128)(2,1)S(1)} all-to-all(bf16[32,48,512]{2,1,0:T(8,128)(2,1)S(1)} %bitcast.13), channel_id=1, replica_groups=mesh['z'=4,'xl'=2,'y'=4,'c'=2,'h'=2] {'z','xl','y'}, dimensions={0} | all-to-all | bytes 3145728 | tf_op jit(solution)/shard_map/all_to_all | solution.py:192
  43.3 1.5 shard_map.84
  44.9 5.7 %all-to-all-start.1 = ((bf16[32,48,512]{2,1,0:T(8,128)(2,1)}), bf16[32,48,512]{2,1,0:T(8,128)(2,1)S(1)}, u32[]{:S(2)}, u32[]{:S(2)}) async-start(bf16[32,48,512]{2,1,0:T(8,128)(2,1)} %shard_map.84), calls=%async_computation.1 | async-start | bytes 3145728 | tf_op jit(solution)/shard_map/all_to_all | solution.py:194
  50.6 0.0 copy-start.2
  50.6 3.5 %dynamic_slice.3 = bf16[512,2560]{1,0:T(8,128)(2,1)} dynamic-slice(bf16[1024,5120]{1,0:T(8,128)(2,1)} %w_own.1, s32[]{:T(128)S(6)} %select_n.6, s32[]{:T(128)S(6)} %select_n.7), dynamic_slice_sizes={512,2560} | dynamic-slice | bytes 5242884 | tf_op jit(solution)/shard_map/dynamic_slice | solution.py:215
  54.1 2.5 %collective-permute-start.8 = (bf16[512,2560]{1,0:T(8,128)(2,1)}, bf16[512,2560]{1,0:T(8,128)(2,1)}, u32[]{:S(2)}, u32[]{:S(2)}) collective-permute-start(bf16[512,2560]{1,0:T(8,128)(2,1)} %dynamic_slice.3), channel_id=1, source_target_pairs={{0,17},{17,0},{1,16},{16,1},{2,19},{19,2},{3,18},{18,3},{4,21},{21... | collective-permute-start | bytes 7864328 | tf_op jit(solution)/shard_map/ppermute | solution.py:216
  56.6 14.9 %all-to-all-done.1 = bf16[32,48,512]{2,1,0:T(8,128)(2,1)S(1)} async-done(((bf16[32,48,512]{2,1,0:T(8,128)(2,1)}), bf16[32,48,512]{2,1,0:T(8,128)(2,1)S(1)}, u32[]{:S(2)}, u32[]{:S(2)}) %all-to-all-start.1) | async-done | bytes 1572896 | tf_op jit(solution)/shard_map/all_to_all | solution.py:194
  71.5 0.0 copy-start.4
  71.5 0.0 copy-start.10
  71.5 0.0 copy-done.2
  71.5 2.3 %shard_map.85 = (f32[768,1024]{1,0:T(8,128)}, f32[8,128]{1,0:T(8,128)S(1)}) custom-call(bf16[768,1024]{1,0:T(8,128)(2,1)S(1)} %copy-done.2, bf16[2,768,512]{2,1,0:T(8,128)(2,1)S(1)} %bitcast.10), custom_call_target="tpu_custom_call" | custom-call | flops 4194304 | bytes 8388608 | tf_op jit(solution)/shard_map/pallas_call | solution.py:229
  73.8 2.4 %collective-permute-start.2 = (f32[8,128]{1,0:T(8,128)S(1)}, f32[8,128]{1,0:T(8,128)S(1)}, u32[]{:S(2)}, u32[]{:S(2)}) collective-permute-start(f32[8,128]{1,0:T(8,128)S(1)} %get-tuple-element.19.sq_own), channel_id=1, source_target_pairs={{0,2},{2,0},{1,3},{3,1},{4,6},{6,4},{5,7},{7,5},{8,10},{10,8},{9,1... | collective-permute-start | bytes 12296 | tf_op jit(solution)/shard_map/ppermute | solution.py:199
  76.3 0.8 collective-permute-done.2.sq_oth
  77.1 0.0 copy-done.4
  77.1 0.0 copy-done.10
  77.1 7.9 %shard_map.86 = (bf16[2,768,512]{2,1,0:T(8,128)(2,1)S(1)}, f32[768,1024]{1,0:T(8,128)}) custom-call(f32[768,1024]{1,0:T(8,128)} %get-tuple-element.17.moved, f32[8,128]{1,0:T(8,128)S(1)} %get-tuple-element.18.norm, f32[8,128]{1,0:T(8,128)S(1)} %get-tuple-element.19.sq_own, f32[8,128]{1,0:T(8,128)S(1)} %collective-permute-done.2.sq_oth, ...), custom_call_target="tpu_custom_call" | custom-call | flops 3221225472 | bytes 14680064 | tf_op jit(solution)/shard_map/pallas_call | solution.py:234
  85.0 27.0 %all_to_all.21.arrived = bf16[32,48,512]{2,1,0:T(8,128)(2,1)S(1)} all-to-all(bf16[32,48,512]{2,1,0:T(8,128)(2,1)S(1)} %bitcast.12), channel_id=1, replica_groups=mesh['z'=4,'xl'=2,'y'=4,'c'=2,'h'=2] {'z','xl','y'}, dimensions={0} | all-to-all | bytes 3145728 | tf_op jit(solution)/shard_map/all_to_all | solution.py:192
  112.0 1.5 shard_map.87
  113.5 0.0 copy-start.8
  113.5 6.0 %all-to-all-start.3 = ((bf16[32,48,512]{2,1,0:T(8,128)(2,1)}), bf16[32,48,512]{2,1,0:T(8,128)(2,1)S(1)}, u32[]{:S(2)}, u32[]{:S(2)}) async-start(bf16[32,48,512]{2,1,0:T(8,128)(2,1)} %shard_map.87), calls=%async_computation.3 | async-start | bytes 3145728 | tf_op jit(solution)/shard_map/all_to_all | solution.py:194
  119.5 0.0 copy-done.8
  119.5 1.2 collective-permute-start.4
  120.7 0.0 collective-permute-done.8.w_first
  120.7 0.1 collective-permute-start.9
  120.8 19.6 %all-to-all-done.3 = bf16[32,48,512]{2,1,0:T(8,128)(2,1)S(1)} async-done(((bf16[32,48,512]{2,1,0:T(8,128)(2,1)}), bf16[32,48,512]{2,1,0:T(8,128)(2,1)S(1)}, u32[]{:S(2)}, u32[]{:S(2)}) %all-to-all-start.3) | async-done | bytes 1572896 | tf_op jit(solution)/shard_map/all_to_all | solution.py:194
  140.4 2.7 %shard_map.88 = (f32[768,1024]{1,0:T(8,128)S(1)}, f32[8,128]{1,0:T(8,128)S(1)}) custom-call(f32[768,1024]{1,0:T(8,128)} %get-tuple-element.20.w, bf16[2,768,512]{2,1,0:T(8,128)(2,1)S(1)} %bitcast.11), custom_call_target="tpu_custom_call" | custom-call | flops 4194304 | bytes 8388608 | tf_op jit(solution)/shard_map/pallas_call | solution.py:229
  143.1 0.0 copy-start
  143.1 1.7 copy-done
  144.8 2.5 %collective-permute-start.3 = (f32[8,128]{1,0:T(8,128)S(1)}, f32[8,128]{1,0:T(8,128)S(1)}, u32[]{:S(2)}, u32[]{:S(2)}) collective-permute-start(f32[8,128]{1,0:T(8,128)S(1)} %get-tuple-element.23.sq_own), channel_id=1, source_target_pairs={{0,2},{2,0},{1,3},{3,1},{4,6},{6,4},{5,7},{7,5},{8,10},{10,8},{9,1... | collective-permute-start | bytes 12296 | tf_op jit(solution)/shard_map/ppermute | solution.py:199
  147.3 0.0 collective-permute-done.4.q_oth
  147.3 0.8 collective-permute-done.3.sq_oth
  148.1 3.6 %shard_map.89 = (bf16[256,1024]{1,0:T(8,128)(2,1)S(1)}, bf16[256,512]{1,0:T(8,128)(2,1)S(1)}, bf16[256,512]{1,0:T(8,128)(2,1)S(1)}) custom-call(f32[768,1024]{1,0:T(8,128)} %copy-done, f32[8,128]{1,0:T(8,128)S(1)} %get-tuple-element.18.norm, f32[8,128]{1,0:T(8,128)S(1)} %get-tuple-element.23.sq_own, f32[8,128]{1,0:T(8,128)S(1)} %collective-permute-done.3.sq_oth, ...), custom_call_target="tpu_custom_call" | custom-call | flops 1073741824 | bytes 8388608 | tf_op jit(solution)/shard_map/pallas_call | solution.py:242
  151.7 0.4 collective-permute-start.6
  152.1 0.2 collective-permute-start.5
  152.3 1.8 collective-permute-done.5.hq_got
  154.1 0.0 collective-permute-done.6.w2_got
  154.1 0.7 shard_map.90.o
  154.8 2.5 %collective-permute-start.7 = (bf16[512,1024]{1,0:T(8,128)(2,1)S(1)}, bf16[512,1024]{1,0:T(8,128)(2,1)S(1)}, u32[]{:S(2)}, u32[]{:S(2)}) collective-permute-start(bf16[512,1024]{1,0:T(8,128)(2,1)S(1)} %shard_map.90.o), channel_id=1, source_target_pairs={{0,1},{1,0},{2,3},{3,2},{4,5},{5,4},{6,7},{7,6},{8,9},{9,8},{10,11... | collective-permute-start | bytes 3145736 | tf_op jit(solution)/shard_map/ppermute | solution.py:252
  157.3 0.1 pad_add_fusion.place
  157.4 0.0 collective-permute-done.9.w_second
  157.4 23.4 %collective-permute-done.7.o_first.o_second = bf16[512,1024]{1,0:T(8,128)(2,1)S(1)} collective-permute-done((bf16[512,1024]{1,0:T(8,128)(2,1)S(1)}, bf16[512,1024]{1,0:T(8,128)(2,1)S(1)}, u32[]{:S(2)}, u32[]{:S(2)}) %collective-permute-start.7) | collective-permute-done | bytes 1048608 | tf_op jit(solution)/shard_map/ppermute | solution.py:252
  180.8 10.2 %shard_map.91 = bf16[512,2560]{1,0:T(8,128)(2,1)} custom-call(s32[2]{0:T(128)S(1)} %pad_add_fusion.place, bf16[512,1024]{1,0:T(8,128)(2,1)S(1)} %shard_map.90.o, bf16[1024,5120]{1,0:T(8,128)(2,1)} %w_own.1, bf16[512,1024]{1,0:T(8,128)(2,1)S(1)} %collective-permute-done.7.o_first.o_second, bf16[512,1024]{1,0:T(8,128)(2,1)S(1)} %collective-permute-done.7.o_first.o_second, ...), custom_call_target="tpu_custom_call" | custom-call | flops 5368709120 | bytes 16777216 | tf_op jit(solution)/shard_map/pallas_call | solution.py:166
Async XLA Ops:
  0.0 3.2 %copy-start.5 = (bf16[1,1024,512]{2,1,0:T(8,128)(2,1)S(1)}, bf16[1,1024,512]{2,1,0:T(8,128)(2,1)}, u32[]{:S(2)}) copy-start(bf16[1,1024,512]{2,1,0:T(8,128)(2,1)} %param.12) | copy-start | bytes 3145732
  0.0 3.2 %copy-start.6 = (bf16[1,1024,512]{2,1,0:T(8,128)(2,1)S(1)}, bf16[1,1024,512]{2,1,0:T(8,128)(2,1)}, u32[]{:S(2)}) copy-start(bf16[1,1024,512]{2,1,0:T(8,128)(2,1)} %param.13) | copy-start | bytes 3145732
  1.6 11.4 %copy-start.3 = (bf16[512,1024]{1,0:T(8,128)(2,1)}, bf16[512,1024]{1,0:T(8,128)(2,1)S(1)}, u32[]{:S(2)}) copy-start(bf16[512,1024]{1,0:T(8,128)(2,1)S(1)} %multiply_convert_fusion.u_own) | copy-start | bytes 3145732
  1.6 5.2 %collective-permute-start.1 = (bf16[512,1024]{1,0:T(8,128)(2,1)S(1)}, bf16[512,1024]{1,0:T(8,128)(2,1)}, u32[]{:S(2)}, u32[]{:S(2)}) collective-permute-start(bf16[512,1024]{1,0:T(8,128)(2,1)S(1)} %multiply_convert_fusion.u_own), channel_id=1, source_target_pairs={{0,2},{2,0},{1,3},{3,1},{4,6},{6,4},{5,7},{7,5},{8,10},{10,8},{9,1... | collective-permute-start | bytes 3145736 | tf_op jit(solution)/shard_map/ppermute | solution.py:199
  3.1 4.1 %collective-permute-start = (bf16[512,1024]{1,0:T(8,128)(2,1)}, bf16[512,1024]{1,0:T(8,128)(2,1)}, u32[]{:S(2)}, u32[]{:S(2)}) collective-permute-start(bf16[512,1024]{1,0:T(8,128)(2,1)} %k_own.3), channel_id=1, source_target_pairs={{0,2},{2,0},{1,3},{3,1},{4,6},{6,4},{5,7},{7,5},{8,10},{10,8},{9,1... | collective-permute-start | bytes 3145736 | tf_op jit(solution)/shard_map/ppermute | solution.py:199
  3.2 1.2 copy-start.7
  4.5 2.8 %copy-start.9 = (bf16[512,1024]{1,0:T(8,128)(2,1)S(1)}, bf16[512,1024]{1,0:T(8,128)(2,1)}, u32[]{:S(2)}) copy-start(bf16[512,1024]{1,0:T(8,128)(2,1)} %k_own.3) | copy-start | bytes 3145732
  5.6 1.1 copy-start.1
  44.9 26.6 %all-to-all-start.1 = ((bf16[32,48,512]{2,1,0:T(8,128)(2,1)}), bf16[32,48,512]{2,1,0:T(8,128)(2,1)S(1)}, u32[]{:S(2)}, u32[]{:S(2)}) async-start(bf16[32,48,512]{2,1,0:T(8,128)(2,1)} %shard_map.84), calls=%async_computation.1 | async-start | bytes 3145728 | tf_op jit(solution)/shard_map/all_to_all | solution.py:194
  50.6 20.9 %copy-start.2 = (bf16[768,1024]{1,0:T(8,128)(2,1)S(1)}, bf16[768,1024]{1,0:T(8,128)(2,1)}, u32[]{:S(2)}) copy-start(bf16[768,1024]{1,0:T(8,128)(2,1)} %copy-done.1) | copy-start | bytes 4718596
  54.1 66.6 %collective-permute-start.8 = (bf16[512,2560]{1,0:T(8,128)(2,1)}, bf16[512,2560]{1,0:T(8,128)(2,1)}, u32[]{:S(2)}, u32[]{:S(2)}) collective-permute-start(bf16[512,2560]{1,0:T(8,128)(2,1)} %dynamic_slice.3), channel_id=1, source_target_pairs={{0,17},{17,0},{1,16},{16,1},{2,19},{19,2},{3,18},{18,3},{4,21},{21... | collective-permute-start | bytes 7864328 | tf_op jit(solution)/shard_map/ppermute | solution.py:216
  71.5 5.6 %copy-start.4 = (bf16[512,1024]{1,0:T(8,128)(2,1)S(1)}, bf16[512,1024]{1,0:T(8,128)(2,1)}, u32[]{:S(2)}) copy-start(bf16[512,1024]{1,0:T(8,128)(2,1)} %copy-done.3) | copy-start | bytes 3145732
  71.5 5.6 %copy-start.10 = (bf16[512,1024]{1,0:T(8,128)(2,1)S(1)}, bf16[512,1024]{1,0:T(8,128)(2,1)}, u32[]{:S(2)}) copy-start(bf16[512,1024]{1,0:T(8,128)(2,1)} %k_own.3) | copy-start | bytes 3145732
  73.8 3.3 %collective-permute-start.2 = (f32[8,128]{1,0:T(8,128)S(1)}, f32[8,128]{1,0:T(8,128)S(1)}, u32[]{:S(2)}, u32[]{:S(2)}) collective-permute-start(f32[8,128]{1,0:T(8,128)S(1)} %get-tuple-element.19.sq_own), channel_id=1, source_target_pairs={{0,2},{2,0},{1,3},{3,1},{4,6},{6,4},{5,7},{7,5},{8,10},{10,8},{9,1... | collective-permute-start | bytes 12296 | tf_op jit(solution)/shard_map/ppermute | solution.py:199
  113.5 6.0 %copy-start.8 = (bf16[512,1024]{1,0:T(8,128)(2,1)S(1)}, bf16[512,1024]{1,0:T(8,128)(2,1)}, u32[]{:S(2)}) copy-start(bf16[512,1024]{1,0:T(8,128)(2,1)} %q_own.1) | copy-start | bytes 3145732
  113.5 26.9 %all-to-all-start.3 = ((bf16[32,48,512]{2,1,0:T(8,128)(2,1)}), bf16[32,48,512]{2,1,0:T(8,128)(2,1)S(1)}, u32[]{:S(2)}, u32[]{:S(2)}) async-start(bf16[32,48,512]{2,1,0:T(8,128)(2,1)} %shard_map.87), calls=%async_computation.3 | async-start | bytes 3145728 | tf_op jit(solution)/shard_map/all_to_all | solution.py:194
  119.5 27.8 %collective-permute-start.4 = (bf16[512,1024]{1,0:T(8,128)(2,1)S(1)}, bf16[512,1024]{1,0:T(8,128)(2,1)}, u32[]{:S(2)}, u32[]{:S(2)}) collective-permute-start(bf16[512,1024]{1,0:T(8,128)(2,1)S(1)} %copy-done.8), channel_id=1, source_target_pairs={{0,2},{2,0},{1,3},{3,1},{4,6},{6,4},{5,7},{7,5},{8,10},{10,8},{9,1... | collective-permute-start | bytes 3145736 | tf_op jit(solution)/shard_map/ppermute | solution.py:199
  120.7 36.7 %collective-permute-start.9 = (bf16[512,2560]{1,0:T(8,128)(2,1)}, bf16[512,2560]{1,0:T(8,128)(2,1)}, u32[]{:S(2)}, u32[]{:S(2)}) collective-permute-start(bf16[512,2560]{1,0:T(8,128)(2,1)} %collective-permute-done.8.w_first), channel_id=1, source_target_pairs={{0,2},{2,0},{1,3},{3,1},{4,6},{6,4},{5,7},{7,5},{8,10},{10,8},{9,1... | collective-permute-start | bytes 7864328 | tf_op jit(solution)/shard_map/ppermute | solution.py:199
  143.1 1.7 copy-start
  144.8 3.3 %collective-permute-start.3 = (f32[8,128]{1,0:T(8,128)S(1)}, f32[8,128]{1,0:T(8,128)S(1)}, u32[]{:S(2)}, u32[]{:S(2)}) collective-permute-start(f32[8,128]{1,0:T(8,128)S(1)} %get-tuple-element.23.sq_own), channel_id=1, source_target_pairs={{0,2},{2,0},{1,3},{3,1},{4,6},{6,4},{5,7},{7,5},{8,10},{10,8},{9,1... | collective-permute-start | bytes 12296 | tf_op jit(solution)/shard_map/ppermute | solution.py:199
  151.7 2.4 %collective-permute-start.6 = (bf16[256,1024]{1,0:T(8,128)(2,1)S(1)}, bf16[256,1024]{1,0:T(8,128)(2,1)S(1)}, u32[]{:S(2)}, u32[]{:S(2)}) collective-permute-start(bf16[256,1024]{1,0:T(8,128)(2,1)S(1)} %get-tuple-element.26.w2_own), channel_id=1, source_target_pairs={{0,2},{2,0},{1,3},{3,1},{4,6},{6,4},{5,7},{7,5},{8,10},{10,8},{9,1... | collective-permute-start | bytes 1572872 | tf_op jit(solution)/shard_map/ppermute | solution.py:199
  152.1 1.9 %collective-permute-start.5 = (bf16[256,512]{1,0:T(8,128)(2,1)S(1)}, bf16[256,512]{1,0:T(8,128)(2,1)S(1)}, u32[]{:S(2)}, u32[]{:S(2)}) collective-permute-start(bf16[256,512]{1,0:T(8,128)(2,1)S(1)} %get-tuple-element.25), channel_id=1, source_target_pairs={{0,2},{2,0},{1,3},{3,1},{4,6},{6,4},{5,7},{7,5},{8,10},{10,8},{9,1... | collective-permute-start | bytes 786440 | tf_op jit(solution)/shard_map/ppermute | solution.py:199
  154.8 26.0 %collective-permute-start.7 = (bf16[512,1024]{1,0:T(8,128)(2,1)S(1)}, bf16[512,1024]{1,0:T(8,128)(2,1)S(1)}, u32[]{:S(2)}, u32[]{:S(2)}) collective-permute-start(bf16[512,1024]{1,0:T(8,128)(2,1)S(1)} %shard_map.90.o), channel_id=1, source_target_pairs={{0,1},{1,0},{2,3},{3,2},{4,5},{5,4},{6,7},{7,6},{8,9},{9,8},{10,11... | collective-permute-start | bytes 3145736 | tf_op jit(solution)/shard_map/ppermute | solution.py:252

commit v2 on v1

v2 whole, which is shorter than its diff:
```python
import functools

import jax
import jax.numpy as jnp
from jax import lax
from jax.experimental import pallas as pl
from jax.experimental.pallas import tpu as pltpu
from jax.sharding import Mesh
from jax.sharding import PartitionSpec as P

STEPS = 2
CTX = ("z", "xl", "y", "c")
CHIPS = ("z", "xl", "y")
SWAP = [(0, 1), (1, 0)]
ACROSS = [(0, 3), (3, 0), (1, 2), (2, 1)]
BF = jnp.bfloat16
F32 = jnp.float32
NT = (((1,), (1,)), ((), ()))
TN = (((0,), (0,)), ((), ()))
VMEM = pl.BlockSpec(memory_space=pltpu.VMEM)
SMEM = pl.BlockSpec(memory_space=pltpu.SMEM)
LIMIT = 24 * 1024 * 1024
CHUNKS = 2


def dot(x, y):
    return jnp.dot(x, y, preferred_element_type=F32)


def nt(x, y):
    return lax.dot_general(x, y, NT, preferred_element_type=F32)


def tn(x, y):
    return lax.dot_general(x, y, TN, preferred_element_type=F32)


def call(kernel, outs, n_in, flops, nbytes, smem=0, scratch=()):
    return pl.pallas_call(
        kernel,
        out_shape=outs,
        in_specs=[SMEM] * smem + [VMEM] * (n_in - smem),
        out_specs=jax.tree.map(lambda _: VMEM, outs),
        scratch_shapes=list(scratch),
        compiler_params=pltpu.CompilerParams(vmem_limit_bytes=LIMIT),
        cost_estimate=pl.CostEstimate(flops=flops, bytes_accessed=nbytes, transcendentals=0),
    )


def shape(dims, dtype=BF):
    return jax.ShapeDtypeStruct(dims, dtype)


def prepare_kernel(core, up, gate, down, w0, norm):
    width, hid = up.shape
    half = hid // 2
    total = []
    for w in (up, gate, down):
        full = w[...].astype(F32)
        total.append(jnp.sum(full * full))
    for i, value in enumerate(total):
        norm[i : i + 1, :] = jnp.full((1, 128), value, F32)
    norm[3:8, :] = jnp.zeros((5, 128), F32)
    for c in range(2):

        @pl.when(core[0] == c)
        def _():
            w0[0:half, :] = up[:, c * half : (c + 1) * half].T
            w0[half : 2 * half, :] = gate[:, c * half : (c + 1) * half].T
            w0[2 * half :, :] = down[c * half : (c + 1) * half, :]


def act_grads(wb, keys, targets):
    half = wb.shape[0] // 3
    act = nt(wb[0:half, :], keys)
    lin = nt(wb[half : 2 * half, :], keys)
    err = nt(wb[2 * half :, :], targets)
    sig = jax.nn.sigmoid(act)
    silu = act * sig
    hidden = (silu * lin).astype(BF)
    pgrad = (err * lin * sig * (1.0 + act * (1.0 - sig))).astype(BF)
    qgrad = (err * silu).astype(BF)
    return pgrad, qgrad, hidden


def sums_into(out, own, oth, k_own, k_oth, u_own, u_oth):
    cols = k_own.shape[1] // 2
    half = own[0].shape[0]
    for i in range(3):
        x, y = (k_own, k_oth) if i < 2 else (u_own, u_oth)
        for j in range(2):
            at = slice(j * cols, (j + 1) * cols)
            g = dot(own[i], x[:, at]) + dot(oth[i], y[:, at])
            out[j, i * half : (i + 1) * half, :] = g.astype(BF)


def own_kernel(w0, k_own, u_own, acts):
    half = w0.shape[0] // 3
    for i, x in enumerate(act_grads(w0, k_own[...], u_own[...])):
        acts[i * half : (i + 1) * half, :] = x


def first_kernel(w0, acts, k_own, k_oth, u_own, u_oth, out):
    half = w0.shape[0] // 3
    own = [acts[i * half : (i + 1) * half, :] for i in range(3)]
    oth = act_grads(w0, k_oth[...], u_oth[...])
    sums_into(out, own, oth, k_own, k_oth, u_own, u_oth)


def moved_into(moved, squares, weight, gathered):
    third = moved.shape[0] // 3
    cols = moved.shape[1] // 2
    for i in range(3):
        rows = slice(i * third, (i + 1) * third)
        total = jnp.zeros((), F32)
        for j in range(2):
            at = slice(j * cols, (j + 1) * cols)
            m = weight(i, rows, at) + gathered[j, rows, :].astype(F32)
            moved[rows, at] = m
            total = total + jnp.sum(m * m)
        squares[i : i + 1, :] = jnp.full((1, 128), total, F32)
    squares[3:8, :] = jnp.zeros((5, 128), F32)


def update_kernel(w, gathered, moved, squares):
    moved_into(moved, squares, lambda i, rows, at: w[rows, at].astype(F32), gathered)


def update_again_kernel(before, norm, sq_own, sq_oth, gathered, moved, squares):
    moved_into(
        moved,
        squares,
        lambda i, rows, at: before[rows, at] * factor(i, norm, sq_own, sq_oth),
        gathered,
    )


def factor(i, norm, own, oth):
    size = jnp.sqrt(norm[i : i + 1, 0:1])
    total = own[i : i + 1, 0:1] + oth[i : i + 1, 0:1]
    return size / jnp.sqrt(total + 1e-06)


def scaled(i, moved, norm, own, oth):
    third = moved.shape[0] // 3
    new = moved[i * third : (i + 1) * third, :] * factor(i, norm, own, oth)
    return new.astype(BF)


def next_kernel(moved, norm, sq_own, sq_oth, k_own, k_oth, u_own, u_oth, out, wb):
    third = moved.shape[0] // 3
    for i in range(3):
        wb[i * third : (i + 1) * third, :] = scaled(i, moved, norm, sq_own, sq_oth)
    own = act_grads(wb, k_own[...], u_own[...])
    oth = act_grads(wb, k_oth[...], u_oth[...])
    sums_into(out, own, oth, k_own, k_oth, u_own, u_oth)


def hidden_of(b1, b3, q):
    return (jax.nn.silu(nt(b1, q)) * nt(b3, q)).astype(BF)


def hidden_kernel(moved, norm, sq_own, sq_oth, q_oth, w2, hq_oth, b13):
    half = w2.shape[0]
    w2[...] = scaled(2, moved, norm, sq_own, sq_oth)
    b1 = scaled(0, moved, norm, sq_own, sq_oth)
    b3 = scaled(1, moved, norm, sq_own, sq_oth)
    b13[0:half, :] = b1
    b13[half:, :] = b3
    hq_oth[...] = hidden_of(b1, b3, q_oth[...])


def hidden_own_kernel(b13, q_own, hq_own):
    half = b13.shape[0] // 2
    hq_own[...] = hidden_of(b13[0:half, :], b13[half:, :], q_own[...])


def piece_kernel(hq_own, hq_got, w2_own, w2_got, *pieces):
    count = pieces[0].shape[0]
    for k, o in enumerate(pieces):
        at = slice(k * count, (k + 1) * count)
        o[...] = (tn(hq_own[:, at], w2_own[...]) + tn(hq_got[:, at], w2_got[...])).astype(BF)


def spread_kernel(arrived, out):
    total = arrived[0].astype(F32)
    for i in range(1, arrived.shape[0]):
        total = total + arrived[i].astype(F32)
    rounded = total.astype(BF)
    for i in range(arrived.shape[0]):
        out[i] = rounded


TILE = 512


def partial_kernel(place, *refs):
    *pieces, w_own, out = refs
    count = pieces[0].shape[0]
    for k, o in enumerate(pieces):
        out[k * count : (k + 1) * count, :] = dot(o[...], w_own[...])


def partial_product(place, pieces, w_out):
    count, width = pieces[0].shape
    n = w_out.shape[1] // 2
    steps = n // TILE
    tokens = count * len(pieces)
    return pl.pallas_call(
        partial_kernel,
        out_shape=shape((tokens, n), F32),
        grid_spec=pltpu.PrefetchScalarGridSpec(
            num_scalar_prefetch=1,
            grid=(steps,),
            in_specs=[pl.BlockSpec((count, width), lambda i, s: (0, 0))] * len(pieces)
            + [pl.BlockSpec((width, TILE), lambda i, s: (0, s[0] * steps + i))],
            out_specs=pl.BlockSpec((tokens, TILE), lambda i, s: (0, i)),
        ),
        compiler_params=pltpu.CompilerParams(vmem_limit_bytes=LIMIT),
        cost_estimate=pl.CostEstimate(
            flops=2 * tokens * width * n, bytes_accessed=10 << 20, transcendentals=0
        ),
    )(place, *pieces, w_out)


def finish_kernel(place, part, o_first, o_second, w_first, w_second, *rest):
    out = rest[-1]
    total = part[...] + dot(o_first[...], w_first[...]) + dot(o_second[...], w_second[...])
    out[...] = total.astype(BF)


def finish_product(place, k, part, o_got, w_first, w_second, out):
    count, width = o_got.shape
    tokens, n = part.shape
    args = (place, part, o_got, o_got, w_first, w_second)
    return pl.pallas_call(
        finish_kernel,
        out_shape=shape((tokens, n)),
        grid_spec=pltpu.PrefetchScalarGridSpec(
            num_scalar_prefetch=1,
            grid=(n // TILE,),
            in_specs=[
                pl.BlockSpec((count, TILE), lambda i, s: (k, i)),
                pl.BlockSpec((count, width // 2), lambda i, s: (0, s[1])),
                pl.BlockSpec((count, width // 2), lambda i, s: (0, 1 - s[1])),
                pl.BlockSpec((width // 2, TILE), lambda i, s: (0, i)),
                pl.BlockSpec((width // 2, TILE), lambda i, s: (0, i)),
            ]
            + [pl.BlockSpec(memory_space=pl.ANY)] * (out is not None),
            out_specs=pl.BlockSpec((count, TILE), lambda i, s: (k, i)),
        ),
        input_output_aliases={} if out is None else {len(args): 0},
        compiler_params=pltpu.CompilerParams(vmem_limit_bytes=LIMIT),
        cost_estimate=pl.CostEstimate(
            flops=2 * count * width * n, bytes_accessed=10 << 20, transcendentals=0
        ),
    )(*args, *(() if out is None else (out,)))


def all_reduced(grads):
    peers = lax.axis_size(CHIPS)
    pieces = grads.reshape(peers, -1, grads.shape[2])
    arrived = lax.all_to_all(pieces, CHIPS, 0, 0, tiled=True)
    copies = call(spread_kernel, shape(pieces.shape), 1, pieces.size, 4 * pieces.size)(arrived)
    gathered = lax.all_to_all(copies, CHIPS, 0, 0, tiled=True)
    return gathered.reshape(grads.shape)


def swap(x):
    return lax.ppermute(x, "c", SWAP)


def shards(queries, keys, values, rates, w_up, w_gate, w_down, w_out):
    width, hid = w_up.shape[1:]
    tokens = keys.shape[0]
    half, third = hid // 2, 3 * hid // 2
    core, head = lax.axis_index("c"), lax.axis_index("h")
    n = w_out.shape[1] // 2

    k_oth = swap(keys)
    targets = (rates * values.astype(F32)).astype(BF)
    u_oth = swap(targets)
    kus = (keys, k_oth, targets, u_oth)

    place = jnp.stack([head, core]).astype(jnp.int32)
    sent = lax.dynamic_slice(w_out, (core * (width // 2), (1 - head) * n), (width // 2, n))
    w_first = lax.ppermute(sent, ("xl", "h"), ACROSS)
    w_second = swap(w_first)
    q_oth = swap(queries)

    w0, norm = call(
        prepare_kernel, (shape((third, width)), shape((8, 128), F32)), 4, 1 << 21, 5 << 20, smem=1
    )(core.reshape(1).astype(jnp.int32), w_up[0], w_gate[0], w_down[0])
    flops = 12 * 2 * tokens * width * half
    gshape = shape((2, third, width // 2))
    mshape = (shape((third, width), F32), shape((8, 128), F32))
    acts = call(own_kernel, shape((third, tokens)), 3, flops // 4, 4 << 20)(w0, keys, targets)
    grads = call(first_kernel, gshape, 6, flops * 3 // 4, 8 << 20)(w0, acts, *kus)
    state = None
    for step in range(STEPS):
        gathered = all_reduced(grads)
        if step == 0:
            moved, squares = call(update_kernel, mshape, 2, 1 << 22, 8 << 20)(w0, gathered)
        else:
            moved, squares = call(update_again_kernel, mshape, 5, 1 << 22, 8 << 20)(
                *state, gathered
            )
        state = (moved, norm, squares, swap(squares))
        if step < STEPS - 1:
            grads = call(
                next_kernel, gshape, 8, flops, 14 << 20, scratch=[pltpu.VMEM((third, width), BF)]
            )(*state, *kus)
    hshape = shape((half, tokens))
    w2, hq_oth, b13 = call(
        hidden_kernel,
        (shape((half, width)), hshape, shape((2 * half, width))),
        5,
        flops // 6,
        8 << 20,
    )(*state, q_oth)
    hq_got, w2_got = swap(hq_oth), swap(w2)
    hq_own = call(hidden_own_kernel, hshape, 2, flops // 6, 3 << 20)(b13, queries)
    pieces = call(
        piece_kernel,
        (shape((tokens // CHUNKS, width)),) * CHUNKS,
        4,
        2 * tokens * hid * width,
        4 << 20,
    )(hq_own, hq_got, w2, w2_got)
    pieces_got = [lax.ppermute(o, "h", SWAP) for o in pieces]
    part = partial_product(place, pieces, w_out)
    out = None
    for k, o_got in enumerate(pieces_got):
        out = finish_product(place, k, part, o_got, w_first, w_second, out)
    return out


def solution(mesh):
    finer = Mesh(
        mesh.devices.reshape(4, 2, 4, 2, mesh.shape["head"]),
        ("z", "xl", "y", "c", "h"),
    )
    return jax.shard_map(
        shards,
        mesh=finer,
        in_specs=(
            P(CTX, "h"),
            P(CTX, "h"),
            P(CTX, "h"),
            P(CTX, "h"),
            P("h", None, None),
            P("h", None, None),
            P("h", None, None),
            P("h", None),
        ),
        out_specs=P(CTX, "h"),
        check_vma=False,
    )
```

time: 192 us -> 186 us (0.969)
  waiting for transfers between devices: 61.8 us -> 45.3 us
  local copies, waits for them, and re-layouts: 7.61 us -> 14.4 us
  Pallas kernels: 37.4 us -> 40.1 us
    ppermute x1 -> x2, waiting for transfers between devices: 23.4 us -> 7.99 us  [shards(): pieces_got = [lax.ppermute(o, 'h', SWAP) for o in pieces]]
    unnamed x22 -> x28, local copies, waits for them, and re-layouts: 4.09 us -> 11 us
    pallas_call x7 -> x11, Pallas kernels: 33.2 us -> 37.2 us  [the longest x2 12.1 us: finish_product(): pl.pallas_call(finish_kernel, out_shape=shape((tokens, n)), grid_spec=plt...]
  transfers between devices with their start and end apart: 12 -> 13, of which waited for: 7 -> 7; matrix products, arithmetic and copies ran while one was open for 2% -> 2% of each run, Pallas kernels for 10% -> 15%
where the time goes in v2:
time: 186 us; the launch traced here: 185 us
  blocking collectives  57.3 us (31%)
  waiting for transfers between devices  45.3 us (24%)
  Pallas kernels  40.1 us (22%)
  starting transfers between devices  25.7 us (14%)
  local copies, waits for them, and re-layouts  14.4 us (8%)
    all_to_all x2, blocking collectives, all_reduced(): arrived = lax.all_to_all(pieces, CHIPS, 0, 0, tiled=True)  57.3 us
    all_to_all x2, waiting for transfers between devices, all_reduced(): gathered = lax.all_to_all(copies, CHIPS, 0, 0, tiled=True)  34.7 us
    pallas_call x2, Pallas kernels, finish_product(): pl.pallas_call(finish_kernel, out_shape=shape((tokens, n)), grid_spec=plt...  12.1 us
    all_to_all x2, starting transfers between devices, all_reduced(): gathered = lax.all_to_all(copies, CHIPS, 0, 0, tiled=True)  11.6 us
    unnamed x28, local copies, waits for them, and re-layouts  11 us
    ppermute x8, starting transfers between devices, swap(): return lax.ppermute(x, 'c', SWAP)  8.56 us
    ppermute x2, waiting for transfers between devices, shards(): pieces_got = [lax.ppermute(o, 'h', SWAP) for o in pieces]  7.99 us
    pallas_call x1, Pallas kernels, shards(): call(next_kernel, gshape, 8, flops, 14 << 20, scratch=[pltpu.VMEM((third,...  5.29 us
  transfers between devices with their start and end apart: 13, of which 7 were waited for; matrix products, arithmetic and copies ran while one was open for 2% of the time, Pallas kernels for 15%

profile of v2, /device:TPU:1, one launch (start us, length us, event | category | flops | bytes accessed | tf_op | source)
XLA Modules:
  0.0 184.7 jit_solution(11431044069400565268)
XLA Ops:
  0.0 0.0 copy-start.8
  0.0 1.6 multiply_convert_fusion.u_own
  1.6 0.0 copy-start.4
  1.6 1.5 collective-permute-start.1
  3.1 0.0 copy-done.8
  3.1 0.1 collective-permute-start
  3.2 0.0 copy-done.10
  3.2 1.2 copy-done.11
  4.5 1.2 copy-done.12
  5.7 1.2 shard_map.82
  6.9 0.0 copy-start.1
  6.9 1.1 shard_map.83.acts
  8.0 0.0 collective-permute-done.1.u_oth
  8.0 0.0 collective-permute-done.k_oth
  8.0 0.0 copy-done.4
  8.0 0.0 copy-done.1
  8.0 4.3 %shard_map.84 = bf16[2,768,512]{2,1,0:T(8,128)(2,1)S(1)} custom-call(bf16[768,1024]{1,0:T(8,128)(2,1)S(1)} %get-tuple-element.16.w0.w, bf16[768,512]{1,0:T(8,128)(2,1)S(1)} %shard_map.83.acts, bf16[512,1024]{1,0:T(8,128)(2,1)S(1)} %copy-done.8, bf16[512,1024]{1,0:T(8,128)(2,1)} %collective-permute-done.k_oth, ...), custom_call_target="tpu_custom_call" | custom-call | flops 2415919104 | bytes 8388608 | tf_op jit(solution)/shard_map/pallas_call | solution.py:298
  12.4 30.3 %all_to_all.20.arrived = bf16[32,48,512]{2,1,0:T(8,128)(2,1)S(1)} all-to-all(bf16[32,48,512]{2,1,0:T(8,128)(2,1)S(1)} %bitcast.11), channel_id=1, replica_groups=mesh['z'=4,'xl'=2,'y'=4,'c'=2,'h'=2] {'z','xl','y'}, dimensions={0} | all-to-all | bytes 3145728 | tf_op jit(solution)/shard_map/all_to_all | solution.py:263
  42.6 1.5 shard_map.85
  44.1 5.8 %all-to-all-start.1 = ((bf16[32,48,512]{2,1,0:T(8,128)(2,1)}), bf16[32,48,512]{2,1,0:T(8,128)(2,1)}, u32[]{:S(2)}, u32[]{:S(2)}) async-start(bf16[32,48,512]{2,1,0:T(8,128)(2,1)} %shard_map.85), calls=%async_computation.1 | async-start | bytes 3145728 | tf_op jit(solution)/shard_map/all_to_all | solution.py:265
  49.9 3.4 %dynamic_slice.3 = bf16[512,2560]{1,0:T(8,128)(2,1)} dynamic-slice(bf16[1024,5120]{1,0:T(8,128)(2,1)} %refs_2_.1, s32[]{:T(128)S(6)} %select_n.6, s32[]{:T(128)S(6)} %select_n.7), dynamic_slice_sizes={512,2560} | dynamic-slice | bytes 5242884 | tf_op jit(solution)/shard_map/dynamic_slice | solution.py:286
  53.3 2.4 %collective-permute-start.8 = (bf16[512,2560]{1,0:T(8,128)(2,1)}, bf16[512,2560]{1,0:T(8,128)(2,1)S(1)}, u32[]{:S(2)}, u32[]{:S(2)}) collective-permute-start(bf16[512,2560]{1,0:T(8,128)(2,1)} %dynamic_slice.3), channel_id=1, source_target_pairs={{0,17},{17,0},{1,16},{16,1},{2,19},{19,2},{3,18},{18,3},{4,21},{21... | collective-permute-start | bytes 7864328 | tf_op jit(solution)/shard_map/ppermute | solution.py:287
  55.8 15.1 %all-to-all-done.1 = bf16[32,48,512]{2,1,0:T(8,128)(2,1)} async-done(((bf16[32,48,512]{2,1,0:T(8,128)(2,1)}), bf16[32,48,512]{2,1,0:T(8,128)(2,1)}, u32[]{:S(2)}, u32[]{:S(2)}) %all-to-all-start.1) | async-done | bytes 1572896 | tf_op jit(solution)/shard_map/all_to_all | solution.py:265
  70.9 1.4 copy-done.2
  72.3 2.4 %shard_map.86 = (f32[768,1024]{1,0:T(8,128)S(1)}, f32[8,128]{1,0:T(8,128)S(1)}) custom-call(bf16[768,1024]{1,0:T(8,128)(2,1)S(1)} %copy-done.2, bf16[2,768,512]{2,1,0:T(8,128)(2,1)} %bitcast.7.gathered), custom_call_target="tpu_custom_call" | custom-call | flops 4194304 | bytes 8388608 | tf_op jit(solution)/shard_map/pallas_call | solution.py:303
  74.7 0.0 copy-start.6
  74.7 2.5 %collective-permute-start.2 = (f32[8,128]{1,0:T(8,128)S(1)}, f32[8,128]{1,0:T(8,128)S(1)}, u32[]{:S(2)}, u32[]{:S(2)}) collective-permute-start(f32[8,128]{1,0:T(8,128)S(1)} %get-tuple-element.19.sq_own), channel_id=1, source_target_pairs={{0,2},{2,0},{1,3},{3,1},{4,6},{6,4},{5,7},{7,5},{8,10},{10,8},{9,1... | collective-permute-start | bytes 12296 | tf_op jit(solution)/shard_map/ppermute | solution.py:270
  77.3 0.8 collective-permute-done.2.sq_oth
  78.1 0.0 copy-done.5
  78.1 0.0 copy-done.9
  78.1 5.3 %shard_map.87 = bf16[2,768,512]{2,1,0:T(8,128)(2,1)S(1)} custom-call(f32[768,1024]{1,0:T(8,128)S(1)} %get-tuple-element.17.moved.before, f32[8,128]{1,0:T(8,128)S(1)} %get-tuple-element.18.norm, f32[8,128]{1,0:T(8,128)S(1)} %get-tuple-element.19.sq_own, f32[8,128]{1,0:T(8,128)S(1)} %collective-permute-done.2.sq_oth, bf16[512,1024]{1,0:T(8,128)(2,1)S(1)} %copy-done.9, ...), custom_call_target="tpu_custom_call" | custom-call | flops 3221225472 | bytes 14680064 | tf_op jit(solution)/shard_map/pallas_call | solution.py:310
  83.4 0.0 copy-done.6
  83.4 27.1 %all_to_all.21.arrived = bf16[32,48,512]{2,1,0:T(8,128)(2,1)S(1)} all-to-all(bf16[32,48,512]{2,1,0:T(8,128)(2,1)S(1)} %bitcast.10), channel_id=1, replica_groups=mesh['z'=4,'xl'=2,'y'=4,'c'=2,'h'=2] {'z','xl','y'}, dimensions={0} | all-to-all | bytes 3145728 | tf_op jit(solution)/shard_map/all_to_all | solution.py:263
  110.4 0.3 shard_map.88
  110.8 0.0 copy-start.3
  110.8 1.2 copy-done.3
  112.0 5.8 %all-to-all-start.3 = ((bf16[32,48,512]{2,1,0:T(8,128)(2,1)}), bf16[32,48,512]{2,1,0:T(8,128)(2,1)}, u32[]{:S(2)}, u32[]{:S(2)}) async-start(bf16[32,48,512]{2,1,0:T(8,128)(2,1)} %copy-done.3), calls=%async_computation.3 | async-start | bytes 3145728 | tf_op jit(solution)/shard_map/all_to_all | solution.py:265
  117.8 0.0 collective-permute-done.8.w_first
  117.8 1.2 collective-permute-start.9
  119.0 0.1 collective-permute-start.4
  119.1 19.6 %all-to-all-done.3 = bf16[32,48,512]{2,1,0:T(8,128)(2,1)} async-done(((bf16[32,48,512]{2,1,0:T(8,128)(2,1)}), bf16[32,48,512]{2,1,0:T(8,128)(2,1)}, u32[]{:S(2)}, u32[]{:S(2)}) %all-to-all-start.3) | async-done | bytes 1572896 | tf_op jit(solution)/shard_map/all_to_all | solution.py:265
  138.7 1.9 %copy-done.7 = f32[768,1024]{1,0:T(8,128)S(1)} copy-done((f32[768,1024]{1,0:T(8,128)S(1)}, f32[768,1024]{1,0:T(8,128)}, u32[]{:S(2)}) %copy-start.7) | copy-done | bytes 3145752
  140.6 3.5 %shard_map.89 = (f32[768,1024]{1,0:T(8,128)S(1)}, f32[8,128]{1,0:T(8,128)S(1)}) custom-call(f32[768,1024]{1,0:T(8,128)S(1)} %copy-done.7, f32[8,128]{1,0:T(8,128)S(1)} %get-tuple-element.18.norm, f32[8,128]{1,0:T(8,128)S(1)} %get-tuple-element.19.sq_own, f32[8,128]{1,0:T(8,128)S(1)} %collective-permute-done.2.sq_oth, bf16[2,768,512]{2,1,0:T(8,128)(2,1)} %bitcast.9.gathered), custom_call_target="tpu_custom_call" | custom-call | flops 4194304 | bytes 8388608 | tf_op jit(solution)/shard_map/pallas_call | solution.py:305
  144.1 2.5 %collective-permute-start.3 = (f32[8,128]{1,0:T(8,128)S(1)}, f32[8,128]{1,0:T(8,128)S(1)}, u32[]{:S(2)}, u32[]{:S(2)}) collective-permute-start(f32[8,128]{1,0:T(8,128)S(1)} %get-tuple-element.21.sq_own), channel_id=1, source_target_pairs={{0,2},{2,0},{1,3},{3,1},{4,6},{6,4},{5,7},{7,5},{8,10},{10,8},{9,1... | collective-permute-start | bytes 12296 | tf_op jit(solution)/shard_map/ppermute | solution.py:270
  146.6 0.0 collective-permute-done.4.q_oth
  146.6 0.8 collective-permute-done.3.sq_oth
  147.4 2.2 %shard_map.90 = (bf16[256,1024]{1,0:T(8,128)(2,1)S(1)}, bf16[256,512]{1,0:T(8,128)(2,1)S(1)}, bf16[512,1024]{1,0:T(8,128)(2,1)S(1)}) custom-call(f32[768,1024]{1,0:T(8,128)S(1)} %get-tuple-element.20.moved, f32[8,128]{1,0:T(8,128)S(1)} %get-tuple-element.18.norm, f32[8,128]{1,0:T(8,128)S(1)} %get-tuple-element.21.sq_own, ...), custom_call_target="tpu_custom_call" | custom-call | flops 536870912 | bytes 8388608 | tf_op jit(solution)/shard_map/pallas_call | solution.py:314
  149.6 0.4 collective-permute-start.6
  150.0 0.2 collective-permute-start.5
  150.2 0.0 copy-done.13
  150.2 0.8 shard_map.91.hq_own
  151.0 1.0 collective-permute-done.5.hq_got
  152.0 0.0 collective-permute-done.6.w2_got
  152.0 0.7 shard_map.92
  152.7 2.5 %collective-permute-start.10 = (bf16[256,1024]{1,0:T(8,128)(2,1)S(1)}, bf16[256,1024]{1,0:T(8,128)(2,1)S(1)}, u32[]{:S(2)}, u32[]{:S(2)}) collective-permute-start(bf16[256,1024]{1,0:T(8,128)(2,1)S(1)} %get-tuple-element.25.refs_0_), channel_id=1, source_target_pairs={{0,1},{1,0},{2,3},{3,2},{4,5},{5,4},{6,7},{7,6},{8,9},{9,8},{10,11... | collective-permute-start | bytes 1572872 | tf_op jit(solution)/shard_map/ppermute | solution.py:330
  155.3 0.5 collective-permute-start.7
  155.8 0.1 pad_add_fusion.place
  155.9 4.0 %copy-done = bf16[1024,5120]{1,0:T(8,128)(2,1)S(1)} copy-done((bf16[1024,5120]{1,0:T(8,128)(2,1)S(1)}, bf16[1024,5120]{1,0:T(8,128)(2,1)}, u32[]{:S(2)}) %copy-start) | copy-done | bytes 10485784
  159.8 4.8 %shard_map.93.part = f32[512,2560]{1,0:T(8,128)S(1)} custom-call(s32[2]{0:T(128)S(1)} %pad_add_fusion.place, bf16[256,1024]{1,0:T(8,128)(2,1)S(1)} %get-tuple-element.25.refs_0_, bf16[256,1024]{1,0:T(8,128)(2,1)S(1)} %get-tuple-element.26.refs_1_, bf16[1024,5120]{1,0:T(8,128)(2,1)S(1)} %copy-done), custom_call_target="tpu_custom_call" | custom-call | flops 2684354560 | bytes 10485760 | tf_op jit(solution)/shard_map/pallas_call | solution.py:209
  164.7 0.0 collective-permute-done.9.w_second
  164.7 2.8 %collective-permute-done.10.o_first.o_second = bf16[256,1024]{1,0:T(8,128)(2,1)S(1)} collective-permute-done((bf16[256,1024]{1,0:T(8,128)(2,1)S(1)}, bf16[256,1024]{1,0:T(8,128)(2,1)S(1)}, u32[]{:S(2)}, u32[]{:S(2)}) %collective-permute-start.10) | collective-permute-done | bytes 524320 | tf_op jit(solution)/shard_map/ppermute | solution.py:330
  167.5 6.0 %shard_map.94.rest_0_ = bf16[512,2560]{1,0:T(8,128)(2,1)} custom-call(s32[2]{0:T(128)S(1)} %pad_add_fusion.place, f32[512,2560]{1,0:T(8,128)S(1)} %shard_map.93.part, bf16[256,1024]{1,0:T(8,128)(2,1)S(1)} %collective-permute-done.10.o_first.o_second, bf16[256,1024]{1,0:T(8,128)(2,1)S(1)} %collective-permute-done.10.o_first.o_second, ...), custom_call_target="tpu_custom_call" | custom-call | flops 1342177280 | bytes 10485760 | tf_op jit(solution)/shard_map/pallas_call | solution.py:236
  173.5 5.2 %collective-permute-done.7.o_first.o_second = bf16[256,1024]{1,0:T(8,128)(2,1)S(1)} collective-permute-done((bf16[256,1024]{1,0:T(8,128)(2,1)S(1)}, bf16[256,1024]{1,0:T(8,128)(2,1)S(1)}, u32[]{:S(2)}, u32[]{:S(2)}) %collective-permute-start.7) | collective-permute-done | bytes 524320 | tf_op jit(solution)/shard_map/ppermute | solution.py:330
  178.7 6.0 %shard_map.95 = bf16[512,2560]{1,0:T(8,128)(2,1)} custom-call(s32[2]{0:T(128)S(1)} %pad_add_fusion.place, f32[512,2560]{1,0:T(8,128)S(1)} %shard_map.93.part, bf16[256,1024]{1,0:T(8,128)(2,1)S(1)} %collective-permute-done.7.o_first.o_second, bf16[256,1024]{1,0:T(8,128)(2,1)S(1)} %collective-permute-done.7.o_first.o_second, ...), custom_call_target="tpu_custom_call", output_to_operand_aliasing={{}: (6, {})} | custom-call | flops 1342177280 | bytes 10485760 | tf_op jit(solution)/shard_map/pallas_call | solution.py:236
  (9 shorter events, 0.0 us)
Async XLA Ops:
  0.0 3.1 %copy-start.8 = (bf16[512,1024]{1,0:T(8,128)(2,1)S(1)}, bf16[512,1024]{1,0:T(8,128)(2,1)}, u32[]{:S(2)}) copy-start(bf16[512,1024]{1,0:T(8,128)(2,1)} %k_own.5) | copy-start | bytes 3145732
  0.0 3.2 %copy-start.10 = (bf16[1,1024,512]{2,1,0:T(8,128)(2,1)S(1)}, bf16[1,1024,512]{2,1,0:T(8,128)(2,1)}, u32[]{:S(2)}) copy-start(bf16[1,1024,512]{2,1,0:T(8,128)(2,1)} %param.12) | copy-start | bytes 3145732
  1.6 6.4 %copy-start.4 = (bf16[512,1024]{1,0:T(8,128)(2,1)}, bf16[512,1024]{1,0:T(8,128)(2,1)S(1)}, u32[]{:S(2)}) copy-start(bf16[512,1024]{1,0:T(8,128)(2,1)S(1)} %multiply_convert_fusion.u_own) | copy-start | bytes 3145732
  1.6 6.3 %collective-permute-start.1 = (bf16[512,1024]{1,0:T(8,128)(2,1)S(1)}, bf16[512,1024]{1,0:T(8,128)(2,1)}, u32[]{:S(2)}, u32[]{:S(2)}) collective-permute-start(bf16[512,1024]{1,0:T(8,128)(2,1)S(1)} %multiply_convert_fusion.u_own), channel_id=1, source_target_pairs={{0,2},{2,0},{1,3},{3,1},{4,6},{6,4},{5,7},{7,5},{8,10},{10,8},{9,1... | collective-permute-start | bytes 3145736 | tf_op jit(solution)/shard_map/ppermute | solution.py:270
  3.1 4.8 %collective-permute-start = (bf16[512,1024]{1,0:T(8,128)(2,1)S(1)}, bf16[512,1024]{1,0:T(8,128)(2,1)}, u32[]{:S(2)}, u32[]{:S(2)}) collective-permute-start(bf16[512,1024]{1,0:T(8,128)(2,1)S(1)} %copy-done.8), channel_id=1, source_target_pairs={{0,2},{2,0},{1,3},{3,1},{4,6},{6,4},{5,7},{7,5},{8,10},{10,8},{9,1... | collective-permute-start | bytes 3145736 | tf_op jit(solution)/shard_map/ppermute | solution.py:270
  3.2 1.2 copy-start.11
  4.5 1.2 copy-start.12
  6.9 1.2 copy-start.1
  44.1 26.8 %all-to-all-start.1 = ((bf16[32,48,512]{2,1,0:T(8,128)(2,1)}), bf16[32,48,512]{2,1,0:T(8,128)(2,1)}, u32[]{:S(2)}, u32[]{:S(2)}) async-start(bf16[32,48,512]{2,1,0:T(8,128)(2,1)} %shard_map.85), calls=%async_computation.1 | async-start | bytes 3145728 | tf_op jit(solution)/shard_map/all_to_all | solution.py:265
  53.3 64.4 %collective-permute-start.8 = (bf16[512,2560]{1,0:T(8,128)(2,1)}, bf16[512,2560]{1,0:T(8,128)(2,1)S(1)}, u32[]{:S(2)}, u32[]{:S(2)}) collective-permute-start(bf16[512,2560]{1,0:T(8,128)(2,1)} %dynamic_slice.3), channel_id=1, source_target_pairs={{0,17},{17,0},{1,16},{16,1},{2,19},{19,2},{3,18},{18,3},{4,21},{21... | collective-permute-start | bytes 7864328 | tf_op jit(solution)/shard_map/ppermute | solution.py:287
  70.9 1.4 copy-start.2
  72.3 5.8 %copy-start.5 = (bf16[512,1024]{1,0:T(8,128)(2,1)S(1)}, bf16[512,1024]{1,0:T(8,128)(2,1)}, u32[]{:S(2)}) copy-start(bf16[512,1024]{1,0:T(8,128)(2,1)} %copy-done.4) | copy-start | bytes 3145732
  72.3 5.8 %copy-start.9 = (bf16[512,1024]{1,0:T(8,128)(2,1)S(1)}, bf16[512,1024]{1,0:T(8,128)(2,1)}, u32[]{:S(2)}) copy-start(bf16[512,1024]{1,0:T(8,128)(2,1)} %k_own.5) | copy-start | bytes 3145732
  74.7 8.7 %copy-start.6 = (f32[768,1024]{1,0:T(8,128)}, f32[768,1024]{1,0:T(8,128)S(1)}, u32[]{:S(2)}) copy-start(f32[768,1024]{1,0:T(8,128)S(1)} %get-tuple-element.17.moved.before) | copy-start | bytes 9437188
  74.7 3.4 %collective-permute-start.2 = (f32[8,128]{1,0:T(8,128)S(1)}, f32[8,128]{1,0:T(8,128)S(1)}, u32[]{:S(2)}, u32[]{:S(2)}) collective-permute-start(f32[8,128]{1,0:T(8,128)S(1)} %get-tuple-element.19.sq_own), channel_id=1, source_target_pairs={{0,2},{2,0},{1,3},{3,1},{4,6},{6,4},{5,7},{7,5},{8,10},{10,8},{9,1... | collective-permute-start | bytes 12296 | tf_op jit(solution)/shard_map/ppermute | solution.py:270
  110.8 1.2 copy-start.3
  112.0 26.7 %all-to-all-start.3 = ((bf16[32,48,512]{2,1,0:T(8,128)(2,1)}), bf16[32,48,512]{2,1,0:T(8,128)(2,1)}, u32[]{:S(2)}, u32[]{:S(2)}) async-start(bf16[32,48,512]{2,1,0:T(8,128)(2,1)} %copy-done.3), calls=%async_computation.3 | async-start | bytes 3145728 | tf_op jit(solution)/shard_map/all_to_all | solution.py:265
  117.8 46.9 %collective-permute-start.9 = (bf16[512,2560]{1,0:T(8,128)(2,1)S(1)}, bf16[512,2560]{1,0:T(8,128)(2,1)}, u32[]{:S(2)}, u32[]{:S(2)}) collective-permute-start(bf16[512,2560]{1,0:T(8,128)(2,1)S(1)} %collective-permute-done.8.w_first), channel_id=1, source_target_pairs={{0,2},{2,0},{1,3},{3,1},{4,6},{6,4},{5,7},{7,5},{8,10},{10,8},{9,1... | collective-permute-start | bytes 7864328 | tf_op jit(solution)/shard_map/ppermute | solution.py:270
  119.0 27.6 %collective-permute-start.4 = (bf16[512,1024]{1,0:T(8,128)(2,1)}, bf16[512,1024]{1,0:T(8,128)(2,1)}, u32[]{:S(2)}, u32[]{:S(2)}) collective-permute-start(bf16[512,1024]{1,0:T(8,128)(2,1)} %q_own.1), channel_id=1, source_target_pairs={{0,2},{2,0},{1,3},{3,1},{4,6},{6,4},{5,7},{7,5},{8,10},{10,8},{9,1... | collective-permute-start | bytes 3145736 | tf_op jit(solution)/shard_map/ppermute | solution.py:270
  138.7 1.9 %copy-start.7 = (f32[768,1024]{1,0:T(8,128)S(1)}, f32[768,1024]{1,0:T(8,128)}, u32[]{:S(2)}) copy-start(f32[768,1024]{1,0:T(8,128)} %copy-done.6) | copy-start | bytes 9437188
  144.1 3.4 %collective-permute-start.3 = (f32[8,128]{1,0:T(8,128)S(1)}, f32[8,128]{1,0:T(8,128)S(1)}, u32[]{:S(2)}, u32[]{:S(2)}) collective-permute-start(f32[8,128]{1,0:T(8,128)S(1)} %get-tuple-element.21.sq_own), channel_id=1, source_target_pairs={{0,2},{2,0},{1,3},{3,1},{4,6},{6,4},{5,7},{7,5},{8,10},{10,8},{9,1... | collective-permute-start | bytes 12296 | tf_op jit(solution)/shard_map/ppermute | solution.py:270
  147.4 2.8 %copy-start.13 = (bf16[512,1024]{1,0:T(8,128)(2,1)S(1)}, bf16[512,1024]{1,0:T(8,128)(2,1)}, u32[]{:S(2)}) copy-start(bf16[512,1024]{1,0:T(8,128)(2,1)} %q_own.1) | copy-start | bytes 3145732
  149.6 2.4 %collective-permute-start.6 = (bf16[256,1024]{1,0:T(8,128)(2,1)S(1)}, bf16[256,1024]{1,0:T(8,128)(2,1)S(1)}, u32[]{:S(2)}, u32[]{:S(2)}) collective-permute-start(bf16[256,1024]{1,0:T(8,128)(2,1)S(1)} %get-tuple-element.24.w2_own), channel_id=1, source_target_pairs={{0,2},{2,0},{1,3},{3,1},{4,6},{6,4},{5,7},{7,5},{8,10},{10,8},{9,1... | collective-permute-start | bytes 1572872 | tf_op jit(solution)/shard_map/ppermute | solution.py:270
  150.0 1.9 %collective-permute-start.5 = (bf16[256,512]{1,0:T(8,128)(2,1)S(1)}, bf16[256,512]{1,0:T(8,128)(2,1)S(1)}, u32[]{:S(2)}, u32[]{:S(2)}) collective-permute-start(bf16[256,512]{1,0:T(8,128)(2,1)S(1)} %get-tuple-element.23), channel_id=1, source_target_pairs={{0,2},{2,0},{1,3},{3,1},{4,6},{6,4},{5,7},{7,5},{8,10},{10,8},{9,1... | collective-permute-start | bytes 786440 | tf_op jit(solution)/shard_map/ppermute | solution.py:270
  152.7 14.7 %collective-permute-start.10 = (bf16[256,1024]{1,0:T(8,128)(2,1)S(1)}, bf16[256,1024]{1,0:T(8,128)(2,1)S(1)}, u32[]{:S(2)}, u32[]{:S(2)}) collective-permute-start(bf16[256,1024]{1,0:T(8,128)(2,1)S(1)} %get-tuple-element.25.refs_0_), channel_id=1, source_target_pairs={{0,1},{1,0},{2,3},{3,2},{4,5},{5,4},{6,7},{7,6},{8,9},{9,8},{10,11... | collective-permute-start | bytes 1572872 | tf_op jit(solution)/shard_map/ppermute | solution.py:330
  155.3 23.4 %collective-permute-start.7 = (bf16[256,1024]{1,0:T(8,128)(2,1)S(1)}, bf16[256,1024]{1,0:T(8,128)(2,1)S(1)}, u32[]{:S(2)}, u32[]{:S(2)}) collective-permute-start(bf16[256,1024]{1,0:T(8,128)(2,1)S(1)} %get-tuple-element.26.refs_1_), channel_id=1, source_target_pairs={{0,1},{1,0},{2,3},{3,2},{4,5},{5,4},{6,7},{7,6},{8,9},{9,8},{10,11... | collective-permute-start | bytes 1572872 | tf_op jit(solution)/shard_map/ppermute | solution.py:330
  155.8 4.0 %copy-start = (bf16[1024,5120]{1,0:T(8,128)(2,1)S(1)}, bf16[1024,5120]{1,0:T(8,128)(2,1)}, u32[]{:S(2)}) copy-start(bf16[1024,5120]{1,0:T(8,128)(2,1)} %refs_2_.1) | copy-start | bytes 31457284

commit v3 on v2

v3 whole, which is shorter than its diff:
```python
import functools

import jax
import jax.numpy as jnp
from jax import lax
from jax.experimental import pallas as pl
from jax.experimental.pallas import tpu as pltpu
from jax.sharding import Mesh
from jax.sharding import PartitionSpec as P

STEPS = 2
CTX = ("z", "xl", "y", "c")
CHIPS = ("z", "xl", "y")
SWAP = [(0, 1), (1, 0)]
ACROSS = [(0, 3), (3, 0), (1, 2), (2, 1)]
BF = jnp.bfloat16
F32 = jnp.float32
NT = (((1,), (1,)), ((), ()))
TN = (((0,), (0,)), ((), ()))
VMEM = pl.BlockSpec(memory_space=pltpu.VMEM)
SMEM = pl.BlockSpec(memory_space=pltpu.SMEM)
LIMIT = 24 * 1024 * 1024
CHUNKS = 2


def dot(x, y):
    return jnp.dot(x, y, preferred_element_type=F32)


def nt(x, y):
    return lax.dot_general(x, y, NT, preferred_element_type=F32)


def tn(x, y):
    return lax.dot_general(x, y, TN, preferred_element_type=F32)


def call(kernel, outs, n_in, flops, nbytes, smem=0, scratch=()):
    return pl.pallas_call(
        kernel,
        out_shape=outs,
        in_specs=[SMEM] * smem + [VMEM] * (n_in - smem),
        out_specs=jax.tree.map(lambda _: VMEM, outs),
        scratch_shapes=list(scratch),
        compiler_params=pltpu.CompilerParams(vmem_limit_bytes=LIMIT),
        cost_estimate=pl.CostEstimate(flops=flops, bytes_accessed=nbytes, transcendentals=0),
    )


def shape(dims, dtype=BF):
    return jax.ShapeDtypeStruct(dims, dtype)


def prepare_kernel(core, up, gate, down, w13, w2, norm):
    half = w2.shape[0]
    for i, w in enumerate((up, gate, down)):
        full = w[...].astype(F32)
        norm[i : i + 1, :] = jnp.full((1, 128), jnp.sum(full * full), F32)
    norm[3:8, :] = jnp.zeros((5, 128), F32)
    for c in range(2):

        @pl.when(core[0] == c)
        def _():
            w13[0:half, :] = up[:, c * half : (c + 1) * half].T
            w13[half:, :] = gate[:, c * half : (c + 1) * half].T
            w2[...] = down[c * half : (c + 1) * half, :]


def factor(i, norm, own, oth):
    size = jnp.sqrt(norm[i : i + 1, 0:1])
    total = own[i : i + 1, 0:1] + oth[i : i + 1, 0:1]
    return size / jnp.sqrt(total + 1e-06)


def raw_kernel(w13, w2, keys, targets, raw):
    raw[0 : w13.shape[0], :] = nt(w13[...], keys[...])
    raw[w13.shape[0] :, :] = nt(w2[...], targets[...])


def act_grads(act, lin, err, scale):
    if scale is not None:
        act, lin, err = (x * f for x, f in zip((act, lin, err), scale))
    sig = jax.nn.sigmoid(act)
    silu = act * sig
    hidden = (silu * lin).astype(BF)
    pgrad = (err * lin * sig * (1.0 + act * (1.0 - sig))).astype(BF)
    qgrad = (err * silu).astype(BF)
    return pgrad, qgrad, hidden


def grads_kernel(w13, w2, raw, k_own, k_oth, u_own, u_oth, *rest):
    *state, out = rest
    half = w2.shape[0]
    cols = k_own.shape[1] // 2
    scale = [factor(i, *state) for i in (0, 1, 2)] if state else None
    keys, targets = k_oth[...], u_oth[...]
    oth = act_grads(
        nt(w13[0:half, :], keys), nt(w13[half:, :], keys), nt(w2[...], targets), scale
    )
    own = act_grads(raw[0:half, :], raw[half : 2 * half, :], raw[2 * half :, :], scale)
    for i in range(3):
        x, y = (k_own, k_oth) if i < 2 else (u_own, u_oth)
        for j in range(2):
            at = slice(j * cols, (j + 1) * cols)
            g = dot(own[i], x[:, at]) + dot(oth[i], y[:, at])
            out[j, i * half : (i + 1) * half, :] = g.astype(BF)


ROWS = 16


def update_kernel(w13, w2, gathered, *rest):
    *again, m13, m2, squares = rest
    half = w2.shape[0]
    cols = w2.shape[1] // 2
    for i in range(3):
        src, dst = (w13, m13) if i < 2 else (w2, m2)
        base = (i % 2) * half
        if again:
            scale = jnp.broadcast_to(factor(i, *again[:3]), (ROWS, cols))

        def step(r, total):
            row = pl.multiple_of(base + r * ROWS, ROWS)
            at = pl.multiple_of(i * half + r * ROWS, ROWS)
            for j in range(2):
                side = slice(j * cols, (j + 1) * cols)
                m = src[pl.ds(row, ROWS), side].astype(F32)
                m = m + gathered[j, pl.ds(at, ROWS), :].astype(F32)
                if again:
                    m = m * scale + again[3][j, pl.ds(at, ROWS), :].astype(F32)
                dst[pl.ds(row, ROWS), side] = m.astype(BF)
                total = total + m * m
            return total

        total = lax.fori_loop(0, half // ROWS, step, jnp.zeros((ROWS, cols), F32))
        squares[i : i + 1, :] = jnp.full((1, 128), jnp.sum(total), F32)
    squares[3:8, :] = jnp.zeros((5, 128), F32)


def query_kernel(m13, q_oth, q_own, raw):
    raw[0] = nt(m13[...], q_oth[...])
    raw[1] = nt(m13[...], q_own[...])


def hidden_kernel(k, raw, norm, sq_own, sq_oth, hq):
    half = hq.shape[0]
    act = raw[k, 0:half, :] * factor(0, norm, sq_own, sq_oth)
    lin = raw[k, half:, :] * factor(1, norm, sq_own, sq_oth)
    hq[...] = (jax.nn.silu(act) * lin).astype(BF)


def piece_kernel(hq_own, hq_got, w2_own, w2_got, norm, sq_own, sq_oth, *pieces):
    count = pieces[0].shape[0]
    scale = factor(2, norm, sq_own, sq_oth)
    for k, o in enumerate(pieces):
        at = slice(k * count, (k + 1) * count)
        total = tn(hq_own[:, at], w2_own[...]) + tn(hq_got[:, at], w2_got[...])
        o[...] = (total * scale).astype(BF)


def spread_kernel(arrived, out):
    total = arrived[0].astype(F32)
    for i in range(1, arrived.shape[0]):
        total = total + arrived[i].astype(F32)
    rounded = total.astype(BF)
    for i in range(arrived.shape[0]):
        out[i] = rounded


TILE = 512


def partial_kernel(place, *refs):
    *pieces, w_own, out = refs
    count = pieces[0].shape[0]
    for k, o in enumerate(pieces):
        out[k * count : (k + 1) * count, :] = dot(o[...], w_own[...])


def partial_product(place, pieces, w_out):
    count, width = pieces[0].shape
    n = w_out.shape[1] // 2
    steps = n // TILE
    tokens = count * len(pieces)
    return pl.pallas_call(
        partial_kernel,
        out_shape=shape((tokens, n), F32),
        grid_spec=pltpu.PrefetchScalarGridSpec(
            num_scalar_prefetch=1,
            grid=(steps,),
            in_specs=[pl.BlockSpec((count, width), lambda i, s: (0, 0))] * len(pieces)
            + [pl.BlockSpec((width, TILE), lambda i, s: (0, s[0] * steps + i))],
            out_specs=pl.BlockSpec((tokens, TILE), lambda i, s: (0, i)),
        ),
        compiler_params=pltpu.CompilerParams(vmem_limit_bytes=LIMIT),
        cost_estimate=pl.CostEstimate(
            flops=2 * tokens * width * n, bytes_accessed=10 << 20, transcendentals=0
        ),
    )(place, *pieces, w_out)


def finish_kernel(k, place, part, o_got, w_first, w_second, *rest):
    *_, out, held, sems = rest
    count, width = o_got.shape
    half = width // 2
    rows = slice(k * count, (k + 1) * count)
    o_first = o_got[:, pl.ds(pl.multiple_of(place[1] * half, 128), half)]
    o_second = o_got[:, pl.ds(pl.multiple_of((1 - place[1]) * half, 128), half)]
    copies = []
    for j in range(part.shape[1] // TILE):
        at = slice(j * TILE, (j + 1) * TILE)
        total = part[rows, at] + dot(o_first, w_first[:, at]) + dot(o_second, w_second[:, at])
        held[j] = total.astype(BF)
        copies.append(pltpu.make_async_copy(held.at[j], out.at[rows, at], sems.at[j]))
        copies[-1].start()
    for copy in copies:
        copy.wait()


def finish_product(place, k, part, o_got, w_first, w_second, out):
    count, width = o_got.shape
    tokens, n = part.shape
    near = [pltpu.with_memory_space_constraint(x, pltpu.VMEM) for x in (part, o_got, w_first, w_second)]
    args = (place, *near)
    return pl.pallas_call(
        functools.partial(finish_kernel, k),
        out_shape=shape((tokens, n)),
        in_specs=[SMEM] + [VMEM] * 4 + [pl.BlockSpec(memory_space=pl.ANY)] * (out is not None),
        out_specs=pl.BlockSpec(memory_space=pl.ANY),
        scratch_shapes=[
            pltpu.VMEM((n // TILE, count, TILE), BF),
            pltpu.SemaphoreType.DMA((n // TILE,)),
        ],
        input_output_aliases={} if out is None else {len(args): 0},
        compiler_params=pltpu.CompilerParams(vmem_limit_bytes=LIMIT),
        cost_estimate=pl.CostEstimate(
            flops=2 * count * width * n, bytes_accessed=4 << 20, transcendentals=0
        ),
    )(*args, *(() if out is None else (out,)))


def all_reduced(grads):
    peers = lax.axis_size(CHIPS)
    pieces = grads.reshape(peers, -1, grads.shape[2])
    arrived = lax.all_to_all(pieces, CHIPS, 0, 0, tiled=True)
    copies = call(spread_kernel, shape(pieces.shape), 1, pieces.size, 4 * pieces.size)(arrived)
    gathered = lax.all_to_all(copies, CHIPS, 0, 0, tiled=True)
    return gathered.reshape(grads.shape)


def swap(x):
    return lax.ppermute(x, "c", SWAP)


def shards(queries, keys, values, rates, w_up, w_gate, w_down, w_out):
    width, hid = w_up.shape[1:]
    tokens = keys.shape[0]
    half, third = hid // 2, 3 * hid // 2
    core, head = lax.axis_index("c"), lax.axis_index("h")
    n = w_out.shape[1] // 2

    k_oth = swap(keys)
    targets = (rates * values.astype(F32)).astype(BF)
    u_oth = swap(targets)
    kus = (keys, k_oth, targets, u_oth)

    place = jnp.stack([head, core]).astype(jnp.int32)
    sent = lax.dynamic_slice(w_out, (core * (width // 2), (1 - head) * n), (width // 2, n))
    w_first = lax.ppermute(sent, ("xl", "h"), ACROSS)
    w_second = swap(w_first)
    q_oth = swap(queries)

    wshape = (shape((2 * half, width)), shape((half, width)))
    sshape = shape((8, 128), F32)
    *w, norm = call(prepare_kernel, (*wshape, sshape), 4, 1 << 21, 5 << 20, smem=1)(
        core.reshape(1).astype(jnp.int32), w_up[0], w_gate[0], w_down[0]
    )
    flops = 12 * 2 * tokens * width * half
    state, mats, again = (), w, ()
    for step in range(STEPS):
        raw = call(raw_kernel, shape((third, tokens), F32), 4, flops // 4, 4 << 20)(
            *mats, keys, targets
        )
        grads = call(
            grads_kernel,
            shape((2, third, width // 2)),
            7 + len(state),
            flops * 3 // 4,
            8 << 20,
        )(*mats, raw, keys, k_oth, targets, u_oth, *state)
        gathered = all_reduced(grads)
        first = gathered if step == 0 else first
        again = () if step == 0 else (*state, gathered)
        *mats, squares = call(
            update_kernel, (*wshape, sshape), 3 + len(again), 1 << 22, 5 << 20
        )(*w, first, *again)
        state = (norm, squares, swap(squares))
    w2_got = swap(mats[1])
    hshape = shape((half, tokens))
    raw = call(query_kernel, shape((2, 2 * half, tokens), F32), 3, flops // 3, 5 << 20)(
        mats[0], q_oth, queries
    )
    hq_oth, hq_own = (
        call(functools.partial(hidden_kernel, k), hshape, 4, 1 << 20, 2 << 20)(raw, *state)
        for k in range(2)
    )
    pieces = call(
        piece_kernel,
        (shape((tokens // CHUNKS, width)),) * CHUNKS,
        7,
        2 * tokens * hid * width,
        4 << 20,
    )(hq_own, swap(hq_oth), mats[1], w2_got, *state)
    pieces_got = [lax.ppermute(o, "h", SWAP) for o in pieces]
    part = partial_product(place, pieces, w_out)
    out = None
    for k, o_got in enumerate(pieces_got):
        out = finish_product(place, k, part, o_got, w_first, w_second, out)
    return out


def solution(mesh):
    finer = Mesh(
        mesh.devices.reshape(4, 2, 4, 2, mesh.shape["head"]),
        ("z", "xl", "y", "c", "h"),
    )
    return jax.shard_map(
        shards,
        mesh=finer,
        in_specs=(
            P(CTX, "h"),
            P(CTX, "h"),
            P(CTX, "h"),
            P(CTX, "h"),
            P("h", None, None),
            P("h", None, None),
            P("h", None, None),
            P("h", None),
        ),
        out_specs=P(CTX, "h"),
        check_vma=False,
    )
```

time: 186 us -> 185 us (level)
  Pallas kernels: 40.1 us -> 35.2 us
  waiting for transfers between devices: 45.3 us -> 48.6 us
    ppermute x2, waiting for transfers between devices: 7.99 us -> 13.1 us  [shards(): pieces_got = [lax.ppermute(o, 'h', SWAP) for o in pieces]]
    pallas_call x11 -> x13, Pallas kernels: 33.5 us -> 29.8 us  [the longest x2 9.65 us: finish_product(): pl.pallas_call(functools.partial(finish_kernel, k), out_shape=shape((toke...]
    unnamed x28 -> x36, local copies, waits for them, and re-layouts: 11 us -> 11.5 us
  transfers between devices with their start and end apart: 13 -> 13, of which waited for: 7 -> 5; matrix products, arithmetic and copies ran while one was open for 2% -> 2% of each run, Pallas kernels for 15% -> 14%
where the time goes in v3:
time: 185 us; the launch traced here: 184 us
  blocking collectives  57.5 us (31%)
  waiting for transfers between devices  48.6 us (26%)
  Pallas kernels  35.2 us (19%)
  starting transfers between devices  25.7 us (14%)
  local copies, waits for them, and re-layouts  14.9 us (8%)
    all_to_all x2, blocking collectives, all_reduced(): arrived = lax.all_to_all(pieces, CHIPS, 0, 0, tiled=True)  57.5 us
    all_to_all x2, waiting for transfers between devices, all_reduced(): gathered = lax.all_to_all(copies, CHIPS, 0, 0, tiled=True)  34.5 us
    ppermute x2, waiting for transfers between devices, shards(): pieces_got = [lax.ppermute(o, 'h', SWAP) for o in pieces]  13.1 us
    unnamed x36, local copies, waits for them, and re-layouts  11.5 us
    all_to_all x2, starting transfers between devices, all_reduced(): gathered = lax.all_to_all(copies, CHIPS, 0, 0, tiled=True)  11.4 us
    pallas_call x2, Pallas kernels, finish_product(): pl.pallas_call(functools.partial(finish_kernel, k), out_shape=shape((toke...  9.65 us
    pallas_call x2, Pallas kernels, shards(): call(grads_kernel, shape((2, third, width // 2)), 7 + len(state), flops *...  8.87 us
    ppermute x8, starting transfers between devices, swap(): return lax.ppermute(x, 'c', SWAP)  8.7 us
  transfers between devices with their start and end apart: 13, of which 5 were waited for; matrix products, arithmetic and copies ran while one was open for 2% of the time, Pallas kernels for 14%

profile of v3, /device:TPU:1, one launch (start us, length us, event | category | flops | bytes accessed | tf_op | source)
XLA Modules:
  0.0 184.0 jit_solution(7817124933336917635)
XLA Ops:
  0.0 1.5 multiply_convert_fusion.targets.u_own
  1.6 1.5 collective-permute-start.1
  3.1 0.0 copy-done.9
  3.1 0.1 collective-permute-start
  3.2 1.2 copy-done.12
  4.4 1.2 copy-done.13
  5.6 1.2 copy-done.14
  6.8 1.2 shard_map.82
  8.0 0.0 copy-start.2
  8.0 0.0 copy-start.7
  8.0 1.0 shard_map.83.raw
  9.0 0.0 collective-permute-done.1.u_oth
  9.1 0.0 collective-permute-done.k_oth
  9.1 0.0 copy-done.2
  9.1 4.4 %shard_map.84 = bf16[2,768,512]{2,1,0:T(8,128)(2,1)S(1)} custom-call(bf16[512,1024]{1,0:T(8,128)(2,1)S(1)} %get-tuple-element.16.w13, bf16[256,1024]{1,0:T(8,128)(2,1)S(1)} %get-tuple-element.17.w2, f32[768,512]{1,0:T(8,128)S(1)} %shard_map.83.raw, bf16[512,1024]{1,0:T(8,128)(2,1)S(1)} %copy-done.9, bf16[512,1024]{1,0:T(8,128)(2,1)} %collective-permute-done.k_oth, ...), custom_call_target="tpu_custom_call" | custom-call | flops 2415919104 | bytes 8388608 | tf_op jit(solution)/shard_map/pallas_call | solution.py:284
  13.5 30.2 %all_to_all.20.arrived = bf16[32,48,512]{2,1,0:T(8,128)(2,1)S(1)} all-to-all(bf16[32,48,512]{2,1,0:T(8,128)(2,1)S(1)} %bitcast.15), channel_id=1, replica_groups=mesh['z'=4,'xl'=2,'y'=4,'c'=2,'h'=2] {'z','xl','y'}, dimensions={0} | all-to-all | bytes 3145728 | tf_op jit(solution)/shard_map/all_to_all | solution.py:245
  43.7 0.3 shard_map.85
  44.0 0.0 copy-start.5
  44.0 1.1 copy-done.5
  45.2 5.7 %all-to-all-start.1 = ((bf16[32,48,512]{2,1,0:T(8,128)(2,1)}), bf16[32,48,512]{2,1,0:T(8,128)(2,1)S(1)}, u32[]{:S(2)}, u32[]{:S(2)}) async-start(bf16[32,48,512]{2,1,0:T(8,128)(2,1)} %copy-done.5), calls=%async_computation.1 | async-start | bytes 3145728 | tf_op jit(solution)/shard_map/all_to_all | solution.py:247
  50.9 3.4 %dynamic_slice.3 = bf16[512,2560]{1,0:T(8,128)(2,1)} dynamic-slice(bf16[1024,5120]{1,0:T(8,128)(2,1)} %refs_2_.1, s32[]{:T(128)S(6)} %select_n.6, s32[]{:T(128)S(6)} %select_n.7), dynamic_slice_sizes={512,2560} | dynamic-slice | bytes 5242884 | tf_op jit(solution)/shard_map/dynamic_slice | solution.py:268
  54.3 2.5 %collective-permute-start.8 = (bf16[512,2560]{1,0:T(8,128)(2,1)}, bf16[512,2560]{1,0:T(8,128)(2,1)}, u32[]{:S(2)}, u32[]{:S(2)}) collective-permute-start(bf16[512,2560]{1,0:T(8,128)(2,1)} %dynamic_slice.3), channel_id=1, source_target_pairs={{0,17},{17,0},{1,16},{16,1},{2,19},{19,2},{3,18},{18,3},{4,21},{21... | collective-permute-start | bytes 7864328 | tf_op jit(solution)/shard_map/ppermute | solution.py:269
  56.8 15.0 %all-to-all-done.1 = bf16[32,48,512]{2,1,0:T(8,128)(2,1)S(1)} async-done(((bf16[32,48,512]{2,1,0:T(8,128)(2,1)}), bf16[32,48,512]{2,1,0:T(8,128)(2,1)S(1)}, u32[]{:S(2)}, u32[]{:S(2)}) %all-to-all-start.1) | async-done | bytes 1572896 | tf_op jit(solution)/shard_map/all_to_all | solution.py:247
  71.9 0.0 copy-done.7
  71.9 1.8 copy-done.3
  73.7 1.2 shard_map.86
  74.8 2.5 %collective-permute-start.2 = (f32[8,128]{1,0:T(8,128)S(1)}, f32[8,128]{1,0:T(8,128)S(1)}, u32[]{:S(2)}, u32[]{:S(2)}) collective-permute-start(f32[8,128]{1,0:T(8,128)S(1)} %get-tuple-element.19.rest_1_), channel_id=1, source_target_pairs={{0,2},{2,0},{1,3},{3,1},{4,6},{6,4},{5,7},{7,5},{8,10},{10,8},{9,1... | collective-permute-start | bytes 12296 | tf_op jit(solution)/shard_map/ppermute | solution.py:252
  77.4 0.0 copy-done.10
  77.4 1.0 shard_map.87.raw
  78.4 0.0 collective-permute-done.2.rest_2_
  78.4 4.5 %shard_map.88 = bf16[2,768,512]{2,1,0:T(8,128)(2,1)S(1)} custom-call(bf16[512,1024]{1,0:T(8,128)(2,1)S(1)} %get-tuple-element.20.w13, bf16[256,1024]{1,0:T(8,128)(2,1)S(1)} %get-tuple-element.21.w2, f32[768,512]{1,0:T(8,128)S(1)} %shard_map.87.raw, bf16[512,1024]{1,0:T(8,128)(2,1)S(1)} %copy-done.10, bf16[512,1024]{1,0:T(8,128)(2,1)} %collective-permute-done.k_oth, ...), custom_call_target="tpu_custom_call" | custom-call | flops 2415919104 | bytes 8388608 | tf_op jit(solution)/shard_map/pallas_call | solution.py:284
  82.9 27.3 %all_to_all.21.arrived = bf16[32,48,512]{2,1,0:T(8,128)(2,1)S(1)} all-to-all(bf16[32,48,512]{2,1,0:T(8,128)(2,1)S(1)} %bitcast.14), channel_id=1, replica_groups=mesh['z'=4,'xl'=2,'y'=4,'c'=2,'h'=2] {'z','xl','y'}, dimensions={0} | all-to-all | bytes 3145728 | tf_op jit(solution)/shard_map/all_to_all | solution.py:245
  110.1 0.3 shard_map.89
  110.5 1.2 copy-done.6
  111.6 5.7 %all-to-all-start.3 = ((bf16[32,48,512]{2,1,0:T(8,128)(2,1)}), bf16[32,48,512]{2,1,0:T(8,128)(2,1)}, u32[]{:S(2)}, u32[]{:S(2)}) async-start(bf16[32,48,512]{2,1,0:T(8,128)(2,1)} %copy-done.6), calls=%async_computation.3 | async-start | bytes 3145728 | tf_op jit(solution)/shard_map/all_to_all | solution.py:247
  117.3 0.0 collective-permute-done.8.w_first
  117.3 1.4 collective-permute-start.9
  118.7 0.1 collective-permute-start.3
  118.8 19.5 %all-to-all-done.3 = bf16[32,48,512]{2,1,0:T(8,128)(2,1)} async-done(((bf16[32,48,512]{2,1,0:T(8,128)(2,1)}), bf16[32,48,512]{2,1,0:T(8,128)(2,1)}, u32[]{:S(2)}, u32[]{:S(2)}) %all-to-all-start.3) | async-done | bytes 1572896 | tf_op jit(solution)/shard_map/all_to_all | solution.py:247
  138.3 1.4 copy-done.1
  139.7 1.0 copy-done.8
  140.7 3.1 %shard_map.90 = (bf16[512,1024]{1,0:T(8,128)(2,1)S(1)}, bf16[256,1024]{1,0:T(8,128)(2,1)S(1)}, f32[8,128]{1,0:T(8,128)S(1)}) custom-call(bf16[512,1024]{1,0:T(8,128)(2,1)S(1)} %copy-done.4, bf16[256,1024]{1,0:T(8,128)(2,1)S(1)} %copy-done.8, bf16[2,768,512]{2,1,0:T(8,128)(2,1)S(1)} %bitcast.13, f32[8,128]{1,0:T(8,128)S(1)} %get-tuple-element.18.rest_0_.norm, ...), custom_call_target="tpu_custom_call" | custom-call | flops 4194304 | bytes 5242880 | tf_op jit(solution)/shard_map/pallas_call | solution.py:294
  143.9 2.5 %collective-permute-start.6 = (bf16[256,1024]{1,0:T(8,128)(2,1)S(1)}, bf16[256,1024]{1,0:T(8,128)(2,1)S(1)}, u32[]{:S(2)}, u32[]{:S(2)}) collective-permute-start(bf16[256,1024]{1,0:T(8,128)(2,1)S(1)} %get-tuple-element.24.w2_own), channel_id=1, source_target_pairs={{0,2},{2,0},{1,3},{3,1},{4,6},{6,4},{5,7},{7,5},{8,10},{10,8},{9,1... | collective-permute-start | bytes 1572872 | tf_op jit(solution)/shard_map/ppermute | solution.py:252
  146.4 0.1 collective-permute-start.4
  146.5 0.0 collective-permute-done.3.q_oth
  146.5 1.2 copy-done.11
  147.7 2.7 %shard_map.91.raw = f32[2,512,512]{2,1,0:T(8,128)S(1)} custom-call(bf16[512,1024]{1,0:T(8,128)(2,1)S(1)} %get-tuple-element.22.m13, bf16[512,1024]{1,0:T(8,128)(2,1)} %collective-permute-done.3.q_oth, bf16[512,1024]{1,0:T(8,128)(2,1)S(1)} %copy-done.11), custom_call_target="tpu_custom_call" | custom-call | flops 1073741824 | bytes 5242880 | tf_op jit(solution)/shard_map/pallas_call | solution.py:300
  150.4 0.0 collective-permute-done.4.sq_oth
  150.4 0.2 shard_map.93
  150.6 0.5 collective-permute-start.5
  151.1 0.2 shard_map.92.hq_own
  151.3 1.0 collective-permute-done.5.hq_got
  152.3 0.0 collective-permute-done.6.w2_got
  152.3 0.7 shard_map.94
  153.0 2.6 %collective-permute-start.10 = (bf16[256,1024]{1,0:T(8,128)(2,1)S(1)}, bf16[256,1024]{1,0:T(8,128)(2,1)S(1)}, u32[]{:S(2)}, u32[]{:S(2)}) collective-permute-start(bf16[256,1024]{1,0:T(8,128)(2,1)S(1)} %get-tuple-element.25.refs_0_), channel_id=1, source_target_pairs={{0,1},{1,0},{2,3},{3,2},{4,5},{5,4},{6,7},{7,6},{8,9},{9,8},{10,11... | collective-permute-start | bytes 1572872 | tf_op jit(solution)/shard_map/ppermute | solution.py:314
  155.6 0.5 collective-permute-start.7
  156.1 0.1 pad_add_fusion.place
  156.1 0.0 slice-done.1
  156.1 4.8 %shard_map.95.part = f32[512,2560]{1,0:T(8,128)S(1)} custom-call(s32[2]{0:T(128)S(1)} %pad_add_fusion.place, bf16[256,1024]{1,0:T(8,128)(2,1)S(1)} %get-tuple-element.25.refs_0_, bf16[256,1024]{1,0:T(8,128)(2,1)S(1)} %get-tuple-element.26.refs_1_, bf16[1024,5120]{1,0:T(8,128)(2,1)S(1)} %bitcast.11), custom_call_target="tpu_custom_call" | custom-call | flops 2684354560 | bytes 10485760 | tf_op jit(solution)/shard_map/pallas_call | solution.py:185
  161.0 0.0 collective-permute-done.9.w_second
  161.0 6.7 %collective-permute-done.10.o_got = bf16[256,1024]{1,0:T(8,128)(2,1)S(1)} collective-permute-done((bf16[256,1024]{1,0:T(8,128)(2,1)S(1)}, bf16[256,1024]{1,0:T(8,128)(2,1)S(1)}, u32[]{:S(2)}, u32[]{:S(2)}) %collective-permute-start.10) | collective-permute-done | bytes 524320 | tf_op jit(solution)/shard_map/ppermute | solution.py:314
  167.7 4.8 %shard_map.96.rest_0_ = bf16[512,2560]{1,0:T(8,128)(2,1)} custom-call(s32[2]{0:T(128)S(1)} %pad_add_fusion.place, f32[512,2560]{1,0:T(8,128)S(1)} %shard_map.95.part, bf16[256,1024]{1,0:T(8,128)(2,1)S(1)} %collective-permute-done.10.o_got, bf16[512,2560]{1,0:T(8,128)(2,1)} %collective-permute-done.8.w_first, bf16[512,2560]{1,0:T(8,128)(2,1)} %collective-permute-done.9.w_second), custom_call_target="tpu_custom_call" | custom-call | flops 1342177280 | bytes 4194304 | tf_op jit(solution)/shard_map/pallas_call | solution.py:225
  172.6 6.4 %collective-permute-done.7.o_got = bf16[256,1024]{1,0:T(8,128)(2,1)S(1)} collective-permute-done((bf16[256,1024]{1,0:T(8,128)(2,1)S(1)}, bf16[256,1024]{1,0:T(8,128)(2,1)S(1)}, u32[]{:S(2)}, u32[]{:S(2)}) %collective-permute-start.7) | collective-permute-done | bytes 524320 | tf_op jit(solution)/shard_map/ppermute | solution.py:314
  179.0 4.8 %shard_map.97 = bf16[512,2560]{1,0:T(8,128)(2,1)} custom-call(s32[2]{0:T(128)S(1)} %pad_add_fusion.place, f32[512,2560]{1,0:T(8,128)S(1)} %shard_map.95.part, bf16[256,1024]{1,0:T(8,128)(2,1)S(1)} %collective-permute-done.7.o_got, bf16[512,2560]{1,0:T(8,128)(2,1)} %collective-permute-done.8.w_first, ...), custom_call_target="tpu_custom_call", output_to_operand_aliasing={{}: (5, {})} | custom-call | flops 1342177280 | bytes 4194304 | tf_op jit(solution)/shard_map/pallas_call | solution.py:225
  (20 shorter events, 0.0 us)
Async XLA Ops:
  0.0 3.1 %copy-start.9 = (bf16[512,1024]{1,0:T(8,128)(2,1)S(1)}, bf16[512,1024]{1,0:T(8,128)(2,1)}, u32[]{:S(2)}) copy-start(bf16[512,1024]{1,0:T(8,128)(2,1)} %k_own.3) | copy-start | bytes 3145732
  1.6 7.5 %collective-permute-start.1 = (bf16[512,1024]{1,0:T(8,128)(2,1)S(1)}, bf16[512,1024]{1,0:T(8,128)(2,1)}, u32[]{:S(2)}, u32[]{:S(2)}) collective-permute-start(bf16[512,1024]{1,0:T(8,128)(2,1)S(1)} %multiply_convert_fusion.targets.u_own), channel_id=1, source_target_pairs={{0,2},{2,0},{1,3},{3,1},{4,6},{6,4},{5,7},{7,5},{8,10},{10,8},{9,1... | collective-permute-start | bytes 3145736 | tf_op jit(solution)/shard_map/ppermute | solution.py:252
  3.1 6.0 %collective-permute-start = (bf16[512,1024]{1,0:T(8,128)(2,1)S(1)}, bf16[512,1024]{1,0:T(8,128)(2,1)}, u32[]{:S(2)}, u32[]{:S(2)}) collective-permute-start(bf16[512,1024]{1,0:T(8,128)(2,1)S(1)} %copy-done.9), channel_id=1, source_target_pairs={{0,2},{2,0},{1,3},{3,1},{4,6},{6,4},{5,7},{7,5},{8,10},{10,8},{9,1... | collective-permute-start | bytes 3145736 | tf_op jit(solution)/shard_map/ppermute | solution.py:252
  3.2 1.2 copy-start.12
  4.4 1.2 copy-start.13
  5.6 1.2 copy-start.14
  8.0 1.1 copy-start.2
  8.0 63.8 %copy-start.7 = (bf16[256,1024]{1,0:T(8,128)(2,1)}, bf16[256,1024]{1,0:T(8,128)(2,1)S(1)}, u32[]{:S(2)}) copy-start(bf16[256,1024]{1,0:T(8,128)(2,1)S(1)} %get-tuple-element.17.w2) | copy-start | bytes 1572868
  44.0 1.2 copy-start.5
  45.2 26.7 %all-to-all-start.1 = ((bf16[32,48,512]{2,1,0:T(8,128)(2,1)}), bf16[32,48,512]{2,1,0:T(8,128)(2,1)S(1)}, u32[]{:S(2)}, u32[]{:S(2)}) async-start(bf16[32,48,512]{2,1,0:T(8,128)(2,1)} %copy-done.5), calls=%async_computation.1 | async-start | bytes 3145728 | tf_op jit(solution)/shard_map/all_to_all | solution.py:247
  54.3 63.0 %collective-permute-start.8 = (bf16[512,2560]{1,0:T(8,128)(2,1)}, bf16[512,2560]{1,0:T(8,128)(2,1)}, u32[]{:S(2)}, u32[]{:S(2)}) collective-permute-start(bf16[512,2560]{1,0:T(8,128)(2,1)} %dynamic_slice.3), channel_id=1, source_target_pairs={{0,17},{17,0},{1,16},{16,1},{2,19},{19,2},{3,18},{18,3},{4,21},{21... | collective-permute-start | bytes 7864328 | tf_op jit(solution)/shard_map/ppermute | solution.py:269
  71.9 6.5 %copy-start = (bf16[32,48,512]{2,1,0:T(8,128)(2,1)}, bf16[32,48,512]{2,1,0:T(8,128)(2,1)S(1)}, u32[]{:S(2)}) copy-start(bf16[32,48,512]{2,1,0:T(8,128)(2,1)S(1)} %all-to-all-done.1) | copy-start | bytes 4718596
  71.9 1.8 copy-start.3
  73.7 3.7 %copy-start.10 = (bf16[512,1024]{1,0:T(8,128)(2,1)S(1)}, bf16[512,1024]{1,0:T(8,128)(2,1)}, u32[]{:S(2)}) copy-start(bf16[512,1024]{1,0:T(8,128)(2,1)} %k_own.3) | copy-start | bytes 3145732
  74.8 3.6 %collective-permute-start.2 = (f32[8,128]{1,0:T(8,128)S(1)}, f32[8,128]{1,0:T(8,128)S(1)}, u32[]{:S(2)}, u32[]{:S(2)}) collective-permute-start(f32[8,128]{1,0:T(8,128)S(1)} %get-tuple-element.19.rest_1_), channel_id=1, source_target_pairs={{0,2},{2,0},{1,3},{3,1},{4,6},{6,4},{5,7},{7,5},{8,10},{10,8},{9,1... | collective-permute-start | bytes 12296 | tf_op jit(solution)/shard_map/ppermute | solution.py:252
  110.1 46.0 %slice-start = ((s8[10485760]{0:T(1024)(128)(4,1)}), s8[2097152]{0:T(1024)(128)(4,1)S(1)}, s32[]{:S(2)}) async-start(s8[10485760]{0:T(1024)(128)(4,1)} %bitcast.10), calls=%async_computation.4 | async-start | bytes 4194304
  110.4 1.2 copy-start.6
  111.6 26.7 %copy-start.4 = (bf16[512,1024]{1,0:T(8,128)(2,1)S(1)}, bf16[512,1024]{1,0:T(8,128)(2,1)}, u32[]{:S(2)}) copy-start(bf16[512,1024]{1,0:T(8,128)(2,1)} %copy-done.2) | copy-start | bytes 3145732
  111.6 26.7 %all-to-all-start.3 = ((bf16[32,48,512]{2,1,0:T(8,128)(2,1)}), bf16[32,48,512]{2,1,0:T(8,128)(2,1)}, u32[]{:S(2)}, u32[]{:S(2)}) async-start(bf16[32,48,512]{2,1,0:T(8,128)(2,1)} %copy-done.6), calls=%async_computation.3 | async-start | bytes 3145728 | tf_op jit(solution)/shard_map/all_to_all | solution.py:247
  117.3 43.7 %collective-permute-start.9 = (bf16[512,2560]{1,0:T(8,128)(2,1)}, bf16[512,2560]{1,0:T(8,128)(2,1)}, u32[]{:S(2)}, u32[]{:S(2)}) collective-permute-start(bf16[512,2560]{1,0:T(8,128)(2,1)} %collective-permute-done.8.w_first), channel_id=1, source_target_pairs={{0,2},{2,0},{1,3},{3,1},{4,6},{6,4},{5,7},{7,5},{8,10},{10,8},{9,1... | collective-permute-start | bytes 7864328 | tf_op jit(solution)/shard_map/ppermute | solution.py:252
  118.7 27.8 %collective-permute-start.3 = (bf16[512,1024]{1,0:T(8,128)(2,1)}, bf16[512,1024]{1,0:T(8,128)(2,1)}, u32[]{:S(2)}, u32[]{:S(2)}) collective-permute-start(bf16[512,1024]{1,0:T(8,128)(2,1)} %q_own.1), channel_id=1, source_target_pairs={{0,2},{2,0},{1,3},{3,1},{4,6},{6,4},{5,7},{7,5},{8,10},{10,8},{9,1... | collective-permute-start | bytes 3145736 | tf_op jit(solution)/shard_map/ppermute | solution.py:252
  138.3 1.4 copy-start.1
  139.7 1.0 copy-start.8
  140.7 15.4 %slice-start.1 = ((s8[10485760]{0:T(1024)(128)(4,1)}), s8[4194304]{0:T(1024)(128)(4,1)S(1)}, s32[]{:S(2)}) async-start(s8[10485760]{0:T(1024)(128)(4,1)} %bitcast.10), calls=%async_computation.5 | async-start | bytes 8388608
  143.9 8.4 %collective-permute-start.6 = (bf16[256,1024]{1,0:T(8,128)(2,1)S(1)}, bf16[256,1024]{1,0:T(8,128)(2,1)S(1)}, u32[]{:S(2)}, u32[]{:S(2)}) collective-permute-start(bf16[256,1024]{1,0:T(8,128)(2,1)S(1)} %get-tuple-element.24.w2_own), channel_id=1, source_target_pairs={{0,2},{2,0},{1,3},{3,1},{4,6},{6,4},{5,7},{7,5},{8,10},{10,8},{9,1... | collective-permute-start | bytes 1572872 | tf_op jit(solution)/shard_map/ppermute | solution.py:252
  146.4 4.0 %collective-permute-start.4 = (f32[8,128]{1,0:T(8,128)S(1)}, f32[8,128]{1,0:T(8,128)S(1)}, u32[]{:S(2)}, u32[]{:S(2)}) collective-permute-start(f32[8,128]{1,0:T(8,128)S(1)} %get-tuple-element.23.sq_own), channel_id=1, source_target_pairs={{0,2},{2,0},{1,3},{3,1},{4,6},{6,4},{5,7},{7,5},{8,10},{10,8},{9,1... | collective-permute-start | bytes 12296 | tf_op jit(solution)/shard_map/ppermute | solution.py:252
  146.5 1.2 copy-start.11
  147.7 8.4 %slice-start.2 = ((s8[10485760]{0:T(1024)(128)(4,1)}), s8[4194304]{0:T(1024)(128)(4,1)S(1)}, s32[]{:S(2)}) async-start(s8[10485760]{0:T(1024)(128)(4,1)} %bitcast.10), calls=%async_computation.6 | async-start | bytes 8388608
  150.6 1.7 collective-permute-start.5
  153.0 14.7 %collective-permute-start.10 = (bf16[256,1024]{1,0:T(8,128)(2,1)S(1)}, bf16[256,1024]{1,0:T(8,128)(2,1)S(1)}, u32[]{:S(2)}, u32[]{:S(2)}) collective-permute-start(bf16[256,1024]{1,0:T(8,128)(2,1)S(1)} %get-tuple-element.25.refs_0_), channel_id=1, source_target_pairs={{0,1},{1,0},{2,3},{3,2},{4,5},{5,4},{6,7},{7,6},{8,9},{9,8},{10,11... | collective-permute-start | bytes 1572872 | tf_op jit(solution)/shard_map/ppermute | solution.py:314
  155.6 23.4 %collective-permute-start.7 = (bf16[256,1024]{1,0:T(8,128)(2,1)S(1)}, bf16[256,1024]{1,0:T(8,128)(2,1)S(1)}, u32[]{:S(2)}, u32[]{:S(2)}) collective-permute-start(bf16[256,1024]{1,0:T(8,128)(2,1)S(1)} %get-tuple-element.26.refs_1_), channel_id=1, source_target_pairs={{0,1},{1,0},{2,3},{3,2},{4,5},{5,4},{6,7},{7,6},{8,9},{9,8},{10,11... | collective-permute-start | bytes 1572872 | tf_op jit(solution)/shard_map/ppermute | solution.py:314

commit v4 on v3

--- a/solution.py
+++ b/solution.py
@@ -19,6 +19,8 @@
 TN = (((0,), (0,)), ((), ()))
 VMEM = pl.BlockSpec(memory_space=pltpu.VMEM)
 SMEM = pl.BlockSpec(memory_space=pltpu.SMEM)
+FAR = pl.BlockSpec(memory_space=pltpu.HBM)
+ANY = pl.BlockSpec(memory_space=pl.ANY)
 LIMIT = 24 * 1024 * 1024
 CHUNKS = 2
 
@@ -35,25 +37,54 @@
     return lax.dot_general(x, y, TN, preferred_element_type=F32)
 
 
-def call(kernel, outs, n_in, flops, nbytes, smem=0, scratch=()):
-    return pl.pallas_call(
+def call(kernel, outs, specs, flops, nbytes, scratch=(), far=False):
+    if far:
+        outs = jax.tree.map(lambda x: pltpu.HBM(x.shape, x.dtype), outs)
+    run = pl.pallas_call(
         kernel,
         out_shape=outs,
-        in_specs=[SMEM] * smem + [VMEM] * (n_in - smem),
-        out_specs=jax.tree.map(lambda _: VMEM, outs),
+        in_specs=specs,
+        out_specs=jax.tree.map(lambda _: FAR if far else VMEM, outs),
         scratch_shapes=list(scratch),
         compiler_params=pltpu.CompilerParams(vmem_limit_bytes=LIMIT),
         cost_estimate=pl.CostEstimate(flops=flops, bytes_accessed=nbytes, transcendentals=0),
     )
 
+    def with_places(*args):
+        return run(
+            *(
+                pltpu.with_memory_space_constraint(x, pltpu.HBM) if spec is FAR else x
+                for x, spec in zip(args, specs, strict=True)
+            )
+        )
+
+    return with_places
+
+
+def fetch(pairs, sems):
+    copies = [pltpu.make_async_copy(src, dst, sems.at[i]) for i, (src, dst) in enumerate(pairs)]
+    for copy in copies:
+        copy.start()
+    return copies
+
+
+def buffer(dims, dtype=BF):
+    return pltpu.VMEM(dims, dtype)
+
+
+def semaphores(n):
+    return pltpu.SemaphoreType.DMA((n,))
+
 
 def shape(dims, dtype=BF):
     return jax.ShapeDtypeStruct(dims, dtype)
 
 
-def prepare_kernel(core, up, gate, down, w13, w2, norm):
+def prepare_kernel(core, up_far, gate_far, down_far, w13, w2, norm, up, gate, down, sems):
+    copies = fetch(((up_far, up), (gate_far, gate), (down_far, down)), sems)
     half = w2.shape[0]
     for i, w in enumerate((up, gate, down)):
+        copies[i].wait()
         full = w[...].astype(F32)
         norm[i : i + 1, :] = jnp.full((1, 128), jnp.sum(full * full), F32)
     norm[3:8, :] = jnp.zeros((5, 128), F32)
@@ -88,36 +119,63 @@
     return pgrad, qgrad, hidden
 
 
-def grads_kernel(w13, w2, raw, k_own, k_oth, u_own, u_oth, *rest):
-    *state, out = rest
+def grads_kernel(w13, w2, raw, *rest):
+    far, state = rest[:4], rest[4:-8]
+    out, k_oth, u_oth, k_own, u_own, held, sems, out_sems = rest[-8:]
+    copies = fetch(tuple(zip(far, (k_oth, u_oth, k_own, u_own))), sems)
     half = w2.shape[0]
     cols = k_own.shape[1] // 2
     scale = [factor(i, *state) for i in (0, 1, 2)] if state else None
-    keys, targets = k_oth[...], u_oth[...]
-    oth = act_grads(
-        nt(w13[0:half, :], keys), nt(w13[half:, :], keys), nt(w2[...], targets), scale
-    )
     own = act_grads(raw[0:half, :], raw[half : 2 * half, :], raw[2 * half :, :], scale)
+    copies[0].wait()
+    act, lin = nt(w13[0:half, :], k_oth[...]), nt(w13[half:, :], k_oth[...])
+    copies[1].wait()
+    oth = act_grads(act, lin, nt(w2[...], u_oth[...]), scale)
+    copies[2].wait()
+    copies[3].wait()
+    copies = []
     for i in range(3):
         x, y = (k_own, k_oth) if i < 2 else (u_own, u_oth)
+        rows = slice(i * half, (i + 1) * half)
         for j in range(2):
             at = slice(j * cols, (j + 1) * cols)
             g = dot(own[i], x[:, at]) + dot(oth[i], y[:, at])
-            out[j, i * half : (i + 1) * half, :] = g.astype(BF)
+            held[j, rows, :] = g.astype(BF)
+            copy = pltpu.make_async_copy(
+                held.at[j, rows, :], out.at[j, rows, :], out_sems.at[len(copies)]
+            )
+            copy.start()
+            copies.append(copy)
+    for copy in copies:
+        copy.wait()
 
 
 ROWS = 16
 
 
-def update_kernel(w13, w2, gathered, *rest):
-    *again, m13, m2, squares = rest
+def update_kernel(w13_far, w2_far, gathered_far, *rest):
+    again, rest = rest[:-9], rest[-9:]
+    m13, m2, squares, w13, w2, gathered, later, sems, more = rest
     half = w2.shape[0]
     cols = w2.shape[1] // 2
+    pairs = []
+    for i in range(3):
+        src, dst = (w13_far, w13) if i < 2 else (w2_far, w2)
+        rows = slice((i % 2) * half, (i % 2 + 1) * half)
+        at = slice(i * half, (i + 1) * half)
+        pairs.append(((src.at[rows, :], dst.at[rows, :]),))
+        pairs[-1] += ((gathered_far.at[:, at, :], gathered.at[:, at, :]),)
+        if again:
+            pairs[-1] += ((again[3].at[:, at, :], later.at[:, at, :]),)
+    each = len(pairs[0])
+    copies = fetch([p for group in pairs for p in group], more if again else sems)
     for i in range(3):
         src, dst = (w13, m13) if i < 2 else (w2, m2)
         base = (i % 2) * half
         if again:
             scale = jnp.broadcast_to(factor(i, *again[:3]), (ROWS, cols))
+        for copy in copies[i * each : (i + 1) * each]:
+            copy.wait()
 
         def step(r, total):
             row = pl.multiple_of(base + r * ROWS, ROWS)
@@ -127,7 +185,7 @@
                 m = src[pl.ds(row, ROWS), side].astype(F32)
                 m = m + gathered[j, pl.ds(at, ROWS), :].astype(F32)
                 if again:
-                    m = m * scale + again[3][j, pl.ds(at, ROWS), :].astype(F32)
+                    m = m * scale + later[j, pl.ds(at, ROWS), :].astype(F32)
                 dst[pl.ds(row, ROWS), side] = m.astype(BF)
                 total = total + m * m
             return total
@@ -137,9 +195,12 @@
     squares[3:8, :] = jnp.zeros((5, 128), F32)
 
 
-def query_kernel(m13, q_oth, q_own, raw):
-    raw[0] = nt(m13[...], q_oth[...])
-    raw[1] = nt(m13[...], q_own[...])
+def query_kernel(m13, oth_far, own_far, raw, oth, own, sems):
+    copies = fetch(((oth_far, oth), (own_far, own)), sems)
+    copies[0].wait()
+    raw[0] = nt(m13[...], oth[...])
+    copies[1].wait()
+    raw[1] = nt(m13[...], own[...])
 
 
 def hidden_kernel(k, raw, norm, sq_own, sq_oth, hq):
@@ -158,13 +219,18 @@
         o[...] = (total * scale).astype(BF)
 
 
-def spread_kernel(arrived, out):
+def spread_kernel(arrived, out, rounded, sems):
     total = arrived[0].astype(F32)
     for i in range(1, arrived.shape[0]):
         total = total + arrived[i].astype(F32)
-    rounded = total.astype(BF)
-    for i in range(arrived.shape[0]):
-        out[i] = rounded
+    rounded[...] = total.astype(BF)
+    for copy in fetch([(rounded, out.at[i]) for i in range(arrived.shape[0])], sems):
+        copy.wait()
+
+
+def stage_kernel(after, first_far, second_far, first, second, sems):
+    for copy in fetch(((first_far, first), (second_far, second)), sems):
+        copy.wait()
 
 
 TILE = 512
@@ -220,13 +286,12 @@
 def finish_product(place, k, part, o_got, w_first, w_second, out):
     count, width = o_got.shape
     tokens, n = part.shape
-    near = [pltpu.with_memory_space_constraint(x, pltpu.VMEM) for x in (part, o_got, w_first, w_second)]
-    args = (place, *near)
+    args = (place, part, o_got, w_first, w_second)
     return pl.pallas_call(
         functools.partial(finish_kernel, k),
         out_shape=shape((tokens, n)),
-        in_specs=[SMEM] + [VMEM] * 4 + [pl.BlockSpec(memory_space=pl.ANY)] * (out is not None),
-        out_specs=pl.BlockSpec(memory_space=pl.ANY),
+        in_specs=[SMEM] + [VMEM] * 4 + [FAR] * (out is not None),
+        out_specs=FAR,
         scratch_shapes=[
             pltpu.VMEM((n // TILE, count, TILE), BF),
             pltpu.SemaphoreType.DMA((n // TILE,)),
@@ -243,7 +308,15 @@
     peers = lax.axis_size(CHIPS)
     pieces = grads.reshape(peers, -1, grads.shape[2])
     arrived = lax.all_to_all(pieces, CHIPS, 0, 0, tiled=True)
-    copies = call(spread_kernel, shape(pieces.shape), 1, pieces.size, 4 * pieces.size)(arrived)
+    copies = call(
+        spread_kernel,
+        shape(pieces.shape),
+        [VMEM],
+        pieces.size,
+        4 * pieces.size,
+        (buffer(pieces.shape[1:]), semaphores(peers)),
+        True,
+    )(arrived)
     gathered = lax.all_to_all(copies, CHIPS, 0, 0, tiled=True)
     return gathered.reshape(grads.shape)
 
@@ -272,47 +345,73 @@
 
     wshape = (shape((2 * half, width)), shape((half, width)))
     sshape = shape((8, 128), F32)
-    *w, norm = call(prepare_kernel, (*wshape, sshape), 4, 1 << 21, 5 << 20, smem=1)(
-        core.reshape(1).astype(jnp.int32), w_up[0], w_gate[0], w_down[0]
-    )
+    scratch = (buffer((width, hid)), buffer((width, hid)), buffer((hid, width)), semaphores(3))
+    *w, norm = call(
+        prepare_kernel, (*wshape, sshape), [SMEM, FAR, FAR, FAR], 1 << 21, 5 << 20, scratch
+    )(core.reshape(1).astype(jnp.int32), w_up[0], w_gate[0], w_down[0])
     flops = 12 * 2 * tokens * width * half
-    state, mats, again = (), w, ()
+    gdims = (2, third, width // 2)
+    pair = [buffer((tokens, width))] * 2
+    state, mats = (), w
     for step in range(STEPS):
-        raw = call(raw_kernel, shape((third, tokens), F32), 4, flops // 4, 4 << 20)(
+        raw = call(raw_kernel, shape((third, tokens), F32), [VMEM] * 4, flops // 4, 4 << 20)(
             *mats, keys, targets
         )
         grads = call(
             grads_kernel,
-            shape((2, third, width // 2)),
-            7 + len(state),
+            shape(gdims),
+            [VMEM] * 3 + [ANY] * 2 + [FAR] * 2 + [VMEM] * len(state),
             flops * 3 // 4,
             8 << 20,
-        )(*mats, raw, keys, k_oth, targets, u_oth, *state)
+            (*pair, *pair, buffer(gdims), semaphores(4), semaphores(6)),
+            True,
+        )(*mats, raw, k_oth, u_oth, keys, targets, *state)
         gathered = all_reduced(grads)
         first = gathered if step == 0 else first
         again = () if step == 0 else (*state, gathered)
         *mats, squares = call(
-            update_kernel, (*wshape, sshape), 3 + len(again), 1 << 22, 5 << 20
+            update_kernel,
+            (*wshape, sshape),
+            [FAR] * 2 + ([FAR] + [VMEM] * 3) * step + [ANY],
+            1 << 22,
+            5 << 20,
+            (
+                buffer((2 * half, width)),
+                buffer((half, width)),
+                buffer(gdims),
+                buffer(gdims),
+                semaphores(6),
+                semaphores(9),
+            ),
         )(*w, first, *again)
         state = (norm, squares, swap(squares))
     w2_got = swap(mats[1])
     hshape = shape((half, tokens))
-    raw = call(query_kernel, shape((2, 2 * half, tokens), F32), 3, flops // 3, 5 << 20)(
-        mats[0], q_oth, queries
-    )
+    raw = call(
+        query_kernel,
+        shape((2, 2 * half, tokens), F32),
+        [VMEM, ANY, FAR],
+        flops // 3,
+        5 << 20,
+        (*pair, semaphores(2)),
+    )(mats[0], q_oth, queries)
     hq_oth, hq_own = (
-        call(functools.partial(hidden_kernel, k), hshape, 4, 1 << 20, 2 << 20)(raw, *state)
+        call(functools.partial(hidden_kernel, k), hshape, [VMEM] * 4, 1 << 20, 2 << 20)(raw, *state)
         for k in range(2)
     )
     pieces = call(
         piece_kernel,
         (shape((tokens // CHUNKS, width)),) * CHUNKS,
-        7,
+        [VMEM] * 7,
         2 * tokens * hid * width,
         4 << 20,
     )(hq_own, swap(hq_oth), mats[1], w2_got, *state)
     pieces_got = [lax.ppermute(o, "h", SWAP) for o in pieces]
     part = partial_product(place, pieces, w_out)
+    wide = (shape(w_first.shape),) * 2
+    w_first, w_second = call(stage_kernel, wide, [ANY] * 3, 1 << 20, 5 << 20, [semaphores(2)])(
+        pieces[0], w_first, w_second
+    )
     out = None
     for k, o_got in enumerate(pieces_got):
         out = finish_product(place, k, part, o_got, w_first, w_second, out)

time: 185 us -> 185 us (level)
  blocking collectives: 57.5 us -> 30.5 us
  waiting for transfers between devices: 48.6 us -> 74.2 us
  local copies, waits for them, and re-layouts: 14.9 us -> 3.51 us
  starting transfers between devices: 25.7 us -> 33 us
  Pallas kernels: 35.2 us -> 41.6 us
    all_to_all x2 -> x1, blocking collectives: 57.5 us -> 30.5 us  [all_reduced(): arrived = lax.all_to_all(pieces, CHIPS, 0, 0, tiled=True)]
    ppermute x1, waiting for transfers between devices: 0.01 us -> 23.5 us  [shards(): w_first = lax.ppermute(sent, ('xl', 'h'), ACROSS)]
    unnamed x36 -> x20, local copies, waits for them, and re-layouts: 11.5 us -> 0.11 us
    pallas_call x13 -> x14, Pallas kernels: 20.7 us -> 31 us  [with_places(): run(*(pltpu.with_memory_space_constraint(x, pltpu.HBM) if spec is FAR els...]
    all_to_all x0 -> x1, starting transfers between devices: none -> 5.89 us  [all_reduced(): arrived = lax.all_to_all(pieces, CHIPS, 0, 0, tiled=True)]
    pallas_call x2, Pallas kernels: 9.65 us -> 5.65 us  [finish_product(): pl.pallas_call(functools.partial(finish_kernel, k), out_shape=shape((toke...]
    all_to_all x2, waiting for transfers between devices: 34.5 us -> 37 us  [all_reduced(): gathered = lax.all_to_all(copies, CHIPS, 0, 0, tiled=True)]
  transfers between devices with their start and end apart: 13 -> 14, of which waited for: 5 -> 6; matrix products, arithmetic and copies ran while one was open for 2% -> 2% of each run, Pallas kernels for 14% -> 17%
where the time goes in v4:
time: 185 us
  waiting for transfers between devices  74.2 us (40%)
  Pallas kernels  41.6 us (22%)
  starting transfers between devices  33 us (18%)
  blocking collectives  30.5 us (16%)
  local copies, waits for them, and re-layouts  3.51 us (2%)
    all_to_all x2, waiting for transfers between devices, all_reduced(): gathered = lax.all_to_all(copies, CHIPS, 0, 0, tiled=True)  37 us
    pallas_call x14, Pallas kernels, with_places(): run(*(pltpu.with_memory_space_constraint(x, pltpu.HBM) if spec is FAR els...  31 us
    all_to_all x1, blocking collectives, all_reduced(): arrived = lax.all_to_all(pieces, CHIPS, 0, 0, tiled=True)  30.5 us
    ppermute x1, waiting for transfers between devices, shards(): w_first = lax.ppermute(sent, ('xl', 'h'), ACROSS)  23.5 us
    ppermute x2, waiting for transfers between devices, shards(): pieces_got = [lax.ppermute(o, 'h', SWAP) for o in pieces]  12.7 us
    all_to_all x2, starting transfers between devices, all_reduced(): gathered = lax.all_to_all(copies, CHIPS, 0, 0, tiled=True)  12.5 us
    ppermute x8, starting transfers between devices, swap(): return lax.ppermute(x, 'c', SWAP)  8.53 us
    all_to_all x1, starting transfers between devices, all_reduced(): arrived = lax.all_to_all(pieces, CHIPS, 0, 0, tiled=True)  5.89 us
  transfers between devices with their start and end apart: 14, of which 6 were waited for; matrix products, arithmetic and copies ran while one was open for 2% of the time, Pallas kernels for 17%

profile of v4, /device:TPU:1, one launch (start us, length us, event | category | flops | bytes accessed | tf_op | source)
XLA Modules:
  0.0 184.8 jit_solution(10285858777325237031)
XLA Ops:
  0.0 0.0 copy-start.5
  0.0 1.5 multiply_convert_fusion.targets.rest_3_
  1.6 0.0 copy-start.1
  1.6 1.5 collective-permute-start.1
  3.1 0.0 copy-done.5
  3.1 0.1 collective-permute-start
  3.2 3.6 %shard_map.82 = (bf16[512,1024]{1,0:T(8,128)(2,1)S(1)}, bf16[256,1024]{1,0:T(8,128)(2,1)S(1)}, f32[8,128]{1,0:T(8,128)S(1)}) custom-call(s32[1]{0:T(128)} %bitcast.1.core, bf16[1024,512]{1,0:T(8,128)(2,1)} %bitcast.17, bf16[1024,512]{1,0:T(8,128)(2,1)} %bitcast.18, bf16[512,1024]{1,0:T(8,128)(2,1)} %bitcast.19), custom_call_target="tpu_custom_call" | custom-call | flops 2097152 | bytes 5242880 | tf_op jit(solution)/shard_map/pallas_call | solution.py:54
  6.8 0.0 copy-start.3
  6.8 0.0 copy-start.4
  6.8 1.0 shard_map.83.raw
  7.8 0.0 copy-done.1
  7.8 0.0 collective-permute-done.1.rest_1_
  7.8 0.0 collective-permute-done.rest_0_
  7.8 0.0 copy-done.3
  7.8 0.1 copy-done.4
  7.9 5.1 %shard_map.84 = bf16[2,768,512]{2,1,0:T(8,128)(2,1)} custom-call(bf16[512,1024]{1,0:T(8,128)(2,1)S(1)} %get-tuple-element.18.w13.w13_far, bf16[256,1024]{1,0:T(8,128)(2,1)S(1)} %get-tuple-element.19.w2.w2_far, f32[768,512]{1,0:T(8,128)S(1)} %shard_map.83.raw, bf16[512,1024]{1,0:T(8,128)(2,1)} %collective-permute-done.rest_0_, ...), custom_call_target="tpu_custom_call" | custom-call | flops 2415919104 | bytes 8388608 | tf_op jit(solution)/shard_map/pallas_call | solution.py:54
  13.0 30.5 %all_to_all.20.arrived = bf16[32,48,512]{2,1,0:T(8,128)(2,1)S(1)} all-to-all(bf16[32,48,512]{2,1,0:T(8,128)(2,1)} %bitcast.16), channel_id=1, replica_groups=mesh['z'=4,'xl'=2,'y'=4,'c'=2,'h'=2] {'z','xl','y'}, dimensions={0} | all-to-all | bytes 3145728 | tf_op jit(solution)/shard_map/all_to_all | solution.py:310
  43.5 1.7 shard_map.85
  45.3 5.7 %all-to-all-start.1 = ((bf16[32,48,512]{2,1,0:T(8,128)(2,1)}), bf16[32,48,512]{2,1,0:T(8,128)(2,1)S(1)}, u32[]{:S(2)}, u32[]{:S(2)}) async-start(bf16[32,48,512]{2,1,0:T(8,128)(2,1)} %shard_map.85), calls=%async_computation.1 | async-start | bytes 3145728 | tf_op jit(solution)/shard_map/all_to_all | solution.py:320
  51.0 3.4 %dynamic_slice.3 = bf16[512,2560]{1,0:T(8,128)(2,1)} dynamic-slice(bf16[1024,5120]{1,0:T(8,128)(2,1)} %refs_2_.1, s32[]{:T(128)S(6)} %select_n.6, s32[]{:T(128)S(6)} %select_n.7), dynamic_slice_sizes={512,2560} | dynamic-slice | bytes 5242884 | tf_op jit(solution)/shard_map/dynamic_slice | solution.py:341
  54.4 2.5 %collective-permute-start.8 = (bf16[512,2560]{1,0:T(8,128)(2,1)}, bf16[512,2560]{1,0:T(8,128)(2,1)}, u32[]{:S(2)}, u32[]{:S(2)}) collective-permute-start(bf16[512,2560]{1,0:T(8,128)(2,1)} %dynamic_slice.3), channel_id=1, source_target_pairs={{0,17},{17,0},{1,16},{16,1},{2,19},{19,2},{3,18},{18,3},{4,21},{21... | collective-permute-start | bytes 7864328 | tf_op jit(solution)/shard_map/ppermute | solution.py:342
  56.9 15.0 %all-to-all-done.1 = bf16[32,48,512]{2,1,0:T(8,128)(2,1)S(1)} async-done(((bf16[32,48,512]{2,1,0:T(8,128)(2,1)}), bf16[32,48,512]{2,1,0:T(8,128)(2,1)S(1)}, u32[]{:S(2)}, u32[]{:S(2)}) %all-to-all-start.1) | async-done | bytes 1572896 | tf_op jit(solution)/shard_map/all_to_all | solution.py:320
  71.9 2.8 %shard_map.86 = (bf16[512,1024]{1,0:T(8,128)(2,1)S(1)}, bf16[256,1024]{1,0:T(8,128)(2,1)S(1)}, f32[8,128]{1,0:T(8,128)S(1)}) custom-call(bf16[512,1024]{1,0:T(8,128)(2,1)} %copy-done.3, bf16[256,1024]{1,0:T(8,128)(2,1)} %copy-done.4, bf16[2,768,512]{2,1,0:T(8,128)(2,1)S(1)} %bitcast.12), custom_call_target="tpu_custom_call" | custom-call | flops 4194304 | bytes 5242880 | tf_op jit(solution)/shard_map/pallas_call | solution.py:54
  74.7 2.7 %collective-permute-start.2 = (f32[8,128]{1,0:T(8,128)S(1)}, f32[8,128]{1,0:T(8,128)S(1)}, u32[]{:S(2)}, u32[]{:S(2)}) collective-permute-start(f32[8,128]{1,0:T(8,128)S(1)} %get-tuple-element.21.rest_5_.rest_1_), channel_id=1, source_target_pairs={{0,2},{2,0},{1,3},{3,1},{4,6},{6,4},{5,7},{7,5},{8,10},{10,8},{9,1... | collective-permute-start | bytes 12296 | tf_op jit(solution)/shard_map/ppermute | solution.py:325
  77.5 0.0 copy-done.2
  77.5 0.0 copy-done.6
  77.5 1.0 shard_map.87.raw
  78.5 0.0 copy-done
  78.5 0.0 collective-permute-done.2.rest_6_.rest_2_
  78.5 5.2 %shard_map.88 = bf16[2,768,512]{2,1,0:T(8,128)(2,1)} custom-call(bf16[512,1024]{1,0:T(8,128)(2,1)S(1)} %get-tuple-element.22.w13, bf16[256,1024]{1,0:T(8,128)(2,1)S(1)} %get-tuple-element.23.w2, f32[768,512]{1,0:T(8,128)S(1)} %shard_map.87.raw, bf16[512,1024]{1,0:T(8,128)(2,1)} %collective-permute-done.rest_0_, ...), custom_call_target="tpu_custom_call" | custom-call | flops 2415919104 | bytes 8388608 | tf_op jit(solution)/shard_map/pallas_call | solution.py:54
  83.7 5.9 %all-to-all-start.2 = ((bf16[32,48,512]{2,1,0:T(8,128)(2,1)}), bf16[32,48,512]{2,1,0:T(8,128)(2,1)S(1)}, u32[]{:S(2)}, u32[]{:S(2)}) async-start(bf16[32,48,512]{2,1,0:T(8,128)(2,1)} %bitcast.15), calls=%async_computation.2 | async-start | bytes 3145728 | tf_op jit(solution)/shard_map/all_to_all | solution.py:310
  89.6 23.5 %collective-permute-done.8.first_far = bf16[512,2560]{1,0:T(8,128)(2,1)} collective-permute-done((bf16[512,2560]{1,0:T(8,128)(2,1)}, bf16[512,2560]{1,0:T(8,128)(2,1)}, u32[]{:S(2)}, u32[]{:S(2)}) %collective-permute-start.8) | collective-permute-done | bytes 2621472 | tf_op jit(solution)/shard_map/ppermute | solution.py:342
  113.1 2.1 %collective-permute-start.9 = (bf16[512,2560]{1,0:T(8,128)(2,1)}, bf16[512,2560]{1,0:T(8,128)(2,1)}, u32[]{:S(2)}, u32[]{:S(2)}) collective-permute-start(bf16[512,2560]{1,0:T(8,128)(2,1)} %collective-permute-done.8.first_far), channel_id=1, source_target_pairs={{0,2},{2,0},{1,3},{3,1},{4,6},{6,4},{5,7},{7,5},{8,10},{10,8},{9,1... | collective-permute-start | bytes 7864328 | tf_op jit(solution)/shard_map/ppermute | solution.py:325
  115.2 0.0 all-to-all-done.2.arrived
  115.2 1.6 shard_map.89
  116.8 6.8 %all-to-all-start.3 = ((bf16[32,48,512]{2,1,0:T(8,128)(2,1)}), bf16[32,48,512]{2,1,0:T(8,128)(2,1)S(1)}, u32[]{:S(2)}, u32[]{:S(2)}) async-start(bf16[32,48,512]{2,1,0:T(8,128)(2,1)} %shard_map.89), calls=%async_computation.3 | async-start | bytes 3145728 | tf_op jit(solution)/shard_map/all_to_all | solution.py:320
  123.6 0.4 collective-permute-start.3
  124.0 21.9 %all-to-all-done.3 = bf16[32,48,512]{2,1,0:T(8,128)(2,1)S(1)} async-done(((bf16[32,48,512]{2,1,0:T(8,128)(2,1)}), bf16[32,48,512]{2,1,0:T(8,128)(2,1)S(1)}, u32[]{:S(2)}, u32[]{:S(2)}) %all-to-all-start.3) | async-done | bytes 1572896 | tf_op jit(solution)/shard_map/all_to_all | solution.py:320
  145.9 3.0 %shard_map.90 = (bf16[512,1024]{1,0:T(8,128)(2,1)S(1)}, bf16[256,1024]{1,0:T(8,128)(2,1)S(1)}, f32[8,128]{1,0:T(8,128)S(1)}) custom-call(bf16[512,1024]{1,0:T(8,128)(2,1)} %copy-done.3, bf16[256,1024]{1,0:T(8,128)(2,1)} %copy-done.4, bf16[2,768,512]{2,1,0:T(8,128)(2,1)} %bitcast.13, f32[8,128]{1,0:T(8,128)S(1)} %get-tuple-element.20.rest_4_.rest_0_.norm, ...), custom_call_target="tpu_custom_call" | custom-call | flops 4194304 | bytes 5242880 | tf_op jit(solution)/shard_map/pallas_call | solution.py:54
  148.9 1.2 collective-permute-start.6
  150.1 0.1 collective-permute-start.4
  150.2 0.0 collective-permute-done.3.oth_far
  150.2 2.2 %shard_map.91.raw = f32[2,512,512]{2,1,0:T(8,128)S(1)} custom-call(bf16[512,1024]{1,0:T(8,128)(2,1)S(1)} %get-tuple-element.24.m13, bf16[512,1024]{1,0:T(8,128)(2,1)S(1)} %collective-permute-done.3.oth_far, bf16[512,1024]{1,0:T(8,128)(2,1)} %own_far.1), custom_call_target="tpu_custom_call" | custom-call | flops 1073741824 | bytes 5242880 | tf_op jit(solution)/shard_map/pallas_call | solution.py:54
  152.5 0.0 collective-permute-done.4.sq_oth
  152.5 0.2 shard_map.93
  152.7 0.5 collective-permute-start.5
  153.2 0.2 shard_map.92.hq_own
  153.4 0.0 slice-start.2
  153.4 0.9 collective-permute-done.5.hq_got
  154.3 0.0 collective-permute-done.6.w2_got
  154.3 0.7 shard_map.94
  155.1 3.5 %collective-permute-start.10 = (bf16[256,1024]{1,0:T(8,128)(2,1)S(1)}, bf16[256,1024]{1,0:T(8,128)(2,1)S(1)}, u32[]{:S(2)}, u32[]{:S(2)}) collective-permute-start(bf16[256,1024]{1,0:T(8,128)(2,1)S(1)} %get-tuple-element.27.refs_0_.after), channel_id=1, source_target_pairs={{0,1},{1,0},{2,3},{3,2},{4,5},{5,4},{6,7},{7,6},{8,9},{9,8},{10,11... | collective-permute-start | bytes 1572872 | tf_op jit(solution)/shard_map/ppermute | solution.py:409
  158.5 0.1 collective-permute-start.7
  158.6 0.1 pad_add_fusion.place
  158.7 0.0 collective-permute-done.9.second_far
  158.7 2.5 %shard_map.96 = (bf16[512,2560]{1,0:T(8,128)(2,1)S(1)}, bf16[512,2560]{1,0:T(8,128)(2,1)S(1)}) custom-call(bf16[256,1024]{1,0:T(8,128)(2,1)S(1)} %get-tuple-element.27.refs_0_.after, bf16[512,2560]{1,0:T(8,128)(2,1)} %collective-permute-done.8.first_far, bf16[512,2560]{1,0:T(8,128)(2,1)} %collective-permute-done.9.second_far), custom_call_target="tpu_custom_call" | custom-call | flops 1048576 | bytes 5242880 | tf_op jit(solution)/shard_map/pallas_call | solution.py:54
  161.3 0.0 slice-done
  161.3 0.0 slice-done.1
  161.3 0.0 slice-done.2
  161.3 4.9 %shard_map.95.part = f32[512,2560]{1,0:T(8,128)S(1)} custom-call(s32[2]{0:T(128)S(1)} %pad_add_fusion.place, bf16[256,1024]{1,0:T(8,128)(2,1)S(1)} %get-tuple-element.27.refs_0_.after, bf16[256,1024]{1,0:T(8,128)(2,1)S(1)} %get-tuple-element.28.refs_1_, bf16[1024,5120]{1,0:T(8,128)(2,1)S(1)} %bitcast.11), custom_call_target="tpu_custom_call" | custom-call | flops 2684354560 | bytes 10485760 | tf_op jit(solution)/shard_map/pallas_call | solution.py:251
  166.2 4.3 %collective-permute-done.10.o_got = bf16[256,1024]{1,0:T(8,128)(2,1)S(1)} collective-permute-done((bf16[256,1024]{1,0:T(8,128)(2,1)S(1)}, bf16[256,1024]{1,0:T(8,128)(2,1)S(1)}, u32[]{:S(2)}, u32[]{:S(2)}) %collective-permute-start.10) | collective-permute-done | bytes 524320 | tf_op jit(solution)/shard_map/ppermute | solution.py:409
  170.5 2.8 %shard_map.97.rest_0_ = bf16[512,2560]{1,0:T(8,128)(2,1)} custom-call(s32[2]{0:T(128)S(1)} %pad_add_fusion.place, f32[512,2560]{1,0:T(8,128)S(1)} %shard_map.95.part, bf16[256,1024]{1,0:T(8,128)(2,1)S(1)} %collective-permute-done.10.o_got, bf16[512,2560]{1,0:T(8,128)(2,1)S(1)} %get-tuple-element.29.w_first, bf16[512,2560]{1,0:T(8,128)(2,1)S(1)} %get-tuple-element.30.w_second), custom_call_target="tpu_custom_call" | custom-call | flops 1342177280 | bytes 4194304 | tf_op jit(solution)/shard_map/pallas_call | solution.py:290
  173.4 8.4 %collective-permute-done.7.o_got = bf16[256,1024]{1,0:T(8,128)(2,1)S(1)} collective-permute-done((bf16[256,1024]{1,0:T(8,128)(2,1)S(1)}, bf16[256,1024]{1,0:T(8,128)(2,1)S(1)}, u32[]{:S(2)}, u32[]{:S(2)}) %collective-permute-start.7) | collective-permute-done | bytes 524320 | tf_op jit(solution)/shard_map/ppermute | solution.py:409
  181.8 2.8 %shard_map.98 = bf16[512,2560]{1,0:T(8,128)(2,1)} custom-call(s32[2]{0:T(128)S(1)} %pad_add_fusion.place, f32[512,2560]{1,0:T(8,128)S(1)} %shard_map.95.part, bf16[256,1024]{1,0:T(8,128)(2,1)S(1)} %collective-permute-done.7.o_got, bf16[512,2560]{1,0:T(8,128)(2,1)S(1)} %get-tuple-element.29.w_first, ...), custom_call_target="tpu_custom_call", output_to_operand_aliasing={{}: (5, {})} | custom-call | flops 1342177280 | bytes 4194304 | tf_op jit(solution)/shard_map/pallas_call | solution.py:290
  (6 shorter events, 0.0 us)
Async XLA Ops:
  0.0 3.1 %copy-start.5 = (bf16[512,1024]{1,0:T(8,128)(2,1)S(1)}, bf16[512,1024]{1,0:T(8,128)(2,1)}, u32[]{:S(2)}) copy-start(bf16[512,1024]{1,0:T(8,128)(2,1)} %rest_2_.3) | copy-start | bytes 3145732
  1.6 6.2 %copy-start.1 = (bf16[512,1024]{1,0:T(8,128)(2,1)}, bf16[512,1024]{1,0:T(8,128)(2,1)S(1)}, u32[]{:S(2)}) copy-start(bf16[512,1024]{1,0:T(8,128)(2,1)S(1)} %multiply_convert_fusion.targets.rest_3_) | copy-start | bytes 3145732
  1.6 6.2 %collective-permute-start.1 = (bf16[512,1024]{1,0:T(8,128)(2,1)S(1)}, bf16[512,1024]{1,0:T(8,128)(2,1)}, u32[]{:S(2)}, u32[]{:S(2)}) collective-permute-start(bf16[512,1024]{1,0:T(8,128)(2,1)S(1)} %multiply_convert_fusion.targets.rest_3_), channel_id=1, source_target_pairs={{0,2},{2,0},{1,3},{3,1},{4,6},{6,4},{5,7},{7,5},{8,10},{10,8},{9,1... | collective-permute-start | bytes 3145736 | tf_op jit(solution)/shard_map/ppermute | solution.py:325
  3.1 4.7 %collective-permute-start = (bf16[512,1024]{1,0:T(8,128)(2,1)S(1)}, bf16[512,1024]{1,0:T(8,128)(2,1)}, u32[]{:S(2)}, u32[]{:S(2)}) collective-permute-start(bf16[512,1024]{1,0:T(8,128)(2,1)S(1)} %copy-done.5), channel_id=1, source_target_pairs={{0,2},{2,0},{1,3},{3,1},{4,6},{6,4},{5,7},{7,5},{8,10},{10,8},{9,1... | collective-permute-start | bytes 3145736 | tf_op jit(solution)/shard_map/ppermute | solution.py:325
  6.8 1.1 copy-start.3
  6.8 1.1 copy-start.4
  45.3 26.6 %all-to-all-start.1 = ((bf16[32,48,512]{2,1,0:T(8,128)(2,1)}), bf16[32,48,512]{2,1,0:T(8,128)(2,1)S(1)}, u32[]{:S(2)}, u32[]{:S(2)}) async-start(bf16[32,48,512]{2,1,0:T(8,128)(2,1)} %shard_map.85), calls=%async_computation.1 | async-start | bytes 3145728 | tf_op jit(solution)/shard_map/all_to_all | solution.py:320
  54.4 23.1 %copy-start.2 = (bf16[512,1024]{1,0:T(8,128)(2,1)S(1)}, bf16[512,1024]{1,0:T(8,128)(2,1)}, u32[]{:S(2)}) copy-start(bf16[512,1024]{1,0:T(8,128)(2,1)} %copy-done.1) | copy-start | bytes 3145732
  54.4 58.7 %collective-permute-start.8 = (bf16[512,2560]{1,0:T(8,128)(2,1)}, bf16[512,2560]{1,0:T(8,128)(2,1)}, u32[]{:S(2)}, u32[]{:S(2)}) collective-permute-start(bf16[512,2560]{1,0:T(8,128)(2,1)} %dynamic_slice.3), channel_id=1, source_target_pairs={{0,17},{17,0},{1,16},{16,1},{2,19},{19,2},{3,18},{18,3},{4,21},{21... | collective-permute-start | bytes 7864328 | tf_op jit(solution)/shard_map/ppermute | solution.py:342
  71.9 6.6 %copy-start = (bf16[32,48,512]{2,1,0:T(8,128)(2,1)}, bf16[32,48,512]{2,1,0:T(8,128)(2,1)S(1)}, u32[]{:S(2)}) copy-start(bf16[32,48,512]{2,1,0:T(8,128)(2,1)S(1)} %all-to-all-done.1) | copy-start | bytes 4718596
  71.9 5.6 %copy-start.6 = (bf16[512,1024]{1,0:T(8,128)(2,1)S(1)}, bf16[512,1024]{1,0:T(8,128)(2,1)}, u32[]{:S(2)}) copy-start(bf16[512,1024]{1,0:T(8,128)(2,1)} %rest_2_.3) | copy-start | bytes 3145732
  74.7 3.8 %collective-permute-start.2 = (f32[8,128]{1,0:T(8,128)S(1)}, f32[8,128]{1,0:T(8,128)S(1)}, u32[]{:S(2)}, u32[]{:S(2)}) collective-permute-start(f32[8,128]{1,0:T(8,128)S(1)} %get-tuple-element.21.rest_5_.rest_1_), channel_id=1, source_target_pairs={{0,2},{2,0},{1,3},{3,1},{4,6},{6,4},{5,7},{7,5},{8,10},{10,8},{9,1... | collective-permute-start | bytes 12296 | tf_op jit(solution)/shard_map/ppermute | solution.py:325
  83.7 31.5 %all-to-all-start.2 = ((bf16[32,48,512]{2,1,0:T(8,128)(2,1)}), bf16[32,48,512]{2,1,0:T(8,128)(2,1)S(1)}, u32[]{:S(2)}, u32[]{:S(2)}) async-start(bf16[32,48,512]{2,1,0:T(8,128)(2,1)} %bitcast.15), calls=%async_computation.2 | async-start | bytes 3145728 | tf_op jit(solution)/shard_map/all_to_all | solution.py:310
  113.1 45.6 %collective-permute-start.9 = (bf16[512,2560]{1,0:T(8,128)(2,1)}, bf16[512,2560]{1,0:T(8,128)(2,1)}, u32[]{:S(2)}, u32[]{:S(2)}) collective-permute-start(bf16[512,2560]{1,0:T(8,128)(2,1)} %collective-permute-done.8.first_far), channel_id=1, source_target_pairs={{0,2},{2,0},{1,3},{3,1},{4,6},{6,4},{5,7},{7,5},{8,10},{10,8},{9,1... | collective-permute-start | bytes 7864328 | tf_op jit(solution)/shard_map/ppermute | solution.py:325
  116.8 29.1 %all-to-all-start.3 = ((bf16[32,48,512]{2,1,0:T(8,128)(2,1)}), bf16[32,48,512]{2,1,0:T(8,128)(2,1)S(1)}, u32[]{:S(2)}, u32[]{:S(2)}) async-start(bf16[32,48,512]{2,1,0:T(8,128)(2,1)} %shard_map.89), calls=%async_computation.3 | async-start | bytes 3145728 | tf_op jit(solution)/shard_map/all_to_all | solution.py:320
  123.6 26.6 %collective-permute-start.3 = (bf16[512,1024]{1,0:T(8,128)(2,1)}, bf16[512,1024]{1,0:T(8,128)(2,1)S(1)}, u32[]{:S(2)}, u32[]{:S(2)}) collective-permute-start(bf16[512,1024]{1,0:T(8,128)(2,1)} %own_far.1), channel_id=1, source_target_pairs={{0,2},{2,0},{1,3},{3,1},{4,6},{6,4},{5,7},{7,5},{8,10},{10,8},{9,1... | collective-permute-start | bytes 3145736 | tf_op jit(solution)/shard_map/ppermute | solution.py:325
  145.9 15.4 %slice-start = ((s8[10485760]{0:T(1024)(128)(4,1)}), s8[4194304]{0:T(1024)(128)(4,1)S(1)}, s32[]{:S(2)}) async-start(s8[10485760]{0:T(1024)(128)(4,1)} %bitcast.10), calls=%async_computation.4 | async-start | bytes 8388608
  148.9 5.4 %collective-permute-start.6 = (bf16[256,1024]{1,0:T(8,128)(2,1)S(1)}, bf16[256,1024]{1,0:T(8,128)(2,1)S(1)}, u32[]{:S(2)}, u32[]{:S(2)}) collective-permute-start(bf16[256,1024]{1,0:T(8,128)(2,1)S(1)} %get-tuple-element.26.w2_own), channel_id=1, source_target_pairs={{0,2},{2,0},{1,3},{3,1},{4,6},{6,4},{5,7},{7,5},{8,10},{10,8},{9,1... | collective-permute-start | bytes 1572872 | tf_op jit(solution)/shard_map/ppermute | solution.py:325
  150.1 2.3 %collective-permute-start.4 = (f32[8,128]{1,0:T(8,128)S(1)}, f32[8,128]{1,0:T(8,128)S(1)}, u32[]{:S(2)}, u32[]{:S(2)}) collective-permute-start(f32[8,128]{1,0:T(8,128)S(1)} %get-tuple-element.25.sq_own), channel_id=1, source_target_pairs={{0,2},{2,0},{1,3},{3,1},{4,6},{6,4},{5,7},{7,5},{8,10},{10,8},{9,1... | collective-permute-start | bytes 12296 | tf_op jit(solution)/shard_map/ppermute | solution.py:325
  150.2 11.0 %slice-start.1 = ((s8[10485760]{0:T(1024)(128)(4,1)}), s8[4194304]{0:T(1024)(128)(4,1)S(1)}, s32[]{:S(2)}) async-start(s8[10485760]{0:T(1024)(128)(4,1)} %bitcast.10), calls=%async_computation.5 | async-start | bytes 8388608
  152.7 1.7 collective-permute-start.5
  153.4 7.9 %slice-start.2 = ((s8[10485760]{0:T(1024)(128)(4,1)}), s8[2097152]{0:T(1024)(128)(4,1)S(1)}, s32[]{:S(2)}) async-start(s8[10485760]{0:T(1024)(128)(4,1)} %bitcast.10), calls=%async_computation.6 | async-start | bytes 4194304
  155.1 15.4 %collective-permute-start.10 = (bf16[256,1024]{1,0:T(8,128)(2,1)S(1)}, bf16[256,1024]{1,0:T(8,128)(2,1)S(1)}, u32[]{:S(2)}, u32[]{:S(2)}) collective-permute-start(bf16[256,1024]{1,0:T(8,128)(2,1)S(1)} %get-tuple-element.27.refs_0_.after), channel_id=1, source_target_pairs={{0,1},{1,0},{2,3},{3,2},{4,5},{5,4},{6,7},{7,6},{8,9},{9,8},{10,11... | collective-permute-start | bytes 1572872 | tf_op jit(solution)/shard_map/ppermute | solution.py:409
  158.5 23.2 %collective-permute-start.7 = (bf16[256,1024]{1,0:T(8,128)(2,1)S(1)}, bf16[256,1024]{1,0:T(8,128)(2,1)S(1)}, u32[]{:S(2)}, u32[]{:S(2)}) collective-permute-start(bf16[256,1024]{1,0:T(8,128)(2,1)S(1)} %get-tuple-element.28.refs_1_), channel_id=1, source_target_pairs={{0,1},{1,0},{2,3},{3,2},{4,5},{5,4},{6,7},{7,6},{8,9},{9,8},{10,11... | collective-permute-start | bytes 1572872 | tf_op jit(solution)/shard_map/ppermute | solution.py:409

commit v5 on v4

--- a/solution.py
+++ b/solution.py
@@ -21,6 +21,8 @@
 SMEM = pl.BlockSpec(memory_space=pltpu.SMEM)
 FAR = pl.BlockSpec(memory_space=pltpu.HBM)
 ANY = pl.BlockSpec(memory_space=pl.ANY)
+NEAR = pl.BlockSpec(memory_space=pltpu.VMEM)
+HELD = {id(FAR): pltpu.HBM, id(NEAR): pltpu.VMEM}
 LIMIT = 24 * 1024 * 1024
 CHUNKS = 2
 
@@ -53,7 +55,7 @@
     def with_places(*args):
         return run(
             *(
-                pltpu.with_memory_space_constraint(x, pltpu.HBM) if spec is FAR else x
+                pltpu.with_memory_space_constraint(x, HELD[id(spec)]) if id(spec) in HELD else x
                 for x, spec in zip(args, specs, strict=True)
             )
         )
@@ -119,43 +121,29 @@
     return pgrad, qgrad, hidden
 
 
-def grads_kernel(w13, w2, raw, *rest):
-    far, state = rest[:4], rest[4:-8]
-    out, k_oth, u_oth, k_own, u_own, held, sems, out_sems = rest[-8:]
-    copies = fetch(tuple(zip(far, (k_oth, u_oth, k_own, u_own))), sems)
+def grads_kernel(w13, w2, raw, k_own, k_oth, u_own, u_oth, *rest):
+    *state, out = rest
     half = w2.shape[0]
     cols = k_own.shape[1] // 2
     scale = [factor(i, *state) for i in (0, 1, 2)] if state else None
+    keys, targets = k_oth[...], u_oth[...]
+    oth = act_grads(
+        nt(w13[0:half, :], keys), nt(w13[half:, :], keys), nt(w2[...], targets), scale
+    )
     own = act_grads(raw[0:half, :], raw[half : 2 * half, :], raw[2 * half :, :], scale)
-    copies[0].wait()
-    act, lin = nt(w13[0:half, :], k_oth[...]), nt(w13[half:, :], k_oth[...])
-    copies[1].wait()
-    oth = act_grads(act, lin, nt(w2[...], u_oth[...]), scale)
-    copies[2].wait()
-    copies[3].wait()
-    copies = []
     for i in range(3):
         x, y = (k_own, k_oth) if i < 2 else (u_own, u_oth)
-        rows = slice(i * half, (i + 1) * half)
         for j in range(2):
             at = slice(j * cols, (j + 1) * cols)
             g = dot(own[i], x[:, at]) + dot(oth[i], y[:, at])
-            held[j, rows, :] = g.astype(BF)
-            copy = pltpu.make_async_copy(
-                held.at[j, rows, :], out.at[j, rows, :], out_sems.at[len(copies)]
-            )
-            copy.start()
-            copies.append(copy)
-    for copy in copies:
-        copy.wait()
+            out[j, i * half : (i + 1) * half, :] = g.astype(BF)
 
 
 ROWS = 16
 
 
-def update_kernel(w13_far, w2_far, gathered_far, *rest):
-    again, rest = rest[:-9], rest[-9:]
-    m13, m2, squares, w13, w2, gathered, later, sems, more = rest
+def update_kernel(w13_far, w2_far, *rest):
+    *again, gathered, m13, m2, squares, w13, w2, first, sems = rest
     half = w2.shape[0]
     cols = w2.shape[1] // 2
     pairs = []
@@ -163,17 +151,16 @@
         src, dst = (w13_far, w13) if i < 2 else (w2_far, w2)
         rows = slice((i % 2) * half, (i % 2 + 1) * half)
         at = slice(i * half, (i + 1) * half)
-        pairs.append(((src.at[rows, :], dst.at[rows, :]),))
-        pairs[-1] += ((gathered_far.at[:, at, :], gathered.at[:, at, :]),)
+        pairs.append((src.at[rows, :], dst.at[rows, :]))
         if again:
-            pairs[-1] += ((again[3].at[:, at, :], later.at[:, at, :]),)
-    each = len(pairs[0])
-    copies = fetch([p for group in pairs for p in group], more if again else sems)
+            pairs.append((again[0].at[:, at, :], first.at[:, at, :]))
+    each = len(pairs) // 3
+    copies = fetch(pairs, sems)
     for i in range(3):
         src, dst = (w13, m13) if i < 2 else (w2, m2)
         base = (i % 2) * half
         if again:
-            scale = jnp.broadcast_to(factor(i, *again[:3]), (ROWS, cols))
+            scale = jnp.broadcast_to(factor(i, *again[1:]), (ROWS, cols))
         for copy in copies[i * each : (i + 1) * each]:
             copy.wait()
 
@@ -183,9 +170,9 @@
             for j in range(2):
                 side = slice(j * cols, (j + 1) * cols)
                 m = src[pl.ds(row, ROWS), side].astype(F32)
+                if again:
+                    m = (m + first[j, pl.ds(at, ROWS), :].astype(F32)) * scale
                 m = m + gathered[j, pl.ds(at, ROWS), :].astype(F32)
-                if again:
-                    m = m * scale + later[j, pl.ds(at, ROWS), :].astype(F32)
                 dst[pl.ds(row, ROWS), side] = m.astype(BF)
                 total = total + m * m
             return total
@@ -219,13 +206,13 @@
         o[...] = (total * scale).astype(BF)
 
 
-def spread_kernel(arrived, out, rounded, sems):
+def spread_kernel(arrived, out):
     total = arrived[0].astype(F32)
     for i in range(1, arrived.shape[0]):
         total = total + arrived[i].astype(F32)
-    rounded[...] = total.astype(BF)
-    for copy in fetch([(rounded, out.at[i]) for i in range(arrived.shape[0])], sems):
-        copy.wait()
+    rounded = total.astype(BF)
+    for i in range(arrived.shape[0]):
+        out[i] = rounded
 
 
 def stage_kernel(after, first_far, second_far, first, second, sems):
@@ -304,7 +291,7 @@
     )(*args, *(() if out is None else (out,)))
 
 
-def all_reduced(grads):
+def all_reduced(grads, beside=None):
     peers = lax.axis_size(CHIPS)
     pieces = grads.reshape(peers, -1, grads.shape[2])
     arrived = lax.all_to_all(pieces, CHIPS, 0, 0, tiled=True)
@@ -314,11 +301,11 @@
         [VMEM],
         pieces.size,
         4 * pieces.size,
-        (buffer(pieces.shape[1:]), semaphores(peers)),
-        True,
     )(arrived)
+    if beside is not None:
+        beside, _ = lax.optimization_barrier((beside, copies))
     gathered = lax.all_to_all(copies, CHIPS, 0, 0, tiled=True)
-    return gathered.reshape(grads.shape)
+    return gathered.reshape(grads.shape), beside
 
 
 def swap(x):
@@ -340,7 +327,6 @@
     place = jnp.stack([head, core]).astype(jnp.int32)
     sent = lax.dynamic_slice(w_out, (core * (width // 2), (1 - head) * n), (width // 2, n))
     w_first = lax.ppermute(sent, ("xl", "h"), ACROSS)
-    w_second = swap(w_first)
     q_oth = swap(queries)
 
     wshape = (shape((2 * half, width)), shape((half, width)))
@@ -360,31 +346,28 @@
         grads = call(
             grads_kernel,
             shape(gdims),
-            [VMEM] * 3 + [ANY] * 2 + [FAR] * 2 + [VMEM] * len(state),
+            [VMEM] * (7 + len(state)),
             flops * 3 // 4,
             8 << 20,
-            (*pair, *pair, buffer(gdims), semaphores(4), semaphores(6)),
-            True,
-        )(*mats, raw, k_oth, u_oth, keys, targets, *state)
-        gathered = all_reduced(grads)
-        first = gathered if step == 0 else first
-        again = () if step == 0 else (*state, gathered)
+        )(*mats, raw, keys, k_oth, targets, u_oth, *state)
+        gathered, w_late = all_reduced(grads, w_first if step else None)
+        again = () if step == 0 else (first, *state)
         *mats, squares = call(
             update_kernel,
             (*wshape, sshape),
-            [FAR] * 2 + ([FAR] + [VMEM] * 3) * step + [ANY],
+            [FAR] * 2 + ([FAR] + [VMEM] * 3) * step + [NEAR],
             1 << 22,
             5 << 20,
             (
                 buffer((2 * half, width)),
                 buffer((half, width)),
                 buffer(gdims),
-                buffer(gdims),
-                semaphores(6),
-                semaphores(9),
+                semaphores(3 + 3 * step),
             ),
-        )(*w, first, *again)
+        )(*w, *again, gathered)
+        first = gathered
         state = (norm, squares, swap(squares))
+    w_second = swap(w_late)
     w2_got = swap(mats[1])
     hshape = shape((half, tokens))
     raw = call(

time: 185 us -> 178 us (0.962)
  blocking collectives: 30.5 us -> 57.6 us
  waiting for transfers between devices: 74.2 us -> 48.3 us
  starting transfers between devices: 33 us -> 25.3 us
  Pallas kernels: 41.6 us -> 38.7 us
  local copies, waits for them, and re-layouts: 3.51 us -> 5.86 us
    all_to_all x1 -> x2, blocking collectives: 30.5 us -> 57.6 us  [all_reduced(): arrived = lax.all_to_all(pieces, CHIPS, 0, 0, tiled=True)]
    ppermute x1, waiting for transfers between devices: 23.5 us -> 0.01 us  [shards(): w_first = lax.ppermute(sent, ('xl', 'h'), ACROSS)]
    all_to_all x1 -> x0, starting transfers between devices: 5.89 us -> none  [all_reduced(): arrived = lax.all_to_all(pieces, CHIPS, 0, 0, tiled=True)]
    pallas_call x14, Pallas kernels: 31 us -> 28.2 us  [with_places(): run(*(pltpu.with_memory_space_constraint(x, HELD[id(spec)]) if id(spec) i...]
    unnamed x20, local copies, waits for them, and re-layouts: 0.11 us -> 2.45 us
    all_to_all x2, waiting for transfers between devices: 37 us -> 34.7 us  [all_reduced(): gathered = lax.all_to_all(copies, CHIPS, 0, 0, tiled=True)]
  transfers between devices with their start and end apart: 14 -> 13, of which waited for: 6 -> 5; matrix products, arithmetic and copies ran while one was open for 2% -> 2% of each run, Pallas kernels for 17% -> 18%
where the time goes in v5:
time: 178 us
  blocking collectives  57.6 us (32%)
  waiting for transfers between devices  48.3 us (27%)
  Pallas kernels  38.7 us (22%)
  starting transfers between devices  25.3 us (14%)
  local copies, waits for them, and re-layouts  5.86 us (3%)
    all_to_all x2, blocking collectives, all_reduced(): arrived = lax.all_to_all(pieces, CHIPS, 0, 0, tiled=True)  57.6 us
    all_to_all x2, waiting for transfers between devices, all_reduced(): gathered = lax.all_to_all(copies, CHIPS, 0, 0, tiled=True)  34.7 us
    pallas_call x14, Pallas kernels, with_places(): run(*(pltpu.with_memory_space_constraint(x, HELD[id(spec)]) if id(spec) i...  28.2 us
    ppermute x2, waiting for transfers between devices, shards(): pieces_got = [lax.ppermute(o, 'h', SWAP) for o in pieces]  12.6 us
    all_to_all x2, starting transfers between devices, all_reduced(): gathered = lax.all_to_all(copies, CHIPS, 0, 0, tiled=True)  11.3 us
    ppermute x8, starting transfers between devices, swap(): return lax.ppermute(x, 'c', SWAP)  8.53 us
    pallas_call x2, Pallas kernels, finish_product(): pl.pallas_call(functools.partial(finish_kernel, k), out_shape=shape((toke...  5.62 us
    pallas_call x1, Pallas kernels, partial_product(): pl.pallas_call(partial_kernel, out_shape=shape((tokens, n), F32), grid_sp...  4.82 us
  transfers between devices with their start and end apart: 13, of which 5 were waited for; matrix products, arithmetic and copies ran while one was open for 2% of the time, Pallas kernels for 18%

profile of v5, /device:TPU:1, one launch (start us, length us, event | category | flops | bytes accessed | tf_op | source)
XLA Modules:
  0.0 177.7 jit_solution(2445377080256465043)
XLA Ops:
  0.0 1.5 multiply_convert_fusion.targets.u_own
  1.6 1.5 collective-permute-start.1
  3.1 0.0 copy-done.5
  3.1 0.1 collective-permute-start
  3.2 3.6 %shard_map.82 = (bf16[512,1024]{1,0:T(8,128)(2,1)S(1)}, bf16[256,1024]{1,0:T(8,128)(2,1)S(1)}, f32[8,128]{1,0:T(8,128)S(1)}) custom-call(s32[1]{0:T(128)} %bitcast.1.core, bf16[1024,512]{1,0:T(8,128)(2,1)} %bitcast.16, bf16[1024,512]{1,0:T(8,128)(2,1)} %bitcast.17, bf16[512,1024]{1,0:T(8,128)(2,1)} %bitcast.18), custom_call_target="tpu_custom_call" | custom-call | flops 2097152 | bytes 5242880 | tf_op jit(solution)/shard_map/pallas_call | solution.py:56
  6.7 0.0 copy-start.1
  6.8 0.0 copy-start.4
  6.8 1.0 shard_map.83.raw
  7.8 0.0 collective-permute-done.1.u_oth
  7.8 0.0 collective-permute-done.k_oth
  7.8 0.0 copy-done.1
  7.8 0.1 copy-done.4
  7.9 4.4 %shard_map.84 = bf16[2,768,512]{2,1,0:T(8,128)(2,1)S(1)} custom-call(bf16[512,1024]{1,0:T(8,128)(2,1)S(1)} %get-tuple-element.19.w13.w13_far, bf16[256,1024]{1,0:T(8,128)(2,1)S(1)} %get-tuple-element.20.w2.w2_far, f32[768,512]{1,0:T(8,128)S(1)} %shard_map.83.raw, bf16[512,1024]{1,0:T(8,128)(2,1)S(1)} %copy-done.5, ...), custom_call_target="tpu_custom_call" | custom-call | flops 2415919104 | bytes 8388608 | tf_op jit(solution)/shard_map/pallas_call | solution.py:56
  12.3 30.3 %all_to_all.20.arrived = bf16[32,48,512]{2,1,0:T(8,128)(2,1)S(1)} all-to-all(bf16[32,48,512]{2,1,0:T(8,128)(2,1)S(1)} %bitcast.15), channel_id=1, replica_groups=mesh['z'=4,'xl'=2,'y'=4,'c'=2,'h'=2] {'z','xl','y'}, dimensions={0} | all-to-all | bytes 3145728 | tf_op jit(solution)/shard_map/all_to_all | solution.py:297
  42.6 0.3 shard_map.85
  42.9 0.0 copy-start.2
  42.9 1.1 copy-done.2
  44.1 5.7 %all-to-all-start.1 = ((bf16[32,48,512]{2,1,0:T(8,128)(2,1)}), bf16[32,48,512]{2,1,0:T(8,128)(2,1)S(1)}, u32[]{:S(2)}, u32[]{:S(2)}) async-start(bf16[32,48,512]{2,1,0:T(8,128)(2,1)} %copy-done.2), calls=%async_computation.1 | async-start | bytes 3145728 | tf_op jit(solution)/shard_map/all_to_all | solution.py:307
  49.8 3.4 %dynamic_slice.3 = bf16[512,2560]{1,0:T(8,128)(2,1)} dynamic-slice(bf16[1024,5120]{1,0:T(8,128)(2,1)} %refs_2_.1, s32[]{:T(128)S(6)} %select_n.6, s32[]{:T(128)S(6)} %select_n.7), dynamic_slice_sizes={512,2560} | dynamic-slice | bytes 5242884 | tf_op jit(solution)/shard_map/dynamic_slice | solution.py:328
  53.2 2.5 %collective-permute-start.8 = (bf16[512,2560]{1,0:T(8,128)(2,1)}, bf16[512,2560]{1,0:T(8,128)(2,1)}, u32[]{:S(2)}, u32[]{:S(2)}) collective-permute-start(bf16[512,2560]{1,0:T(8,128)(2,1)} %dynamic_slice.3), channel_id=1, source_target_pairs={{0,17},{17,0},{1,16},{16,1},{2,19},{19,2},{3,18},{18,3},{4,21},{21... | collective-permute-start | bytes 7864328 | tf_op jit(solution)/shard_map/ppermute | solution.py:329
  55.7 15.0 %all-to-all-done.1 = bf16[32,48,512]{2,1,0:T(8,128)(2,1)S(1)} async-done(((bf16[32,48,512]{2,1,0:T(8,128)(2,1)}), bf16[32,48,512]{2,1,0:T(8,128)(2,1)S(1)}, u32[]{:S(2)}, u32[]{:S(2)}) %all-to-all-start.1) | async-done | bytes 1572896 | tf_op jit(solution)/shard_map/all_to_all | solution.py:307
  70.7 0.0 copy-start
  70.7 0.0 copy-start.6
  70.7 2.7 %shard_map.86 = (bf16[512,1024]{1,0:T(8,128)(2,1)S(1)}, bf16[256,1024]{1,0:T(8,128)(2,1)S(1)}, f32[8,128]{1,0:T(8,128)S(1)}) custom-call(bf16[512,1024]{1,0:T(8,128)(2,1)} %copy-done.1, bf16[256,1024]{1,0:T(8,128)(2,1)} %copy-done.4, bf16[2,768,512]{2,1,0:T(8,128)(2,1)S(1)} %bitcast.12), custom_call_target="tpu_custom_call" | custom-call | flops 4194304 | bytes 5242880 | tf_op jit(solution)/shard_map/pallas_call | solution.py:56
  73.4 2.5 %collective-permute-start.2 = (f32[8,128]{1,0:T(8,128)S(1)}, f32[8,128]{1,0:T(8,128)S(1)}, u32[]{:S(2)}, u32[]{:S(2)}) collective-permute-start(f32[8,128]{1,0:T(8,128)S(1)} %get-tuple-element.22.rest_1_.rest_2_), channel_id=1, source_target_pairs={{0,2},{2,0},{1,3},{3,1},{4,6},{6,4},{5,7},{7,5},{8,10},{10,8},{9,1... | collective-permute-start | bytes 12296 | tf_op jit(solution)/shard_map/ppermute | solution.py:312
  76.0 0.0 copy-done.6
  76.0 1.0 shard_map.87.raw
  77.0 0.0 copy-done
  77.0 0.0 collective-permute-done.2.rest_2_.rest_3_
  77.0 4.5 %shard_map.88 = bf16[2,768,512]{2,1,0:T(8,128)(2,1)S(1)} custom-call(bf16[512,1024]{1,0:T(8,128)(2,1)S(1)} %get-tuple-element.23.w13, bf16[256,1024]{1,0:T(8,128)(2,1)S(1)} %get-tuple-element.24.w2, f32[768,512]{1,0:T(8,128)S(1)} %shard_map.87.raw, bf16[512,1024]{1,0:T(8,128)(2,1)S(1)} %copy-done.6, bf16[512,1024]{1,0:T(8,128)(2,1)} %collective-permute-done.k_oth, ...), custom_call_target="tpu_custom_call" | custom-call | flops 2415919104 | bytes 8388608 | tf_op jit(solution)/shard_map/pallas_call | solution.py:56
  81.5 27.3 %all_to_all.21.arrived = bf16[32,48,512]{2,1,0:T(8,128)(2,1)S(1)} all-to-all(bf16[32,48,512]{2,1,0:T(8,128)(2,1)S(1)} %bitcast.14), channel_id=1, replica_groups=mesh['z'=4,'xl'=2,'y'=4,'c'=2,'h'=2] {'z','xl','y'}, dimensions={0} | all-to-all | bytes 3145728 | tf_op jit(solution)/shard_map/all_to_all | solution.py:297
  108.8 0.3 shard_map.89
  109.1 0.0 copy-start.3
  109.1 1.2 copy-done.3
  110.3 5.6 %all-to-all-start.3 = ((bf16[32,48,512]{2,1,0:T(8,128)(2,1)}), bf16[32,48,512]{2,1,0:T(8,128)(2,1)}, u32[]{:S(2)}, u32[]{:S(2)}) async-start(bf16[32,48,512]{2,1,0:T(8,128)(2,1)} %copy-done.3), calls=%async_computation.3 | async-start | bytes 3145728 | tf_op jit(solution)/shard_map/all_to_all | solution.py:307
  115.9 0.0 collective-permute-done.8.first_far
  115.9 1.2 collective-permute-start.9
  117.1 0.1 collective-permute-start.3
  117.2 19.6 %all-to-all-done.3 = bf16[32,48,512]{2,1,0:T(8,128)(2,1)} async-done(((bf16[32,48,512]{2,1,0:T(8,128)(2,1)}), bf16[32,48,512]{2,1,0:T(8,128)(2,1)}, u32[]{:S(2)}, u32[]{:S(2)}) %all-to-all-start.3) | async-done | bytes 1572896 | tf_op jit(solution)/shard_map/all_to_all | solution.py:307
  136.8 4.5 %shard_map.90 = (bf16[512,1024]{1,0:T(8,128)(2,1)S(1)}, bf16[256,1024]{1,0:T(8,128)(2,1)S(1)}, f32[8,128]{1,0:T(8,128)S(1)}) custom-call(bf16[512,1024]{1,0:T(8,128)(2,1)} %copy-done.1, bf16[256,1024]{1,0:T(8,128)(2,1)} %copy-done.4, bf16[2,768,512]{2,1,0:T(8,128)(2,1)} %bitcast.13, f32[8,128]{1,0:T(8,128)S(1)} %get-tuple-element.21.rest_0_.rest_1_.norm, ...), custom_call_target="tpu_custom_call" | custom-call | flops 4194304 | bytes 5242880 | tf_op jit(solution)/shard_map/pallas_call | solution.py:56
  141.4 2.5 %collective-permute-start.6 = (bf16[256,1024]{1,0:T(8,128)(2,1)S(1)}, bf16[256,1024]{1,0:T(8,128)(2,1)S(1)}, u32[]{:S(2)}, u32[]{:S(2)}) collective-permute-start(bf16[256,1024]{1,0:T(8,128)(2,1)S(1)} %get-tuple-element.27.w2_own), channel_id=1, source_target_pairs={{0,2},{2,0},{1,3},{3,1},{4,6},{6,4},{5,7},{7,5},{8,10},{10,8},{9,1... | collective-permute-start | bytes 1572872 | tf_op jit(solution)/shard_map/ppermute | solution.py:312
  143.9 0.1 collective-permute-start.4
  144.0 0.0 collective-permute-done.3.oth_far
  144.0 2.2 %shard_map.91.raw = f32[2,512,512]{2,1,0:T(8,128)S(1)} custom-call(bf16[512,1024]{1,0:T(8,128)(2,1)S(1)} %get-tuple-element.25.m13, bf16[512,1024]{1,0:T(8,128)(2,1)S(1)} %collective-permute-done.3.oth_far, bf16[512,1024]{1,0:T(8,128)(2,1)} %own_far.1), custom_call_target="tpu_custom_call" | custom-call | flops 1073741824 | bytes 5242880 | tf_op jit(solution)/shard_map/pallas_call | solution.py:56
  146.2 0.0 collective-permute-done.4.sq_oth
  146.2 0.2 shard_map.93
  146.4 0.5 collective-permute-start.5
  146.9 0.2 shard_map.92.hq_own
  147.1 1.0 collective-permute-done.5.hq_got
  148.1 0.0 collective-permute-done.6.w2_got
  148.1 0.7 shard_map.94
  148.8 2.5 %collective-permute-start.10 = (bf16[256,1024]{1,0:T(8,128)(2,1)S(1)}, bf16[256,1024]{1,0:T(8,128)(2,1)S(1)}, u32[]{:S(2)}, u32[]{:S(2)}) collective-permute-start(bf16[256,1024]{1,0:T(8,128)(2,1)S(1)} %get-tuple-element.28.refs_0_.after), channel_id=1, source_target_pairs={{0,1},{1,0},{2,3},{3,2},{4,5},{5,4},{6,7},{7,6},{8,9},{9,8},{10,11... | collective-permute-start | bytes 1572872 | tf_op jit(solution)/shard_map/ppermute | solution.py:392
  151.3 0.5 collective-permute-start.7
  151.9 0.1 pad_add_fusion.place
  151.9 0.0 slice-done
  151.9 0.0 slice-done.1
  151.9 0.0 slice-done.2
  151.9 4.8 %shard_map.95.part = f32[512,2560]{1,0:T(8,128)S(1)} custom-call(s32[2]{0:T(128)S(1)} %pad_add_fusion.place, bf16[256,1024]{1,0:T(8,128)(2,1)S(1)} %get-tuple-element.28.refs_0_.after, bf16[256,1024]{1,0:T(8,128)(2,1)S(1)} %get-tuple-element.29.refs_1_, bf16[1024,5120]{1,0:T(8,128)(2,1)S(1)} %bitcast.11), custom_call_target="tpu_custom_call" | custom-call | flops 2684354560 | bytes 10485760 | tf_op jit(solution)/shard_map/pallas_call | solution.py:238
  156.8 0.0 collective-permute-done.9.second_far
  156.8 2.5 %shard_map.96 = (bf16[512,2560]{1,0:T(8,128)(2,1)S(1)}, bf16[512,2560]{1,0:T(8,128)(2,1)S(1)}) custom-call(bf16[256,1024]{1,0:T(8,128)(2,1)S(1)} %get-tuple-element.28.refs_0_.after, bf16[512,2560]{1,0:T(8,128)(2,1)} %collective-permute-done.8.first_far, bf16[512,2560]{1,0:T(8,128)(2,1)} %collective-permute-done.9.second_far), custom_call_target="tpu_custom_call" | custom-call | flops 1048576 | bytes 5242880 | tf_op jit(solution)/shard_map/pallas_call | solution.py:56
  159.3 4.2 %collective-permute-done.10.o_got = bf16[256,1024]{1,0:T(8,128)(2,1)S(1)} collective-permute-done((bf16[256,1024]{1,0:T(8,128)(2,1)S(1)}, bf16[256,1024]{1,0:T(8,128)(2,1)S(1)}, u32[]{:S(2)}, u32[]{:S(2)}) %collective-permute-start.10) | collective-permute-done | bytes 524320 | tf_op jit(solution)/shard_map/ppermute | solution.py:392
  163.5 2.8 %shard_map.97.rest_0_ = bf16[512,2560]{1,0:T(8,128)(2,1)} custom-call(s32[2]{0:T(128)S(1)} %pad_add_fusion.place, f32[512,2560]{1,0:T(8,128)S(1)} %shard_map.95.part, bf16[256,1024]{1,0:T(8,128)(2,1)S(1)} %collective-permute-done.10.o_got, bf16[512,2560]{1,0:T(8,128)(2,1)S(1)} %get-tuple-element.31.w_first, bf16[512,2560]{1,0:T(8,128)(2,1)S(1)} %get-tuple-element.32.w_second), custom_call_target="tpu_custom_call" | custom-call | flops 1342177280 | bytes 4194304 | tf_op jit(solution)/shard_map/pallas_call | solution.py:277
  166.3 8.4 %collective-permute-done.7.o_got = bf16[256,1024]{1,0:T(8,128)(2,1)S(1)} collective-permute-done((bf16[256,1024]{1,0:T(8,128)(2,1)S(1)}, bf16[256,1024]{1,0:T(8,128)(2,1)S(1)}, u32[]{:S(2)}, u32[]{:S(2)}) %collective-permute-start.7) | collective-permute-done | bytes 524320 | tf_op jit(solution)/shard_map/ppermute | solution.py:392
  174.8 2.8 %shard_map.98 = bf16[512,2560]{1,0:T(8,128)(2,1)} custom-call(s32[2]{0:T(128)S(1)} %pad_add_fusion.place, f32[512,2560]{1,0:T(8,128)S(1)} %shard_map.95.part, bf16[256,1024]{1,0:T(8,128)(2,1)S(1)} %collective-permute-done.7.o_got, bf16[512,2560]{1,0:T(8,128)(2,1)S(1)} %get-tuple-element.31.w_first, ...), custom_call_target="tpu_custom_call", output_to_operand_aliasing={{}: (5, {})} | custom-call | flops 1342177280 | bytes 4194304 | tf_op jit(solution)/shard_map/pallas_call | solution.py:277
  (5 shorter events, 0.0 us)
Async XLA Ops:
  0.0 3.1 %copy-start.5 = (bf16[512,1024]{1,0:T(8,128)(2,1)S(1)}, bf16[512,1024]{1,0:T(8,128)(2,1)}, u32[]{:S(2)}) copy-start(bf16[512,1024]{1,0:T(8,128)(2,1)} %k_own.3) | copy-start | bytes 3145732
  1.6 6.2 %collective-permute-start.1 = (bf16[512,1024]{1,0:T(8,128)(2,1)S(1)}, bf16[512,1024]{1,0:T(8,128)(2,1)}, u32[]{:S(2)}, u32[]{:S(2)}) collective-permute-start(bf16[512,1024]{1,0:T(8,128)(2,1)S(1)} %multiply_convert_fusion.targets.u_own), channel_id=1, source_target_pairs={{0,2},{2,0},{1,3},{3,1},{4,6},{6,4},{5,7},{7,5},{8,10},{10,8},{9,1... | collective-permute-start | bytes 3145736 | tf_op jit(solution)/shard_map/ppermute | solution.py:312
  3.1 4.7 %collective-permute-start = (bf16[512,1024]{1,0:T(8,128)(2,1)S(1)}, bf16[512,1024]{1,0:T(8,128)(2,1)}, u32[]{:S(2)}, u32[]{:S(2)}) collective-permute-start(bf16[512,1024]{1,0:T(8,128)(2,1)S(1)} %copy-done.5), channel_id=1, source_target_pairs={{0,2},{2,0},{1,3},{3,1},{4,6},{6,4},{5,7},{7,5},{8,10},{10,8},{9,1... | collective-permute-start | bytes 3145736 | tf_op jit(solution)/shard_map/ppermute | solution.py:312
  6.7 1.1 copy-start.1
  6.8 1.1 copy-start.4
  42.9 1.2 copy-start.2
  44.1 26.6 %all-to-all-start.1 = ((bf16[32,48,512]{2,1,0:T(8,128)(2,1)}), bf16[32,48,512]{2,1,0:T(8,128)(2,1)S(1)}, u32[]{:S(2)}, u32[]{:S(2)}) async-start(bf16[32,48,512]{2,1,0:T(8,128)(2,1)} %copy-done.2), calls=%async_computation.1 | async-start | bytes 3145728 | tf_op jit(solution)/shard_map/all_to_all | solution.py:307
  53.2 62.7 %collective-permute-start.8 = (bf16[512,2560]{1,0:T(8,128)(2,1)}, bf16[512,2560]{1,0:T(8,128)(2,1)}, u32[]{:S(2)}, u32[]{:S(2)}) collective-permute-start(bf16[512,2560]{1,0:T(8,128)(2,1)} %dynamic_slice.3), channel_id=1, source_target_pairs={{0,17},{17,0},{1,16},{16,1},{2,19},{19,2},{3,18},{18,3},{4,21},{21... | collective-permute-start | bytes 7864328 | tf_op jit(solution)/shard_map/ppermute | solution.py:329
  70.7 6.3 %copy-start = (bf16[32,48,512]{2,1,0:T(8,128)(2,1)}, bf16[32,48,512]{2,1,0:T(8,128)(2,1)S(1)}, u32[]{:S(2)}) copy-start(bf16[32,48,512]{2,1,0:T(8,128)(2,1)S(1)} %all-to-all-done.1) | copy-start | bytes 4718596
  70.7 5.3 %copy-start.6 = (bf16[512,1024]{1,0:T(8,128)(2,1)S(1)}, bf16[512,1024]{1,0:T(8,128)(2,1)}, u32[]{:S(2)}) copy-start(bf16[512,1024]{1,0:T(8,128)(2,1)} %k_own.3) | copy-start | bytes 3145732
  73.4 3.6 %collective-permute-start.2 = (f32[8,128]{1,0:T(8,128)S(1)}, f32[8,128]{1,0:T(8,128)S(1)}, u32[]{:S(2)}, u32[]{:S(2)}) collective-permute-start(f32[8,128]{1,0:T(8,128)S(1)} %get-tuple-element.22.rest_1_.rest_2_), channel_id=1, source_target_pairs={{0,2},{2,0},{1,3},{3,1},{4,6},{6,4},{5,7},{7,5},{8,10},{10,8},{9,1... | collective-permute-start | bytes 12296 | tf_op jit(solution)/shard_map/ppermute | solution.py:312
  108.8 43.1 %slice-start = ((s8[10485760]{0:T(1024)(128)(4,1)}), s8[2097152]{0:T(1024)(128)(4,1)S(1)}, s32[]{:S(2)}) async-start(s8[10485760]{0:T(1024)(128)(4,1)} %bitcast.10), calls=%async_computation.4 | async-start | bytes 4194304
  109.1 1.2 copy-start.3
  110.3 26.5 %all-to-all-start.3 = ((bf16[32,48,512]{2,1,0:T(8,128)(2,1)}), bf16[32,48,512]{2,1,0:T(8,128)(2,1)}, u32[]{:S(2)}, u32[]{:S(2)}) async-start(bf16[32,48,512]{2,1,0:T(8,128)(2,1)} %copy-done.3), calls=%async_computation.3 | async-start | bytes 3145728 | tf_op jit(solution)/shard_map/all_to_all | solution.py:307
  115.9 40.9 %collective-permute-start.9 = (bf16[512,2560]{1,0:T(8,128)(2,1)}, bf16[512,2560]{1,0:T(8,128)(2,1)}, u32[]{:S(2)}, u32[]{:S(2)}) collective-permute-start(bf16[512,2560]{1,0:T(8,128)(2,1)} %collective-permute-done.8.first_far), channel_id=1, source_target_pairs={{0,2},{2,0},{1,3},{3,1},{4,6},{6,4},{5,7},{7,5},{8,10},{10,8},{9,1... | collective-permute-start | bytes 7864328 | tf_op jit(solution)/shard_map/ppermute | solution.py:312
  117.1 26.9 %collective-permute-start.3 = (bf16[512,1024]{1,0:T(8,128)(2,1)}, bf16[512,1024]{1,0:T(8,128)(2,1)S(1)}, u32[]{:S(2)}, u32[]{:S(2)}) collective-permute-start(bf16[512,1024]{1,0:T(8,128)(2,1)} %own_far.1), channel_id=1, source_target_pairs={{0,2},{2,0},{1,3},{3,1},{4,6},{6,4},{5,7},{7,5},{8,10},{10,8},{9,1... | collective-permute-start | bytes 3145736 | tf_op jit(solution)/shard_map/ppermute | solution.py:312
  136.8 15.1 %slice-start.1 = ((s8[10485760]{0:T(1024)(128)(4,1)}), s8[4194304]{0:T(1024)(128)(4,1)S(1)}, s32[]{:S(2)}) async-start(s8[10485760]{0:T(1024)(128)(4,1)} %bitcast.10), calls=%async_computation.5 | async-start | bytes 8388608
  141.4 6.7 %collective-permute-start.6 = (bf16[256,1024]{1,0:T(8,128)(2,1)S(1)}, bf16[256,1024]{1,0:T(8,128)(2,1)S(1)}, u32[]{:S(2)}, u32[]{:S(2)}) collective-permute-start(bf16[256,1024]{1,0:T(8,128)(2,1)S(1)} %get-tuple-element.27.w2_own), channel_id=1, source_target_pairs={{0,2},{2,0},{1,3},{3,1},{4,6},{6,4},{5,7},{7,5},{8,10},{10,8},{9,1... | collective-permute-start | bytes 1572872 | tf_op jit(solution)/shard_map/ppermute | solution.py:312
  143.9 2.3 %collective-permute-start.4 = (f32[8,128]{1,0:T(8,128)S(1)}, f32[8,128]{1,0:T(8,128)S(1)}, u32[]{:S(2)}, u32[]{:S(2)}) collective-permute-start(f32[8,128]{1,0:T(8,128)S(1)} %get-tuple-element.26.sq_own), channel_id=1, source_target_pairs={{0,2},{2,0},{1,3},{3,1},{4,6},{6,4},{5,7},{7,5},{8,10},{10,8},{9,1... | collective-permute-start | bytes 12296 | tf_op jit(solution)/shard_map/ppermute | solution.py:312
  144.0 8.0 %slice-start.2 = ((s8[10485760]{0:T(1024)(128)(4,1)}), s8[4194304]{0:T(1024)(128)(4,1)S(1)}, s32[]{:S(2)}) async-start(s8[10485760]{0:T(1024)(128)(4,1)} %bitcast.10), calls=%async_computation.6 | async-start | bytes 8388608
  146.4 1.7 collective-permute-start.5
  148.8 14.7 %collective-permute-start.10 = (bf16[256,1024]{1,0:T(8,128)(2,1)S(1)}, bf16[256,1024]{1,0:T(8,128)(2,1)S(1)}, u32[]{:S(2)}, u32[]{:S(2)}) collective-permute-start(bf16[256,1024]{1,0:T(8,128)(2,1)S(1)} %get-tuple-element.28.refs_0_.after), channel_id=1, source_target_pairs={{0,1},{1,0},{2,3},{3,2},{4,5},{5,4},{6,7},{7,6},{8,9},{9,8},{10,11... | collective-permute-start | bytes 1572872 | tf_op jit(solution)/shard_map/ppermute | solution.py:392
  151.3 23.4 %collective-permute-start.7 = (bf16[256,1024]{1,0:T(8,128)(2,1)S(1)}, bf16[256,1024]{1,0:T(8,128)(2,1)S(1)}, u32[]{:S(2)}, u32[]{:S(2)}) collective-permute-start(bf16[256,1024]{1,0:T(8,128)(2,1)S(1)} %get-tuple-element.29.refs_1_), channel_id=1, source_target_pairs={{0,1},{1,0},{2,3},{3,2},{4,5},{5,4},{6,7},{7,6},{8,9},{9,8},{10,11... | collective-permute-start | bytes 1572872 | tf_op jit(solution)/shard_map/ppermute | solution.py:392

commit v6 on v5

--- a/solution.py
+++ b/solution.py
@@ -24,7 +24,6 @@
 NEAR = pl.BlockSpec(memory_space=pltpu.VMEM)
 HELD = {id(FAR): pltpu.HBM, id(NEAR): pltpu.VMEM}
 LIMIT = 24 * 1024 * 1024
-CHUNKS = 2
 
 
 def dot(x, y):
@@ -143,7 +142,11 @@
 
 
 def update_kernel(w13_far, w2_far, *rest):
-    *again, gathered, m13, m2, squares, w13, w2, first, sems = rest
+    if len(rest) > 8:
+        first_far, *state, gathered_far, m13, m2, squares, w13, w2, first, gathered, sems = rest
+    else:
+        gathered, m13, m2, squares, w13, w2, first, sems = rest
+    again = len(rest) > 8
     half = w2.shape[0]
     cols = w2.shape[1] // 2
     pairs = []
@@ -153,14 +156,15 @@
         at = slice(i * half, (i + 1) * half)
         pairs.append((src.at[rows, :], dst.at[rows, :]))
         if again:
-            pairs.append((again[0].at[:, at, :], first.at[:, at, :]))
+            pairs.append((first_far.at[:, at, :], first.at[:, at, :]))
+            pairs.append((gathered_far.at[:, at, :], gathered.at[:, at, :]))
     each = len(pairs) // 3
     copies = fetch(pairs, sems)
     for i in range(3):
         src, dst = (w13, m13) if i < 2 else (w2, m2)
         base = (i % 2) * half
         if again:
-            scale = jnp.broadcast_to(factor(i, *again[1:]), (ROWS, cols))
+            scale = jnp.broadcast_to(factor(i, *state), (ROWS, cols))
         for copy in copies[i * each : (i + 1) * each]:
             copy.wait()
 
@@ -194,16 +198,11 @@
     half = hq.shape[0]
     act = raw[k, 0:half, :] * factor(0, norm, sq_own, sq_oth)
     lin = raw[k, half:, :] * factor(1, norm, sq_own, sq_oth)
-    hq[...] = (jax.nn.silu(act) * lin).astype(BF)
-
-
-def piece_kernel(hq_own, hq_got, w2_own, w2_got, norm, sq_own, sq_oth, *pieces):
-    count = pieces[0].shape[0]
-    scale = factor(2, norm, sq_own, sq_oth)
-    for k, o in enumerate(pieces):
-        at = slice(k * count, (k + 1) * count)
-        total = tn(hq_own[:, at], w2_own[...]) + tn(hq_got[:, at], w2_got[...])
-        o[...] = (total * scale).astype(BF)
+    hq[...] = (jax.nn.silu(act) * lin * factor(2, norm, sq_own, sq_oth)).astype(BF)
+
+
+def piece_kernel(hq_own, hq_got, w2_own, w2_got, o):
+    o[...] = (tn(hq_own[...], w2_own[...]) + tn(hq_got[...], w2_got[...])).astype(BF)
 
 
 def spread_kernel(arrived, out):
@@ -223,72 +222,68 @@
 TILE = 512
 
 
-def partial_kernel(place, *refs):
-    *pieces, w_own, out = refs
-    count = pieces[0].shape[0]
-    for k, o in enumerate(pieces):
-        out[k * count : (k + 1) * count, :] = dot(o[...], w_own[...])
-
-
-def partial_product(place, pieces, w_out):
-    count, width = pieces[0].shape
+def partial_kernel(place, o, w_own, out):
+    out[...] = dot(o[...], w_own[...])
+
+
+def partial_product(place, o, w_out):
+    tokens, width = o.shape
     n = w_out.shape[1] // 2
     steps = n // TILE
-    tokens = count * len(pieces)
     return pl.pallas_call(
         partial_kernel,
         out_shape=shape((tokens, n), F32),
         grid_spec=pltpu.PrefetchScalarGridSpec(
             num_scalar_prefetch=1,
             grid=(steps,),
-            in_specs=[pl.BlockSpec((count, width), lambda i, s: (0, 0))] * len(pieces)
-            + [pl.BlockSpec((width, TILE), lambda i, s: (0, s[0] * steps + i))],
+            in_specs=[
+                pl.BlockSpec((tokens, width), lambda i, s: (0, 0)),
+                pl.BlockSpec((width, TILE), lambda i, s: (0, s[0] * steps + i)),
+            ],
             out_specs=pl.BlockSpec((tokens, TILE), lambda i, s: (0, i)),
         ),
         compiler_params=pltpu.CompilerParams(vmem_limit_bytes=LIMIT),
         cost_estimate=pl.CostEstimate(
-            flops=2 * tokens * width * n, bytes_accessed=10 << 20, transcendentals=0
+            flops=1 << 20, bytes_accessed=1 << 16, transcendentals=0
         ),
-    )(place, *pieces, w_out)
-
-
-def finish_kernel(k, place, part, o_got, w_first, w_second, *rest):
-    *_, out, held, sems = rest
-    count, width = o_got.shape
-    half = width // 2
-    rows = slice(k * count, (k + 1) * count)
-    o_first = o_got[:, pl.ds(pl.multiple_of(place[1] * half, 128), half)]
-    o_second = o_got[:, pl.ds(pl.multiple_of((1 - place[1]) * half, 128), half)]
+    )(place, o, w_out)
+
+
+def finish_kernel(place, part, hq_a, hq_b, *rest):
+    w2_a, w2_b, w_first, w_second, out, o, held, sems = rest
+    half = o.shape[1] // 2
+    o[...] = (tn(hq_a[...], w2_a[...]) + tn(hq_b[...], w2_b[...])).astype(BF)
+    o_first = o[:, pl.ds(pl.multiple_of(place[1] * half, half), half)]
+    o_second = o[:, pl.ds(pl.multiple_of((1 - place[1]) * half, half), half)]
     copies = []
     for j in range(part.shape[1] // TILE):
         at = slice(j * TILE, (j + 1) * TILE)
-        total = part[rows, at] + dot(o_first, w_first[:, at]) + dot(o_second, w_second[:, at])
+        total = part[:, at] + dot(o_first, w_first[:, at]) + dot(o_second, w_second[:, at])
         held[j] = total.astype(BF)
-        copies.append(pltpu.make_async_copy(held.at[j], out.at[rows, at], sems.at[j]))
+        copies.append(pltpu.make_async_copy(held.at[j], out.at[:, at], sems.at[j]))
         copies[-1].start()
     for copy in copies:
         copy.wait()
 
 
-def finish_product(place, k, part, o_got, w_first, w_second, out):
-    count, width = o_got.shape
+def finish_product(place, part, hqs, w2s, w_first, w_second):
     tokens, n = part.shape
-    args = (place, part, o_got, w_first, w_second)
+    width = w2s[0].shape[1]
     return pl.pallas_call(
-        functools.partial(finish_kernel, k),
+        finish_kernel,
         out_shape=shape((tokens, n)),
-        in_specs=[SMEM] + [VMEM] * 4 + [FAR] * (out is not None),
+        in_specs=[SMEM] + [VMEM] * 7,
         out_specs=FAR,
         scratch_shapes=[
-            pltpu.VMEM((n // TILE, count, TILE), BF),
-            pltpu.SemaphoreType.DMA((n // TILE,)),
+            buffer((tokens, width)),
+            buffer((n // TILE, tokens, TILE)),
+            semaphores(n // TILE),
         ],
-        input_output_aliases={} if out is None else {len(args): 0},
         compiler_params=pltpu.CompilerParams(vmem_limit_bytes=LIMIT),
         cost_estimate=pl.CostEstimate(
-            flops=2 * count * width * n, bytes_accessed=4 << 20, transcendentals=0
+            flops=2 * tokens * width * (n + width // 2), bytes_accessed=6 << 20, transcendentals=0
         ),
-    )(*args, *(() if out is None else (out,)))
+    )(place, part, *hqs, *w2s, w_first, w_second)
 
 
 def all_reduced(grads, beside=None):
@@ -327,7 +322,6 @@
     place = jnp.stack([head, core]).astype(jnp.int32)
     sent = lax.dynamic_slice(w_out, (core * (width // 2), (1 - head) * n), (width // 2, n))
     w_first = lax.ppermute(sent, ("xl", "h"), ACROSS)
-    q_oth = swap(queries)
 
     wshape = (shape((2 * half, width)), shape((half, width)))
     sshape = shape((8, 128), F32)
@@ -355,19 +349,22 @@
         *mats, squares = call(
             update_kernel,
             (*wshape, sshape),
-            [FAR] * 2 + ([FAR] + [VMEM] * 3) * step + [NEAR],
+            [FAR] * 2 + ([FAR] + [VMEM] * 3) * step + [ANY if step else NEAR],
             1 << 22,
             5 << 20,
             (
                 buffer((2 * half, width)),
                 buffer((half, width)),
                 buffer(gdims),
-                semaphores(3 + 3 * step),
+                *([buffer(gdims)] * step),
+                semaphores(3 + 6 * step),
             ),
         )(*w, *again, gathered)
         first = gathered
         state = (norm, squares, swap(squares))
+    crossed = lax.ppermute(mats[1], ("xl", "h"), ACROSS)
     w_second = swap(w_late)
+    q_oth = swap(queries)
     w2_got = swap(mats[1])
     hshape = shape((half, tokens))
     raw = call(
@@ -382,23 +379,18 @@
         call(functools.partial(hidden_kernel, k), hshape, [VMEM] * 4, 1 << 20, 2 << 20)(raw, *state)
         for k in range(2)
     )
-    pieces = call(
-        piece_kernel,
-        (shape((tokens // CHUNKS, width)),) * CHUNKS,
-        [VMEM] * 7,
-        2 * tokens * hid * width,
-        4 << 20,
-    )(hq_own, swap(hq_oth), mats[1], w2_got, *state)
-    pieces_got = [lax.ppermute(o, "h", SWAP) for o in pieces]
-    part = partial_product(place, pieces, w_out)
+    hq_got = swap(hq_oth)
+    hqs = [lax.ppermute(x, "h", SWAP) for x in (hq_own, hq_got)]
+    o = call(piece_kernel, shape((tokens, width)), [VMEM] * 4, 1 << 20, 1 << 16)(
+        hq_own, hq_got, mats[1], w2_got
+    )
+    part = partial_product(place, o, w_out)
     wide = (shape(w_first.shape),) * 2
-    w_first, w_second = call(stage_kernel, wide, [ANY] * 3, 1 << 20, 5 << 20, [semaphores(2)])(
-        pieces[0], w_first, w_second
-    )
-    out = None
-    for k, o_got in enumerate(pieces_got):
-        out = finish_product(place, k, part, o_got, w_first, w_second, out)
-    return out
+    w_first, w_second = call(stage_kernel, wide, [ANY] * 3, 1 << 16, 1 << 16, [semaphores(2)])(
+        hqs[0], w_first, w_second
+    )
+    crossed, *hqs, _, _ = lax.optimization_barrier((crossed, *hqs, part, w_first))
+    return finish_product(place, part, hqs, (crossed, swap(crossed)), w_first, w_second)
 
 
 def solution(mesh):

time: 178 us -> 180 us (1.011)
  starting transfers between devices: 25.3 us -> 31.2 us
  Pallas kernels: 38.7 us -> 36.8 us
  waiting for transfers between devices: 48.3 us -> 46.4 us
    ppermute x2 -> x3, waiting for transfers between devices: 12.6 us -> 5.9 us  [the longest x1 5.08 us: shards(): crossed = lax.ppermute(mats[1], ('xl', 'h'), ACROSS)]
    ppermute x8 -> x9, starting transfers between devices: 8.53 us -> 10.9 us  [swap(): return lax.ppermute(x, 'c', SWAP)]
    all_to_all x2, waiting for transfers between devices: 34.7 us -> 37 us  [all_reduced(): gathered = lax.all_to_all(copies, CHIPS, 0, 0, tiled=True)]
    ppermute x2 -> x3, starting transfers between devices: 3.05 us -> 5.26 us  [the longest x2 2.74 us: shards(): hqs = [lax.ppermute(x, 'h', SWAP) for x in (hq_own, hq_got)]]
    pallas_call x2 -> x1, Pallas kernels: 5.62 us -> 5 us  [finish_product(): pl.pallas_call(finish_kernel, out_shape=shape((tokens, n)), in_specs=[SME...]
  transfers between devices with their start and end apart: 13 -> 15, of which waited for: 5 -> 7; matrix products, arithmetic and copies ran while one was open for 2% -> 2% of each run, Pallas kernels for 18% -> 15%
where the time goes in v6:
time: 180 us
  blocking collectives  57.6 us (32%)
  waiting for transfers between devices  46.4 us (26%)
  Pallas kernels  36.8 us (20%)
  starting transfers between devices  31.2 us (17%)
  local copies, waits for them, and re-layouts  5.82 us (3%)
    all_to_all x2, blocking collectives, all_reduced(): arrived = lax.all_to_all(pieces, CHIPS, 0, 0, tiled=True)  57.6 us
    all_to_all x2, waiting for transfers between devices, all_reduced(): gathered = lax.all_to_all(copies, CHIPS, 0, 0, tiled=True)  37 us
    pallas_call x14, Pallas kernels, with_places(): run(*(pltpu.with_memory_space_constraint(x, HELD[id(spec)]) if id(spec) i...  27 us
    all_to_all x2, starting transfers between devices, all_reduced(): gathered = lax.all_to_all(copies, CHIPS, 0, 0, tiled=True)  12.6 us
    ppermute x9, starting transfers between devices, swap(): return lax.ppermute(x, 'c', SWAP)  10.9 us
    ppermute x1, waiting for transfers between devices, shards(): crossed = lax.ppermute(mats[1], ('xl', 'h'), ACROSS)  5.08 us
    pallas_call x1, Pallas kernels, finish_product(): pl.pallas_call(finish_kernel, out_shape=shape((tokens, n)), in_specs=[SME...  5 us
    pallas_call x1, Pallas kernels, partial_product(): pl.pallas_call(partial_kernel, out_shape=shape((tokens, n), F32), grid_sp...  4.82 us
  transfers between devices with their start and end apart: 15, of which 7 were waited for; matrix products, arithmetic and copies ran while one was open for 2% of the time, Pallas kernels for 15%

profile of v6, /device:TPU:1, one launch (start us, length us, event | category | flops | bytes accessed | tf_op | source)
XLA Modules:
  0.0 179.9 jit_solution(13333922269761169912)
XLA Ops:
  0.0 1.5 multiply_convert_fusion.targets.u_own
  1.6 1.5 collective-permute-start.1
  3.1 0.0 copy-done.5
  3.1 0.1 collective-permute-start
  3.2 3.6 %shard_map.82 = (bf16[512,1024]{1,0:T(8,128)(2,1)S(1)}, bf16[256,1024]{1,0:T(8,128)(2,1)S(1)}, f32[8,128]{1,0:T(8,128)S(1)}) custom-call(s32[1]{0:T(128)} %bitcast.1.core, bf16[1024,512]{1,0:T(8,128)(2,1)} %bitcast.16, bf16[1024,512]{1,0:T(8,128)(2,1)} %bitcast.17, bf16[512,1024]{1,0:T(8,128)(2,1)} %bitcast.18), custom_call_target="tpu_custom_call" | custom-call | flops 2097152 | bytes 5242880 | tf_op jit(solution)/shard_map/pallas_call | solution.py:55
  6.7 0.0 copy-start.1
  6.8 0.0 copy-start.4
  6.8 1.0 shard_map.83.raw
  7.8 0.0 collective-permute-done.1.u_oth
  7.8 0.0 collective-permute-done.k_oth
  7.8 0.0 copy-done.1
  7.8 0.1 copy-done.4
  7.9 4.4 %shard_map.84 = bf16[2,768,512]{2,1,0:T(8,128)(2,1)S(1)} custom-call(bf16[512,1024]{1,0:T(8,128)(2,1)S(1)} %get-tuple-element.20.w13.w13_far, bf16[256,1024]{1,0:T(8,128)(2,1)S(1)} %get-tuple-element.21.w2.w2_far, f32[768,512]{1,0:T(8,128)S(1)} %shard_map.83.raw, bf16[512,1024]{1,0:T(8,128)(2,1)S(1)} %copy-done.5, ...), custom_call_target="tpu_custom_call" | custom-call | flops 2415919104 | bytes 8388608 | tf_op jit(solution)/shard_map/pallas_call | solution.py:55
  12.3 30.3 %all_to_all.20.arrived = bf16[32,48,512]{2,1,0:T(8,128)(2,1)S(1)} all-to-all(bf16[32,48,512]{2,1,0:T(8,128)(2,1)S(1)} %bitcast.15), channel_id=1, replica_groups=mesh['z'=4,'xl'=2,'y'=4,'c'=2,'h'=2] {'z','xl','y'}, dimensions={0} | all-to-all | bytes 3145728 | tf_op jit(solution)/shard_map/all_to_all | solution.py:292
  42.6 0.3 shard_map.85
  42.9 0.0 copy-start.2
  42.9 1.1 copy-done.2
  44.1 5.7 %all-to-all-start.1 = ((bf16[32,48,512]{2,1,0:T(8,128)(2,1)}), bf16[32,48,512]{2,1,0:T(8,128)(2,1)S(1)}, u32[]{:S(2)}, u32[]{:S(2)}) async-start(bf16[32,48,512]{2,1,0:T(8,128)(2,1)} %copy-done.2), calls=%async_computation.1 | async-start | bytes 3145728 | tf_op jit(solution)/shard_map/all_to_all | solution.py:302
  49.7 3.4 %dynamic_slice.3 = bf16[512,2560]{1,0:T(8,128)(2,1)} dynamic-slice(bf16[1024,5120]{1,0:T(8,128)(2,1)} %w_own.1, s32[]{:T(128)S(6)} %select_n.6, s32[]{:T(128)S(6)} %select_n.7), dynamic_slice_sizes={512,2560} | dynamic-slice | bytes 5242884 | tf_op jit(solution)/shard_map/dynamic_slice | solution.py:323
  53.2 2.5 %collective-permute-start.10 = (bf16[512,2560]{1,0:T(8,128)(2,1)}, bf16[512,2560]{1,0:T(8,128)(2,1)}, u32[]{:S(2)}, u32[]{:S(2)}) collective-permute-start(bf16[512,2560]{1,0:T(8,128)(2,1)} %dynamic_slice.3), channel_id=1, source_target_pairs={{0,17},{17,0},{1,16},{16,1},{2,19},{19,2},{3,18},{18,3},{4,21},{21... | collective-permute-start | bytes 7864328 | tf_op jit(solution)/shard_map/ppermute | solution.py:324
  55.6 15.0 %all-to-all-done.1 = bf16[32,48,512]{2,1,0:T(8,128)(2,1)S(1)} async-done(((bf16[32,48,512]{2,1,0:T(8,128)(2,1)}), bf16[32,48,512]{2,1,0:T(8,128)(2,1)S(1)}, u32[]{:S(2)}, u32[]{:S(2)}) %all-to-all-start.1) | async-done | bytes 1572896 | tf_op jit(solution)/shard_map/all_to_all | solution.py:302
  70.7 2.7 %shard_map.86 = (bf16[512,1024]{1,0:T(8,128)(2,1)S(1)}, bf16[256,1024]{1,0:T(8,128)(2,1)S(1)}, f32[8,128]{1,0:T(8,128)S(1)}) custom-call(bf16[512,1024]{1,0:T(8,128)(2,1)} %copy-done.1, bf16[256,1024]{1,0:T(8,128)(2,1)} %copy-done.4, bf16[2,768,512]{2,1,0:T(8,128)(2,1)S(1)} %bitcast.12), custom_call_target="tpu_custom_call" | custom-call | flops 4194304 | bytes 5242880 | tf_op jit(solution)/shard_map/pallas_call | solution.py:55
  73.4 2.5 %collective-permute-start.2 = (f32[8,128]{1,0:T(8,128)S(1)}, f32[8,128]{1,0:T(8,128)S(1)}, u32[]{:S(2)}, u32[]{:S(2)}) collective-permute-start(f32[8,128]{1,0:T(8,128)S(1)} %get-tuple-element.23.rest_1_.rest_2_), channel_id=1, source_target_pairs={{0,2},{2,0},{1,3},{3,1},{4,6},{6,4},{5,7},{7,5},{8,10},{10,8},{9,1... | collective-permute-start | bytes 12296 | tf_op jit(solution)/shard_map/ppermute | solution.py:307
  76.0 0.0 copy-done.6
  76.0 1.0 shard_map.87.raw
  77.0 0.0 copy-done
  77.0 0.0 collective-permute-done.2.rest_2_.rest_3_
  77.0 4.5 %shard_map.88 = bf16[2,768,512]{2,1,0:T(8,128)(2,1)S(1)} custom-call(bf16[512,1024]{1,0:T(8,128)(2,1)S(1)} %get-tuple-element.24.w13, bf16[256,1024]{1,0:T(8,128)(2,1)S(1)} %get-tuple-element.25.w2, f32[768,512]{1,0:T(8,128)S(1)} %shard_map.87.raw, bf16[512,1024]{1,0:T(8,128)(2,1)S(1)} %copy-done.6, bf16[512,1024]{1,0:T(8,128)(2,1)} %collective-permute-done.k_oth, ...), custom_call_target="tpu_custom_call" | custom-call | flops 2415919104 | bytes 8388608 | tf_op jit(solution)/shard_map/pallas_call | solution.py:55
  81.5 27.3 %all_to_all.21.arrived = bf16[32,48,512]{2,1,0:T(8,128)(2,1)S(1)} all-to-all(bf16[32,48,512]{2,1,0:T(8,128)(2,1)S(1)} %bitcast.14), channel_id=1, replica_groups=mesh['z'=4,'xl'=2,'y'=4,'c'=2,'h'=2] {'z','xl','y'}, dimensions={0} | all-to-all | bytes 3145728 | tf_op jit(solution)/shard_map/all_to_all | solution.py:292
  108.8 0.3 shard_map.89
  109.1 0.0 copy-start.3
  109.1 1.2 copy-done.3
  110.3 1.6 collective-permute-done.10.first_far
  111.9 2.1 %collective-permute-start.11 = (bf16[512,2560]{1,0:T(8,128)(2,1)}, bf16[512,2560]{1,0:T(8,128)(2,1)}, u32[]{:S(2)}, u32[]{:S(2)}) collective-permute-start(bf16[512,2560]{1,0:T(8,128)(2,1)} %collective-permute-done.10.first_far), channel_id=1, source_target_pairs={{0,2},{2,0},{1,3},{3,1},{4,6},{6,4},{5,7},{7,5},{8,10},{10,8},{9,1... | collective-permute-start | bytes 7864328 | tf_op jit(solution)/shard_map/ppermute | solution.py:307
  114.0 6.9 %all-to-all-start.3 = ((bf16[32,48,512]{2,1,0:T(8,128)(2,1)}), bf16[32,48,512]{2,1,0:T(8,128)(2,1)}, u32[]{:S(2)}, u32[]{:S(2)}) async-start(bf16[32,48,512]{2,1,0:T(8,128)(2,1)} %copy-done.3), calls=%async_computation.3 | async-start | bytes 3145728 | tf_op jit(solution)/shard_map/all_to_all | solution.py:302
  120.9 0.4 collective-permute-start.3
  121.3 21.9 %all-to-all-done.3 = bf16[32,48,512]{2,1,0:T(8,128)(2,1)} async-done(((bf16[32,48,512]{2,1,0:T(8,128)(2,1)}), bf16[32,48,512]{2,1,0:T(8,128)(2,1)}, u32[]{:S(2)}, u32[]{:S(2)}) %all-to-all-start.3) | async-done | bytes 1572896 | tf_op jit(solution)/shard_map/all_to_all | solution.py:302
  143.2 3.1 %shard_map.90 = (bf16[512,1024]{1,0:T(8,128)(2,1)S(1)}, bf16[256,1024]{1,0:T(8,128)(2,1)S(1)}, f32[8,128]{1,0:T(8,128)S(1)}) custom-call(bf16[512,1024]{1,0:T(8,128)(2,1)} %copy-done.1, bf16[256,1024]{1,0:T(8,128)(2,1)} %copy-done.4, bf16[2,768,512]{2,1,0:T(8,128)(2,1)} %bitcast.13, f32[8,128]{1,0:T(8,128)S(1)} %get-tuple-element.22.rest_0_.rest_1_.norm, ...), custom_call_target="tpu_custom_call" | custom-call | flops 4194304 | bytes 5242880 | tf_op jit(solution)/shard_map/pallas_call | solution.py:55
  146.3 2.5 %collective-permute-start.7 = (bf16[256,1024]{1,0:T(8,128)(2,1)S(1)}, bf16[256,1024]{1,0:T(8,128)(2,1)S(1)}, u32[]{:S(2)}, u32[]{:S(2)}) collective-permute-start(bf16[256,1024]{1,0:T(8,128)(2,1)S(1)} %get-tuple-element.28.w2_own), channel_id=1, source_target_pairs={{0,17},{17,0},{1,16},{16,1},{2,19},{19,2},{3,18},{18,3},{4,21},{21... | collective-permute-start | bytes 1572872 | tf_op jit(solution)/shard_map/ppermute | solution.py:365
  148.8 1.7 collective-permute-start.6
  150.5 0.0 collective-permute-start.4
  150.5 0.0 collective-permute-done.3.oth_far
  150.5 2.2 %shard_map.91.raw = f32[2,512,512]{2,1,0:T(8,128)S(1)} custom-call(bf16[512,1024]{1,0:T(8,128)(2,1)S(1)} %get-tuple-element.26.m13, bf16[512,1024]{1,0:T(8,128)(2,1)S(1)} %collective-permute-done.3.oth_far, bf16[512,1024]{1,0:T(8,128)(2,1)} %own_far.1), custom_call_target="tpu_custom_call" | custom-call | flops 1073741824 | bytes 5242880 | tf_op jit(solution)/shard_map/pallas_call | solution.py:55
  152.7 0.0 collective-permute-done.4.sq_oth
  152.7 0.3 shard_map.93
  153.0 0.6 collective-permute-start.5
  153.6 0.3 shard_map.92.hq_own
  153.9 0.6 collective-permute-start.8
  154.5 0.3 collective-permute-done.5.hq_got
  154.8 2.2 %collective-permute-start.9 = (bf16[256,512]{1,0:T(8,128)(2,1)S(1)}, bf16[256,512]{1,0:T(8,128)(2,1)S(1)}, u32[]{:S(2)}, u32[]{:S(2)}) collective-permute-start(bf16[256,512]{1,0:T(8,128)(2,1)S(1)} %collective-permute-done.5.hq_got), channel_id=1, source_target_pairs={{0,1},{1,0},{2,3},{3,2},{4,5},{5,4},{6,7},{7,6},{8,9},{9,8},{10,11... | collective-permute-start | bytes 786440 | tf_op jit(solution)/shard_map/ppermute | solution.py:383
  157.0 0.1 pad_add_fusion.place
  157.0 0.0 collective-permute-done.6.w2_got
  157.0 0.7 shard_map.94.o
  157.8 0.0 slice-done
  157.8 0.0 slice-done.1
  157.8 4.8 %shard_map.95.part = f32[512,2560]{1,0:T(8,128)S(1)} custom-call(s32[2]{0:T(128)S(1)} %pad_add_fusion.place, bf16[512,1024]{1,0:T(8,128)(2,1)S(1)} %shard_map.94.o, bf16[1024,5120]{1,0:T(8,128)(2,1)S(1)} %bitcast.11), custom_call_target="tpu_custom_call" | custom-call | flops 1048576 | bytes 65536 | tf_op jit(solution)/shard_map/pallas_call | solution.py:233
  162.6 0.8 collective-permute-done.8.after.hq_a
  163.5 0.0 collective-permute-done.11.second_far
  163.5 2.5 %shard_map.96 = (bf16[512,2560]{1,0:T(8,128)(2,1)S(1)}, bf16[512,2560]{1,0:T(8,128)(2,1)S(1)}) custom-call(bf16[256,512]{1,0:T(8,128)(2,1)S(1)} %collective-permute-done.8.after.hq_a, bf16[512,2560]{1,0:T(8,128)(2,1)} %collective-permute-done.10.first_far, bf16[512,2560]{1,0:T(8,128)(2,1)} %collective-permute-done.11.second_far), custom_call_target="tpu_custom_call" | custom-call | flops 65536 | bytes 65536 | tf_op jit(solution)/shard_map/pallas_call | solution.py:55
  166.0 5.1 %collective-permute-done.7.rest_0_ = bf16[256,1024]{1,0:T(8,128)(2,1)S(1)} collective-permute-done((bf16[256,1024]{1,0:T(8,128)(2,1)S(1)}, bf16[256,1024]{1,0:T(8,128)(2,1)S(1)}, u32[]{:S(2)}, u32[]{:S(2)}) %collective-permute-start.7) | collective-permute-done | bytes 524320 | tf_op jit(solution)/shard_map/ppermute | solution.py:365
  171.1 0.0 collective-permute-done.9.hq_b
  171.1 2.1 %collective-permute-start.12 = (bf16[256,1024]{1,0:T(8,128)(2,1)S(1)}, bf16[256,1024]{1,0:T(8,128)(2,1)S(1)}, u32[]{:S(2)}, u32[]{:S(2)}) collective-permute-start(bf16[256,1024]{1,0:T(8,128)(2,1)S(1)} %collective-permute-done.7.rest_0_), channel_id=1, source_target_pairs={{0,2},{2,0},{1,3},{3,1},{4,6},{6,4},{5,7},{7,5},{8,10},{10,8},{9,1... | collective-permute-start | bytes 1572872 | tf_op jit(solution)/shard_map/ppermute | solution.py:307
  173.2 1.5 collective-permute-done.12.rest_1_
  174.7 5.0 %shard_map.97 = bf16[512,2560]{1,0:T(8,128)(2,1)} custom-call(s32[2]{0:T(128)S(1)} %pad_add_fusion.place, f32[512,2560]{1,0:T(8,128)S(1)} %shard_map.95.part, bf16[256,512]{1,0:T(8,128)(2,1)S(1)} %collective-permute-done.8.after.hq_a, bf16[256,512]{1,0:T(8,128)(2,1)S(1)} %collective-permute-done.9.hq_b, ...), custom_call_target="tpu_custom_call" | custom-call | flops 3221225472 | bytes 6291456 | tf_op jit(solution)/shard_map/pallas_call | solution.py:272
  (8 shorter events, 0.0 us)
Async XLA Ops:
  0.0 3.1 %copy-start.5 = (bf16[512,1024]{1,0:T(8,128)(2,1)S(1)}, bf16[512,1024]{1,0:T(8,128)(2,1)}, u32[]{:S(2)}) copy-start(bf16[512,1024]{1,0:T(8,128)(2,1)} %k_own.3) | copy-start | bytes 3145732
  1.6 6.2 %collective-permute-start.1 = (bf16[512,1024]{1,0:T(8,128)(2,1)S(1)}, bf16[512,1024]{1,0:T(8,128)(2,1)}, u32[]{:S(2)}, u32[]{:S(2)}) collective-permute-start(bf16[512,1024]{1,0:T(8,128)(2,1)S(1)} %multiply_convert_fusion.targets.u_own), channel_id=1, source_target_pairs={{0,2},{2,0},{1,3},{3,1},{4,6},{6,4},{5,7},{7,5},{8,10},{10,8},{9,1... | collective-permute-start | bytes 3145736 | tf_op jit(solution)/shard_map/ppermute | solution.py:307
  3.1 4.7 %collective-permute-start = (bf16[512,1024]{1,0:T(8,128)(2,1)S(1)}, bf16[512,1024]{1,0:T(8,128)(2,1)}, u32[]{:S(2)}, u32[]{:S(2)}) collective-permute-start(bf16[512,1024]{1,0:T(8,128)(2,1)S(1)} %copy-done.5), channel_id=1, source_target_pairs={{0,2},{2,0},{1,3},{3,1},{4,6},{6,4},{5,7},{7,5},{8,10},{10,8},{9,1... | collective-permute-start | bytes 3145736 | tf_op jit(solution)/shard_map/ppermute | solution.py:307
  6.7 1.1 copy-start.1
  6.8 1.1 copy-start.4
  42.9 1.1 copy-start.2
  44.1 26.6 %all-to-all-start.1 = ((bf16[32,48,512]{2,1,0:T(8,128)(2,1)}), bf16[32,48,512]{2,1,0:T(8,128)(2,1)S(1)}, u32[]{:S(2)}, u32[]{:S(2)}) async-start(bf16[32,48,512]{2,1,0:T(8,128)(2,1)} %copy-done.2), calls=%async_computation.1 | async-start | bytes 3145728 | tf_op jit(solution)/shard_map/all_to_all | solution.py:302
  53.2 58.7 %collective-permute-start.10 = (bf16[512,2560]{1,0:T(8,128)(2,1)}, bf16[512,2560]{1,0:T(8,128)(2,1)}, u32[]{:S(2)}, u32[]{:S(2)}) collective-permute-start(bf16[512,2560]{1,0:T(8,128)(2,1)} %dynamic_slice.3), channel_id=1, source_target_pairs={{0,17},{17,0},{1,16},{16,1},{2,19},{19,2},{3,18},{18,3},{4,21},{21... | collective-permute-start | bytes 7864328 | tf_op jit(solution)/shard_map/ppermute | solution.py:324
  70.7 6.3 %copy-start = (bf16[32,48,512]{2,1,0:T(8,128)(2,1)}, bf16[32,48,512]{2,1,0:T(8,128)(2,1)S(1)}, u32[]{:S(2)}) copy-start(bf16[32,48,512]{2,1,0:T(8,128)(2,1)S(1)} %all-to-all-done.1) | copy-start | bytes 4718596
  70.7 5.3 %copy-start.6 = (bf16[512,1024]{1,0:T(8,128)(2,1)S(1)}, bf16[512,1024]{1,0:T(8,128)(2,1)}, u32[]{:S(2)}) copy-start(bf16[512,1024]{1,0:T(8,128)(2,1)} %k_own.3) | copy-start | bytes 3145732
  73.4 3.6 %collective-permute-start.2 = (f32[8,128]{1,0:T(8,128)S(1)}, f32[8,128]{1,0:T(8,128)S(1)}, u32[]{:S(2)}, u32[]{:S(2)}) collective-permute-start(f32[8,128]{1,0:T(8,128)S(1)} %get-tuple-element.23.rest_1_.rest_2_), channel_id=1, source_target_pairs={{0,2},{2,0},{1,3},{3,1},{4,6},{6,4},{5,7},{7,5},{8,10},{10,8},{9,1... | collective-permute-start | bytes 12296 | tf_op jit(solution)/shard_map/ppermute | solution.py:307
  108.8 49.0 %slice-start = ((s8[10485760]{0:T(1024)(128)(4,1)}), s8[2097152]{0:T(1024)(128)(4,1)S(1)}, s32[]{:S(2)}) async-start(s8[10485760]{0:T(1024)(128)(4,1)} %bitcast.10), calls=%async_computation.4 | async-start | bytes 4194304
  109.1 1.2 copy-start.3
  111.9 51.6 %collective-permute-start.11 = (bf16[512,2560]{1,0:T(8,128)(2,1)}, bf16[512,2560]{1,0:T(8,128)(2,1)}, u32[]{:S(2)}, u32[]{:S(2)}) collective-permute-start(bf16[512,2560]{1,0:T(8,128)(2,1)} %collective-permute-done.10.first_far), channel_id=1, source_target_pairs={{0,2},{2,0},{1,3},{3,1},{4,6},{6,4},{5,7},{7,5},{8,10},{10,8},{9,1... | collective-permute-start | bytes 7864328 | tf_op jit(solution)/shard_map/ppermute | solution.py:307
  114.0 29.2 %all-to-all-start.3 = ((bf16[32,48,512]{2,1,0:T(8,128)(2,1)}), bf16[32,48,512]{2,1,0:T(8,128)(2,1)}, u32[]{:S(2)}, u32[]{:S(2)}) async-start(bf16[32,48,512]{2,1,0:T(8,128)(2,1)} %copy-done.3), calls=%async_computation.3 | async-start | bytes 3145728 | tf_op jit(solution)/shard_map/all_to_all | solution.py:302
  120.9 29.6 %collective-permute-start.3 = (bf16[512,1024]{1,0:T(8,128)(2,1)}, bf16[512,1024]{1,0:T(8,128)(2,1)S(1)}, u32[]{:S(2)}, u32[]{:S(2)}) collective-permute-start(bf16[512,1024]{1,0:T(8,128)(2,1)} %own_far.1), channel_id=1, source_target_pairs={{0,2},{2,0},{1,3},{3,1},{4,6},{6,4},{5,7},{7,5},{8,10},{10,8},{9,1... | collective-permute-start | bytes 3145736 | tf_op jit(solution)/shard_map/ppermute | solution.py:307
  143.2 14.6 %slice-start.1 = ((s8[10485760]{0:T(1024)(128)(4,1)}), s8[4194304]{0:T(1024)(128)(4,1)S(1)}, s32[]{:S(2)}) async-start(s8[10485760]{0:T(1024)(128)(4,1)} %bitcast.10), calls=%async_computation.5 | async-start | bytes 8388608
  146.3 24.8 %collective-permute-start.7 = (bf16[256,1024]{1,0:T(8,128)(2,1)S(1)}, bf16[256,1024]{1,0:T(8,128)(2,1)S(1)}, u32[]{:S(2)}, u32[]{:S(2)}) collective-permute-start(bf16[256,1024]{1,0:T(8,128)(2,1)S(1)} %get-tuple-element.28.w2_own), channel_id=1, source_target_pairs={{0,17},{17,0},{1,16},{16,1},{2,19},{19,2},{3,18},{18,3},{4,21},{21... | collective-permute-start | bytes 1572872 | tf_op jit(solution)/shard_map/ppermute | solution.py:365
  148.8 8.2 %collective-permute-start.6 = (bf16[256,1024]{1,0:T(8,128)(2,1)S(1)}, bf16[256,1024]{1,0:T(8,128)(2,1)S(1)}, u32[]{:S(2)}, u32[]{:S(2)}) collective-permute-start(bf16[256,1024]{1,0:T(8,128)(2,1)S(1)} %get-tuple-element.28.w2_own), channel_id=1, source_target_pairs={{0,2},{2,0},{1,3},{3,1},{4,6},{6,4},{5,7},{7,5},{8,10},{10,8},{9,1... | collective-permute-start | bytes 1572872 | tf_op jit(solution)/shard_map/ppermute | solution.py:307
  150.5 2.2 %collective-permute-start.4 = (f32[8,128]{1,0:T(8,128)S(1)}, f32[8,128]{1,0:T(8,128)S(1)}, u32[]{:S(2)}, u32[]{:S(2)}) collective-permute-start(f32[8,128]{1,0:T(8,128)S(1)} %get-tuple-element.27.sq_own), channel_id=1, source_target_pairs={{0,2},{2,0},{1,3},{3,1},{4,6},{6,4},{5,7},{7,5},{8,10},{10,8},{9,1... | collective-permute-start | bytes 12296 | tf_op jit(solution)/shard_map/ppermute | solution.py:307
  150.5 7.3 %slice-start.2 = ((s8[10485760]{0:T(1024)(128)(4,1)}), s8[4194304]{0:T(1024)(128)(4,1)S(1)}, s32[]{:S(2)}) async-start(s8[10485760]{0:T(1024)(128)(4,1)} %bitcast.10), calls=%async_computation.6 | async-start | bytes 8388608
  153.0 1.7 collective-permute-start.5
  153.9 9.6 %collective-permute-start.8 = (bf16[256,512]{1,0:T(8,128)(2,1)S(1)}, bf16[256,512]{1,0:T(8,128)(2,1)S(1)}, u32[]{:S(2)}, u32[]{:S(2)}) collective-permute-start(bf16[256,512]{1,0:T(8,128)(2,1)S(1)} %shard_map.92.hq_own), channel_id=1, source_target_pairs={{0,1},{1,0},{2,3},{3,2},{4,5},{5,4},{6,7},{7,6},{8,9},{9,8},{10,11... | collective-permute-start | bytes 786440 | tf_op jit(solution)/shard_map/ppermute | solution.py:383
  154.8 16.3 %collective-permute-start.9 = (bf16[256,512]{1,0:T(8,128)(2,1)S(1)}, bf16[256,512]{1,0:T(8,128)(2,1)S(1)}, u32[]{:S(2)}, u32[]{:S(2)}) collective-permute-start(bf16[256,512]{1,0:T(8,128)(2,1)S(1)} %collective-permute-done.5.hq_got), channel_id=1, source_target_pairs={{0,1},{1,0},{2,3},{3,2},{4,5},{5,4},{6,7},{7,6},{8,9},{9,8},{10,11... | collective-permute-start | bytes 786440 | tf_op jit(solution)/shard_map/ppermute | solution.py:383
  171.1 3.6 %collective-permute-start.12 = (bf16[256,1024]{1,0:T(8,128)(2,1)S(1)}, bf16[256,1024]{1,0:T(8,128)(2,1)S(1)}, u32[]{:S(2)}, u32[]{:S(2)}) collective-permute-start(bf16[256,1024]{1,0:T(8,128)(2,1)S(1)} %collective-permute-done.7.rest_0_), channel_id=1, source_target_pairs={{0,2},{2,0},{1,3},{3,1},{4,6},{6,4},{5,7},{7,5},{8,10},{10,8},{9,1... | collective-permute-start | bytes 1572872 | tf_op jit(solution)/shard_map/ppermute | solution.py:307

commit v7 on v6

--- a/solution.py
+++ b/solution.py
@@ -214,8 +214,11 @@
         out[i] = rounded
 
 
-def stage_kernel(after, first_far, second_far, first, second, sems):
-    for copy in fetch(((first_far, first), (second_far, second)), sems):
+def stage_kernel(after, first_a, first_b, second_a, second_b, first, second, sems):
+    rows = first_a.shape[0]
+    pairs = [(first_a, first.at[0:rows, :]), (first_b, first.at[rows:, :])]
+    pairs += [(second_a, second.at[0:rows, :]), (second_b, second.at[rows:, :])]
+    for copy in fetch(pairs, sems):
         copy.wait()
 
 
@@ -320,8 +323,15 @@
     kus = (keys, k_oth, targets, u_oth)
 
     place = jnp.stack([head, core]).astype(jnp.int32)
-    sent = lax.dynamic_slice(w_out, (core * (width // 2), (1 - head) * n), (width // 2, n))
-    w_first = lax.ppermute(sent, ("xl", "h"), ACROSS)
+    rows = width // 4
+
+    def sent(part):
+        return lax.dynamic_slice(
+            w_out, ((2 * core + part) * rows, (1 - head) * n), (rows, n)
+        )
+
+    w_a = lax.ppermute(sent(0), ("xl", "h"), ACROSS)
+    w_b = lax.ppermute(lax.optimization_barrier((sent(1), w_a))[0], ("xl", "h"), ACROSS)
 
     wshape = (shape((2 * half, width)), shape((half, width)))
     sshape = shape((8, 128), F32)
@@ -344,7 +354,7 @@
             flops * 3 // 4,
             8 << 20,
         )(*mats, raw, keys, k_oth, targets, u_oth, *state)
-        gathered, w_late = all_reduced(grads, w_first if step else None)
+        gathered, w_late = all_reduced(grads, (w_a, w_b) if step else None)
         again = () if step == 0 else (first, *state)
         *mats, squares = call(
             update_kernel,
@@ -363,7 +373,7 @@
         first = gathered
         state = (norm, squares, swap(squares))
     crossed = lax.ppermute(mats[1], ("xl", "h"), ACROSS)
-    w_second = swap(w_late)
+    w_parts = (w_a, w_b, *map(swap, w_late))
     q_oth = swap(queries)
     w2_got = swap(mats[1])
     hshape = shape((half, tokens))
@@ -385,9 +395,9 @@
         hq_own, hq_got, mats[1], w2_got
     )
     part = partial_product(place, o, w_out)
-    wide = (shape(w_first.shape),) * 2
-    w_first, w_second = call(stage_kernel, wide, [ANY] * 3, 1 << 16, 1 << 16, [semaphores(2)])(
-        hqs[0], w_first, w_second
+    wide = (shape((width // 2, n)),) * 2
+    w_first, w_second = call(stage_kernel, wide, [ANY] * 5, 1 << 16, 1 << 16, [semaphores(4)])(
+        hqs[0], *w_parts
     )
     crossed, *hqs, _, _ = lax.optimization_barrier((crossed, *hqs, part, w_first))
     return finish_product(place, part, hqs, (crossed, swap(crossed)), w_first, w_second)

time: 180 us -> 177 us (0.983)
  blocking collectives: 57.6 us -> 30.3 us
  waiting for transfers between devices: 46.4 us -> 60.8 us
  starting transfers between devices: 31.2 us -> 39 us
  Pallas kernels: 36.8 us -> 39.5 us
    all_to_all x2 -> x1, blocking collectives: 57.6 us -> 30.3 us  [all_reduced(): arrived = lax.all_to_all(pieces, CHIPS, 0, 0, tiled=True)]
    all_to_all x0 -> x1, waiting for transfers between devices: none -> 19.5 us  [all_reduced(): arrived = lax.all_to_all(pieces, CHIPS, 0, 0, tiled=True)]
    all_to_all x0 -> x1, starting transfers between devices: none -> 5.89 us  [all_reduced(): arrived = lax.all_to_all(pieces, CHIPS, 0, 0, tiled=True)]
    ppermute x2, waiting for transfers between devices: 0.82 us -> 6.43 us  [shards(): hqs = [lax.ppermute(x, 'h', SWAP) for x in (hq_own, hq_got)]]
    ppermute x1, waiting for transfers between devices: 5.08 us -> 0.01 us  [shards(): crossed = lax.ppermute(mats[1], ('xl', 'h'), ACROSS)]
    all_to_all x2, waiting for transfers between devices: 37 us -> 33 us  [all_reduced(): gathered = lax.all_to_all(copies, CHIPS, 0, 0, tiled=True)]
    pallas_call x14, Pallas kernels: 27 us -> 29.7 us  [with_places(): run(*(pltpu.with_memory_space_constraint(x, HELD[id(spec)]) if id(spec) i...]
    ppermute x1 -> x2, starting transfers between devices: 2.49 us -> 5.08 us  [the longest x1 2.58 us: shards(): lax.ppermute(lax.optimization_barrier((sent(1), w_a))[0], ('xl', 'h'), AC...]
  transfers between devices with their start and end apart: 15 -> 18, of which waited for: 7 -> 6; matrix products, arithmetic and copies ran while one was open for 2% -> 2% of each run, Pallas kernels for 15% -> 17%
where the time goes in v7:
time: 177 us; the launch traced here: 176 us
  waiting for transfers between devices  60.8 us (34%)
  Pallas kernels  39.5 us (22%)
  starting transfers between devices  39 us (22%)
  blocking collectives  30.3 us (17%)
  local copies, waits for them, and re-layouts  4.68 us (3%)
    all_to_all x2, waiting for transfers between devices, all_reduced(): gathered = lax.all_to_all(copies, CHIPS, 0, 0, tiled=True)  33 us
    all_to_all x1, blocking collectives, all_reduced(): arrived = lax.all_to_all(pieces, CHIPS, 0, 0, tiled=True)  30.3 us
    pallas_call x14, Pallas kernels, with_places(): run(*(pltpu.with_memory_space_constraint(x, HELD[id(spec)]) if id(spec) i...  29.7 us
    all_to_all x1, waiting for transfers between devices, all_reduced(): arrived = lax.all_to_all(pieces, CHIPS, 0, 0, tiled=True)  19.5 us
    all_to_all x2, starting transfers between devices, all_reduced(): gathered = lax.all_to_all(copies, CHIPS, 0, 0, tiled=True)  12 us
    ppermute x10, starting transfers between devices, swap(): return lax.ppermute(x, 'c', SWAP)  11.4 us
    ppermute x2, waiting for transfers between devices, shards(): hqs = [lax.ppermute(x, 'h', SWAP) for x in (hq_own, hq_got)]  6.43 us
    all_to_all x1, starting transfers between devices, all_reduced(): arrived = lax.all_to_all(pieces, CHIPS, 0, 0, tiled=True)  5.89 us
  transfers between devices with their start and end apart: 18, of which 6 were waited for; matrix products, arithmetic and copies ran while one was open for 2% of the time, Pallas kernels for 17%

profile of v7, /device:TPU:1, one launch (start us, length us, event | category | flops | bytes accessed | tf_op | source)
XLA Modules:
  0.0 176.3 jit_solution(9417984488417942930)
XLA Ops:
  0.0 1.5 multiply_convert_fusion.targets.u_own
  1.6 1.5 collective-permute-start.1
  3.1 0.0 copy-done.4
  3.1 0.1 collective-permute-start
  3.2 3.6 %shard_map.82 = (bf16[512,1024]{1,0:T(8,128)(2,1)S(1)}, bf16[256,1024]{1,0:T(8,128)(2,1)S(1)}, f32[8,128]{1,0:T(8,128)S(1)}) custom-call(s32[1]{0:T(128)} %bitcast.1.core, bf16[1024,512]{1,0:T(8,128)(2,1)} %bitcast.16, bf16[1024,512]{1,0:T(8,128)(2,1)} %bitcast.17, bf16[512,1024]{1,0:T(8,128)(2,1)} %bitcast.18), custom_call_target="tpu_custom_call" | custom-call | flops 2097152 | bytes 5242880 | tf_op jit(solution)/shard_map/pallas_call | solution.py:55
  6.7 0.0 copy-start.1
  6.8 0.0 copy-start.3
  6.8 1.0 shard_map.83.raw
  7.8 0.0 collective-permute-done.1.u_oth
  7.8 0.0 collective-permute-done.k_oth
  7.8 0.0 copy-done.1
  7.8 0.1 copy-done.3
  7.9 4.6 %shard_map.84 = bf16[2,768,512]{2,1,0:T(8,128)(2,1)S(1)} custom-call(bf16[512,1024]{1,0:T(8,128)(2,1)S(1)} %get-tuple-element.22.w13.w13_far, bf16[256,1024]{1,0:T(8,128)(2,1)S(1)} %get-tuple-element.23.w2.w2_far, f32[768,512]{1,0:T(8,128)S(1)} %shard_map.83.raw, bf16[512,1024]{1,0:T(8,128)(2,1)S(1)} %copy-done.4, ...), custom_call_target="tpu_custom_call" | custom-call | flops 2415919104 | bytes 8388608 | tf_op jit(solution)/shard_map/pallas_call | solution.py:55
  12.5 30.3 %all_to_all.20.arrived = bf16[32,48,512]{2,1,0:T(8,128)(2,1)S(1)} all-to-all(bf16[32,48,512]{2,1,0:T(8,128)(2,1)S(1)} %bitcast.15), channel_id=1, replica_groups=mesh['z'=4,'xl'=2,'y'=4,'c'=2,'h'=2] {'z','xl','y'}, dimensions={0} | all-to-all | bytes 3145728 | tf_op jit(solution)/shard_map/all_to_all | solution.py:295
  42.7 0.3 shard_map.85
  43.1 0.0 copy-start.2
  43.1 1.1 copy-done.2
  44.2 5.7 %all-to-all-start.1 = ((bf16[32,48,512]{2,1,0:T(8,128)(2,1)}), bf16[32,48,512]{2,1,0:T(8,128)(2,1)S(1)}, u32[]{:S(2)}, u32[]{:S(2)}) async-start(bf16[32,48,512]{2,1,0:T(8,128)(2,1)} %copy-done.2), calls=%async_computation.1 | async-start | bytes 3145728 | tf_op jit(solution)/shard_map/all_to_all | solution.py:305
  49.9 3.4 %fusion = (bf16[256,2560]{1,0:T(8,128)(2,1)}, bf16[256,2560]{1,0:T(8,128)(2,1)}) fusion(bf16[1024,5120]{1,0:T(8,128)(2,1)} %w_own.1, s32[]{:T(128)S(6)} %select_n.12, s32[]{:T(128)S(6)} %select_n.11, s32[]{:T(128)S(6)} %select_n.10), kind=kLoop, calls=%fused_computation.2 | loop fusion | bytes 5242892 | tf_op jit(solution)/shard_map/dynamic_slice | solution.py:329
  53.3 2.5 %collective-permute-start.10 = (bf16[256,2560]{1,0:T(8,128)(2,1)}, bf16[256,2560]{1,0:T(8,128)(2,1)}, u32[]{:S(2)}, u32[]{:S(2)}) collective-permute-start(bf16[256,2560]{1,0:T(8,128)(2,1)} %get-tuple-element.40), channel_id=1, source_target_pairs={{0,17},{17,0},{1,16},{16,1},{2,19},{19,2},{3,18},{18,3},{4,21},{21... | collective-permute-start | bytes 3932168 | tf_op jit(solution)/shard_map/ppermute | solution.py:333
  55.8 15.0 %all-to-all-done.1 = bf16[32,48,512]{2,1,0:T(8,128)(2,1)S(1)} async-done(((bf16[32,48,512]{2,1,0:T(8,128)(2,1)}), bf16[32,48,512]{2,1,0:T(8,128)(2,1)S(1)}, u32[]{:S(2)}, u32[]{:S(2)}) %all-to-all-start.1) | async-done | bytes 1572896 | tf_op jit(solution)/shard_map/all_to_all | solution.py:305
  70.8 2.7 %shard_map.86 = (bf16[512,1024]{1,0:T(8,128)(2,1)S(1)}, bf16[256,1024]{1,0:T(8,128)(2,1)S(1)}, f32[8,128]{1,0:T(8,128)S(1)}) custom-call(bf16[512,1024]{1,0:T(8,128)(2,1)} %copy-done.1, bf16[256,1024]{1,0:T(8,128)(2,1)} %copy-done.3, bf16[2,768,512]{2,1,0:T(8,128)(2,1)S(1)} %bitcast.12), custom_call_target="tpu_custom_call" | custom-call | flops 4194304 | bytes 5242880 | tf_op jit(solution)/shard_map/pallas_call | solution.py:55
  73.6 0.0 copy-done
  73.6 2.5 %collective-permute-start.2 = (f32[8,128]{1,0:T(8,128)S(1)}, f32[8,128]{1,0:T(8,128)S(1)}, u32[]{:S(2)}, u32[]{:S(2)}) collective-permute-start(f32[8,128]{1,0:T(8,128)S(1)} %get-tuple-element.25.rest_1_.rest_2_), channel_id=1, source_target_pairs={{0,2},{2,0},{1,3},{3,1},{4,6},{6,4},{5,7},{7,5},{8,10},{10,8},{9,1... | collective-permute-start | bytes 12296 | tf_op jit(solution)/shard_map/ppermute | solution.py:310
  76.1 1.0 shard_map.87.raw
  77.1 0.0 collective-permute-done.2.rest_2_.rest_3_
  77.1 5.7 %shard_map.88 = bf16[2,768,512]{2,1,0:T(8,128)(2,1)} custom-call(bf16[512,1024]{1,0:T(8,128)(2,1)S(1)} %get-tuple-element.26.w13, bf16[256,1024]{1,0:T(8,128)(2,1)S(1)} %get-tuple-element.27.w2, f32[768,512]{1,0:T(8,128)S(1)} %shard_map.87.raw, bf16[512,1024]{1,0:T(8,128)(2,1)S(1)} %copy-done.5, bf16[512,1024]{1,0:T(8,128)(2,1)} %collective-permute-done.k_oth, ...), custom_call_target="tpu_custom_call" | custom-call | flops 2415919104 | bytes 8388608 | tf_op jit(solution)/shard_map/pallas_call | solution.py:55
  82.9 5.9 %all-to-all-start.2 = ((bf16[32,48,512]{2,1,0:T(8,128)(2,1)}), bf16[32,48,512]{2,1,0:T(8,128)(2,1)S(1)}, u32[]{:S(2)}, u32[]{:S(2)}) async-start(bf16[32,48,512]{2,1,0:T(8,128)(2,1)} %bitcast.8), calls=%async_computation.2 | async-start | bytes 3145728 | tf_op jit(solution)/shard_map/all_to_all | solution.py:295
  88.8 0.0 collective-permute-done.10.first_a
  88.8 2.6 %collective-permute-start.11 = (bf16[256,2560]{1,0:T(8,128)(2,1)}, bf16[256,2560]{1,0:T(8,128)(2,1)S(1)}, u32[]{:S(2)}, u32[]{:S(2)}) collective-permute-start(bf16[256,2560]{1,0:T(8,128)(2,1)} %get-tuple-element.31), channel_id=1, source_target_pairs={{0,17},{17,0},{1,16},{16,1},{2,19},{19,2},{3,18},{18,3},{4,21},{21... | collective-permute-start | bytes 3932168 | tf_op jit(solution)/shard_map/ppermute | solution.py:334
  91.4 19.5 %all-to-all-done.2.arrived = bf16[32,48,512]{2,1,0:T(8,128)(2,1)S(1)} async-done(((bf16[32,48,512]{2,1,0:T(8,128)(2,1)}), bf16[32,48,512]{2,1,0:T(8,128)(2,1)S(1)}, u32[]{:S(2)}, u32[]{:S(2)}) %all-to-all-start.2) | async-done | bytes 1572896 | tf_op jit(solution)/shard_map/all_to_all | solution.py:295
  110.8 1.5 shard_map.89
  112.3 6.3 %all-to-all-start.3 = ((bf16[32,48,512]{2,1,0:T(8,128)(2,1)}), bf16[32,48,512]{2,1,0:T(8,128)(2,1)S(1)}, u32[]{:S(2)}, u32[]{:S(2)}) async-start(bf16[32,48,512]{2,1,0:T(8,128)(2,1)} %shard_map.89), calls=%async_computation.3 | async-start | bytes 3145728 | tf_op jit(solution)/shard_map/all_to_all | solution.py:305
  118.6 1.3 collective-permute-start.3
  120.0 0.3 collective-permute-done.11.first_b
  120.3 1.2 collective-permute-start.12
  121.5 0.0 collective-permute-start.13
  121.5 18.0 %all-to-all-done.3 = bf16[32,48,512]{2,1,0:T(8,128)(2,1)S(1)} async-done(((bf16[32,48,512]{2,1,0:T(8,128)(2,1)}), bf16[32,48,512]{2,1,0:T(8,128)(2,1)S(1)}, u32[]{:S(2)}, u32[]{:S(2)}) %all-to-all-start.3) | async-done | bytes 1572896 | tf_op jit(solution)/shard_map/all_to_all | solution.py:305
  139.5 2.9 %shard_map.90 = (bf16[512,1024]{1,0:T(8,128)(2,1)S(1)}, bf16[256,1024]{1,0:T(8,128)(2,1)S(1)}, f32[8,128]{1,0:T(8,128)S(1)}) custom-call(bf16[512,1024]{1,0:T(8,128)(2,1)} %copy-done.1, bf16[256,1024]{1,0:T(8,128)(2,1)} %copy-done.3, bf16[2,768,512]{2,1,0:T(8,128)(2,1)} %bitcast.13, f32[8,128]{1,0:T(8,128)S(1)} %get-tuple-element.24.rest_0_.rest_1_.norm, ...), custom_call_target="tpu_custom_call" | custom-call | flops 4194304 | bytes 5242880 | tf_op jit(solution)/shard_map/pallas_call | solution.py:55
  142.4 1.6 collective-permute-start.7
  144.0 2.8 %collective-permute-start.6 = (bf16[256,1024]{1,0:T(8,128)(2,1)S(1)}, bf16[256,1024]{1,0:T(8,128)(2,1)S(1)}, u32[]{:S(2)}, u32[]{:S(2)}) collective-permute-start(bf16[256,1024]{1,0:T(8,128)(2,1)S(1)} %get-tuple-element.30.w2_own), channel_id=1, source_target_pairs={{0,2},{2,0},{1,3},{3,1},{4,6},{6,4},{5,7},{7,5},{8,10},{10,8},{9,1... | collective-permute-start | bytes 1572872 | tf_op jit(solution)/shard_map/ppermute | solution.py:310
  146.9 0.0 collective-permute-done.3.oth_far
  146.9 0.0 collective-permute-start.4
  146.9 2.9 %shard_map.91.raw = f32[2,512,512]{2,1,0:T(8,128)S(1)} custom-call(bf16[512,1024]{1,0:T(8,128)(2,1)S(1)} %get-tuple-element.28.m13, bf16[512,1024]{1,0:T(8,128)(2,1)} %collective-permute-done.3.oth_far, bf16[512,1024]{1,0:T(8,128)(2,1)} %own_far.1), custom_call_target="tpu_custom_call" | custom-call | flops 1073741824 | bytes 5242880 | tf_op jit(solution)/shard_map/pallas_call | solution.py:55
  149.8 0.0 collective-permute-done.4.sq_oth
  149.8 0.3 shard_map.93
  150.1 0.6 collective-permute-start.5
  150.7 0.3 shard_map.92.hq_own
  150.9 0.0 collective-permute-done.12.second_a
  151.0 0.8 collective-permute-start.8
  151.8 0.0 collective-permute-done.5.hq_got
  151.8 2.2 %collective-permute-start.9 = (bf16[256,512]{1,0:T(8,128)(2,1)S(1)}, bf16[256,512]{1,0:T(8,128)(2,1)S(1)}, u32[]{:S(2)}, u32[]{:S(2)}) collective-permute-start(bf16[256,512]{1,0:T(8,128)(2,1)S(1)} %collective-permute-done.5.hq_got), channel_id=1, source_target_pairs={{0,1},{1,0},{2,3},{3,2},{4,5},{5,4},{6,7},{7,6},{8,9},{9,8},{10,11... | collective-permute-start | bytes 786440 | tf_op jit(solution)/shard_map/ppermute | solution.py:393
  154.0 0.1 pad_add_fusion.place
  154.1 0.0 collective-permute-done.13.second_b
  154.1 6.4 %collective-permute-done.8.after.hq_a = bf16[256,512]{1,0:T(8,128)(2,1)S(1)} collective-permute-done((bf16[256,512]{1,0:T(8,128)(2,1)S(1)}, bf16[256,512]{1,0:T(8,128)(2,1)S(1)}, u32[]{:S(2)}, u32[]{:S(2)}) %collective-permute-start.8) | collective-permute-done | bytes 262176 | tf_op jit(solution)/shard_map/ppermute | solution.py:393
  160.5 2.2 %shard_map.96 = (bf16[512,2560]{1,0:T(8,128)(2,1)S(1)}, bf16[512,2560]{1,0:T(8,128)(2,1)S(1)}) custom-call(bf16[256,512]{1,0:T(8,128)(2,1)S(1)} %collective-permute-done.8.after.hq_a, bf16[256,2560]{1,0:T(8,128)(2,1)} %collective-permute-done.10.first_a, bf16[256,2560]{1,0:T(8,128)(2,1)S(1)} %collective-permute-done.11.first_b, ...), custom_call_target="tpu_custom_call" | custom-call | flops 65536 | bytes 65536 | tf_op jit(solution)/shard_map/pallas_call | solution.py:55
  162.7 0.0 collective-permute-done.6.w2_got
  162.7 0.7 shard_map.94.o
  163.5 4.8 %shard_map.95.part = f32[512,2560]{1,0:T(8,128)S(1)} custom-call(s32[2]{0:T(128)S(1)} %pad_add_fusion.place, bf16[512,1024]{1,0:T(8,128)(2,1)S(1)} %shard_map.94.o, bf16[1024,5120]{1,0:T(8,128)(2,1)S(1)} %bitcast.11), custom_call_target="tpu_custom_call" | custom-call | flops 1048576 | bytes 65536 | tf_op jit(solution)/shard_map/pallas_call | solution.py:236
  168.3 0.0 collective-permute-done.7.rest_0_
  168.3 0.0 collective-permute-done.9.hq_b
  168.3 1.3 collective-permute-start.14
  169.7 1.5 collective-permute-done.14.rest_1_
  171.2 5.0 %shard_map.97 = bf16[512,2560]{1,0:T(8,128)(2,1)} custom-call(s32[2]{0:T(128)S(1)} %pad_add_fusion.place, f32[512,2560]{1,0:T(8,128)S(1)} %shard_map.95.part, bf16[256,512]{1,0:T(8,128)(2,1)S(1)} %collective-permute-done.8.after.hq_a, bf16[256,512]{1,0:T(8,128)(2,1)S(1)} %collective-permute-done.9.hq_b, ...), custom_call_target="tpu_custom_call" | custom-call | flops 3221225472 | bytes 6291456 | tf_op jit(solution)/shard_map/pallas_call | solution.py:275
  (11 shorter events, 0.0 us)
Async XLA Ops:
  0.0 3.1 %copy-start.4 = (bf16[512,1024]{1,0:T(8,128)(2,1)S(1)}, bf16[512,1024]{1,0:T(8,128)(2,1)}, u32[]{:S(2)}) copy-start(bf16[512,1024]{1,0:T(8,128)(2,1)} %k_own.3) | copy-start | bytes 3145732
  1.6 6.2 %collective-permute-start.1 = (bf16[512,1024]{1,0:T(8,128)(2,1)S(1)}, bf16[512,1024]{1,0:T(8,128)(2,1)}, u32[]{:S(2)}, u32[]{:S(2)}) collective-permute-start(bf16[512,1024]{1,0:T(8,128)(2,1)S(1)} %multiply_convert_fusion.targets.u_own), channel_id=1, source_target_pairs={{0,2},{2,0},{1,3},{3,1},{4,6},{6,4},{5,7},{7,5},{8,10},{10,8},{9,1... | collective-permute-start | bytes 3145736 | tf_op jit(solution)/shard_map/ppermute | solution.py:310
  3.1 4.7 %collective-permute-start = (bf16[512,1024]{1,0:T(8,128)(2,1)S(1)}, bf16[512,1024]{1,0:T(8,128)(2,1)}, u32[]{:S(2)}, u32[]{:S(2)}) collective-permute-start(bf16[512,1024]{1,0:T(8,128)(2,1)S(1)} %copy-done.4), channel_id=1, source_target_pairs={{0,2},{2,0},{1,3},{3,1},{4,6},{6,4},{5,7},{7,5},{8,10},{10,8},{9,1... | collective-permute-start | bytes 3145736 | tf_op jit(solution)/shard_map/ppermute | solution.py:310
  6.7 1.1 copy-start.1
  6.8 1.2 copy-start.3
  43.1 1.1 copy-start.2
  44.2 26.6 %all-to-all-start.1 = ((bf16[32,48,512]{2,1,0:T(8,128)(2,1)}), bf16[32,48,512]{2,1,0:T(8,128)(2,1)S(1)}, u32[]{:S(2)}, u32[]{:S(2)}) async-start(bf16[32,48,512]{2,1,0:T(8,128)(2,1)} %copy-done.2), calls=%async_computation.1 | async-start | bytes 3145728 | tf_op jit(solution)/shard_map/all_to_all | solution.py:305
  53.3 35.5 %collective-permute-start.10 = (bf16[256,2560]{1,0:T(8,128)(2,1)}, bf16[256,2560]{1,0:T(8,128)(2,1)}, u32[]{:S(2)}, u32[]{:S(2)}) collective-permute-start(bf16[256,2560]{1,0:T(8,128)(2,1)} %get-tuple-element.40), channel_id=1, source_target_pairs={{0,17},{17,0},{1,16},{16,1},{2,19},{19,2},{3,18},{18,3},{4,21},{21... | collective-permute-start | bytes 3932168 | tf_op jit(solution)/shard_map/ppermute | solution.py:333
  70.8 2.7 %copy-start = (bf16[32,48,512]{2,1,0:T(8,128)(2,1)}, bf16[32,48,512]{2,1,0:T(8,128)(2,1)S(1)}, u32[]{:S(2)}) copy-start(bf16[32,48,512]{2,1,0:T(8,128)(2,1)S(1)} %all-to-all-done.1) | copy-start | bytes 4718596
  70.8 5.3 %copy-start.5 = (bf16[512,1024]{1,0:T(8,128)(2,1)S(1)}, bf16[512,1024]{1,0:T(8,128)(2,1)}, u32[]{:S(2)}) copy-start(bf16[512,1024]{1,0:T(8,128)(2,1)} %k_own.3) | copy-start | bytes 3145732
  73.6 3.6 %collective-permute-start.2 = (f32[8,128]{1,0:T(8,128)S(1)}, f32[8,128]{1,0:T(8,128)S(1)}, u32[]{:S(2)}, u32[]{:S(2)}) collective-permute-start(f32[8,128]{1,0:T(8,128)S(1)} %get-tuple-element.25.rest_1_.rest_2_), channel_id=1, source_target_pairs={{0,2},{2,0},{1,3},{3,1},{4,6},{6,4},{5,7},{7,5},{8,10},{10,8},{9,1... | collective-permute-start | bytes 12296 | tf_op jit(solution)/shard_map/ppermute | solution.py:310
  82.9 28.0 %all-to-all-start.2 = ((bf16[32,48,512]{2,1,0:T(8,128)(2,1)}), bf16[32,48,512]{2,1,0:T(8,128)(2,1)S(1)}, u32[]{:S(2)}, u32[]{:S(2)}) async-start(bf16[32,48,512]{2,1,0:T(8,128)(2,1)} %bitcast.8), calls=%async_computation.2 | async-start | bytes 3145728 | tf_op jit(solution)/shard_map/all_to_all | solution.py:295
  88.8 31.5 %collective-permute-start.11 = (bf16[256,2560]{1,0:T(8,128)(2,1)}, bf16[256,2560]{1,0:T(8,128)(2,1)S(1)}, u32[]{:S(2)}, u32[]{:S(2)}) collective-permute-start(bf16[256,2560]{1,0:T(8,128)(2,1)} %get-tuple-element.31), channel_id=1, source_target_pairs={{0,17},{17,0},{1,16},{16,1},{2,19},{19,2},{3,18},{18,3},{4,21},{21... | collective-permute-start | bytes 3932168 | tf_op jit(solution)/shard_map/ppermute | solution.py:334
  112.3 27.1 %all-to-all-start.3 = ((bf16[32,48,512]{2,1,0:T(8,128)(2,1)}), bf16[32,48,512]{2,1,0:T(8,128)(2,1)S(1)}, u32[]{:S(2)}, u32[]{:S(2)}) async-start(bf16[32,48,512]{2,1,0:T(8,128)(2,1)} %shard_map.89), calls=%async_computation.3 | async-start | bytes 3145728 | tf_op jit(solution)/shard_map/all_to_all | solution.py:305
  118.6 28.2 %collective-permute-start.3 = (bf16[512,1024]{1,0:T(8,128)(2,1)}, bf16[512,1024]{1,0:T(8,128)(2,1)}, u32[]{:S(2)}, u32[]{:S(2)}) collective-permute-start(bf16[512,1024]{1,0:T(8,128)(2,1)} %own_far.1), channel_id=1, source_target_pairs={{0,2},{2,0},{1,3},{3,1},{4,6},{6,4},{5,7},{7,5},{8,10},{10,8},{9,1... | collective-permute-start | bytes 3145736 | tf_op jit(solution)/shard_map/ppermute | solution.py:310
  120.3 30.7 %collective-permute-start.12 = (bf16[256,2560]{1,0:T(8,128)(2,1)}, bf16[256,2560]{1,0:T(8,128)(2,1)}, u32[]{:S(2)}, u32[]{:S(2)}) collective-permute-start(bf16[256,2560]{1,0:T(8,128)(2,1)} %collective-permute-done.10.first_a), channel_id=1, source_target_pairs={{0,2},{2,0},{1,3},{3,1},{4,6},{6,4},{5,7},{7,5},{8,10},{10,8},{9,1... | collective-permute-start | bytes 3932168 | tf_op jit(solution)/shard_map/ppermute | solution.py:310
  121.5 32.6 %collective-permute-start.13 = (bf16[256,2560]{1,0:T(8,128)(2,1)S(1)}, bf16[256,2560]{1,0:T(8,128)(2,1)}, u32[]{:S(2)}, u32[]{:S(2)}) collective-permute-start(bf16[256,2560]{1,0:T(8,128)(2,1)S(1)} %collective-permute-done.11.first_b), channel_id=1, source_target_pairs={{0,2},{2,0},{1,3},{3,1},{4,6},{6,4},{5,7},{7,5},{8,10},{10,8},{9,1... | collective-permute-start | bytes 3932168 | tf_op jit(solution)/shard_map/ppermute | solution.py:310
  139.5 24.0 %slice-start = ((s8[10485760]{0:T(1024)(128)(4,1)}), s8[4194304]{0:T(1024)(128)(4,1)S(1)}, s32[]{:S(2)}) async-start(s8[10485760]{0:T(1024)(128)(4,1)} %bitcast.10), calls=%async_computation.4 | async-start | bytes 8388608
  142.4 25.9 %collective-permute-start.7 = (bf16[256,1024]{1,0:T(8,128)(2,1)S(1)}, bf16[256,1024]{1,0:T(8,128)(2,1)S(1)}, u32[]{:S(2)}, u32[]{:S(2)}) collective-permute-start(bf16[256,1024]{1,0:T(8,128)(2,1)S(1)} %get-tuple-element.30.w2_own), channel_id=1, source_target_pairs={{0,17},{17,0},{1,16},{16,1},{2,19},{19,2},{3,18},{18,3},{4,21},{21... | collective-permute-start | bytes 1572872 | tf_op jit(solution)/shard_map/ppermute | solution.py:375
  144.0 18.7 %collective-permute-start.6 = (bf16[256,1024]{1,0:T(8,128)(2,1)S(1)}, bf16[256,1024]{1,0:T(8,128)(2,1)S(1)}, u32[]{:S(2)}, u32[]{:S(2)}) collective-permute-start(bf16[256,1024]{1,0:T(8,128)(2,1)S(1)} %get-tuple-element.30.w2_own), channel_id=1, source_target_pairs={{0,2},{2,0},{1,3},{3,1},{4,6},{6,4},{5,7},{7,5},{8,10},{10,8},{9,1... | collective-permute-start | bytes 1572872 | tf_op jit(solution)/shard_map/ppermute | solution.py:310
  146.9 2.9 %collective-permute-start.4 = (f32[8,128]{1,0:T(8,128)S(1)}, f32[8,128]{1,0:T(8,128)S(1)}, u32[]{:S(2)}, u32[]{:S(2)}) collective-permute-start(f32[8,128]{1,0:T(8,128)S(1)} %get-tuple-element.29.sq_own), channel_id=1, source_target_pairs={{0,2},{2,0},{1,3},{3,1},{4,6},{6,4},{5,7},{7,5},{8,10},{10,8},{9,1... | collective-permute-start | bytes 12296 | tf_op jit(solution)/shard_map/ppermute | solution.py:310
  146.9 16.6 %slice-start.1 = ((s8[10485760]{0:T(1024)(128)(4,1)}), s8[4194304]{0:T(1024)(128)(4,1)S(1)}, s32[]{:S(2)}) async-start(s8[10485760]{0:T(1024)(128)(4,1)} %bitcast.10), calls=%async_computation.5 | async-start | bytes 8388608
  150.1 1.7 collective-permute-start.5
  151.0 9.6 %collective-permute-start.8 = (bf16[256,512]{1,0:T(8,128)(2,1)S(1)}, bf16[256,512]{1,0:T(8,128)(2,1)S(1)}, u32[]{:S(2)}, u32[]{:S(2)}) collective-permute-start(bf16[256,512]{1,0:T(8,128)(2,1)S(1)} %shard_map.92.hq_own), channel_id=1, source_target_pairs={{0,1},{1,0},{2,3},{3,2},{4,5},{5,4},{6,7},{7,6},{8,9},{9,8},{10,11... | collective-permute-start | bytes 786440 | tf_op jit(solution)/shard_map/ppermute | solution.py:393
  151.8 16.5 %collective-permute-start.9 = (bf16[256,512]{1,0:T(8,128)(2,1)S(1)}, bf16[256,512]{1,0:T(8,128)(2,1)S(1)}, u32[]{:S(2)}, u32[]{:S(2)}) collective-permute-start(bf16[256,512]{1,0:T(8,128)(2,1)S(1)} %collective-permute-done.5.hq_got), channel_id=1, source_target_pairs={{0,1},{1,0},{2,3},{3,2},{4,5},{5,4},{6,7},{7,6},{8,9},{9,8},{10,11... | collective-permute-start | bytes 786440 | tf_op jit(solution)/shard_map/ppermute | solution.py:393
  154.1 9.4 %slice-start.2 = ((s8[10485760]{0:T(1024)(128)(4,1)}), s8[2097152]{0:T(1024)(128)(4,1)S(1)}, s32[]{:S(2)}) async-start(s8[10485760]{0:T(1024)(128)(4,1)} %bitcast.10), calls=%async_computation.6 | async-start | bytes 4194304
  168.3 2.9 %collective-permute-start.14 = (bf16[256,1024]{1,0:T(8,128)(2,1)S(1)}, bf16[256,1024]{1,0:T(8,128)(2,1)S(1)}, u32[]{:S(2)}, u32[]{:S(2)}) collective-permute-start(bf16[256,1024]{1,0:T(8,128)(2,1)S(1)} %collective-permute-done.7.rest_0_), channel_id=1, source_target_pairs={{0,2},{2,0},{1,3},{3,1},{4,6},{6,4},{5,7},{7,5},{8,10},{10,8},{9,1... | collective-permute-start | bytes 1572872 | tf_op jit(solution)/shard_map/ppermute | solution.py:310

commit v8 on v7

--- a/solution.py
+++ b/solution.py
@@ -381,12 +381,12 @@
         query_kernel,
         shape((2, 2 * half, tokens), F32),
         [VMEM, ANY, FAR],
-        flops // 3,
-        5 << 20,
+        1 << 16,
+        1 << 16,
         (*pair, semaphores(2)),
     )(mats[0], q_oth, queries)
     hq_oth, hq_own = (
-        call(functools.partial(hidden_kernel, k), hshape, [VMEM] * 4, 1 << 20, 2 << 20)(raw, *state)
+        call(functools.partial(hidden_kernel, k), hshape, [VMEM] * 4, 1 << 16, 1 << 16)(raw, *state)
         for k in range(2)
     )
     hq_got = swap(hq_oth)
@@ -394,10 +394,10 @@
     o = call(piece_kernel, shape((tokens, width)), [VMEM] * 4, 1 << 20, 1 << 16)(
         hq_own, hq_got, mats[1], w2_got
     )
-    part = partial_product(place, o, w_out)
+    part = partial_product(place, lax.optimization_barrier((o, crossed))[0], w_out)
     wide = (shape((width // 2, n)),) * 2
     w_first, w_second = call(stage_kernel, wide, [ANY] * 5, 1 << 16, 1 << 16, [semaphores(4)])(
-        hqs[0], *w_parts
+        o, *w_parts
     )
     crossed, *hqs, _, _ = lax.optimization_barrier((crossed, *hqs, part, w_first))
     return finish_product(place, part, hqs, (crossed, swap(crossed)), w_first, w_second)

time: 177 us -> 184 us (1.040)
  waiting for transfers between devices: 60.8 us -> 68.1 us
    ppermute x1, waiting for transfers between devices: 0.01 us -> 12.9 us  [shards(): crossed = lax.ppermute(mats[1], ('xl', 'h'), ACROSS)]
    ppermute x2, waiting for transfers between devices: 6.43 us -> 0.01 us  [shards(): hqs = [lax.ppermute(x, 'h', SWAP) for x in (hq_own, hq_got)]]
  transfers between devices with their start and end apart: 18 -> 18, of which waited for: 6 -> 7; matrix products, arithmetic and copies ran while one was open for 2% -> 2% of each run, Pallas kernels for 17% -> 16%
where the time goes in v8:
time: 184 us
  waiting for transfers between devices  68.1 us (37%)
  Pallas kernels  39.5 us (21%)
  starting transfers between devices  39 us (21%)
  blocking collectives  30.3 us (16%)
  local copies, waits for them, and re-layouts  4.68 us (3%)
    all_to_all x2, waiting for transfers between devices, all_reduced(): gathered = lax.all_to_all(copies, CHIPS, 0, 0, tiled=True)  33 us
    all_to_all x1, blocking collectives, all_reduced(): arrived = lax.all_to_all(pieces, CHIPS, 0, 0, tiled=True)  30.3 us
    pallas_call x14, Pallas kernels, with_places(): run(*(pltpu.with_memory_space_constraint(x, HELD[id(spec)]) if id(spec) i...  29.7 us
    all_to_all x1, waiting for transfers between devices, all_reduced(): arrived = lax.all_to_all(pieces, CHIPS, 0, 0, tiled=True)  19.5 us
    ppermute x1, waiting for transfers between devices, shards(): crossed = lax.ppermute(mats[1], ('xl', 'h'), ACROSS)  12.9 us
    all_to_all x2, starting transfers between devices, all_reduced(): gathered = lax.all_to_all(copies, CHIPS, 0, 0, tiled=True)  12 us
    ppermute x10, starting transfers between devices, swap(): return lax.ppermute(x, 'c', SWAP)  11.5 us
    all_to_all x1, starting transfers between devices, all_reduced(): arrived = lax.all_to_all(pieces, CHIPS, 0, 0, tiled=True)  5.89 us
  transfers between devices with their start and end apart: 18, of which 7 were waited for; matrix products, arithmetic and copies ran while one was open for 2% of the time, Pallas kernels for 16%

profile of v8, /device:TPU:1, one launch (start us, length us, event | category | flops | bytes accessed | tf_op | source)
XLA Modules:
  0.0 183.6 jit_solution(15178922816944067989)
XLA Ops:
  0.0 1.5 multiply_convert_fusion.targets.u_own
  1.6 1.5 collective-permute-start.1
  3.1 0.0 copy-done.4
  3.1 0.1 collective-permute-start
  3.2 3.6 %shard_map.82 = (bf16[512,1024]{1,0:T(8,128)(2,1)S(1)}, bf16[256,1024]{1,0:T(8,128)(2,1)S(1)}, f32[8,128]{1,0:T(8,128)S(1)}) custom-call(s32[1]{0:T(128)} %bitcast.1.core, bf16[1024,512]{1,0:T(8,128)(2,1)} %bitcast.16, bf16[1024,512]{1,0:T(8,128)(2,1)} %bitcast.17, bf16[512,1024]{1,0:T(8,128)(2,1)} %bitcast.18), custom_call_target="tpu_custom_call" | custom-call | flops 2097152 | bytes 5242880 | tf_op jit(solution)/shard_map/pallas_call | solution.py:55
  6.7 0.0 copy-start.1
  6.8 0.0 copy-start.3
  6.8 1.0 shard_map.83.raw
  7.8 0.0 collective-permute-done.1.u_oth
  7.8 0.0 collective-permute-done.k_oth
  7.8 0.0 copy-done.1
  7.8 0.1 copy-done.3
  7.9 4.6 %shard_map.84 = bf16[2,768,512]{2,1,0:T(8,128)(2,1)S(1)} custom-call(bf16[512,1024]{1,0:T(8,128)(2,1)S(1)} %get-tuple-element.23.w13.w13_far, bf16[256,1024]{1,0:T(8,128)(2,1)S(1)} %get-tuple-element.24.w2.w2_far, f32[768,512]{1,0:T(8,128)S(1)} %shard_map.83.raw, bf16[512,1024]{1,0:T(8,128)(2,1)S(1)} %copy-done.4, ...), custom_call_target="tpu_custom_call" | custom-call | flops 2415919104 | bytes 8388608 | tf_op jit(solution)/shard_map/pallas_call | solution.py:55
  12.5 30.3 %all_to_all.20.arrived = bf16[32,48,512]{2,1,0:T(8,128)(2,1)S(1)} all-to-all(bf16[32,48,512]{2,1,0:T(8,128)(2,1)S(1)} %bitcast.15), channel_id=1, replica_groups=mesh['z'=4,'xl'=2,'y'=4,'c'=2,'h'=2] {'z','xl','y'}, dimensions={0} | all-to-all | bytes 3145728 | tf_op jit(solution)/shard_map/all_to_all | solution.py:295
  42.7 0.3 shard_map.85
  43.1 0.0 copy-start.2
  43.1 1.1 copy-done.2
  44.2 5.7 %all-to-all-start.1 = ((bf16[32,48,512]{2,1,0:T(8,128)(2,1)}), bf16[32,48,512]{2,1,0:T(8,128)(2,1)S(1)}, u32[]{:S(2)}, u32[]{:S(2)}) async-start(bf16[32,48,512]{2,1,0:T(8,128)(2,1)} %copy-done.2), calls=%async_computation.1 | async-start | bytes 3145728 | tf_op jit(solution)/shard_map/all_to_all | solution.py:305
  49.9 3.4 %fusion = (bf16[256,2560]{1,0:T(8,128)(2,1)}, bf16[256,2560]{1,0:T(8,128)(2,1)}) fusion(bf16[1024,5120]{1,0:T(8,128)(2,1)} %w_own.1, s32[]{:T(128)S(6)} %select_n.12, s32[]{:T(128)S(6)} %select_n.11, s32[]{:T(128)S(6)} %select_n.10), kind=kLoop, calls=%fused_computation.2 | loop fusion | bytes 5242892 | tf_op jit(solution)/shard_map/dynamic_slice | solution.py:329
  53.3 2.5 %collective-permute-start.10 = (bf16[256,2560]{1,0:T(8,128)(2,1)}, bf16[256,2560]{1,0:T(8,128)(2,1)}, u32[]{:S(2)}, u32[]{:S(2)}) collective-permute-start(bf16[256,2560]{1,0:T(8,128)(2,1)} %get-tuple-element.42), channel_id=1, source_target_pairs={{0,17},{17,0},{1,16},{16,1},{2,19},{19,2},{3,18},{18,3},{4,21},{21... | collective-permute-start | bytes 3932168 | tf_op jit(solution)/shard_map/ppermute | solution.py:333
  55.8 15.0 %all-to-all-done.1 = bf16[32,48,512]{2,1,0:T(8,128)(2,1)S(1)} async-done(((bf16[32,48,512]{2,1,0:T(8,128)(2,1)}), bf16[32,48,512]{2,1,0:T(8,128)(2,1)S(1)}, u32[]{:S(2)}, u32[]{:S(2)}) %all-to-all-start.1) | async-done | bytes 1572896 | tf_op jit(solution)/shard_map/all_to_all | solution.py:305
  70.8 2.7 %shard_map.86 = (bf16[512,1024]{1,0:T(8,128)(2,1)S(1)}, bf16[256,1024]{1,0:T(8,128)(2,1)S(1)}, f32[8,128]{1,0:T(8,128)S(1)}) custom-call(bf16[512,1024]{1,0:T(8,128)(2,1)} %copy-done.1, bf16[256,1024]{1,0:T(8,128)(2,1)} %copy-done.3, bf16[2,768,512]{2,1,0:T(8,128)(2,1)S(1)} %bitcast.12), custom_call_target="tpu_custom_call" | custom-call | flops 4194304 | bytes 5242880 | tf_op jit(solution)/shard_map/pallas_call | solution.py:55
  73.6 2.5 %collective-permute-start.2 = (f32[8,128]{1,0:T(8,128)S(1)}, f32[8,128]{1,0:T(8,128)S(1)}, u32[]{:S(2)}, u32[]{:S(2)}) collective-permute-start(f32[8,128]{1,0:T(8,128)S(1)} %get-tuple-element.26.rest_1_.rest_2_), channel_id=1, source_target_pairs={{0,2},{2,0},{1,3},{3,1},{4,6},{6,4},{5,7},{7,5},{8,10},{10,8},{9,1... | collective-permute-start | bytes 12296 | tf_op jit(solution)/shard_map/ppermute | solution.py:310
  76.1 1.0 shard_map.87.raw
  77.1 0.0 collective-permute-done.2.rest_2_.rest_3_
  77.1 5.7 %shard_map.88 = bf16[2,768,512]{2,1,0:T(8,128)(2,1)} custom-call(bf16[512,1024]{1,0:T(8,128)(2,1)S(1)} %get-tuple-element.27.w13, bf16[256,1024]{1,0:T(8,128)(2,1)S(1)} %get-tuple-element.28.w2, f32[768,512]{1,0:T(8,128)S(1)} %shard_map.87.raw, bf16[512,1024]{1,0:T(8,128)(2,1)S(1)} %copy-done.5, bf16[512,1024]{1,0:T(8,128)(2,1)} %collective-permute-done.k_oth, ...), custom_call_target="tpu_custom_call" | custom-call | flops 2415919104 | bytes 8388608 | tf_op jit(solution)/shard_map/pallas_call | solution.py:55
  82.9 5.9 %all-to-all-start.2 = ((bf16[32,48,512]{2,1,0:T(8,128)(2,1)}), bf16[32,48,512]{2,1,0:T(8,128)(2,1)S(1)}, u32[]{:S(2)}, u32[]{:S(2)}) async-start(bf16[32,48,512]{2,1,0:T(8,128)(2,1)} %bitcast.8), calls=%async_computation.2 | async-start | bytes 3145728 | tf_op jit(solution)/shard_map/all_to_all | solution.py:295
  88.8 0.0 collective-permute-done.10.first_a
  88.8 2.6 %collective-permute-start.11 = (bf16[256,2560]{1,0:T(8,128)(2,1)}, bf16[256,2560]{1,0:T(8,128)(2,1)S(1)}, u32[]{:S(2)}, u32[]{:S(2)}) collective-permute-start(bf16[256,2560]{1,0:T(8,128)(2,1)} %get-tuple-element.33), channel_id=1, source_target_pairs={{0,17},{17,0},{1,16},{16,1},{2,19},{19,2},{3,18},{18,3},{4,21},{21... | collective-permute-start | bytes 3932168 | tf_op jit(solution)/shard_map/ppermute | solution.py:334
  91.4 19.5 %all-to-all-done.2.arrived = bf16[32,48,512]{2,1,0:T(8,128)(2,1)S(1)} async-done(((bf16[32,48,512]{2,1,0:T(8,128)(2,1)}), bf16[32,48,512]{2,1,0:T(8,128)(2,1)S(1)}, u32[]{:S(2)}, u32[]{:S(2)}) %all-to-all-start.2) | async-done | bytes 1572896 | tf_op jit(solution)/shard_map/all_to_all | solution.py:295
  110.8 1.5 shard_map.89
  112.3 6.3 %all-to-all-start.3 = ((bf16[32,48,512]{2,1,0:T(8,128)(2,1)}), bf16[32,48,512]{2,1,0:T(8,128)(2,1)S(1)}, u32[]{:S(2)}, u32[]{:S(2)}) async-start(bf16[32,48,512]{2,1,0:T(8,128)(2,1)} %shard_map.89), calls=%async_computation.3 | async-start | bytes 3145728 | tf_op jit(solution)/shard_map/all_to_all | solution.py:305
  118.6 1.3 collective-permute-start.3
  120.0 0.3 collective-permute-done.11.first_b
  120.3 1.2 collective-permute-start.12
  121.5 0.0 collective-permute-start.13
  121.5 18.0 %all-to-all-done.3 = bf16[32,48,512]{2,1,0:T(8,128)(2,1)S(1)} async-done(((bf16[32,48,512]{2,1,0:T(8,128)(2,1)}), bf16[32,48,512]{2,1,0:T(8,128)(2,1)S(1)}, u32[]{:S(2)}, u32[]{:S(2)}) %all-to-all-start.3) | async-done | bytes 1572896 | tf_op jit(solution)/shard_map/all_to_all | solution.py:305
  139.5 2.9 %shard_map.90 = (bf16[512,1024]{1,0:T(8,128)(2,1)S(1)}, bf16[256,1024]{1,0:T(8,128)(2,1)S(1)}, f32[8,128]{1,0:T(8,128)S(1)}) custom-call(bf16[512,1024]{1,0:T(8,128)(2,1)} %copy-done.1, bf16[256,1024]{1,0:T(8,128)(2,1)} %copy-done.3, bf16[2,768,512]{2,1,0:T(8,128)(2,1)} %bitcast.13, f32[8,128]{1,0:T(8,128)S(1)} %get-tuple-element.25.rest_0_.rest_1_.norm, ...), custom_call_target="tpu_custom_call" | custom-call | flops 4194304 | bytes 5242880 | tf_op jit(solution)/shard_map/pallas_call | solution.py:55
  142.4 2.7 %collective-permute-start.6 = (bf16[256,1024]{1,0:T(8,128)(2,1)S(1)}, bf16[256,1024]{1,0:T(8,128)(2,1)S(1)}, u32[]{:S(2)}, u32[]{:S(2)}) collective-permute-start(bf16[256,1024]{1,0:T(8,128)(2,1)S(1)} %get-tuple-element.31.w2_own), channel_id=1, source_target_pairs={{0,2},{2,0},{1,3},{3,1},{4,6},{6,4},{5,7},{7,5},{8,10},{10,8},{9,1... | collective-permute-start | bytes 1572872 | tf_op jit(solution)/shard_map/ppermute | solution.py:310
  145.1 0.1 collective-permute-start.4
  145.2 0.0 collective-permute-done.3.oth_far
  145.2 1.5 collective-permute-start.7
  146.7 2.9 %shard_map.91.raw = f32[2,512,512]{2,1,0:T(8,128)S(1)} custom-call(bf16[512,1024]{1,0:T(8,128)(2,1)S(1)} %get-tuple-element.29.m13, bf16[512,1024]{1,0:T(8,128)(2,1)} %collective-permute-done.3.oth_far, bf16[512,1024]{1,0:T(8,128)(2,1)} %own_far.1), custom_call_target="tpu_custom_call" | custom-call | flops 65536 | bytes 65536 | tf_op jit(solution)/shard_map/pallas_call | solution.py:55
  149.6 0.0 collective-permute-done.4.sq_oth
  149.6 0.3 shard_map.93
  149.9 0.8 collective-permute-start.5
  150.7 0.3 shard_map.92.hq_own
  150.9 0.9 collective-permute-done.5.hq_got
  151.8 0.7 collective-permute-start.8
  152.5 0.0 collective-permute-done.6.w2_got
  152.5 2.3 %collective-permute-start.9 = (bf16[256,512]{1,0:T(8,128)(2,1)S(1)}, bf16[256,512]{1,0:T(8,128)(2,1)S(1)}, u32[]{:S(2)}, u32[]{:S(2)}) collective-permute-start(bf16[256,512]{1,0:T(8,128)(2,1)S(1)} %collective-permute-done.5.hq_got), channel_id=1, source_target_pairs={{0,1},{1,0},{2,3},{3,2},{4,5},{5,4},{6,7},{7,6},{8,9},{9,8},{10,11... | collective-permute-start | bytes 786440 | tf_op jit(solution)/shard_map/ppermute | solution.py:393
  154.8 0.1 pad_add_fusion.place
  154.9 0.7 shard_map.94.o.after
  155.6 0.0 collective-permute-done.12.second_a
  155.6 0.0 collective-permute-done.13.second_b
  155.6 2.2 %shard_map.96 = (bf16[512,2560]{1,0:T(8,128)(2,1)S(1)}, bf16[512,2560]{1,0:T(8,128)(2,1)S(1)}) custom-call(bf16[512,1024]{1,0:T(8,128)(2,1)S(1)} %shard_map.94.o.after, bf16[256,2560]{1,0:T(8,128)(2,1)} %collective-permute-done.10.first_a, bf16[256,2560]{1,0:T(8,128)(2,1)S(1)} %collective-permute-done.11.first_b, ...), custom_call_target="tpu_custom_call" | custom-call | flops 65536 | bytes 65536 | tf_op jit(solution)/shard_map/pallas_call | solution.py:55
  157.8 12.9 %collective-permute-done.7.rest_0_ = bf16[256,1024]{1,0:T(8,128)(2,1)S(1)} collective-permute-done((bf16[256,1024]{1,0:T(8,128)(2,1)S(1)}, bf16[256,1024]{1,0:T(8,128)(2,1)S(1)}, u32[]{:S(2)}, u32[]{:S(2)}) %collective-permute-start.7) | collective-permute-done | bytes 524320 | tf_op jit(solution)/shard_map/ppermute | solution.py:375
  170.7 0.0 slice-done.2
  170.7 4.8 %shard_map.95.part = f32[512,2560]{1,0:T(8,128)S(1)} custom-call(s32[2]{0:T(128)S(1)} %pad_add_fusion.place, bf16[512,1024]{1,0:T(8,128)(2,1)S(1)} %shard_map.94.o.after, bf16[1024,5120]{1,0:T(8,128)(2,1)S(1)} %bitcast.11), custom_call_target="tpu_custom_call" | custom-call | flops 1048576 | bytes 65536 | tf_op jit(solution)/shard_map/pallas_call | solution.py:236
  175.6 0.0 collective-permute-done.8.hq_a
  175.6 0.0 collective-permute-done.9.hq_b
  175.6 1.3 collective-permute-start.14
  176.9 1.5 collective-permute-done.14.rest_1_
  178.5 5.0 %shard_map.97 = bf16[512,2560]{1,0:T(8,128)(2,1)} custom-call(s32[2]{0:T(128)S(1)} %pad_add_fusion.place, f32[512,2560]{1,0:T(8,128)S(1)} %shard_map.95.part, bf16[256,512]{1,0:T(8,128)(2,1)S(1)} %collective-permute-done.8.hq_a, bf16[256,512]{1,0:T(8,128)(2,1)S(1)} %collective-permute-done.9.hq_b, bf16[256,1024]{1,0:T(8,128)(2,1)S(1)} %collective-permute-done.7.rest_0_, ...), custom_call_target="tpu_custom_call" | custom-call | flops 3221225472 | bytes 6291456 | tf_op jit(solution)/shard_map/pallas_call | solution.py:275
  (11 shorter events, 0.0 us)
Async XLA Ops:
  0.0 3.1 %copy-start.4 = (bf16[512,1024]{1,0:T(8,128)(2,1)S(1)}, bf16[512,1024]{1,0:T(8,128)(2,1)}, u32[]{:S(2)}) copy-start(bf16[512,1024]{1,0:T(8,128)(2,1)} %k_own.3) | copy-start | bytes 3145732
  1.6 6.2 %collective-permute-start.1 = (bf16[512,1024]{1,0:T(8,128)(2,1)S(1)}, bf16[512,1024]{1,0:T(8,128)(2,1)}, u32[]{:S(2)}, u32[]{:S(2)}) collective-permute-start(bf16[512,1024]{1,0:T(8,128)(2,1)S(1)} %multiply_convert_fusion.targets.u_own), channel_id=1, source_target_pairs={{0,2},{2,0},{1,3},{3,1},{4,6},{6,4},{5,7},{7,5},{8,10},{10,8},{9,1... | collective-permute-start | bytes 3145736 | tf_op jit(solution)/shard_map/ppermute | solution.py:310
  3.1 4.7 %collective-permute-start = (bf16[512,1024]{1,0:T(8,128)(2,1)S(1)}, bf16[512,1024]{1,0:T(8,128)(2,1)}, u32[]{:S(2)}, u32[]{:S(2)}) collective-permute-start(bf16[512,1024]{1,0:T(8,128)(2,1)S(1)} %copy-done.4), channel_id=1, source_target_pairs={{0,2},{2,0},{1,3},{3,1},{4,6},{6,4},{5,7},{7,5},{8,10},{10,8},{9,1... | collective-permute-start | bytes 3145736 | tf_op jit(solution)/shard_map/ppermute | solution.py:310
  6.7 1.1 copy-start.1
  6.8 1.2 copy-start.3
  43.1 1.1 copy-start.2
  44.2 26.6 %all-to-all-start.1 = ((bf16[32,48,512]{2,1,0:T(8,128)(2,1)}), bf16[32,48,512]{2,1,0:T(8,128)(2,1)S(1)}, u32[]{:S(2)}, u32[]{:S(2)}) async-start(bf16[32,48,512]{2,1,0:T(8,128)(2,1)} %copy-done.2), calls=%async_computation.1 | async-start | bytes 3145728 | tf_op jit(solution)/shard_map/all_to_all | solution.py:305
  53.3 35.5 %collective-permute-start.10 = (bf16[256,2560]{1,0:T(8,128)(2,1)}, bf16[256,2560]{1,0:T(8,128)(2,1)}, u32[]{:S(2)}, u32[]{:S(2)}) collective-permute-start(bf16[256,2560]{1,0:T(8,128)(2,1)} %get-tuple-element.42), channel_id=1, source_target_pairs={{0,17},{17,0},{1,16},{16,1},{2,19},{19,2},{3,18},{18,3},{4,21},{21... | collective-permute-start | bytes 3932168 | tf_op jit(solution)/shard_map/ppermute | solution.py:333
  70.8 2.7 %copy-start = (bf16[32,48,512]{2,1,0:T(8,128)(2,1)}, bf16[32,48,512]{2,1,0:T(8,128)(2,1)S(1)}, u32[]{:S(2)}) copy-start(bf16[32,48,512]{2,1,0:T(8,128)(2,1)S(1)} %all-to-all-done.1) | copy-start | bytes 4718596
  70.8 5.3 %copy-start.5 = (bf16[512,1024]{1,0:T(8,128)(2,1)S(1)}, bf16[512,1024]{1,0:T(8,128)(2,1)}, u32[]{:S(2)}) copy-start(bf16[512,1024]{1,0:T(8,128)(2,1)} %k_own.3) | copy-start | bytes 3145732
  73.6 3.6 %collective-permute-start.2 = (f32[8,128]{1,0:T(8,128)S(1)}, f32[8,128]{1,0:T(8,128)S(1)}, u32[]{:S(2)}, u32[]{:S(2)}) collective-permute-start(f32[8,128]{1,0:T(8,128)S(1)} %get-tuple-element.26.rest_1_.rest_2_), channel_id=1, source_target_pairs={{0,2},{2,0},{1,3},{3,1},{4,6},{6,4},{5,7},{7,5},{8,10},{10,8},{9,1... | collective-permute-start | bytes 12296 | tf_op jit(solution)/shard_map/ppermute | solution.py:310
  82.9 28.0 %all-to-all-start.2 = ((bf16[32,48,512]{2,1,0:T(8,128)(2,1)}), bf16[32,48,512]{2,1,0:T(8,128)(2,1)S(1)}, u32[]{:S(2)}, u32[]{:S(2)}) async-start(bf16[32,48,512]{2,1,0:T(8,128)(2,1)} %bitcast.8), calls=%async_computation.2 | async-start | bytes 3145728 | tf_op jit(solution)/shard_map/all_to_all | solution.py:295
  88.8 31.5 %collective-permute-start.11 = (bf16[256,2560]{1,0:T(8,128)(2,1)}, bf16[256,2560]{1,0:T(8,128)(2,1)S(1)}, u32[]{:S(2)}, u32[]{:S(2)}) collective-permute-start(bf16[256,2560]{1,0:T(8,128)(2,1)} %get-tuple-element.33), channel_id=1, source_target_pairs={{0,17},{17,0},{1,16},{16,1},{2,19},{19,2},{3,18},{18,3},{4,21},{21... | collective-permute-start | bytes 3932168 | tf_op jit(solution)/shard_map/ppermute | solution.py:334
  112.3 27.1 %all-to-all-start.3 = ((bf16[32,48,512]{2,1,0:T(8,128)(2,1)}), bf16[32,48,512]{2,1,0:T(8,128)(2,1)S(1)}, u32[]{:S(2)}, u32[]{:S(2)}) async-start(bf16[32,48,512]{2,1,0:T(8,128)(2,1)} %shard_map.89), calls=%async_computation.3 | async-start | bytes 3145728 | tf_op jit(solution)/shard_map/all_to_all | solution.py:305
  118.6 26.5 %collective-permute-start.3 = (bf16[512,1024]{1,0:T(8,128)(2,1)}, bf16[512,1024]{1,0:T(8,128)(2,1)}, u32[]{:S(2)}, u32[]{:S(2)}) collective-permute-start(bf16[512,1024]{1,0:T(8,128)(2,1)} %own_far.1), channel_id=1, source_target_pairs={{0,2},{2,0},{1,3},{3,1},{4,6},{6,4},{5,7},{7,5},{8,10},{10,8},{9,1... | collective-permute-start | bytes 3145736 | tf_op jit(solution)/shard_map/ppermute | solution.py:310
  120.3 35.3 %collective-permute-start.12 = (bf16[256,2560]{1,0:T(8,128)(2,1)}, bf16[256,2560]{1,0:T(8,128)(2,1)}, u32[]{:S(2)}, u32[]{:S(2)}) collective-permute-start(bf16[256,2560]{1,0:T(8,128)(2,1)} %collective-permute-done.10.first_a), channel_id=1, source_target_pairs={{0,2},{2,0},{1,3},{3,1},{4,6},{6,4},{5,7},{7,5},{8,10},{10,8},{9,1... | collective-permute-start | bytes 3932168 | tf_op jit(solution)/shard_map/ppermute | solution.py:310
  121.5 34.1 %collective-permute-start.13 = (bf16[256,2560]{1,0:T(8,128)(2,1)S(1)}, bf16[256,2560]{1,0:T(8,128)(2,1)}, u32[]{:S(2)}, u32[]{:S(2)}) collective-permute-start(bf16[256,2560]{1,0:T(8,128)(2,1)S(1)} %collective-permute-done.11.first_b), channel_id=1, source_target_pairs={{0,2},{2,0},{1,3},{3,1},{4,6},{6,4},{5,7},{7,5},{8,10},{10,8},{9,1... | collective-permute-start | bytes 3932168 | tf_op jit(solution)/shard_map/ppermute | solution.py:310
  139.5 31.2 %slice-start = ((s8[10485760]{0:T(1024)(128)(4,1)}), s8[4194304]{0:T(1024)(128)(4,1)S(1)}, s32[]{:S(2)}) async-start(s8[10485760]{0:T(1024)(128)(4,1)} %bitcast.10), calls=%async_computation.4 | async-start | bytes 8388608
  142.4 10.1 %collective-permute-start.6 = (bf16[256,1024]{1,0:T(8,128)(2,1)S(1)}, bf16[256,1024]{1,0:T(8,128)(2,1)S(1)}, u32[]{:S(2)}, u32[]{:S(2)}) collective-permute-start(bf16[256,1024]{1,0:T(8,128)(2,1)S(1)} %get-tuple-element.31.w2_own), channel_id=1, source_target_pairs={{0,2},{2,0},{1,3},{3,1},{4,6},{6,4},{5,7},{7,5},{8,10},{10,8},{9,1... | collective-permute-start | bytes 1572872 | tf_op jit(solution)/shard_map/ppermute | solution.py:310
  145.1 4.5 %collective-permute-start.4 = (f32[8,128]{1,0:T(8,128)S(1)}, f32[8,128]{1,0:T(8,128)S(1)}, u32[]{:S(2)}, u32[]{:S(2)}) collective-permute-start(f32[8,128]{1,0:T(8,128)S(1)} %get-tuple-element.30.sq_own), channel_id=1, source_target_pairs={{0,2},{2,0},{1,3},{3,1},{4,6},{6,4},{5,7},{7,5},{8,10},{10,8},{9,1... | collective-permute-start | bytes 12296 | tf_op jit(solution)/shard_map/ppermute | solution.py:310
  145.2 25.5 %collective-permute-start.7 = (bf16[256,1024]{1,0:T(8,128)(2,1)S(1)}, bf16[256,1024]{1,0:T(8,128)(2,1)S(1)}, u32[]{:S(2)}, u32[]{:S(2)}) collective-permute-start(bf16[256,1024]{1,0:T(8,128)(2,1)S(1)} %get-tuple-element.31.w2_own), channel_id=1, source_target_pairs={{0,17},{17,0},{1,16},{16,1},{2,19},{19,2},{3,18},{18,3},{4,21},{21... | collective-permute-start | bytes 1572872 | tf_op jit(solution)/shard_map/ppermute | solution.py:375
  146.7 24.0 %slice-start.1 = ((s8[10485760]{0:T(1024)(128)(4,1)}), s8[4194304]{0:T(1024)(128)(4,1)S(1)}, s32[]{:S(2)}) async-start(s8[10485760]{0:T(1024)(128)(4,1)} %bitcast.10), calls=%async_computation.5 | async-start | bytes 8388608
  149.9 1.9 %collective-permute-start.5 = (bf16[256,512]{1,0:T(8,128)(2,1)S(1)}, bf16[256,512]{1,0:T(8,128)(2,1)S(1)}, u32[]{:S(2)}, u32[]{:S(2)}) collective-permute-start(bf16[256,512]{1,0:T(8,128)(2,1)S(1)} %shard_map.93), channel_id=1, source_target_pairs={{0,2},{2,0},{1,3},{3,1},{4,6},{6,4},{5,7},{7,5},{8,10},{10,8},{9,1... | collective-permute-start | bytes 786440 | tf_op jit(solution)/shard_map/ppermute | solution.py:310
  151.8 23.8 %collective-permute-start.8 = (bf16[256,512]{1,0:T(8,128)(2,1)S(1)}, bf16[256,512]{1,0:T(8,128)(2,1)S(1)}, u32[]{:S(2)}, u32[]{:S(2)}) collective-permute-start(bf16[256,512]{1,0:T(8,128)(2,1)S(1)} %shard_map.92.hq_own), channel_id=1, source_target_pairs={{0,1},{1,0},{2,3},{3,2},{4,5},{5,4},{6,7},{7,6},{8,9},{9,8},{10,11... | collective-permute-start | bytes 786440 | tf_op jit(solution)/shard_map/ppermute | solution.py:393
  152.5 23.1 %collective-permute-start.9 = (bf16[256,512]{1,0:T(8,128)(2,1)S(1)}, bf16[256,512]{1,0:T(8,128)(2,1)S(1)}, u32[]{:S(2)}, u32[]{:S(2)}) collective-permute-start(bf16[256,512]{1,0:T(8,128)(2,1)S(1)} %collective-permute-done.5.hq_got), channel_id=1, source_target_pairs={{0,1},{1,0},{2,3},{3,2},{4,5},{5,4},{6,7},{7,6},{8,9},{9,8},{10,11... | collective-permute-start | bytes 786440 | tf_op jit(solution)/shard_map/ppermute | solution.py:393
  154.9 15.8 %slice-start.2 = ((s8[10485760]{0:T(1024)(128)(4,1)}), s8[2097152]{0:T(1024)(128)(4,1)S(1)}, s32[]{:S(2)}) async-start(s8[10485760]{0:T(1024)(128)(4,1)} %bitcast.10), calls=%async_computation.6 | async-start | bytes 4194304
  175.6 2.9 %collective-permute-start.14 = (bf16[256,1024]{1,0:T(8,128)(2,1)S(1)}, bf16[256,1024]{1,0:T(8,128)(2,1)S(1)}, u32[]{:S(2)}, u32[]{:S(2)}) collective-permute-start(bf16[256,1024]{1,0:T(8,128)(2,1)S(1)} %collective-permute-done.7.rest_0_), channel_id=1, source_target_pairs={{0,2},{2,0},{1,3},{3,1},{4,6},{6,4},{5,7},{7,5},{8,10},{10,8},{9,1... | collective-permute-start | bytes 1572872 | tf_op jit(solution)/shard_map/ppermute | solution.py:310

commit v9 on v8

--- a/solution.py
+++ b/solution.py
@@ -394,10 +394,10 @@
     o = call(piece_kernel, shape((tokens, width)), [VMEM] * 4, 1 << 20, 1 << 16)(
         hq_own, hq_got, mats[1], w2_got
     )
-    part = partial_product(place, lax.optimization_barrier((o, crossed))[0], w_out)
+    part = partial_product(place, o, w_out)
     wide = (shape((width // 2, n)),) * 2
     w_first, w_second = call(stage_kernel, wide, [ANY] * 5, 1 << 16, 1 << 16, [semaphores(4)])(
-        o, *w_parts
+        hq_got, *w_parts
     )
     crossed, *hqs, _, _ = lax.optimization_barrier((crossed, *hqs, part, w_first))
     return finish_product(place, part, hqs, (crossed, swap(crossed)), w_first, w_second)

time: 184 us -> 179 us (0.973)
  waiting for transfers between devices: 68.1 us -> 63.1 us
    ppermute x1, waiting for transfers between devices: 12.9 us -> 8.66 us  [shards(): crossed = lax.ppermute(mats[1], ('xl', 'h'), ACROSS)]
  transfers between devices with their start and end apart: 18 -> 18, of which waited for: 7 -> 7; matrix products, arithmetic and copies ran while one was open for 2% -> 2% of each run, Pallas kernels for 16% -> 17%
where the time goes in v9:
time: 179 us
  waiting for transfers between devices  63.1 us (35%)
  Pallas kernels  39.7 us (22%)
  starting transfers between devices  38.9 us (22%)
  blocking collectives  30.3 us (17%)
  local copies, waits for them, and re-layouts  4.68 us (3%)
    all_to_all x2, waiting for transfers between devices, all_reduced(): gathered = lax.all_to_all(copies, CHIPS, 0, 0, tiled=True)  33 us
    all_to_all x1, blocking collectives, all_reduced(): arrived = lax.all_to_all(pieces, CHIPS, 0, 0, tiled=True)  30.3 us
    pallas_call x14, Pallas kernels, with_places(): run(*(pltpu.with_memory_space_constraint(x, HELD[id(spec)]) if id(spec) i...  29.8 us
    all_to_all x1, waiting for transfers between devices, all_reduced(): arrived = lax.all_to_all(pieces, CHIPS, 0, 0, tiled=True)  19.5 us
    all_to_all x2, starting transfers between devices, all_reduced(): gathered = lax.all_to_all(copies, CHIPS, 0, 0, tiled=True)  12 us
    ppermute x10, starting transfers between devices, swap(): return lax.ppermute(x, 'c', SWAP)  11.5 us
    ppermute x1, waiting for transfers between devices, shards(): crossed = lax.ppermute(mats[1], ('xl', 'h'), ACROSS)  8.66 us
    all_to_all x1, starting transfers between devices, all_reduced(): arrived = lax.all_to_all(pieces, CHIPS, 0, 0, tiled=True)  5.89 us
  transfers between devices with their start and end apart: 18, of which 7 were waited for; matrix products, arithmetic and copies ran while one was open for 2% of the time, Pallas kernels for 17%

profile of v9, /device:TPU:1, one launch (start us, length us, event | category | flops | bytes accessed | tf_op | source)
XLA Modules:
  0.0 178.6 jit_solution(14386101710609424991)
XLA Ops:
  0.0 1.5 multiply_convert_fusion.targets.u_own
  1.6 1.5 collective-permute-start.1
  3.1 0.0 copy-done.4
  3.1 0.1 collective-permute-start
  3.2 3.6 %shard_map.82 = (bf16[512,1024]{1,0:T(8,128)(2,1)S(1)}, bf16[256,1024]{1,0:T(8,128)(2,1)S(1)}, f32[8,128]{1,0:T(8,128)S(1)}) custom-call(s32[1]{0:T(128)} %bitcast.1.core, bf16[1024,512]{1,0:T(8,128)(2,1)} %bitcast.16, bf16[1024,512]{1,0:T(8,128)(2,1)} %bitcast.17, bf16[512,1024]{1,0:T(8,128)(2,1)} %bitcast.18), custom_call_target="tpu_custom_call" | custom-call | flops 2097152 | bytes 5242880 | tf_op jit(solution)/shard_map/pallas_call | solution.py:55
  6.7 0.0 copy-start.1
  6.8 0.0 copy-start.3
  6.8 1.0 shard_map.83.raw
  7.8 0.0 collective-permute-done.1.u_oth
  7.8 0.0 collective-permute-done.k_oth
  7.8 0.0 copy-done.1
  7.8 0.1 copy-done.3
  7.9 4.6 %shard_map.84 = bf16[2,768,512]{2,1,0:T(8,128)(2,1)S(1)} custom-call(bf16[512,1024]{1,0:T(8,128)(2,1)S(1)} %get-tuple-element.22.w13.w13_far, bf16[256,1024]{1,0:T(8,128)(2,1)S(1)} %get-tuple-element.23.w2.w2_far, f32[768,512]{1,0:T(8,128)S(1)} %shard_map.83.raw, bf16[512,1024]{1,0:T(8,128)(2,1)S(1)} %copy-done.4, ...), custom_call_target="tpu_custom_call" | custom-call | flops 2415919104 | bytes 8388608 | tf_op jit(solution)/shard_map/pallas_call | solution.py:55
  12.5 30.3 %all_to_all.20.arrived = bf16[32,48,512]{2,1,0:T(8,128)(2,1)S(1)} all-to-all(bf16[32,48,512]{2,1,0:T(8,128)(2,1)S(1)} %bitcast.15), channel_id=1, replica_groups=mesh['z'=4,'xl'=2,'y'=4,'c'=2,'h'=2] {'z','xl','y'}, dimensions={0} | all-to-all | bytes 3145728 | tf_op jit(solution)/shard_map/all_to_all | solution.py:295
  42.7 0.3 shard_map.85
  43.1 0.0 copy-start.2
  43.1 1.1 copy-done.2
  44.2 5.7 %all-to-all-start.1 = ((bf16[32,48,512]{2,1,0:T(8,128)(2,1)}), bf16[32,48,512]{2,1,0:T(8,128)(2,1)S(1)}, u32[]{:S(2)}, u32[]{:S(2)}) async-start(bf16[32,48,512]{2,1,0:T(8,128)(2,1)} %copy-done.2), calls=%async_computation.1 | async-start | bytes 3145728 | tf_op jit(solution)/shard_map/all_to_all | solution.py:305
  49.9 3.4 %fusion = (bf16[256,2560]{1,0:T(8,128)(2,1)}, bf16[256,2560]{1,0:T(8,128)(2,1)}) fusion(bf16[1024,5120]{1,0:T(8,128)(2,1)} %w_own.1, s32[]{:T(128)S(6)} %select_n.12, s32[]{:T(128)S(6)} %select_n.11, s32[]{:T(128)S(6)} %select_n.10), kind=kLoop, calls=%fused_computation.2 | loop fusion | bytes 5242892 | tf_op jit(solution)/shard_map/dynamic_slice | solution.py:329
  53.3 2.5 %collective-permute-start.10 = (bf16[256,2560]{1,0:T(8,128)(2,1)}, bf16[256,2560]{1,0:T(8,128)(2,1)}, u32[]{:S(2)}, u32[]{:S(2)}) collective-permute-start(bf16[256,2560]{1,0:T(8,128)(2,1)} %get-tuple-element.40), channel_id=1, source_target_pairs={{0,17},{17,0},{1,16},{16,1},{2,19},{19,2},{3,18},{18,3},{4,21},{21... | collective-permute-start | bytes 3932168 | tf_op jit(solution)/shard_map/ppermute | solution.py:333
  55.8 15.0 %all-to-all-done.1 = bf16[32,48,512]{2,1,0:T(8,128)(2,1)S(1)} async-done(((bf16[32,48,512]{2,1,0:T(8,128)(2,1)}), bf16[32,48,512]{2,1,0:T(8,128)(2,1)S(1)}, u32[]{:S(2)}, u32[]{:S(2)}) %all-to-all-start.1) | async-done | bytes 1572896 | tf_op jit(solution)/shard_map/all_to_all | solution.py:305
  70.8 2.7 %shard_map.86 = (bf16[512,1024]{1,0:T(8,128)(2,1)S(1)}, bf16[256,1024]{1,0:T(8,128)(2,1)S(1)}, f32[8,128]{1,0:T(8,128)S(1)}) custom-call(bf16[512,1024]{1,0:T(8,128)(2,1)} %copy-done.1, bf16[256,1024]{1,0:T(8,128)(2,1)} %copy-done.3, bf16[2,768,512]{2,1,0:T(8,128)(2,1)S(1)} %bitcast.12), custom_call_target="tpu_custom_call" | custom-call | flops 4194304 | bytes 5242880 | tf_op jit(solution)/shard_map/pallas_call | solution.py:55
  73.6 0.0 copy-done
  73.6 2.5 %collective-permute-start.2 = (f32[8,128]{1,0:T(8,128)S(1)}, f32[8,128]{1,0:T(8,128)S(1)}, u32[]{:S(2)}, u32[]{:S(2)}) collective-permute-start(f32[8,128]{1,0:T(8,128)S(1)} %get-tuple-element.25.rest_1_.rest_2_), channel_id=1, source_target_pairs={{0,2},{2,0},{1,3},{3,1},{4,6},{6,4},{5,7},{7,5},{8,10},{10,8},{9,1... | collective-permute-start | bytes 12296 | tf_op jit(solution)/shard_map/ppermute | solution.py:310
  76.1 1.0 shard_map.87.raw
  77.1 0.0 collective-permute-done.2.rest_2_.rest_3_
  77.1 5.7 %shard_map.88 = bf16[2,768,512]{2,1,0:T(8,128)(2,1)} custom-call(bf16[512,1024]{1,0:T(8,128)(2,1)S(1)} %get-tuple-element.26.w13, bf16[256,1024]{1,0:T(8,128)(2,1)S(1)} %get-tuple-element.27.w2, f32[768,512]{1,0:T(8,128)S(1)} %shard_map.87.raw, bf16[512,1024]{1,0:T(8,128)(2,1)S(1)} %copy-done.5, bf16[512,1024]{1,0:T(8,128)(2,1)} %collective-permute-done.k_oth, ...), custom_call_target="tpu_custom_call" | custom-call | flops 2415919104 | bytes 8388608 | tf_op jit(solution)/shard_map/pallas_call | solution.py:55
  82.9 5.9 %all-to-all-start.2 = ((bf16[32,48,512]{2,1,0:T(8,128)(2,1)}), bf16[32,48,512]{2,1,0:T(8,128)(2,1)S(1)}, u32[]{:S(2)}, u32[]{:S(2)}) async-start(bf16[32,48,512]{2,1,0:T(8,128)(2,1)} %bitcast.8), calls=%async_computation.2 | async-start | bytes 3145728 | tf_op jit(solution)/shard_map/all_to_all | solution.py:295
  88.8 0.0 collective-permute-done.10.first_a
  88.8 2.6 %collective-permute-start.11 = (bf16[256,2560]{1,0:T(8,128)(2,1)}, bf16[256,2560]{1,0:T(8,128)(2,1)S(1)}, u32[]{:S(2)}, u32[]{:S(2)}) collective-permute-start(bf16[256,2560]{1,0:T(8,128)(2,1)} %get-tuple-element.31), channel_id=1, source_target_pairs={{0,17},{17,0},{1,16},{16,1},{2,19},{19,2},{3,18},{18,3},{4,21},{21... | collective-permute-start | bytes 3932168 | tf_op jit(solution)/shard_map/ppermute | solution.py:334
  91.4 19.5 %all-to-all-done.2.arrived = bf16[32,48,512]{2,1,0:T(8,128)(2,1)S(1)} async-done(((bf16[32,48,512]{2,1,0:T(8,128)(2,1)}), bf16[32,48,512]{2,1,0:T(8,128)(2,1)S(1)}, u32[]{:S(2)}, u32[]{:S(2)}) %all-to-all-start.2) | async-done | bytes 1572896 | tf_op jit(solution)/shard_map/all_to_all | solution.py:295
  110.8 1.5 shard_map.89
  112.3 6.3 %all-to-all-start.3 = ((bf16[32,48,512]{2,1,0:T(8,128)(2,1)}), bf16[32,48,512]{2,1,0:T(8,128)(2,1)S(1)}, u32[]{:S(2)}, u32[]{:S(2)}) async-start(bf16[32,48,512]{2,1,0:T(8,128)(2,1)} %shard_map.89), calls=%async_computation.3 | async-start | bytes 3145728 | tf_op jit(solution)/shard_map/all_to_all | solution.py:305
  118.6 1.3 collective-permute-start.3
  120.0 0.3 collective-permute-done.11.first_b
  120.3 1.2 collective-permute-start.12
  121.5 0.0 collective-permute-start.13
  121.5 18.0 %all-to-all-done.3 = bf16[32,48,512]{2,1,0:T(8,128)(2,1)S(1)} async-done(((bf16[32,48,512]{2,1,0:T(8,128)(2,1)}), bf16[32,48,512]{2,1,0:T(8,128)(2,1)S(1)}, u32[]{:S(2)}, u32[]{:S(2)}) %all-to-all-start.3) | async-done | bytes 1572896 | tf_op jit(solution)/shard_map/all_to_all | solution.py:305
  139.5 2.9 %shard_map.90 = (bf16[512,1024]{1,0:T(8,128)(2,1)S(1)}, bf16[256,1024]{1,0:T(8,128)(2,1)S(1)}, f32[8,128]{1,0:T(8,128)S(1)}) custom-call(bf16[512,1024]{1,0:T(8,128)(2,1)} %copy-done.1, bf16[256,1024]{1,0:T(8,128)(2,1)} %copy-done.3, bf16[2,768,512]{2,1,0:T(8,128)(2,1)} %bitcast.13, f32[8,128]{1,0:T(8,128)S(1)} %get-tuple-element.24.rest_0_.rest_1_.norm, ...), custom_call_target="tpu_custom_call" | custom-call | flops 4194304 | bytes 5242880 | tf_op jit(solution)/shard_map/pallas_call | solution.py:55
  142.4 2.7 %collective-permute-start.4 = (f32[8,128]{1,0:T(8,128)S(1)}, f32[8,128]{1,0:T(8,128)S(1)}, u32[]{:S(2)}, u32[]{:S(2)}) collective-permute-start(f32[8,128]{1,0:T(8,128)S(1)} %get-tuple-element.29.sq_own), channel_id=1, source_target_pairs={{0,2},{2,0},{1,3},{3,1},{4,6},{6,4},{5,7},{7,5},{8,10},{10,8},{9,1... | collective-permute-start | bytes 12296 | tf_op jit(solution)/shard_map/ppermute | solution.py:310
  145.1 0.1 collective-permute-start.6
  145.2 0.0 collective-permute-done.3.oth_far
  145.2 1.5 collective-permute-start.7
  146.7 2.9 %shard_map.91.raw = f32[2,512,512]{2,1,0:T(8,128)S(1)} custom-call(bf16[512,1024]{1,0:T(8,128)(2,1)S(1)} %get-tuple-element.28.m13, bf16[512,1024]{1,0:T(8,128)(2,1)} %collective-permute-done.3.oth_far, bf16[512,1024]{1,0:T(8,128)(2,1)} %own_far.1), custom_call_target="tpu_custom_call" | custom-call | flops 65536 | bytes 65536 | tf_op jit(solution)/shard_map/pallas_call | solution.py:55
  149.6 0.0 collective-permute-done.4.sq_oth
  149.6 0.3 shard_map.93
  149.9 0.8 collective-permute-start.5
  150.7 0.3 shard_map.92.hq_own
  150.9 0.0 collective-permute-done.12.second_a
  151.0 0.8 collective-permute-start.8
  151.7 0.1 collective-permute-done.5.hq_got.after
  151.8 2.2 %collective-permute-start.9 = (bf16[256,512]{1,0:T(8,128)(2,1)S(1)}, bf16[256,512]{1,0:T(8,128)(2,1)S(1)}, u32[]{:S(2)}, u32[]{:S(2)}) collective-permute-start(bf16[256,512]{1,0:T(8,128)(2,1)S(1)} %collective-permute-done.5.hq_got.after), channel_id=1, source_target_pairs={{0,1},{1,0},{2,3},{3,2},{4,5},{5,4},{6,7},{7,6},{8,9},{9,8},{10,11... | collective-permute-start | bytes 786440 | tf_op jit(solution)/shard_map/ppermute | solution.py:393
  154.0 0.1 pad_add_fusion.place
  154.1 0.0 collective-permute-done.13.second_b
  154.1 2.3 %shard_map.96 = (bf16[512,2560]{1,0:T(8,128)(2,1)S(1)}, bf16[512,2560]{1,0:T(8,128)(2,1)S(1)}) custom-call(bf16[256,512]{1,0:T(8,128)(2,1)S(1)} %collective-permute-done.5.hq_got.after, bf16[256,2560]{1,0:T(8,128)(2,1)} %collective-permute-done.10.first_a, bf16[256,2560]{1,0:T(8,128)(2,1)S(1)} %collective-permute-done.11.first_b, ...), custom_call_target="tpu_custom_call" | custom-call | flops 65536 | bytes 65536 | tf_op jit(solution)/shard_map/pallas_call | solution.py:55
  156.4 0.0 collective-permute-done.6.w2_got
  156.4 0.7 shard_map.94.o
  157.2 4.8 %shard_map.95.part = f32[512,2560]{1,0:T(8,128)S(1)} custom-call(s32[2]{0:T(128)S(1)} %pad_add_fusion.place, bf16[512,1024]{1,0:T(8,128)(2,1)S(1)} %shard_map.94.o, bf16[1024,5120]{1,0:T(8,128)(2,1)S(1)} %bitcast.11), custom_call_target="tpu_custom_call" | custom-call | flops 1048576 | bytes 65536 | tf_op jit(solution)/shard_map/pallas_call | solution.py:236
  162.0 0.0 collective-permute-done.8.hq_a
  162.0 8.7 %collective-permute-done.7.rest_0_ = bf16[256,1024]{1,0:T(8,128)(2,1)S(1)} collective-permute-done((bf16[256,1024]{1,0:T(8,128)(2,1)S(1)}, bf16[256,1024]{1,0:T(8,128)(2,1)S(1)}, u32[]{:S(2)}, u32[]{:S(2)}) %collective-permute-start.7) | collective-permute-done | bytes 524320 | tf_op jit(solution)/shard_map/ppermute | solution.py:375
  170.7 0.0 collective-permute-done.9.hq_b
  170.7 1.3 collective-permute-start.14
  172.0 1.5 collective-permute-done.14.rest_1_
  173.5 5.0 %shard_map.97 = bf16[512,2560]{1,0:T(8,128)(2,1)} custom-call(s32[2]{0:T(128)S(1)} %pad_add_fusion.place, f32[512,2560]{1,0:T(8,128)S(1)} %shard_map.95.part, bf16[256,512]{1,0:T(8,128)(2,1)S(1)} %collective-permute-done.8.hq_a, bf16[256,512]{1,0:T(8,128)(2,1)S(1)} %collective-permute-done.9.hq_b, bf16[256,1024]{1,0:T(8,128)(2,1)S(1)} %collective-permute-done.7.rest_0_, ...), custom_call_target="tpu_custom_call" | custom-call | flops 3221225472 | bytes 6291456 | tf_op jit(solution)/shard_map/pallas_call | solution.py:275
  (11 shorter events, 0.0 us)
Async XLA Ops:
  0.0 3.1 %copy-start.4 = (bf16[512,1024]{1,0:T(8,128)(2,1)S(1)}, bf16[512,1024]{1,0:T(8,128)(2,1)}, u32[]{:S(2)}) copy-start(bf16[512,1024]{1,0:T(8,128)(2,1)} %k_own.3) | copy-start | bytes 3145732
  1.6 6.2 %collective-permute-start.1 = (bf16[512,1024]{1,0:T(8,128)(2,1)S(1)}, bf16[512,1024]{1,0:T(8,128)(2,1)}, u32[]{:S(2)}, u32[]{:S(2)}) collective-permute-start(bf16[512,1024]{1,0:T(8,128)(2,1)S(1)} %multiply_convert_fusion.targets.u_own), channel_id=1, source_target_pairs={{0,2},{2,0},{1,3},{3,1},{4,6},{6,4},{5,7},{7,5},{8,10},{10,8},{9,1... | collective-permute-start | bytes 3145736 | tf_op jit(solution)/shard_map/ppermute | solution.py:310
  3.1 4.7 %collective-permute-start = (bf16[512,1024]{1,0:T(8,128)(2,1)S(1)}, bf16[512,1024]{1,0:T(8,128)(2,1)}, u32[]{:S(2)}, u32[]{:S(2)}) collective-permute-start(bf16[512,1024]{1,0:T(8,128)(2,1)S(1)} %copy-done.4), channel_id=1, source_target_pairs={{0,2},{2,0},{1,3},{3,1},{4,6},{6,4},{5,7},{7,5},{8,10},{10,8},{9,1... | collective-permute-start | bytes 3145736 | tf_op jit(solution)/shard_map/ppermute | solution.py:310
  6.7 1.1 copy-start.1
  6.8 1.2 copy-start.3
  43.1 1.1 copy-start.2
  44.2 26.6 %all-to-all-start.1 = ((bf16[32,48,512]{2,1,0:T(8,128)(2,1)}), bf16[32,48,512]{2,1,0:T(8,128)(2,1)S(1)}, u32[]{:S(2)}, u32[]{:S(2)}) async-start(bf16[32,48,512]{2,1,0:T(8,128)(2,1)} %copy-done.2), calls=%async_computation.1 | async-start | bytes 3145728 | tf_op jit(solution)/shard_map/all_to_all | solution.py:305
  53.3 35.5 %collective-permute-start.10 = (bf16[256,2560]{1,0:T(8,128)(2,1)}, bf16[256,2560]{1,0:T(8,128)(2,1)}, u32[]{:S(2)}, u32[]{:S(2)}) collective-permute-start(bf16[256,2560]{1,0:T(8,128)(2,1)} %get-tuple-element.40), channel_id=1, source_target_pairs={{0,17},{17,0},{1,16},{16,1},{2,19},{19,2},{3,18},{18,3},{4,21},{21... | collective-permute-start | bytes 3932168 | tf_op jit(solution)/shard_map/ppermute | solution.py:333
  70.8 2.7 %copy-start = (bf16[32,48,512]{2,1,0:T(8,128)(2,1)}, bf16[32,48,512]{2,1,0:T(8,128)(2,1)S(1)}, u32[]{:S(2)}) copy-start(bf16[32,48,512]{2,1,0:T(8,128)(2,1)S(1)} %all-to-all-done.1) | copy-start | bytes 4718596
  70.8 5.3 %copy-start.5 = (bf16[512,1024]{1,0:T(8,128)(2,1)S(1)}, bf16[512,1024]{1,0:T(8,128)(2,1)}, u32[]{:S(2)}) copy-start(bf16[512,1024]{1,0:T(8,128)(2,1)} %k_own.3) | copy-start | bytes 3145732
  73.6 3.6 %collective-permute-start.2 = (f32[8,128]{1,0:T(8,128)S(1)}, f32[8,128]{1,0:T(8,128)S(1)}, u32[]{:S(2)}, u32[]{:S(2)}) collective-permute-start(f32[8,128]{1,0:T(8,128)S(1)} %get-tuple-element.25.rest_1_.rest_2_), channel_id=1, source_target_pairs={{0,2},{2,0},{1,3},{3,1},{4,6},{6,4},{5,7},{7,5},{8,10},{10,8},{9,1... | collective-permute-start | bytes 12296 | tf_op jit(solution)/shard_map/ppermute | solution.py:310
  82.9 28.0 %all-to-all-start.2 = ((bf16[32,48,512]{2,1,0:T(8,128)(2,1)}), bf16[32,48,512]{2,1,0:T(8,128)(2,1)S(1)}, u32[]{:S(2)}, u32[]{:S(2)}) async-start(bf16[32,48,512]{2,1,0:T(8,128)(2,1)} %bitcast.8), calls=%async_computation.2 | async-start | bytes 3145728 | tf_op jit(solution)/shard_map/all_to_all | solution.py:295
  88.8 31.5 %collective-permute-start.11 = (bf16[256,2560]{1,0:T(8,128)(2,1)}, bf16[256,2560]{1,0:T(8,128)(2,1)S(1)}, u32[]{:S(2)}, u32[]{:S(2)}) collective-permute-start(bf16[256,2560]{1,0:T(8,128)(2,1)} %get-tuple-element.31), channel_id=1, source_target_pairs={{0,17},{17,0},{1,16},{16,1},{2,19},{19,2},{3,18},{18,3},{4,21},{21... | collective-permute-start | bytes 3932168 | tf_op jit(solution)/shard_map/ppermute | solution.py:334
  112.3 27.1 %all-to-all-start.3 = ((bf16[32,48,512]{2,1,0:T(8,128)(2,1)}), bf16[32,48,512]{2,1,0:T(8,128)(2,1)S(1)}, u32[]{:S(2)}, u32[]{:S(2)}) async-start(bf16[32,48,512]{2,1,0:T(8,128)(2,1)} %shard_map.89), calls=%async_computation.3 | async-start | bytes 3145728 | tf_op jit(solution)/shard_map/all_to_all | solution.py:305
  118.6 26.5 %collective-permute-start.3 = (bf16[512,1024]{1,0:T(8,128)(2,1)}, bf16[512,1024]{1,0:T(8,128)(2,1)}, u32[]{:S(2)}, u32[]{:S(2)}) collective-permute-start(bf16[512,1024]{1,0:T(8,128)(2,1)} %own_far.1), channel_id=1, source_target_pairs={{0,2},{2,0},{1,3},{3,1},{4,6},{6,4},{5,7},{7,5},{8,10},{10,8},{9,1... | collective-permute-start | bytes 3145736 | tf_op jit(solution)/shard_map/ppermute | solution.py:310
  120.3 30.7 %collective-permute-start.12 = (bf16[256,2560]{1,0:T(8,128)(2,1)}, bf16[256,2560]{1,0:T(8,128)(2,1)}, u32[]{:S(2)}, u32[]{:S(2)}) collective-permute-start(bf16[256,2560]{1,0:T(8,128)(2,1)} %collective-permute-done.10.first_a), channel_id=1, source_target_pairs={{0,2},{2,0},{1,3},{3,1},{4,6},{6,4},{5,7},{7,5},{8,10},{10,8},{9,1... | collective-permute-start | bytes 3932168 | tf_op jit(solution)/shard_map/ppermute | solution.py:310
  121.5 32.6 %collective-permute-start.13 = (bf16[256,2560]{1,0:T(8,128)(2,1)S(1)}, bf16[256,2560]{1,0:T(8,128)(2,1)}, u32[]{:S(2)}, u32[]{:S(2)}) collective-permute-start(bf16[256,2560]{1,0:T(8,128)(2,1)S(1)} %collective-permute-done.11.first_b), channel_id=1, source_target_pairs={{0,2},{2,0},{1,3},{3,1},{4,6},{6,4},{5,7},{7,5},{8,10},{10,8},{9,1... | collective-permute-start | bytes 3932168 | tf_op jit(solution)/shard_map/ppermute | solution.py:310
  139.5 17.7 %slice-start = ((s8[10485760]{0:T(1024)(128)(4,1)}), s8[4194304]{0:T(1024)(128)(4,1)S(1)}, s32[]{:S(2)}) async-start(s8[10485760]{0:T(1024)(128)(4,1)} %bitcast.10), calls=%async_computation.4 | async-start | bytes 8388608
  142.4 7.2 %collective-permute-start.4 = (f32[8,128]{1,0:T(8,128)S(1)}, f32[8,128]{1,0:T(8,128)S(1)}, u32[]{:S(2)}, u32[]{:S(2)}) collective-permute-start(f32[8,128]{1,0:T(8,128)S(1)} %get-tuple-element.29.sq_own), channel_id=1, source_target_pairs={{0,2},{2,0},{1,3},{3,1},{4,6},{6,4},{5,7},{7,5},{8,10},{10,8},{9,1... | collective-permute-start | bytes 12296 | tf_op jit(solution)/shard_map/ppermute | solution.py:310
  145.1 11.3 %collective-permute-start.6 = (bf16[256,1024]{1,0:T(8,128)(2,1)S(1)}, bf16[256,1024]{1,0:T(8,128)(2,1)S(1)}, u32[]{:S(2)}, u32[]{:S(2)}) collective-permute-start(bf16[256,1024]{1,0:T(8,128)(2,1)S(1)} %get-tuple-element.30.w2_own), channel_id=1, source_target_pairs={{0,2},{2,0},{1,3},{3,1},{4,6},{6,4},{5,7},{7,5},{8,10},{10,8},{9,1... | collective-permute-start | bytes 1572872 | tf_op jit(solution)/shard_map/ppermute | solution.py:310
  145.2 25.5 %collective-permute-start.7 = (bf16[256,1024]{1,0:T(8,128)(2,1)S(1)}, bf16[256,1024]{1,0:T(8,128)(2,1)S(1)}, u32[]{:S(2)}, u32[]{:S(2)}) collective-permute-start(bf16[256,1024]{1,0:T(8,128)(2,1)S(1)} %get-tuple-element.30.w2_own), channel_id=1, source_target_pairs={{0,17},{17,0},{1,16},{16,1},{2,19},{19,2},{3,18},{18,3},{4,21},{21... | collective-permute-start | bytes 1572872 | tf_op jit(solution)/shard_map/ppermute | solution.py:375
  146.7 10.5 %slice-start.1 = ((s8[10485760]{0:T(1024)(128)(4,1)}), s8[4194304]{0:T(1024)(128)(4,1)S(1)}, s32[]{:S(2)}) async-start(s8[10485760]{0:T(1024)(128)(4,1)} %bitcast.10), calls=%async_computation.5 | async-start | bytes 8388608
  149.9 1.9 %collective-permute-start.5 = (bf16[256,512]{1,0:T(8,128)(2,1)S(1)}, bf16[256,512]{1,0:T(8,128)(2,1)S(1)}, u32[]{:S(2)}, u32[]{:S(2)}) collective-permute-start(bf16[256,512]{1,0:T(8,128)(2,1)S(1)} %shard_map.93), channel_id=1, source_target_pairs={{0,2},{2,0},{1,3},{3,1},{4,6},{6,4},{5,7},{7,5},{8,10},{10,8},{9,1... | collective-permute-start | bytes 786440 | tf_op jit(solution)/shard_map/ppermute | solution.py:310
  151.0 11.1 %collective-permute-start.8 = (bf16[256,512]{1,0:T(8,128)(2,1)S(1)}, bf16[256,512]{1,0:T(8,128)(2,1)S(1)}, u32[]{:S(2)}, u32[]{:S(2)}) collective-permute-start(bf16[256,512]{1,0:T(8,128)(2,1)S(1)} %shard_map.92.hq_own), channel_id=1, source_target_pairs={{0,1},{1,0},{2,3},{3,2},{4,5},{5,4},{6,7},{7,6},{8,9},{9,8},{10,11... | collective-permute-start | bytes 786440 | tf_op jit(solution)/shard_map/ppermute | solution.py:393
  151.8 18.9 %collective-permute-start.9 = (bf16[256,512]{1,0:T(8,128)(2,1)S(1)}, bf16[256,512]{1,0:T(8,128)(2,1)S(1)}, u32[]{:S(2)}, u32[]{:S(2)}) collective-permute-start(bf16[256,512]{1,0:T(8,128)(2,1)S(1)} %collective-permute-done.5.hq_got.after), channel_id=1, source_target_pairs={{0,1},{1,0},{2,3},{3,2},{4,5},{5,4},{6,7},{7,6},{8,9},{9,8},{10,11... | collective-permute-start | bytes 786440 | tf_op jit(solution)/shard_map/ppermute | solution.py:393
  154.1 3.1 %slice-start.2 = ((s8[10485760]{0:T(1024)(128)(4,1)}), s8[2097152]{0:T(1024)(128)(4,1)S(1)}, s32[]{:S(2)}) async-start(s8[10485760]{0:T(1024)(128)(4,1)} %bitcast.10), calls=%async_computation.6 | async-start | bytes 4194304
  170.7 2.8 %collective-permute-start.14 = (bf16[256,1024]{1,0:T(8,128)(2,1)S(1)}, bf16[256,1024]{1,0:T(8,128)(2,1)S(1)}, u32[]{:S(2)}, u32[]{:S(2)}) collective-permute-start(bf16[256,1024]{1,0:T(8,128)(2,1)S(1)} %collective-permute-done.7.rest_0_), channel_id=1, source_target_pairs={{0,2},{2,0},{1,3},{3,1},{4,6},{6,4},{5,7},{7,5},{8,10},{10,8},{9,1... | collective-permute-start | bytes 1572872 | tf_op jit(solution)/shard_map/ppermute | solution.py:310

commit v10 on v7

--- a/solution.py
+++ b/solution.py
@@ -141,49 +141,57 @@
 ROWS = 16
 
 
-def update_kernel(w13_far, w2_far, *rest):
-    if len(rest) > 8:
-        first_far, *state, gathered_far, m13, m2, squares, w13, w2, first, gathered, sems = rest
-    else:
-        gathered, m13, m2, squares, w13, w2, first, sems = rest
-    again = len(rest) > 8
+def moved_rows(i, base, src, terms, scale, dst, cols, half):
+    def step(r, total):
+        row = pl.multiple_of(base + r * ROWS, ROWS)
+        at = pl.multiple_of(i * half + r * ROWS, ROWS)
+        for j in range(2):
+            side = slice(j * cols, (j + 1) * cols)
+            m = src[pl.ds(row, ROWS), side].astype(F32)
+            m = m + terms[0][j, pl.ds(at, ROWS), :].astype(F32)
+            if scale is not None:
+                m = m * scale + terms[1][j, pl.ds(at, ROWS), :].astype(F32)
+            dst[pl.ds(row, ROWS), side] = m.astype(BF)
+            total = total + m * m
+        return total
+
+    total = lax.fori_loop(0, half // ROWS, step, jnp.zeros((ROWS, cols), F32))
+    return jnp.full((1, 128), jnp.sum(total), F32)
+
+
+def update_kernel(w13_far, w2_far, gathered, m13, m2, squares, w13, w2, sems):
     half = w2.shape[0]
     cols = w2.shape[1] // 2
-    pairs = []
-    for i in range(3):
-        src, dst = (w13_far, w13) if i < 2 else (w2_far, w2)
-        rows = slice((i % 2) * half, (i % 2 + 1) * half)
-        at = slice(i * half, (i + 1) * half)
-        pairs.append((src.at[rows, :], dst.at[rows, :]))
-        if again:
-            pairs.append((first_far.at[:, at, :], first.at[:, at, :]))
-            pairs.append((gathered_far.at[:, at, :], gathered.at[:, at, :]))
-    each = len(pairs) // 3
-    copies = fetch(pairs, sems)
+    pairs = [(w13_far.at[r, :], w13.at[r, :]) for r in (slice(0, half), slice(half, 2 * half))]
+    copies = fetch([*pairs, (w2_far, w2)], sems)
     for i in range(3):
         src, dst = (w13, m13) if i < 2 else (w2, m2)
-        base = (i % 2) * half
-        if again:
-            scale = jnp.broadcast_to(factor(i, *state), (ROWS, cols))
-        for copy in copies[i * each : (i + 1) * each]:
+        copies[i].wait()
+        squares[i : i + 1, :] = moved_rows(
+            i, (i % 2) * half, src, (gathered,), None, dst, cols, half
+        )
+    squares[3:8, :] = jnp.zeros((5, 128), F32)
+
+
+def later_kernel(parts, w_far, first_far, norm, own, oth, gathered_far, *rest):
+    *before, m, squares, w, first, gathered, sems = rest
+    half = w.shape[0] // len(parts)
+    cols = w.shape[1] // 2
+    pairs = []
+    for k, i in enumerate(parts):
+        rows, at = slice(k * half, (k + 1) * half), slice(i * half, (i + 1) * half)
+        pairs.append((w_far.at[rows, :], w.at[rows, :]))
+        pairs.append((first_far.at[:, at, :], first.at[:, at, :]))
+        pairs.append((gathered_far.at[:, at, :], gathered.at[:, at, :]))
+    copies = fetch(pairs, sems)
+    squares[...] = before[0][...] if before else jnp.zeros(squares.shape, F32)
+    for k, i in enumerate(parts):
+        scale = jnp.broadcast_to(factor(i, norm, own, oth), (ROWS, cols))
+        for copy in copies[3 * k : 3 * k + 3]:
             copy.wait()
-
-        def step(r, total):
-            row = pl.multiple_of(base + r * ROWS, ROWS)
-            at = pl.multiple_of(i * half + r * ROWS, ROWS)
-            for j in range(2):
-                side = slice(j * cols, (j + 1) * cols)
-                m = src[pl.ds(row, ROWS), side].astype(F32)
-                if again:
-                    m = (m + first[j, pl.ds(at, ROWS), :].astype(F32)) * scale
-                m = m + gathered[j, pl.ds(at, ROWS), :].astype(F32)
-                dst[pl.ds(row, ROWS), side] = m.astype(BF)
-                total = total + m * m
-            return total
-
-        total = lax.fori_loop(0, half // ROWS, step, jnp.zeros((ROWS, cols), F32))
-        squares[i : i + 1, :] = jnp.full((1, 128), jnp.sum(total), F32)
-    squares[3:8, :] = jnp.zeros((5, 128), F32)
+        squares[i : i + 1, :] = moved_rows(
+            i, k * half, w, (first, gathered), scale, m, cols, half
+        )
 
 
 def query_kernel(m13, oth_far, own_far, raw, oth, own, sems):
@@ -355,22 +363,34 @@
             8 << 20,
         )(*mats, raw, keys, k_oth, targets, u_oth, *state)
         gathered, w_late = all_reduced(grads, (w_a, w_b) if step else None)
-        again = () if step == 0 else (first, *state)
-        *mats, squares = call(
-            update_kernel,
-            (*wshape, sshape),
-            [FAR] * 2 + ([FAR] + [VMEM] * 3) * step + [ANY if step else NEAR],
-            1 << 22,
-            5 << 20,
-            (
-                buffer((2 * half, width)),
-                buffer((half, width)),
-                buffer(gdims),
-                *([buffer(gdims)] * step),
-                semaphores(3 + 6 * step),
-            ),
-        )(*w, *again, gathered)
-        first = gathered
+        if step == 0:
+            *mats, squares = call(
+                update_kernel,
+                (*wshape, sshape),
+                [FAR] * 2 + [NEAR],
+                1 << 22,
+                5 << 20,
+                (buffer((2 * half, width)), buffer((half, width)), semaphores(3)),
+            )(*w, gathered)
+            first = gathered
+        else:
+            before, mats = (), []
+            for k, parts in ((1, (2,)), (0, (0, 1))):
+                m, *before = call(
+                    functools.partial(later_kernel, parts),
+                    (wshape[k], sshape),
+                    [FAR] * 2 + [VMEM] * 3 + [ANY] + [VMEM] * len(before),
+                    1 << 20,
+                    1 << 20,
+                    (
+                        buffer(wshape[k].shape),
+                        buffer(gdims),
+                        buffer(gdims),
+                        semaphores(3 * len(parts)),
+                    ),
+                )(w[k], first, *state, gathered, *before)
+                mats.insert(0, m)
+            squares = before[0]
         state = (norm, squares, swap(squares))
     crossed = lax.ppermute(mats[1], ("xl", "h"), ACROSS)
     w_parts = (w_a, w_b, *map(swap, w_late))
@@ -397,7 +417,7 @@
     part = partial_product(place, o, w_out)
     wide = (shape((width // 2, n)),) * 2
     w_first, w_second = call(stage_kernel, wide, [ANY] * 5, 1 << 16, 1 << 16, [semaphores(4)])(
-        hqs[0], *w_parts
+        hq_got, *w_parts
     )
     crossed, *hqs, _, _ = lax.optimization_barrier((crossed, *hqs, part, w_first))
     return finish_product(place, part, hqs, (crossed, swap(crossed)), w_first, w_second)

time: 177 us -> 175 us (0.989)
  waiting for transfers between devices: 60.8 us -> 58 us
    ppermute x2, waiting for transfers between devices: 6.43 us -> 4.01 us  [shards(): hqs = [lax.ppermute(x, 'h', SWAP) for x in (hq_own, hq_got)]]
    pallas_call x14 -> x15, Pallas kernels: 29.7 us -> 31.1 us  [with_places(): run(*(pltpu.with_memory_space_constraint(x, HELD[id(spec)]) if id(spec) i...]
  transfers between devices with their start and end apart: 18 -> 18, of which waited for: 6 -> 6; matrix products, arithmetic and copies ran while one was open for 2% -> 2% of each run, Pallas kernels for 17% -> 18%
where the time goes in v10:
time: 175 us
  waiting for transfers between devices  58 us (33%)
  Pallas kernels  40.9 us (23%)
  starting transfers between devices  38.8 us (22%)
  blocking collectives  30.3 us (17%)
  local copies, waits for them, and re-layouts  4.68 us (3%)
    all_to_all x2, waiting for transfers between devices, all_reduced(): gathered = lax.all_to_all(copies, CHIPS, 0, 0, tiled=True)  32.9 us
    pallas_call x15, Pallas kernels, with_places(): run(*(pltpu.with_memory_space_constraint(x, HELD[id(spec)]) if id(spec) i...  31.1 us
    all_to_all x1, blocking collectives, all_reduced(): arrived = lax.all_to_all(pieces, CHIPS, 0, 0, tiled=True)  30.3 us
    all_to_all x1, waiting for transfers between devices, all_reduced(): arrived = lax.all_to_all(pieces, CHIPS, 0, 0, tiled=True)  19.3 us
    all_to_all x2, starting transfers between devices, all_reduced(): gathered = lax.all_to_all(copies, CHIPS, 0, 0, tiled=True)  12.1 us
    ppermute x10, starting transfers between devices, swap(): return lax.ppermute(x, 'c', SWAP)  11.1 us
    all_to_all x1, starting transfers between devices, all_reduced(): arrived = lax.all_to_all(pieces, CHIPS, 0, 0, tiled=True)  5.85 us
    pallas_call x1, Pallas kernels, finish_product(): pl.pallas_call(finish_kernel, out_shape=shape((tokens, n)), in_specs=[SME...  4.98 us
  transfers between devices with their start and end apart: 18, of which 6 were waited for; matrix products, arithmetic and copies ran while one was open for 2% of the time, Pallas kernels for 18%

profile of v10, /device:TPU:1, one launch (start us, length us, event | category | flops | bytes accessed | tf_op | source)
XLA Modules:
  0.0 174.7 jit_solution(14962108401539604299)
XLA Ops:
  0.0 1.5 multiply_convert_fusion.targets.u_own
  1.6 1.5 collective-permute-start.1
  3.1 0.0 copy-done.4
  3.1 0.1 collective-permute-start
  3.2 3.6 %shard_map.82 = (bf16[512,1024]{1,0:T(8,128)(2,1)S(1)}, bf16[256,1024]{1,0:T(8,128)(2,1)S(1)}, f32[8,128]{1,0:T(8,128)S(1)}) custom-call(s32[1]{0:T(128)} %bitcast.1.core, bf16[1024,512]{1,0:T(8,128)(2,1)} %bitcast.18, bf16[1024,512]{1,0:T(8,128)(2,1)} %bitcast.19, bf16[512,1024]{1,0:T(8,128)(2,1)} %bitcast.20), custom_call_target="tpu_custom_call" | custom-call | flops 2097152 | bytes 5242880 | tf_op jit(solution)/shard_map/pallas_call | solution.py:55
  6.7 0.0 copy-start.1
  6.8 1.0 shard_map.83.raw
  7.8 0.0 collective-permute-done.1.u_oth
  7.8 0.0 collective-permute-done.k_oth
  7.8 0.0 copy-done.1
  7.8 0.1 copy-done.3
  7.9 4.5 %shard_map.84 = bf16[2,768,512]{2,1,0:T(8,128)(2,1)S(1)} custom-call(bf16[512,1024]{1,0:T(8,128)(2,1)S(1)} %get-tuple-element.23.w13.w13_far.w_far, bf16[256,1024]{1,0:T(8,128)(2,1)S(1)} %get-tuple-element.24.w2.w2_far.w_far, f32[768,512]{1,0:T(8,128)S(1)} %shard_map.83.raw, bf16[512,1024]{1,0:T(8,128)(2,1)S(1)} %copy-done.4, ...), custom_call_target="tpu_custom_call" | custom-call | flops 2415919104 | bytes 8388608 | tf_op jit(solution)/shard_map/pallas_call | solution.py:55
  12.5 30.3 %all_to_all.20.arrived = bf16[32,48,512]{2,1,0:T(8,128)(2,1)S(1)} all-to-all(bf16[32,48,512]{2,1,0:T(8,128)(2,1)S(1)} %bitcast.17), channel_id=1, replica_groups=mesh['z'=4,'xl'=2,'y'=4,'c'=2,'h'=2] {'z','xl','y'}, dimensions={0} | all-to-all | bytes 3145728 | tf_op jit(solution)/shard_map/all_to_all | solution.py:303
  42.8 0.3 shard_map.85
  43.1 0.0 copy-start.2
  43.1 1.1 copy-done.2
  44.2 5.7 %all-to-all-start.1 = ((bf16[32,48,512]{2,1,0:T(8,128)(2,1)}), bf16[32,48,512]{2,1,0:T(8,128)(2,1)S(1)}, u32[]{:S(2)}, u32[]{:S(2)}) async-start(bf16[32,48,512]{2,1,0:T(8,128)(2,1)} %copy-done.2), calls=%async_computation.1 | async-start | bytes 3145728 | tf_op jit(solution)/shard_map/all_to_all | solution.py:313
  49.9 3.4 %fusion = (bf16[256,2560]{1,0:T(8,128)(2,1)}, bf16[256,2560]{1,0:T(8,128)(2,1)}) fusion(bf16[1024,5120]{1,0:T(8,128)(2,1)} %w_own.1, s32[]{:T(128)S(6)} %select_n.12, s32[]{:T(128)S(6)} %select_n.11, s32[]{:T(128)S(6)} %select_n.10), kind=kLoop, calls=%fused_computation.2 | loop fusion | bytes 5242892 | tf_op jit(solution)/shard_map/dynamic_slice | solution.py:337
  53.3 2.5 %collective-permute-start.10 = (bf16[256,2560]{1,0:T(8,128)(2,1)}, bf16[256,2560]{1,0:T(8,128)(2,1)}, u32[]{:S(2)}, u32[]{:S(2)}) collective-permute-start(bf16[256,2560]{1,0:T(8,128)(2,1)} %get-tuple-element.42), channel_id=1, source_target_pairs={{0,17},{17,0},{1,16},{16,1},{2,19},{19,2},{3,18},{18,3},{4,21},{21... | collective-permute-start | bytes 3932168 | tf_op jit(solution)/shard_map/ppermute | solution.py:341
  55.8 15.0 %all-to-all-done.1 = bf16[32,48,512]{2,1,0:T(8,128)(2,1)S(1)} async-done(((bf16[32,48,512]{2,1,0:T(8,128)(2,1)}), bf16[32,48,512]{2,1,0:T(8,128)(2,1)S(1)}, u32[]{:S(2)}, u32[]{:S(2)}) %all-to-all-start.1) | async-done | bytes 1572896 | tf_op jit(solution)/shard_map/all_to_all | solution.py:313
  70.8 2.7 %shard_map.86 = (bf16[512,1024]{1,0:T(8,128)(2,1)S(1)}, bf16[256,1024]{1,0:T(8,128)(2,1)S(1)}, f32[8,128]{1,0:T(8,128)S(1)}) custom-call(bf16[512,1024]{1,0:T(8,128)(2,1)} %copy-done.1, bf16[256,1024]{1,0:T(8,128)(2,1)} %copy-done.3, bf16[2,768,512]{2,1,0:T(8,128)(2,1)S(1)} %bitcast.10), custom_call_target="tpu_custom_call" | custom-call | flops 4194304 | bytes 5242880 | tf_op jit(solution)/shard_map/pallas_call | solution.py:55
  73.6 2.5 %collective-permute-start.2 = (f32[8,128]{1,0:T(8,128)S(1)}, f32[8,128]{1,0:T(8,128)S(1)}, u32[]{:S(2)}, u32[]{:S(2)}) collective-permute-start(f32[8,128]{1,0:T(8,128)S(1)} %get-tuple-element.26.rest_1_.own), channel_id=1, source_target_pairs={{0,2},{2,0},{1,3},{3,1},{4,6},{6,4},{5,7},{7,5},{8,10},{10,8},{9,1... | collective-permute-start | bytes 12296 | tf_op jit(solution)/shard_map/ppermute | solution.py:318
  76.1 1.0 shard_map.87.raw
  77.1 0.0 collective-permute-done.2.rest_2_.oth
  77.2 5.8 %shard_map.88 = bf16[2,768,512]{2,1,0:T(8,128)(2,1)} custom-call(bf16[512,1024]{1,0:T(8,128)(2,1)S(1)} %get-tuple-element.27.w13, bf16[256,1024]{1,0:T(8,128)(2,1)S(1)} %get-tuple-element.28.w2, f32[768,512]{1,0:T(8,128)S(1)} %shard_map.87.raw, bf16[512,1024]{1,0:T(8,128)(2,1)S(1)} %copy-done.5, bf16[512,1024]{1,0:T(8,128)(2,1)} %collective-permute-done.k_oth, ...), custom_call_target="tpu_custom_call" | custom-call | flops 2415919104 | bytes 8388608 | tf_op jit(solution)/shard_map/pallas_call | solution.py:55
  82.9 5.8 %all-to-all-start.2 = ((bf16[32,48,512]{2,1,0:T(8,128)(2,1)}), bf16[32,48,512]{2,1,0:T(8,128)(2,1)S(1)}, u32[]{:S(2)}, u32[]{:S(2)}) async-start(bf16[32,48,512]{2,1,0:T(8,128)(2,1)} %bitcast.8), calls=%async_computation.2 | async-start | bytes 3145728 | tf_op jit(solution)/shard_map/all_to_all | solution.py:303
  88.8 0.0 collective-permute-done.10.first_a
  88.8 2.6 %collective-permute-start.11 = (bf16[256,2560]{1,0:T(8,128)(2,1)}, bf16[256,2560]{1,0:T(8,128)(2,1)S(1)}, u32[]{:S(2)}, u32[]{:S(2)}) collective-permute-start(bf16[256,2560]{1,0:T(8,128)(2,1)} %get-tuple-element.33), channel_id=1, source_target_pairs={{0,17},{17,0},{1,16},{16,1},{2,19},{19,2},{3,18},{18,3},{4,21},{21... | collective-permute-start | bytes 3932168 | tf_op jit(solution)/shard_map/ppermute | solution.py:342
  91.3 19.3 %all-to-all-done.2.arrived = bf16[32,48,512]{2,1,0:T(8,128)(2,1)S(1)} async-done(((bf16[32,48,512]{2,1,0:T(8,128)(2,1)}), bf16[32,48,512]{2,1,0:T(8,128)(2,1)S(1)}, u32[]{:S(2)}, u32[]{:S(2)}) %all-to-all-start.2) | async-done | bytes 1572896 | tf_op jit(solution)/shard_map/all_to_all | solution.py:303
  110.6 1.5 shard_map.89
  112.1 6.4 %all-to-all-start.3 = ((bf16[32,48,512]{2,1,0:T(8,128)(2,1)}), bf16[32,48,512]{2,1,0:T(8,128)(2,1)S(1)}, u32[]{:S(2)}, u32[]{:S(2)}) async-start(bf16[32,48,512]{2,1,0:T(8,128)(2,1)} %shard_map.89), calls=%async_computation.3 | async-start | bytes 3145728 | tf_op jit(solution)/shard_map/all_to_all | solution.py:313
  118.6 1.4 collective-permute-start.3
  120.0 0.2 collective-permute-done.11.first_b
  120.2 1.3 collective-permute-start.12
  121.5 0.0 collective-permute-start.13
  121.5 17.9 %all-to-all-done.3 = bf16[32,48,512]{2,1,0:T(8,128)(2,1)S(1)} async-done(((bf16[32,48,512]{2,1,0:T(8,128)(2,1)}), bf16[32,48,512]{2,1,0:T(8,128)(2,1)S(1)}, u32[]{:S(2)}, u32[]{:S(2)}) %all-to-all-start.3) | async-done | bytes 1572896 | tf_op jit(solution)/shard_map/all_to_all | solution.py:313
  139.3 1.7 shard_map.90
  141.1 1.6 collective-permute-start.7
  142.7 2.8 %collective-permute-start.6 = (bf16[256,1024]{1,0:T(8,128)(2,1)S(1)}, bf16[256,1024]{1,0:T(8,128)(2,1)S(1)}, u32[]{:S(2)}, u32[]{:S(2)}) collective-permute-start(bf16[256,1024]{1,0:T(8,128)(2,1)S(1)} %get-tuple-element.32.w2_own), channel_id=1, source_target_pairs={{0,2},{2,0},{1,3},{3,1},{4,6},{6,4},{5,7},{7,5},{8,10},{10,8},{9,1... | collective-permute-start | bytes 1572872 | tf_op jit(solution)/shard_map/ppermute | solution.py:318
  145.5 2.4 %shard_map.91 = (bf16[512,1024]{1,0:T(8,128)(2,1)S(1)}, f32[8,128]{1,0:T(8,128)S(1)}) custom-call(bf16[512,1024]{1,0:T(8,128)(2,1)} %copy-done.1, bf16[2,768,512]{2,1,0:T(8,128)(2,1)} %bitcast.12, f32[8,128]{1,0:T(8,128)S(1)} %get-tuple-element.25.rest_0_.norm, f32[8,128]{1,0:T(8,128)S(1)} %get-tuple-element.26.rest_1_.own, ...), custom_call_target="tpu_custom_call" | custom-call | flops 1048576 | bytes 1048576 | tf_op jit(solution)/shard_map/pallas_call | solution.py:55
  147.9 0.0 collective-permute-done.3.oth_far
  147.9 0.1 collective-permute-start.4
  148.0 0.0 slice-start.1
  148.1 2.9 %shard_map.92.raw = f32[2,512,512]{2,1,0:T(8,128)S(1)} custom-call(bf16[512,1024]{1,0:T(8,128)(2,1)S(1)} %get-tuple-element.30.m13, bf16[512,1024]{1,0:T(8,128)(2,1)} %collective-permute-done.3.oth_far, bf16[512,1024]{1,0:T(8,128)(2,1)} %own_far.1), custom_call_target="tpu_custom_call" | custom-call | flops 1073741824 | bytes 5242880 | tf_op jit(solution)/shard_map/pallas_call | solution.py:55
  151.0 0.0 collective-permute-done.4.sq_oth
  151.0 0.3 shard_map.94
  151.3 0.6 collective-permute-start.5
  151.8 0.3 shard_map.93.hq_own
  152.1 0.0 collective-permute-done.12.second_a
  152.1 0.9 collective-permute-start.8
  153.0 0.0 collective-permute-done.5.hq_got.after
  153.0 2.2 %collective-permute-start.9 = (bf16[256,512]{1,0:T(8,128)(2,1)S(1)}, bf16[256,512]{1,0:T(8,128)(2,1)S(1)}, u32[]{:S(2)}, u32[]{:S(2)}) collective-permute-start(bf16[256,512]{1,0:T(8,128)(2,1)S(1)} %collective-permute-done.5.hq_got.after), channel_id=1, source_target_pairs={{0,1},{1,0},{2,3},{3,2},{4,5},{5,4},{6,7},{7,6},{8,9},{9,8},{10,11... | collective-permute-start | bytes 786440 | tf_op jit(solution)/shard_map/ppermute | solution.py:413
  155.2 0.1 pad_add_fusion.place
  155.3 0.0 collective-permute-done.13.second_b
  155.3 2.3 %shard_map.97 = (bf16[512,2560]{1,0:T(8,128)(2,1)S(1)}, bf16[512,2560]{1,0:T(8,128)(2,1)S(1)}) custom-call(bf16[256,512]{1,0:T(8,128)(2,1)S(1)} %collective-permute-done.5.hq_got.after, bf16[256,2560]{1,0:T(8,128)(2,1)} %collective-permute-done.10.first_a, bf16[256,2560]{1,0:T(8,128)(2,1)S(1)} %collective-permute-done.11.first_b, ...), custom_call_target="tpu_custom_call" | custom-call | flops 65536 | bytes 65536 | tf_op jit(solution)/shard_map/pallas_call | solution.py:55
  157.6 0.0 collective-permute-done.6.w2_got
  157.6 0.7 shard_map.95.o
  158.3 4.8 %shard_map.96.part = f32[512,2560]{1,0:T(8,128)S(1)} custom-call(s32[2]{0:T(128)S(1)} %pad_add_fusion.place, bf16[512,1024]{1,0:T(8,128)(2,1)S(1)} %shard_map.95.o, bf16[1024,5120]{1,0:T(8,128)(2,1)S(1)} %bitcast.14), custom_call_target="tpu_custom_call" | custom-call | flops 1048576 | bytes 65536 | tf_op jit(solution)/shard_map/pallas_call | solution.py:244
  163.2 0.0 collective-permute-done.8.hq_a
  163.2 0.0 collective-permute-done.7.rest_0_
  163.2 4.0 %collective-permute-done.9.hq_b = bf16[256,512]{1,0:T(8,128)(2,1)S(1)} collective-permute-done((bf16[256,512]{1,0:T(8,128)(2,1)S(1)}, bf16[256,512]{1,0:T(8,128)(2,1)S(1)}, u32[]{:S(2)}, u32[]{:S(2)}) %collective-permute-start.9) | collective-permute-done | bytes 262176 | tf_op jit(solution)/shard_map/ppermute | solution.py:413
  167.2 0.8 collective-permute-start.14
  168.0 1.5 collective-permute-done.14.rest_1_
  169.6 5.0 %shard_map.98 = bf16[512,2560]{1,0:T(8,128)(2,1)} custom-call(s32[2]{0:T(128)S(1)} %pad_add_fusion.place, f32[512,2560]{1,0:T(8,128)S(1)} %shard_map.96.part, bf16[256,512]{1,0:T(8,128)(2,1)S(1)} %collective-permute-done.8.hq_a, bf16[256,512]{1,0:T(8,128)(2,1)S(1)} %collective-permute-done.9.hq_b, bf16[256,1024]{1,0:T(8,128)(2,1)S(1)} %collective-permute-done.7.rest_0_, ...), custom_call_target="tpu_custom_call" | custom-call | flops 3221225472 | bytes 6291456 | tf_op jit(solution)/shard_map/pallas_call | solution.py:283
  (12 shorter events, 0.0 us)
Async XLA Ops:
  0.0 3.1 %copy-start.4 = (bf16[512,1024]{1,0:T(8,128)(2,1)S(1)}, bf16[512,1024]{1,0:T(8,128)(2,1)}, u32[]{:S(2)}) copy-start(bf16[512,1024]{1,0:T(8,128)(2,1)} %k_own.3) | copy-start | bytes 3145732
  1.6 6.2 %collective-permute-start.1 = (bf16[512,1024]{1,0:T(8,128)(2,1)S(1)}, bf16[512,1024]{1,0:T(8,128)(2,1)}, u32[]{:S(2)}, u32[]{:S(2)}) collective-permute-start(bf16[512,1024]{1,0:T(8,128)(2,1)S(1)} %multiply_convert_fusion.targets.u_own), channel_id=1, source_target_pairs={{0,2},{2,0},{1,3},{3,1},{4,6},{6,4},{5,7},{7,5},{8,10},{10,8},{9,1... | collective-permute-start | bytes 3145736 | tf_op jit(solution)/shard_map/ppermute | solution.py:318
  3.1 4.7 %collective-permute-start = (bf16[512,1024]{1,0:T(8,128)(2,1)S(1)}, bf16[512,1024]{1,0:T(8,128)(2,1)}, u32[]{:S(2)}, u32[]{:S(2)}) collective-permute-start(bf16[512,1024]{1,0:T(8,128)(2,1)S(1)} %copy-done.4), channel_id=1, source_target_pairs={{0,2},{2,0},{1,3},{3,1},{4,6},{6,4},{5,7},{7,5},{8,10},{10,8},{9,1... | collective-permute-start | bytes 3145736 | tf_op jit(solution)/shard_map/ppermute | solution.py:318
  6.7 1.1 copy-start.1
  6.8 1.2 copy-start.3
  43.1 1.1 copy-start.2
  44.2 26.6 %all-to-all-start.1 = ((bf16[32,48,512]{2,1,0:T(8,128)(2,1)}), bf16[32,48,512]{2,1,0:T(8,128)(2,1)S(1)}, u32[]{:S(2)}, u32[]{:S(2)}) async-start(bf16[32,48,512]{2,1,0:T(8,128)(2,1)} %copy-done.2), calls=%async_computation.1 | async-start | bytes 3145728 | tf_op jit(solution)/shard_map/all_to_all | solution.py:313
  53.3 35.5 %collective-permute-start.10 = (bf16[256,2560]{1,0:T(8,128)(2,1)}, bf16[256,2560]{1,0:T(8,128)(2,1)}, u32[]{:S(2)}, u32[]{:S(2)}) collective-permute-start(bf16[256,2560]{1,0:T(8,128)(2,1)} %get-tuple-element.42), channel_id=1, source_target_pairs={{0,17},{17,0},{1,16},{16,1},{2,19},{19,2},{3,18},{18,3},{4,21},{21... | collective-permute-start | bytes 3932168 | tf_op jit(solution)/shard_map/ppermute | solution.py:341
  70.8 2.7 %copy-start = (bf16[32,48,512]{2,1,0:T(8,128)(2,1)}, bf16[32,48,512]{2,1,0:T(8,128)(2,1)S(1)}, u32[]{:S(2)}) copy-start(bf16[32,48,512]{2,1,0:T(8,128)(2,1)S(1)} %all-to-all-done.1) | copy-start | bytes 4718596
  70.8 5.3 %copy-start.5 = (bf16[512,1024]{1,0:T(8,128)(2,1)S(1)}, bf16[512,1024]{1,0:T(8,128)(2,1)}, u32[]{:S(2)}) copy-start(bf16[512,1024]{1,0:T(8,128)(2,1)} %k_own.3) | copy-start | bytes 3145732
  73.6 3.6 %collective-permute-start.2 = (f32[8,128]{1,0:T(8,128)S(1)}, f32[8,128]{1,0:T(8,128)S(1)}, u32[]{:S(2)}, u32[]{:S(2)}) collective-permute-start(f32[8,128]{1,0:T(8,128)S(1)} %get-tuple-element.26.rest_1_.own), channel_id=1, source_target_pairs={{0,2},{2,0},{1,3},{3,1},{4,6},{6,4},{5,7},{7,5},{8,10},{10,8},{9,1... | collective-permute-start | bytes 12296 | tf_op jit(solution)/shard_map/ppermute | solution.py:318
  82.9 27.7 %all-to-all-start.2 = ((bf16[32,48,512]{2,1,0:T(8,128)(2,1)}), bf16[32,48,512]{2,1,0:T(8,128)(2,1)S(1)}, u32[]{:S(2)}, u32[]{:S(2)}) async-start(bf16[32,48,512]{2,1,0:T(8,128)(2,1)} %bitcast.8), calls=%async_computation.2 | async-start | bytes 3145728 | tf_op jit(solution)/shard_map/all_to_all | solution.py:303
  88.8 31.4 %collective-permute-start.11 = (bf16[256,2560]{1,0:T(8,128)(2,1)}, bf16[256,2560]{1,0:T(8,128)(2,1)S(1)}, u32[]{:S(2)}, u32[]{:S(2)}) collective-permute-start(bf16[256,2560]{1,0:T(8,128)(2,1)} %get-tuple-element.33), channel_id=1, source_target_pairs={{0,17},{17,0},{1,16},{16,1},{2,19},{19,2},{3,18},{18,3},{4,21},{21... | collective-permute-start | bytes 3932168 | tf_op jit(solution)/shard_map/ppermute | solution.py:342
  112.1 27.2 %all-to-all-start.3 = ((bf16[32,48,512]{2,1,0:T(8,128)(2,1)}), bf16[32,48,512]{2,1,0:T(8,128)(2,1)S(1)}, u32[]{:S(2)}, u32[]{:S(2)}) async-start(bf16[32,48,512]{2,1,0:T(8,128)(2,1)} %shard_map.89), calls=%async_computation.3 | async-start | bytes 3145728 | tf_op jit(solution)/shard_map/all_to_all | solution.py:313
  118.6 29.3 %collective-permute-start.3 = (bf16[512,1024]{1,0:T(8,128)(2,1)}, bf16[512,1024]{1,0:T(8,128)(2,1)}, u32[]{:S(2)}, u32[]{:S(2)}) collective-permute-start(bf16[512,1024]{1,0:T(8,128)(2,1)} %own_far.1), channel_id=1, source_target_pairs={{0,2},{2,0},{1,3},{3,1},{4,6},{6,4},{5,7},{7,5},{8,10},{10,8},{9,1... | collective-permute-start | bytes 3145736 | tf_op jit(solution)/shard_map/ppermute | solution.py:318
  120.2 31.9 %collective-permute-start.12 = (bf16[256,2560]{1,0:T(8,128)(2,1)}, bf16[256,2560]{1,0:T(8,128)(2,1)}, u32[]{:S(2)}, u32[]{:S(2)}) collective-permute-start(bf16[256,2560]{1,0:T(8,128)(2,1)} %collective-permute-done.10.first_a), channel_id=1, source_target_pairs={{0,2},{2,0},{1,3},{3,1},{4,6},{6,4},{5,7},{7,5},{8,10},{10,8},{9,1... | collective-permute-start | bytes 3932168 | tf_op jit(solution)/shard_map/ppermute | solution.py:318
  121.5 33.8 %collective-permute-start.13 = (bf16[256,2560]{1,0:T(8,128)(2,1)S(1)}, bf16[256,2560]{1,0:T(8,128)(2,1)}, u32[]{:S(2)}, u32[]{:S(2)}) collective-permute-start(bf16[256,2560]{1,0:T(8,128)(2,1)S(1)} %collective-permute-done.11.first_b), channel_id=1, source_target_pairs={{0,2},{2,0},{1,3},{3,1},{4,6},{6,4},{5,7},{7,5},{8,10},{10,8},{9,1... | collective-permute-start | bytes 3932168 | tf_op jit(solution)/shard_map/ppermute | solution.py:318
  141.1 22.1 %collective-permute-start.7 = (bf16[256,1024]{1,0:T(8,128)(2,1)S(1)}, bf16[256,1024]{1,0:T(8,128)(2,1)S(1)}, u32[]{:S(2)}, u32[]{:S(2)}) collective-permute-start(bf16[256,1024]{1,0:T(8,128)(2,1)S(1)} %get-tuple-element.32.w2_own), channel_id=1, source_target_pairs={{0,17},{17,0},{1,16},{16,1},{2,19},{19,2},{3,18},{18,3},{4,21},{21... | collective-permute-start | bytes 1572872 | tf_op jit(solution)/shard_map/ppermute | solution.py:395
  142.7 14.8 %collective-permute-start.6 = (bf16[256,1024]{1,0:T(8,128)(2,1)S(1)}, bf16[256,1024]{1,0:T(8,128)(2,1)S(1)}, u32[]{:S(2)}, u32[]{:S(2)}) collective-permute-start(bf16[256,1024]{1,0:T(8,128)(2,1)S(1)} %get-tuple-element.32.w2_own), channel_id=1, source_target_pairs={{0,2},{2,0},{1,3},{3,1},{4,6},{6,4},{5,7},{7,5},{8,10},{10,8},{9,1... | collective-permute-start | bytes 1572872 | tf_op jit(solution)/shard_map/ppermute | solution.py:318
  145.5 12.8 %slice-start = ((s8[10485760]{0:T(1024)(128)(4,1)}), s8[4194304]{0:T(1024)(128)(4,1)S(1)}, s32[]{:S(2)}) async-start(s8[10485760]{0:T(1024)(128)(4,1)} %bitcast.13), calls=%async_computation.4 | async-start | bytes 8388608
  147.9 3.0 %collective-permute-start.4 = (f32[8,128]{1,0:T(8,128)S(1)}, f32[8,128]{1,0:T(8,128)S(1)}, u32[]{:S(2)}, u32[]{:S(2)}) collective-permute-start(f32[8,128]{1,0:T(8,128)S(1)} %get-tuple-element.31.sq_own), channel_id=1, source_target_pairs={{0,2},{2,0},{1,3},{3,1},{4,6},{6,4},{5,7},{7,5},{8,10},{10,8},{9,1... | collective-permute-start | bytes 12296 | tf_op jit(solution)/shard_map/ppermute | solution.py:318
  148.0 10.3 %slice-start.1 = ((s8[10485760]{0:T(1024)(128)(4,1)}), s8[4194304]{0:T(1024)(128)(4,1)S(1)}, s32[]{:S(2)}) async-start(s8[10485760]{0:T(1024)(128)(4,1)} %bitcast.13), calls=%async_computation.5 | async-start | bytes 8388608
  151.3 1.7 collective-permute-start.5
  152.1 11.1 %collective-permute-start.8 = (bf16[256,512]{1,0:T(8,128)(2,1)S(1)}, bf16[256,512]{1,0:T(8,128)(2,1)S(1)}, u32[]{:S(2)}, u32[]{:S(2)}) collective-permute-start(bf16[256,512]{1,0:T(8,128)(2,1)S(1)} %shard_map.93.hq_own), channel_id=1, source_target_pairs={{0,1},{1,0},{2,3},{3,2},{4,5},{5,4},{6,7},{7,6},{8,9},{9,8},{10,11... | collective-permute-start | bytes 786440 | tf_op jit(solution)/shard_map/ppermute | solution.py:413
  153.0 14.2 %collective-permute-start.9 = (bf16[256,512]{1,0:T(8,128)(2,1)S(1)}, bf16[256,512]{1,0:T(8,128)(2,1)S(1)}, u32[]{:S(2)}, u32[]{:S(2)}) collective-permute-start(bf16[256,512]{1,0:T(8,128)(2,1)S(1)} %collective-permute-done.5.hq_got.after), channel_id=1, source_target_pairs={{0,1},{1,0},{2,3},{3,2},{4,5},{5,4},{6,7},{7,6},{8,9},{9,8},{10,11... | collective-permute-start | bytes 786440 | tf_op jit(solution)/shard_map/ppermute | solution.py:413
  155.3 3.1 %slice-start.2 = ((s8[10485760]{0:T(1024)(128)(4,1)}), s8[2097152]{0:T(1024)(128)(4,1)S(1)}, s32[]{:S(2)}) async-start(s8[10485760]{0:T(1024)(128)(4,1)} %bitcast.13), calls=%async_computation.6 | async-start | bytes 4194304
  167.2 2.4 %collective-permute-start.14 = (bf16[256,1024]{1,0:T(8,128)(2,1)S(1)}, bf16[256,1024]{1,0:T(8,128)(2,1)S(1)}, u32[]{:S(2)}, u32[]{:S(2)}) collective-permute-start(bf16[256,1024]{1,0:T(8,128)(2,1)S(1)} %collective-permute-done.7.rest_0_), channel_id=1, source_target_pairs={{0,2},{2,0},{1,3},{3,1},{4,6},{6,4},{5,7},{7,5},{8,10},{10,8},{9,1... | collective-permute-start | bytes 1572872 | tf_op jit(solution)/shard_map/ppermute | solution.py:318

commit v11 on v10

--- a/solution.py
+++ b/solution.py
@@ -222,12 +222,18 @@
         out[i] = rounded
 
 
-def stage_kernel(after, first_a, first_b, second_a, second_b, first, second, sems):
+def stage_kernel(place, after, first_a, first_b, second_a, second_b, w, sems):
     rows = first_a.shape[0]
-    pairs = [(first_a, first.at[0:rows, :]), (first_b, first.at[rows:, :])]
-    pairs += [(second_a, second.at[0:rows, :]), (second_b, second.at[rows:, :])]
-    for copy in fetch(pairs, sems):
-        copy.wait()
+    for c in range(2):
+
+        @pl.when(place[1] == c)
+        def _():
+            parts = (first_a, first_b, second_a, second_b)
+            if c == 1:
+                parts = parts[2:] + parts[:2]
+            pairs = [(x, w.at[k * rows : (k + 1) * rows, :]) for k, x in enumerate(parts)]
+            for copy in fetch(pairs, sems):
+                copy.wait()
 
 
 TILE = 512
@@ -260,16 +266,13 @@
     )(place, o, w_out)
 
 
-def finish_kernel(place, part, hq_a, hq_b, *rest):
-    w2_a, w2_b, w_first, w_second, out, o, held, sems = rest
-    half = o.shape[1] // 2
+def finish_kernel(part, hq_a, hq_b, *rest):
+    w2_a, w2_b, w, out, o, held, sems = rest
     o[...] = (tn(hq_a[...], w2_a[...]) + tn(hq_b[...], w2_b[...])).astype(BF)
-    o_first = o[:, pl.ds(pl.multiple_of(place[1] * half, half), half)]
-    o_second = o[:, pl.ds(pl.multiple_of((1 - place[1]) * half, half), half)]
     copies = []
     for j in range(part.shape[1] // TILE):
         at = slice(j * TILE, (j + 1) * TILE)
-        total = part[:, at] + dot(o_first, w_first[:, at]) + dot(o_second, w_second[:, at])
+        total = part[:, at] + dot(o[...], w[:, at])
         held[j] = total.astype(BF)
         copies.append(pltpu.make_async_copy(held.at[j], out.at[:, at], sems.at[j]))
         copies[-1].start()
@@ -277,13 +280,13 @@
         copy.wait()
 
 
-def finish_product(place, part, hqs, w2s, w_first, w_second):
+def finish_product(part, hqs, w2s, w):
     tokens, n = part.shape
     width = w2s[0].shape[1]
     return pl.pallas_call(
         finish_kernel,
         out_shape=shape((tokens, n)),
-        in_specs=[SMEM] + [VMEM] * 7,
+        in_specs=[VMEM] * 6,
         out_specs=FAR,
         scratch_shapes=[
             buffer((tokens, width)),
@@ -294,7 +297,7 @@
         cost_estimate=pl.CostEstimate(
             flops=2 * tokens * width * (n + width // 2), bytes_accessed=6 << 20, transcendentals=0
         ),
-    )(place, part, *hqs, *w2s, w_first, w_second)
+    )(part, *hqs, *w2s, w)
 
 
 def all_reduced(grads, beside=None):
@@ -415,12 +418,11 @@
         hq_own, hq_got, mats[1], w2_got
     )
     part = partial_product(place, o, w_out)
-    wide = (shape((width // 2, n)),) * 2
-    w_first, w_second = call(stage_kernel, wide, [ANY] * 5, 1 << 16, 1 << 16, [semaphores(4)])(
-        hq_got, *w_parts
-    )
-    crossed, *hqs, _, _ = lax.optimization_barrier((crossed, *hqs, part, w_first))
-    return finish_product(place, part, hqs, (crossed, swap(crossed)), w_first, w_second)
+    w_other = call(
+        stage_kernel, shape((width, n)), [SMEM] + [ANY] * 5, 1 << 16, 1 << 16, [semaphores(4)]
+    )(place, hq_got, *w_parts)
+    crossed, *hqs, _, _ = lax.optimization_barrier((crossed, *hqs, part, w_other))
+    return finish_product(part, hqs, (crossed, swap(crossed)), w_other)
 
 
 def solution(mesh):

time: 175 us -> 175 us (level)
  no operation moved by 1% of the time
where the time goes in v11:
time: 175 us; the launch traced here: 174 us
  waiting for transfers between devices  57.9 us (33%)
  Pallas kernels  40.5 us (23%)
  starting transfers between devices  38.6 us (22%)
  blocking collectives  30.3 us (17%)
  local copies, waits for them, and re-layouts  4.69 us (3%)
    all_to_all x2, waiting for transfers between devices, all_reduced(): gathered = lax.all_to_all(copies, CHIPS, 0, 0, tiled=True)  33 us
    pallas_call x15, Pallas kernels, with_places(): run(*(pltpu.with_memory_space_constraint(x, HELD[id(spec)]) if id(spec) i...  31.4 us
    all_to_all x1, blocking collectives, all_reduced(): arrived = lax.all_to_all(pieces, CHIPS, 0, 0, tiled=True)  30.3 us
    all_to_all x1, waiting for transfers between devices, all_reduced(): arrived = lax.all_to_all(pieces, CHIPS, 0, 0, tiled=True)  19.5 us
    all_to_all x2, starting transfers between devices, all_reduced(): gathered = lax.all_to_all(copies, CHIPS, 0, 0, tiled=True)  12 us
    ppermute x10, starting transfers between devices, swap(): return lax.ppermute(x, 'c', SWAP)  11 us
    all_to_all x1, starting transfers between devices, all_reduced(): arrived = lax.all_to_all(pieces, CHIPS, 0, 0, tiled=True)  5.89 us
    pallas_call x1, Pallas kernels, partial_product(): pl.pallas_call(partial_kernel, out_shape=shape((tokens, n), F32), grid_sp...  4.85 us
  transfers between devices with their start and end apart: 18, of which 6 were waited for; matrix products, arithmetic and copies ran while one was open for 2% of the time, Pallas kernels for 18%

profile of v11, /device:TPU:1, one launch (start us, length us, event | category | flops | bytes accessed | tf_op | source)
XLA Modules:
  0.0 174.1 jit_solution(3093873550212583418)
XLA Ops:
  0.0 1.5 multiply_convert_fusion.targets.u_own
  1.6 1.5 collective-permute-start.1
  3.1 0.1 collective-permute-start
  3.2 3.6 %shard_map.82 = (bf16[512,1024]{1,0:T(8,128)(2,1)S(1)}, bf16[256,1024]{1,0:T(8,128)(2,1)S(1)}, f32[8,128]{1,0:T(8,128)S(1)}) custom-call(s32[1]{0:T(128)} %bitcast.1.core, bf16[1024,512]{1,0:T(8,128)(2,1)} %bitcast.18, bf16[1024,512]{1,0:T(8,128)(2,1)} %bitcast.19, bf16[512,1024]{1,0:T(8,128)(2,1)} %bitcast.20), custom_call_target="tpu_custom_call" | custom-call | flops 2097152 | bytes 5242880 | tf_op jit(solution)/shard_map/pallas_call | solution.py:55
  6.8 1.0 shard_map.83.raw
  7.8 0.0 collective-permute-done.1.u_oth
  7.8 0.0 collective-permute-done.k_oth
  7.8 0.0 copy-done.1
  7.8 0.1 copy-done.3
  7.9 4.6 %shard_map.84 = bf16[2,768,512]{2,1,0:T(8,128)(2,1)S(1)} custom-call(bf16[512,1024]{1,0:T(8,128)(2,1)S(1)} %get-tuple-element.21.w13.w13_far.w_far, bf16[256,1024]{1,0:T(8,128)(2,1)S(1)} %get-tuple-element.22.w2.w2_far.w_far, f32[768,512]{1,0:T(8,128)S(1)} %shard_map.83.raw, bf16[512,1024]{1,0:T(8,128)(2,1)S(1)} %copy-done.4, ...), custom_call_target="tpu_custom_call" | custom-call | flops 2415919104 | bytes 8388608 | tf_op jit(solution)/shard_map/pallas_call | solution.py:55
  12.5 30.3 %all_to_all.20.arrived = bf16[32,48,512]{2,1,0:T(8,128)(2,1)S(1)} all-to-all(bf16[32,48,512]{2,1,0:T(8,128)(2,1)S(1)} %bitcast.17), channel_id=1, replica_groups=mesh['z'=4,'xl'=2,'y'=4,'c'=2,'h'=2] {'z','xl','y'}, dimensions={0} | all-to-all | bytes 3145728 | tf_op jit(solution)/shard_map/all_to_all | solution.py:306
  42.7 0.3 shard_map.85
  43.1 0.0 copy-start.2
  43.1 1.1 copy-done.2
  44.2 5.7 %all-to-all-start.1 = ((bf16[32,48,512]{2,1,0:T(8,128)(2,1)}), bf16[32,48,512]{2,1,0:T(8,128)(2,1)S(1)}, u32[]{:S(2)}, u32[]{:S(2)}) async-start(bf16[32,48,512]{2,1,0:T(8,128)(2,1)} %copy-done.2), calls=%async_computation.1 | async-start | bytes 3145728 | tf_op jit(solution)/shard_map/all_to_all | solution.py:316
  49.9 3.4 %fusion = (bf16[256,2560]{1,0:T(8,128)(2,1)}, bf16[256,2560]{1,0:T(8,128)(2,1)}) fusion(bf16[1024,5120]{1,0:T(8,128)(2,1)} %w_own.1, s32[]{:T(128)S(6)} %select_n.12, s32[]{:T(128)S(6)} %select_n.11, s32[]{:T(128)S(6)} %select_n.10), kind=kLoop, calls=%fused_computation.2 | loop fusion | bytes 5242892 | tf_op jit(solution)/shard_map/dynamic_slice | solution.py:340
  53.3 2.5 %collective-permute-start.10 = (bf16[256,2560]{1,0:T(8,128)(2,1)}, bf16[256,2560]{1,0:T(8,128)(2,1)}, u32[]{:S(2)}, u32[]{:S(2)}) collective-permute-start(bf16[256,2560]{1,0:T(8,128)(2,1)} %get-tuple-element.38), channel_id=1, source_target_pairs={{0,17},{17,0},{1,16},{16,1},{2,19},{19,2},{3,18},{18,3},{4,21},{21... | collective-permute-start | bytes 3932168 | tf_op jit(solution)/shard_map/ppermute | solution.py:344
  55.8 15.0 %all-to-all-done.1 = bf16[32,48,512]{2,1,0:T(8,128)(2,1)S(1)} async-done(((bf16[32,48,512]{2,1,0:T(8,128)(2,1)}), bf16[32,48,512]{2,1,0:T(8,128)(2,1)S(1)}, u32[]{:S(2)}, u32[]{:S(2)}) %all-to-all-start.1) | async-done | bytes 1572896 | tf_op jit(solution)/shard_map/all_to_all | solution.py:316
  70.8 2.7 %shard_map.86 = (bf16[512,1024]{1,0:T(8,128)(2,1)S(1)}, bf16[256,1024]{1,0:T(8,128)(2,1)S(1)}, f32[8,128]{1,0:T(8,128)S(1)}) custom-call(bf16[512,1024]{1,0:T(8,128)(2,1)} %copy-done.1, bf16[256,1024]{1,0:T(8,128)(2,1)} %copy-done.3, bf16[2,768,512]{2,1,0:T(8,128)(2,1)S(1)} %bitcast.10), custom_call_target="tpu_custom_call" | custom-call | flops 4194304 | bytes 5242880 | tf_op jit(solution)/shard_map/pallas_call | solution.py:55
  73.6 2.5 %collective-permute-start.2 = (f32[8,128]{1,0:T(8,128)S(1)}, f32[8,128]{1,0:T(8,128)S(1)}, u32[]{:S(2)}, u32[]{:S(2)}) collective-permute-start(f32[8,128]{1,0:T(8,128)S(1)} %get-tuple-element.24.rest_1_.own), channel_id=1, source_target_pairs={{0,2},{2,0},{1,3},{3,1},{4,6},{6,4},{5,7},{7,5},{8,10},{10,8},{9,1... | collective-permute-start | bytes 12296 | tf_op jit(solution)/shard_map/ppermute | solution.py:321
  76.1 1.0 shard_map.87.raw
  77.1 0.0 collective-permute-done.2.rest_2_.oth
  77.1 5.7 %shard_map.88 = bf16[2,768,512]{2,1,0:T(8,128)(2,1)} custom-call(bf16[512,1024]{1,0:T(8,128)(2,1)S(1)} %get-tuple-element.25.w13, bf16[256,1024]{1,0:T(8,128)(2,1)S(1)} %get-tuple-element.26.w2, f32[768,512]{1,0:T(8,128)S(1)} %shard_map.87.raw, bf16[512,1024]{1,0:T(8,128)(2,1)S(1)} %copy-done.5, bf16[512,1024]{1,0:T(8,128)(2,1)} %collective-permute-done.k_oth, ...), custom_call_target="tpu_custom_call" | custom-call | flops 2415919104 | bytes 8388608 | tf_op jit(solution)/shard_map/pallas_call | solution.py:55
  82.9 5.9 %all-to-all-start.2 = ((bf16[32,48,512]{2,1,0:T(8,128)(2,1)}), bf16[32,48,512]{2,1,0:T(8,128)(2,1)S(1)}, u32[]{:S(2)}, u32[]{:S(2)}) async-start(bf16[32,48,512]{2,1,0:T(8,128)(2,1)} %bitcast.8), calls=%async_computation.2 | async-start | bytes 3145728 | tf_op jit(solution)/shard_map/all_to_all | solution.py:306
  88.8 0.0 collective-permute-done.10.first_a
  88.8 2.6 %collective-permute-start.11 = (bf16[256,2560]{1,0:T(8,128)(2,1)}, bf16[256,2560]{1,0:T(8,128)(2,1)S(1)}, u32[]{:S(2)}, u32[]{:S(2)}) collective-permute-start(bf16[256,2560]{1,0:T(8,128)(2,1)} %get-tuple-element.31), channel_id=1, source_target_pairs={{0,17},{17,0},{1,16},{16,1},{2,19},{19,2},{3,18},{18,3},{4,21},{21... | collective-permute-start | bytes 3932168 | tf_op jit(solution)/shard_map/ppermute | solution.py:345
  91.4 19.5 %all-to-all-done.2.arrived = bf16[32,48,512]{2,1,0:T(8,128)(2,1)S(1)} async-done(((bf16[32,48,512]{2,1,0:T(8,128)(2,1)}), bf16[32,48,512]{2,1,0:T(8,128)(2,1)S(1)}, u32[]{:S(2)}, u32[]{:S(2)}) %all-to-all-start.2) | async-done | bytes 1572896 | tf_op jit(solution)/shard_map/all_to_all | solution.py:306
  110.8 1.5 shard_map.89
  112.3 6.3 %all-to-all-start.3 = ((bf16[32,48,512]{2,1,0:T(8,128)(2,1)}), bf16[32,48,512]{2,1,0:T(8,128)(2,1)S(1)}, u32[]{:S(2)}, u32[]{:S(2)}) async-start(bf16[32,48,512]{2,1,0:T(8,128)(2,1)} %shard_map.89), calls=%async_computation.3 | async-start | bytes 3145728 | tf_op jit(solution)/shard_map/all_to_all | solution.py:316
  118.6 1.3 collective-permute-start.3
  120.0 0.3 collective-permute-done.11.first_b
  120.3 1.2 collective-permute-start.12
  121.5 0.0 collective-permute-start.13
  121.5 18.0 %all-to-all-done.3 = bf16[32,48,512]{2,1,0:T(8,128)(2,1)S(1)} async-done(((bf16[32,48,512]{2,1,0:T(8,128)(2,1)}), bf16[32,48,512]{2,1,0:T(8,128)(2,1)S(1)}, u32[]{:S(2)}, u32[]{:S(2)}) %all-to-all-start.3) | async-done | bytes 1572896 | tf_op jit(solution)/shard_map/all_to_all | solution.py:316
  139.5 1.7 shard_map.90
  141.2 1.6 collective-permute-start.7
  142.8 2.8 %collective-permute-start.6 = (bf16[256,1024]{1,0:T(8,128)(2,1)S(1)}, bf16[256,1024]{1,0:T(8,128)(2,1)S(1)}, u32[]{:S(2)}, u32[]{:S(2)}) collective-permute-start(bf16[256,1024]{1,0:T(8,128)(2,1)S(1)} %get-tuple-element.30.w2_own), channel_id=1, source_target_pairs={{0,2},{2,0},{1,3},{3,1},{4,6},{6,4},{5,7},{7,5},{8,10},{10,8},{9,1... | collective-permute-start | bytes 1572872 | tf_op jit(solution)/shard_map/ppermute | solution.py:321
  145.6 2.3 %shard_map.91 = (bf16[512,1024]{1,0:T(8,128)(2,1)S(1)}, f32[8,128]{1,0:T(8,128)S(1)}) custom-call(bf16[512,1024]{1,0:T(8,128)(2,1)} %copy-done.1, bf16[2,768,512]{2,1,0:T(8,128)(2,1)} %bitcast.12, f32[8,128]{1,0:T(8,128)S(1)} %get-tuple-element.23.rest_0_.norm, f32[8,128]{1,0:T(8,128)S(1)} %get-tuple-element.24.rest_1_.own, ...), custom_call_target="tpu_custom_call" | custom-call | flops 1048576 | bytes 1048576 | tf_op jit(solution)/shard_map/pallas_call | solution.py:55
  147.9 0.0 collective-permute-done.3.oth_far
  147.9 0.1 collective-permute-start.4
  148.0 0.0 slice-start
  148.0 2.9 %shard_map.92.raw = f32[2,512,512]{2,1,0:T(8,128)S(1)} custom-call(bf16[512,1024]{1,0:T(8,128)(2,1)S(1)} %get-tuple-element.28.m13, bf16[512,1024]{1,0:T(8,128)(2,1)} %collective-permute-done.3.oth_far, bf16[512,1024]{1,0:T(8,128)(2,1)} %own_far.1), custom_call_target="tpu_custom_call" | custom-call | flops 1073741824 | bytes 5242880 | tf_op jit(solution)/shard_map/pallas_call | solution.py:55
  150.9 0.0 collective-permute-done.4.sq_oth
  150.9 0.3 shard_map.94
  151.2 0.0 slice-start.1
  151.2 0.6 collective-permute-start.5
  151.8 0.3 shard_map.93.hq_own
  152.1 0.0 collective-permute-done.12.second_a
  152.1 0.8 collective-permute-start.8
  152.9 0.0 collective-permute-done.5.hq_got.after
  153.0 2.2 %collective-permute-start.9 = (bf16[256,512]{1,0:T(8,128)(2,1)S(1)}, bf16[256,512]{1,0:T(8,128)(2,1)S(1)}, u32[]{:S(2)}, u32[]{:S(2)}) collective-permute-start(bf16[256,512]{1,0:T(8,128)(2,1)S(1)} %collective-permute-done.5.hq_got.after), channel_id=1, source_target_pairs={{0,1},{1,0},{2,3},{3,2},{4,5},{5,4},{6,7},{7,6},{8,9},{9,8},{10,11... | collective-permute-start | bytes 786440 | tf_op jit(solution)/shard_map/ppermute | solution.py:416
  155.2 0.1 pad_add_fusion.place
  155.2 0.0 collective-permute-done.13.second_b
  155.2 2.8 %shard_map.97.rest_2_ = bf16[1024,2560]{1,0:T(8,128)(2,1)S(1)} custom-call(s32[2]{0:T(128)S(1)} %pad_add_fusion.place, bf16[256,512]{1,0:T(8,128)(2,1)S(1)} %collective-permute-done.5.hq_got.after, bf16[256,2560]{1,0:T(8,128)(2,1)} %collective-permute-done.10.first_a, bf16[256,2560]{1,0:T(8,128)(2,1)S(1)} %collective-permute-done.11.first_b, ...), custom_call_target="tpu_custom_call" | custom-call | flops 65536 | bytes 65536 | tf_op jit(solution)/shard_map/pallas_call | solution.py:55
  158.0 0.0 collective-permute-done.6.w2_got
  158.0 0.7 shard_map.95.o
  158.8 0.0 slice-done
  158.8 4.8 %shard_map.96.part = f32[512,2560]{1,0:T(8,128)S(1)} custom-call(s32[2]{0:T(128)S(1)} %pad_add_fusion.place, bf16[512,1024]{1,0:T(8,128)(2,1)S(1)} %shard_map.95.o, bf16[1024,5120]{1,0:T(8,128)(2,1)S(1)} %bitcast.14), custom_call_target="tpu_custom_call" | custom-call | flops 1048576 | bytes 65536 | tf_op jit(solution)/shard_map/pallas_call | solution.py:250
  163.7 0.0 collective-permute-done.8.hq_a
  163.7 0.0 collective-permute-done.7.rest_0_
  163.7 3.5 %collective-permute-done.9.hq_b = bf16[256,512]{1,0:T(8,128)(2,1)S(1)} collective-permute-done((bf16[256,512]{1,0:T(8,128)(2,1)S(1)}, bf16[256,512]{1,0:T(8,128)(2,1)S(1)}, u32[]{:S(2)}, u32[]{:S(2)}) %collective-permute-start.9) | collective-permute-done | bytes 262176 | tf_op jit(solution)/shard_map/ppermute | solution.py:416
  167.2 0.8 collective-permute-start.14
  168.0 1.5 collective-permute-done.14.rest_1_
  169.6 4.3 %shard_map.98 = bf16[512,2560]{1,0:T(8,128)(2,1)} custom-call(f32[512,2560]{1,0:T(8,128)S(1)} %shard_map.96.part, bf16[256,512]{1,0:T(8,128)(2,1)S(1)} %collective-permute-done.8.hq_a, bf16[256,512]{1,0:T(8,128)(2,1)S(1)} %collective-permute-done.9.hq_b, bf16[256,1024]{1,0:T(8,128)(2,1)S(1)} %collective-permute-done.7.rest_0_, ...), custom_call_target="tpu_custom_call" | custom-call | flops 3221225472 | bytes 6291456 | tf_op jit(solution)/shard_map/pallas_call | solution.py:286
  (12 shorter events, 0.0 us)
Async XLA Ops:
  0.0 3.1 %copy-start.4 = (bf16[512,1024]{1,0:T(8,128)(2,1)S(1)}, bf16[512,1024]{1,0:T(8,128)(2,1)}, u32[]{:S(2)}) copy-start(bf16[512,1024]{1,0:T(8,128)(2,1)} %k_own.3) | copy-start | bytes 3145732
  1.6 6.2 %collective-permute-start.1 = (bf16[512,1024]{1,0:T(8,128)(2,1)S(1)}, bf16[512,1024]{1,0:T(8,128)(2,1)}, u32[]{:S(2)}, u32[]{:S(2)}) collective-permute-start(bf16[512,1024]{1,0:T(8,128)(2,1)S(1)} %multiply_convert_fusion.targets.u_own), channel_id=1, source_target_pairs={{0,2},{2,0},{1,3},{3,1},{4,6},{6,4},{5,7},{7,5},{8,10},{10,8},{9,1... | collective-permute-start | bytes 3145736 | tf_op jit(solution)/shard_map/ppermute | solution.py:321
  3.1 4.7 %collective-permute-start = (bf16[512,1024]{1,0:T(8,128)(2,1)S(1)}, bf16[512,1024]{1,0:T(8,128)(2,1)}, u32[]{:S(2)}, u32[]{:S(2)}) collective-permute-start(bf16[512,1024]{1,0:T(8,128)(2,1)S(1)} %copy-done.4), channel_id=1, source_target_pairs={{0,2},{2,0},{1,3},{3,1},{4,6},{6,4},{5,7},{7,5},{8,10},{10,8},{9,1... | collective-permute-start | bytes 3145736 | tf_op jit(solution)/shard_map/ppermute | solution.py:321
  6.7 1.1 copy-start.1
  6.8 1.2 copy-start.3
  43.1 1.1 copy-start.2
  44.2 26.6 %all-to-all-start.1 = ((bf16[32,48,512]{2,1,0:T(8,128)(2,1)}), bf16[32,48,512]{2,1,0:T(8,128)(2,1)S(1)}, u32[]{:S(2)}, u32[]{:S(2)}) async-start(bf16[32,48,512]{2,1,0:T(8,128)(2,1)} %copy-done.2), calls=%async_computation.1 | async-start | bytes 3145728 | tf_op jit(solution)/shard_map/all_to_all | solution.py:316
  53.3 35.5 %collective-permute-start.10 = (bf16[256,2560]{1,0:T(8,128)(2,1)}, bf16[256,2560]{1,0:T(8,128)(2,1)}, u32[]{:S(2)}, u32[]{:S(2)}) collective-permute-start(bf16[256,2560]{1,0:T(8,128)(2,1)} %get-tuple-element.38), channel_id=1, source_target_pairs={{0,17},{17,0},{1,16},{16,1},{2,19},{19,2},{3,18},{18,3},{4,21},{21... | collective-permute-start | bytes 3932168 | tf_op jit(solution)/shard_map/ppermute | solution.py:344
  70.8 2.7 %copy-start = (bf16[32,48,512]{2,1,0:T(8,128)(2,1)}, bf16[32,48,512]{2,1,0:T(8,128)(2,1)S(1)}, u32[]{:S(2)}) copy-start(bf16[32,48,512]{2,1,0:T(8,128)(2,1)S(1)} %all-to-all-done.1) | copy-start | bytes 4718596
  70.8 5.3 %copy-start.5 = (bf16[512,1024]{1,0:T(8,128)(2,1)S(1)}, bf16[512,1024]{1,0:T(8,128)(2,1)}, u32[]{:S(2)}) copy-start(bf16[512,1024]{1,0:T(8,128)(2,1)} %k_own.3) | copy-start | bytes 3145732
  73.6 3.6 %collective-permute-start.2 = (f32[8,128]{1,0:T(8,128)S(1)}, f32[8,128]{1,0:T(8,128)S(1)}, u32[]{:S(2)}, u32[]{:S(2)}) collective-permute-start(f32[8,128]{1,0:T(8,128)S(1)} %get-tuple-element.24.rest_1_.own), channel_id=1, source_target_pairs={{0,2},{2,0},{1,3},{3,1},{4,6},{6,4},{5,7},{7,5},{8,10},{10,8},{9,1... | collective-permute-start | bytes 12296 | tf_op jit(solution)/shard_map/ppermute | solution.py:321
  82.9 28.0 %all-to-all-start.2 = ((bf16[32,48,512]{2,1,0:T(8,128)(2,1)}), bf16[32,48,512]{2,1,0:T(8,128)(2,1)S(1)}, u32[]{:S(2)}, u32[]{:S(2)}) async-start(bf16[32,48,512]{2,1,0:T(8,128)(2,1)} %bitcast.8), calls=%async_computation.2 | async-start | bytes 3145728 | tf_op jit(solution)/shard_map/all_to_all | solution.py:306
  88.8 31.5 %collective-permute-start.11 = (bf16[256,2560]{1,0:T(8,128)(2,1)}, bf16[256,2560]{1,0:T(8,128)(2,1)S(1)}, u32[]{:S(2)}, u32[]{:S(2)}) collective-permute-start(bf16[256,2560]{1,0:T(8,128)(2,1)} %get-tuple-element.31), channel_id=1, source_target_pairs={{0,17},{17,0},{1,16},{16,1},{2,19},{19,2},{3,18},{18,3},{4,21},{21... | collective-permute-start | bytes 3932168 | tf_op jit(solution)/shard_map/ppermute | solution.py:345
  112.3 27.1 %all-to-all-start.3 = ((bf16[32,48,512]{2,1,0:T(8,128)(2,1)}), bf16[32,48,512]{2,1,0:T(8,128)(2,1)S(1)}, u32[]{:S(2)}, u32[]{:S(2)}) async-start(bf16[32,48,512]{2,1,0:T(8,128)(2,1)} %shard_map.89), calls=%async_computation.3 | async-start | bytes 3145728 | tf_op jit(solution)/shard_map/all_to_all | solution.py:316
  118.6 29.3 %collective-permute-start.3 = (bf16[512,1024]{1,0:T(8,128)(2,1)}, bf16[512,1024]{1,0:T(8,128)(2,1)}, u32[]{:S(2)}, u32[]{:S(2)}) collective-permute-start(bf16[512,1024]{1,0:T(8,128)(2,1)} %own_far.1), channel_id=1, source_target_pairs={{0,2},{2,0},{1,3},{3,1},{4,6},{6,4},{5,7},{7,5},{8,10},{10,8},{9,1... | collective-permute-start | bytes 3145736 | tf_op jit(solution)/shard_map/ppermute | solution.py:321
  120.3 31.8 %collective-permute-start.12 = (bf16[256,2560]{1,0:T(8,128)(2,1)}, bf16[256,2560]{1,0:T(8,128)(2,1)}, u32[]{:S(2)}, u32[]{:S(2)}) collective-permute-start(bf16[256,2560]{1,0:T(8,128)(2,1)} %collective-permute-done.10.first_a), channel_id=1, source_target_pairs={{0,2},{2,0},{1,3},{3,1},{4,6},{6,4},{5,7},{7,5},{8,10},{10,8},{9,1... | collective-permute-start | bytes 3932168 | tf_op jit(solution)/shard_map/ppermute | solution.py:321
  121.5 33.8 %collective-permute-start.13 = (bf16[256,2560]{1,0:T(8,128)(2,1)S(1)}, bf16[256,2560]{1,0:T(8,128)(2,1)}, u32[]{:S(2)}, u32[]{:S(2)}) collective-permute-start(bf16[256,2560]{1,0:T(8,128)(2,1)S(1)} %collective-permute-done.11.first_b), channel_id=1, source_target_pairs={{0,2},{2,0},{1,3},{3,1},{4,6},{6,4},{5,7},{7,5},{8,10},{10,8},{9,1... | collective-permute-start | bytes 3932168 | tf_op jit(solution)/shard_map/ppermute | solution.py:321
  141.2 22.5 %collective-permute-start.7 = (bf16[256,1024]{1,0:T(8,128)(2,1)S(1)}, bf16[256,1024]{1,0:T(8,128)(2,1)S(1)}, u32[]{:S(2)}, u32[]{:S(2)}) collective-permute-start(bf16[256,1024]{1,0:T(8,128)(2,1)S(1)} %get-tuple-element.30.w2_own), channel_id=1, source_target_pairs={{0,17},{17,0},{1,16},{16,1},{2,19},{19,2},{3,18},{18,3},{4,21},{21... | collective-permute-start | bytes 1572872 | tf_op jit(solution)/shard_map/ppermute | solution.py:398
  142.8 15.2 %collective-permute-start.6 = (bf16[256,1024]{1,0:T(8,128)(2,1)S(1)}, bf16[256,1024]{1,0:T(8,128)(2,1)S(1)}, u32[]{:S(2)}, u32[]{:S(2)}) collective-permute-start(bf16[256,1024]{1,0:T(8,128)(2,1)S(1)} %get-tuple-element.30.w2_own), channel_id=1, source_target_pairs={{0,2},{2,0},{1,3},{3,1},{4,6},{6,4},{5,7},{7,5},{8,10},{10,8},{9,1... | collective-permute-start | bytes 1572872 | tf_op jit(solution)/shard_map/ppermute | solution.py:321
  147.9 3.0 %collective-permute-start.4 = (f32[8,128]{1,0:T(8,128)S(1)}, f32[8,128]{1,0:T(8,128)S(1)}, u32[]{:S(2)}, u32[]{:S(2)}) collective-permute-start(f32[8,128]{1,0:T(8,128)S(1)} %get-tuple-element.29.sq_own), channel_id=1, source_target_pairs={{0,2},{2,0},{1,3},{3,1},{4,6},{6,4},{5,7},{7,5},{8,10},{10,8},{9,1... | collective-permute-start | bytes 12296 | tf_op jit(solution)/shard_map/ppermute | solution.py:321
  148.0 10.8 %slice-start = ((s8[10485760]{0:T(1024)(128)(4,1)}), s8[4194304]{0:T(1024)(128)(4,1)S(1)}, s32[]{:S(2)}) async-start(s8[10485760]{0:T(1024)(128)(4,1)} %bitcast.13), calls=%async_computation.4 | async-start | bytes 8388608
  151.2 7.5 %slice-start.1 = ((s8[10485760]{0:T(1024)(128)(4,1)}), s8[4194304]{0:T(1024)(128)(4,1)S(1)}, s32[]{:S(2)}) async-start(s8[10485760]{0:T(1024)(128)(4,1)} %bitcast.13), calls=%async_computation.5 | async-start | bytes 8388608
  151.2 1.7 collective-permute-start.5
  152.1 11.6 %collective-permute-start.8 = (bf16[256,512]{1,0:T(8,128)(2,1)S(1)}, bf16[256,512]{1,0:T(8,128)(2,1)S(1)}, u32[]{:S(2)}, u32[]{:S(2)}) collective-permute-start(bf16[256,512]{1,0:T(8,128)(2,1)S(1)} %shard_map.93.hq_own), channel_id=1, source_target_pairs={{0,1},{1,0},{2,3},{3,2},{4,5},{5,4},{6,7},{7,6},{8,9},{9,8},{10,11... | collective-permute-start | bytes 786440 | tf_op jit(solution)/shard_map/ppermute | solution.py:416
  153.0 14.2 %collective-permute-start.9 = (bf16[256,512]{1,0:T(8,128)(2,1)S(1)}, bf16[256,512]{1,0:T(8,128)(2,1)S(1)}, u32[]{:S(2)}, u32[]{:S(2)}) collective-permute-start(bf16[256,512]{1,0:T(8,128)(2,1)S(1)} %collective-permute-done.5.hq_got.after), channel_id=1, source_target_pairs={{0,1},{1,0},{2,3},{3,2},{4,5},{5,4},{6,7},{7,6},{8,9},{9,8},{10,11... | collective-permute-start | bytes 786440 | tf_op jit(solution)/shard_map/ppermute | solution.py:416
  155.2 3.5 %slice-start.2 = ((s8[10485760]{0:T(1024)(128)(4,1)}), s8[2097152]{0:T(1024)(128)(4,1)S(1)}, s32[]{:S(2)}) async-start(s8[10485760]{0:T(1024)(128)(4,1)} %bitcast.13), calls=%async_computation.6 | async-start | bytes 4194304
  167.2 2.4 %collective-permute-start.14 = (bf16[256,1024]{1,0:T(8,128)(2,1)S(1)}, bf16[256,1024]{1,0:T(8,128)(2,1)S(1)}, u32[]{:S(2)}, u32[]{:S(2)}) collective-permute-start(bf16[256,1024]{1,0:T(8,128)(2,1)S(1)} %collective-permute-done.7.rest_0_), channel_id=1, source_target_pairs={{0,2},{2,0},{1,3},{3,1},{4,6},{6,4},{5,7},{7,5},{8,10},{10,8},{9,1... | collective-permute-start | bytes 1572872 | tf_op jit(solution)/shard_map/ppermute | solution.py:321

commit v12 on v11

--- a/solution.py
+++ b/solution.py
@@ -263,7 +263,7 @@
         cost_estimate=pl.CostEstimate(
             flops=1 << 20, bytes_accessed=1 << 16, transcendentals=0
         ),
-    )(place, o, w_out)
+    )(place, o, pltpu.with_memory_space_constraint(w_out, pltpu.HBM))
 
 
 def finish_kernel(part, hq_a, hq_b, *rest):

time: 175 us -> 175 us (level)
  waiting for transfers between devices: 57.9 us -> 55.9 us
  transfers between devices with their start and end apart: 18 -> 18, of which waited for: 6 -> 6; matrix products, arithmetic and copies ran while one was open for 2% -> 2% of each run, Pallas kernels for 18% -> 19%
where the time goes in v12:
time: 175 us; the launch traced here: 174 us
  waiting for transfers between devices  55.9 us (32%)
  Pallas kernels  42.1 us (24%)
  starting transfers between devices  39 us (22%)
  blocking collectives  30.3 us (17%)
  local copies, waits for them, and re-layouts  4.68 us (3%)
    all_to_all x2, waiting for transfers between devices, all_reduced(): gathered = lax.all_to_all(copies, CHIPS, 0, 0, tiled=True)  32.9 us
    pallas_call x15, Pallas kernels, with_places(): run(*(pltpu.with_memory_space_constraint(x, HELD[id(spec)]) if id(spec) i...  31.1 us
    all_to_all x1, blocking collectives, all_reduced(): arrived = lax.all_to_all(pieces, CHIPS, 0, 0, tiled=True)  30.3 us
    all_to_all x1, waiting for transfers between devices, all_reduced(): arrived = lax.all_to_all(pieces, CHIPS, 0, 0, tiled=True)  19.2 us
    all_to_all x2, starting transfers between devices, all_reduced(): gathered = lax.all_to_all(copies, CHIPS, 0, 0, tiled=True)  12.1 us
    ppermute x10, starting transfers between devices, swap(): return lax.ppermute(x, 'c', SWAP)  11.1 us
    pallas_call x1, Pallas kernels, partial_product(): pl.pallas_call(partial_kernel, out_shape=shape((tokens, n), F32), grid_sp...  6.59 us
    all_to_all x1, starting transfers between devices, all_reduced(): arrived = lax.all_to_all(pieces, CHIPS, 0, 0, tiled=True)  5.84 us
  transfers between devices with their start and end apart: 18, of which 6 were waited for; matrix products, arithmetic and copies ran while one was open for 2% of the time, Pallas kernels for 19%

profile of v12, /device:TPU:1, one launch (start us, length us, event | category | flops | bytes accessed | tf_op | source)
XLA Modules:
  0.0 174.0 jit_solution(10674983653762855362)
XLA Ops:
  0.0 1.5 multiply_convert_fusion.targets.u_own
  1.6 1.5 collective-permute-start.1
  3.1 0.0 copy-done.4
  3.1 0.1 collective-permute-start
  3.2 3.6 %shard_map.82 = (bf16[512,1024]{1,0:T(8,128)(2,1)S(1)}, bf16[256,1024]{1,0:T(8,128)(2,1)S(1)}, f32[8,128]{1,0:T(8,128)S(1)}) custom-call(s32[1]{0:T(128)} %bitcast.1.core, bf16[1024,512]{1,0:T(8,128)(2,1)} %bitcast.16, bf16[1024,512]{1,0:T(8,128)(2,1)} %bitcast.17, bf16[512,1024]{1,0:T(8,128)(2,1)} %bitcast.18), custom_call_target="tpu_custom_call" | custom-call | flops 2097152 | bytes 5242880 | tf_op jit(solution)/shard_map/pallas_call | solution.py:55
  6.7 0.0 copy-start.1
  6.8 0.0 copy-start.3
  6.8 1.0 shard_map.83.raw
  7.8 0.0 collective-permute-done.1.u_oth
  7.8 0.0 collective-permute-done.k_oth
  7.8 0.0 copy-done.1
  7.8 0.1 copy-done.3
  7.9 4.5 %shard_map.84 = bf16[2,768,512]{2,1,0:T(8,128)(2,1)S(1)} custom-call(bf16[512,1024]{1,0:T(8,128)(2,1)S(1)} %get-tuple-element.21.w13.w13_far.w_far, bf16[256,1024]{1,0:T(8,128)(2,1)S(1)} %get-tuple-element.22.w2.w2_far.w_far, f32[768,512]{1,0:T(8,128)S(1)} %shard_map.83.raw, bf16[512,1024]{1,0:T(8,128)(2,1)S(1)} %copy-done.4, ...), custom_call_target="tpu_custom_call" | custom-call | flops 2415919104 | bytes 8388608 | tf_op jit(solution)/shard_map/pallas_call | solution.py:55
  12.5 30.3 %all_to_all.20.arrived = bf16[32,48,512]{2,1,0:T(8,128)(2,1)S(1)} all-to-all(bf16[32,48,512]{2,1,0:T(8,128)(2,1)S(1)} %bitcast.15), channel_id=1, replica_groups=mesh['z'=4,'xl'=2,'y'=4,'c'=2,'h'=2] {'z','xl','y'}, dimensions={0} | all-to-all | bytes 3145728 | tf_op jit(solution)/shard_map/all_to_all | solution.py:306
  42.8 0.3 shard_map.85
  43.1 0.0 copy-start.2
  43.1 1.1 copy-done.2
  44.2 5.7 %all-to-all-start.1 = ((bf16[32,48,512]{2,1,0:T(8,128)(2,1)}), bf16[32,48,512]{2,1,0:T(8,128)(2,1)S(1)}, u32[]{:S(2)}, u32[]{:S(2)}) async-start(bf16[32,48,512]{2,1,0:T(8,128)(2,1)} %copy-done.2), calls=%async_computation.1 | async-start | bytes 3145728 | tf_op jit(solution)/shard_map/all_to_all | solution.py:316
  49.9 3.4 %fusion = (bf16[256,2560]{1,0:T(8,128)(2,1)}, bf16[256,2560]{1,0:T(8,128)(2,1)}) fusion(bf16[1024,5120]{1,0:T(8,128)(2,1)} %w_own.1, s32[]{:T(128)S(6)} %select_n.12, s32[]{:T(128)S(6)} %select_n.11, s32[]{:T(128)S(6)} %select_n.10), kind=kLoop, calls=%fused_computation.2 | loop fusion | bytes 5242892 | tf_op jit(solution)/shard_map/dynamic_slice | solution.py:340
  53.3 2.5 %collective-permute-start.10 = (bf16[256,2560]{1,0:T(8,128)(2,1)}, bf16[256,2560]{1,0:T(8,128)(2,1)}, u32[]{:S(2)}, u32[]{:S(2)}) collective-permute-start(bf16[256,2560]{1,0:T(8,128)(2,1)} %get-tuple-element.38), channel_id=1, source_target_pairs={{0,17},{17,0},{1,16},{16,1},{2,19},{19,2},{3,18},{18,3},{4,21},{21... | collective-permute-start | bytes 3932168 | tf_op jit(solution)/shard_map/ppermute | solution.py:344
  55.8 15.0 %all-to-all-done.1 = bf16[32,48,512]{2,1,0:T(8,128)(2,1)S(1)} async-done(((bf16[32,48,512]{2,1,0:T(8,128)(2,1)}), bf16[32,48,512]{2,1,0:T(8,128)(2,1)S(1)}, u32[]{:S(2)}, u32[]{:S(2)}) %all-to-all-start.1) | async-done | bytes 1572896 | tf_op jit(solution)/shard_map/all_to_all | solution.py:316
  70.8 2.7 %shard_map.86 = (bf16[512,1024]{1,0:T(8,128)(2,1)S(1)}, bf16[256,1024]{1,0:T(8,128)(2,1)S(1)}, f32[8,128]{1,0:T(8,128)S(1)}) custom-call(bf16[512,1024]{1,0:T(8,128)(2,1)} %copy-done.1, bf16[256,1024]{1,0:T(8,128)(2,1)} %copy-done.3, bf16[2,768,512]{2,1,0:T(8,128)(2,1)S(1)} %bitcast.10), custom_call_target="tpu_custom_call" | custom-call | flops 4194304 | bytes 5242880 | tf_op jit(solution)/shard_map/pallas_call | solution.py:55
  73.6 2.5 %collective-permute-start.2 = (f32[8,128]{1,0:T(8,128)S(1)}, f32[8,128]{1,0:T(8,128)S(1)}, u32[]{:S(2)}, u32[]{:S(2)}) collective-permute-start(f32[8,128]{1,0:T(8,128)S(1)} %get-tuple-element.24.rest_1_.own), channel_id=1, source_target_pairs={{0,2},{2,0},{1,3},{3,1},{4,6},{6,4},{5,7},{7,5},{8,10},{10,8},{9,1... | collective-permute-start | bytes 12296 | tf_op jit(solution)/shard_map/ppermute | solution.py:321
  76.1 1.0 shard_map.87.raw
  77.1 0.0 collective-permute-done.2.rest_2_.oth
  77.2 5.8 %shard_map.88 = bf16[2,768,512]{2,1,0:T(8,128)(2,1)} custom-call(bf16[512,1024]{1,0:T(8,128)(2,1)S(1)} %get-tuple-element.25.w13, bf16[256,1024]{1,0:T(8,128)(2,1)S(1)} %get-tuple-element.26.w2, f32[768,512]{1,0:T(8,128)S(1)} %shard_map.87.raw, bf16[512,1024]{1,0:T(8,128)(2,1)S(1)} %copy-done.5, bf16[512,1024]{1,0:T(8,128)(2,1)} %collective-permute-done.k_oth, ...), custom_call_target="tpu_custom_call" | custom-call | flops 2415919104 | bytes 8388608 | tf_op jit(solution)/shard_map/pallas_call | solution.py:55
  82.9 5.8 %all-to-all-start.2 = ((bf16[32,48,512]{2,1,0:T(8,128)(2,1)}), bf16[32,48,512]{2,1,0:T(8,128)(2,1)S(1)}, u32[]{:S(2)}, u32[]{:S(2)}) async-start(bf16[32,48,512]{2,1,0:T(8,128)(2,1)} %bitcast.8), calls=%async_computation.2 | async-start | bytes 3145728 | tf_op jit(solution)/shard_map/all_to_all | solution.py:306
  88.8 0.0 collective-permute-done.10.first_a
  88.8 2.6 %collective-permute-start.11 = (bf16[256,2560]{1,0:T(8,128)(2,1)}, bf16[256,2560]{1,0:T(8,128)(2,1)S(1)}, u32[]{:S(2)}, u32[]{:S(2)}) collective-permute-start(bf16[256,2560]{1,0:T(8,128)(2,1)} %get-tuple-element.31), channel_id=1, source_target_pairs={{0,17},{17,0},{1,16},{16,1},{2,19},{19,2},{3,18},{18,3},{4,21},{21... | collective-permute-start | bytes 3932168 | tf_op jit(solution)/shard_map/ppermute | solution.py:345
  91.4 19.2 %all-to-all-done.2.arrived = bf16[32,48,512]{2,1,0:T(8,128)(2,1)S(1)} async-done(((bf16[32,48,512]{2,1,0:T(8,128)(2,1)}), bf16[32,48,512]{2,1,0:T(8,128)(2,1)S(1)}, u32[]{:S(2)}, u32[]{:S(2)}) %all-to-all-start.2) | async-done | bytes 1572896 | tf_op jit(solution)/shard_map/all_to_all | solution.py:306
  110.6 1.5 shard_map.89
  112.1 6.4 %all-to-all-start.3 = ((bf16[32,48,512]{2,1,0:T(8,128)(2,1)}), bf16[32,48,512]{2,1,0:T(8,128)(2,1)S(1)}, u32[]{:S(2)}, u32[]{:S(2)}) async-start(bf16[32,48,512]{2,1,0:T(8,128)(2,1)} %shard_map.89), calls=%async_computation.3 | async-start | bytes 3145728 | tf_op jit(solution)/shard_map/all_to_all | solution.py:316
  118.6 1.4 collective-permute-start.3
  120.0 0.2 collective-permute-done.11.first_b
  120.2 1.3 collective-permute-start.12
  121.5 0.0 collective-permute-start.13
  121.5 17.9 %all-to-all-done.3 = bf16[32,48,512]{2,1,0:T(8,128)(2,1)S(1)} async-done(((bf16[32,48,512]{2,1,0:T(8,128)(2,1)}), bf16[32,48,512]{2,1,0:T(8,128)(2,1)S(1)}, u32[]{:S(2)}, u32[]{:S(2)}) %all-to-all-start.3) | async-done | bytes 1572896 | tf_op jit(solution)/shard_map/all_to_all | solution.py:316
  139.3 1.7 shard_map.90
  141.1 1.8 %collective-permute-start.7 = (bf16[256,1024]{1,0:T(8,128)(2,1)S(1)}, bf16[256,1024]{1,0:T(8,128)(2,1)S(1)}, u32[]{:S(2)}, u32[]{:S(2)}) collective-permute-start(bf16[256,1024]{1,0:T(8,128)(2,1)S(1)} %get-tuple-element.30.w2_own), channel_id=1, source_target_pairs={{0,17},{17,0},{1,16},{16,1},{2,19},{19,2},{3,18},{18,3},{4,21},{21... | collective-permute-start | bytes 1572872 | tf_op jit(solution)/shard_map/ppermute | solution.py:398
  142.8 2.8 %collective-permute-start.6 = (bf16[256,1024]{1,0:T(8,128)(2,1)S(1)}, bf16[256,1024]{1,0:T(8,128)(2,1)S(1)}, u32[]{:S(2)}, u32[]{:S(2)}) collective-permute-start(bf16[256,1024]{1,0:T(8,128)(2,1)S(1)} %get-tuple-element.30.w2_own), channel_id=1, source_target_pairs={{0,2},{2,0},{1,3},{3,1},{4,6},{6,4},{5,7},{7,5},{8,10},{10,8},{9,1... | collective-permute-start | bytes 1572872 | tf_op jit(solution)/shard_map/ppermute | solution.py:321
  145.7 2.3 %shard_map.91 = (bf16[512,1024]{1,0:T(8,128)(2,1)S(1)}, f32[8,128]{1,0:T(8,128)S(1)}) custom-call(bf16[512,1024]{1,0:T(8,128)(2,1)} %copy-done.1, bf16[2,768,512]{2,1,0:T(8,128)(2,1)} %bitcast.12, f32[8,128]{1,0:T(8,128)S(1)} %get-tuple-element.23.rest_0_.norm, f32[8,128]{1,0:T(8,128)S(1)} %get-tuple-element.24.rest_1_.own, ...), custom_call_target="tpu_custom_call" | custom-call | flops 1048576 | bytes 1048576 | tf_op jit(solution)/shard_map/pallas_call | solution.py:55
  147.9 0.0 collective-permute-done.3.oth_far
  147.9 0.1 collective-permute-start.4
  148.0 2.7 %shard_map.92.raw = f32[2,512,512]{2,1,0:T(8,128)S(1)} custom-call(bf16[512,1024]{1,0:T(8,128)(2,1)S(1)} %get-tuple-element.28.m13, bf16[512,1024]{1,0:T(8,128)(2,1)} %collective-permute-done.3.oth_far, bf16[512,1024]{1,0:T(8,128)(2,1)} %own_far.1), custom_call_target="tpu_custom_call" | custom-call | flops 1073741824 | bytes 5242880 | tf_op jit(solution)/shard_map/pallas_call | solution.py:55
  150.8 0.0 collective-permute-done.4.sq_oth
  150.8 0.3 shard_map.94
  151.1 0.6 collective-permute-start.5
  151.7 0.3 shard_map.93.hq_own
  152.0 0.0 collective-permute-done.12.second_a
  152.0 0.8 collective-permute-start.8
  152.8 0.0 collective-permute-done.5.hq_got.after
  152.8 2.2 %collective-permute-start.9 = (bf16[256,512]{1,0:T(8,128)(2,1)S(1)}, bf16[256,512]{1,0:T(8,128)(2,1)S(1)}, u32[]{:S(2)}, u32[]{:S(2)}) collective-permute-start(bf16[256,512]{1,0:T(8,128)(2,1)S(1)} %collective-permute-done.5.hq_got.after), channel_id=1, source_target_pairs={{0,1},{1,0},{2,3},{3,2},{4,5},{5,4},{6,7},{7,6},{8,9},{9,8},{10,11... | collective-permute-start | bytes 786440 | tf_op jit(solution)/shard_map/ppermute | solution.py:416
  155.0 0.1 pad_add_fusion.place
  155.1 0.0 collective-permute-done.13.second_b
  155.1 2.7 %shard_map.97.rest_2_ = bf16[1024,2560]{1,0:T(8,128)(2,1)S(1)} custom-call(s32[2]{0:T(128)S(1)} %pad_add_fusion.place, bf16[256,512]{1,0:T(8,128)(2,1)S(1)} %collective-permute-done.5.hq_got.after, bf16[256,2560]{1,0:T(8,128)(2,1)} %collective-permute-done.10.first_a, bf16[256,2560]{1,0:T(8,128)(2,1)S(1)} %collective-permute-done.11.first_b, ...), custom_call_target="tpu_custom_call" | custom-call | flops 65536 | bytes 65536 | tf_op jit(solution)/shard_map/pallas_call | solution.py:55
  157.8 0.0 collective-permute-done.6.w2_got
  157.8 0.7 shard_map.95.o
  158.5 6.6 %shard_map.96.part = f32[512,2560]{1,0:T(8,128)S(1)} custom-call(s32[2]{0:T(128)S(1)} %pad_add_fusion.place, bf16[512,1024]{1,0:T(8,128)(2,1)S(1)} %shard_map.95.o, bf16[1024,5120]{1,0:T(8,128)(2,1)} %w_own.1), custom_call_target="tpu_custom_call" | custom-call | flops 1048576 | bytes 65536 | tf_op jit(solution)/shard_map/pallas_call | solution.py:250
  165.1 0.0 collective-permute-done.8.hq_a
  165.2 0.0 collective-permute-done.7.rest_0_
  165.2 1.9 %collective-permute-done.9.hq_b = bf16[256,512]{1,0:T(8,128)(2,1)S(1)} collective-permute-done((bf16[256,512]{1,0:T(8,128)(2,1)S(1)}, bf16[256,512]{1,0:T(8,128)(2,1)S(1)}, u32[]{:S(2)}, u32[]{:S(2)}) %collective-permute-start.9) | collective-permute-done | bytes 262176 | tf_op jit(solution)/shard_map/ppermute | solution.py:416
  167.1 0.8 collective-permute-start.14
  167.9 1.5 collective-permute-done.14.rest_1_
  169.5 4.3 %shard_map.98 = bf16[512,2560]{1,0:T(8,128)(2,1)} custom-call(f32[512,2560]{1,0:T(8,128)S(1)} %shard_map.96.part, bf16[256,512]{1,0:T(8,128)(2,1)S(1)} %collective-permute-done.8.hq_a, bf16[256,512]{1,0:T(8,128)(2,1)S(1)} %collective-permute-done.9.hq_b, bf16[256,1024]{1,0:T(8,128)(2,1)S(1)} %collective-permute-done.7.rest_0_, ...), custom_call_target="tpu_custom_call" | custom-call | flops 3221225472 | bytes 6291456 | tf_op jit(solution)/shard_map/pallas_call | solution.py:286
  (5 shorter events, 0.0 us)
Async XLA Ops:
  0.0 3.1 %copy-start.4 = (bf16[512,1024]{1,0:T(8,128)(2,1)S(1)}, bf16[512,1024]{1,0:T(8,128)(2,1)}, u32[]{:S(2)}) copy-start(bf16[512,1024]{1,0:T(8,128)(2,1)} %k_own.3) | copy-start | bytes 3145732
  1.6 6.2 %collective-permute-start.1 = (bf16[512,1024]{1,0:T(8,128)(2,1)S(1)}, bf16[512,1024]{1,0:T(8,128)(2,1)}, u32[]{:S(2)}, u32[]{:S(2)}) collective-permute-start(bf16[512,1024]{1,0:T(8,128)(2,1)S(1)} %multiply_convert_fusion.targets.u_own), channel_id=1, source_target_pairs={{0,2},{2,0},{1,3},{3,1},{4,6},{6,4},{5,7},{7,5},{8,10},{10,8},{9,1... | collective-permute-start | bytes 3145736 | tf_op jit(solution)/shard_map/ppermute | solution.py:321
  3.1 4.7 %collective-permute-start = (bf16[512,1024]{1,0:T(8,128)(2,1)S(1)}, bf16[512,1024]{1,0:T(8,128)(2,1)}, u32[]{:S(2)}, u32[]{:S(2)}) collective-permute-start(bf16[512,1024]{1,0:T(8,128)(2,1)S(1)} %copy-done.4), channel_id=1, source_target_pairs={{0,2},{2,0},{1,3},{3,1},{4,6},{6,4},{5,7},{7,5},{8,10},{10,8},{9,1... | collective-permute-start | bytes 3145736 | tf_op jit(solution)/shard_map/ppermute | solution.py:321
  6.7 1.1 copy-start.1
  6.8 1.2 copy-start.3
  43.1 1.1 copy-start.2
  44.2 26.6 %all-to-all-start.1 = ((bf16[32,48,512]{2,1,0:T(8,128)(2,1)}), bf16[32,48,512]{2,1,0:T(8,128)(2,1)S(1)}, u32[]{:S(2)}, u32[]{:S(2)}) async-start(bf16[32,48,512]{2,1,0:T(8,128)(2,1)} %copy-done.2), calls=%async_computation.1 | async-start | bytes 3145728 | tf_op jit(solution)/shard_map/all_to_all | solution.py:316
  53.3 35.4 %collective-permute-start.10 = (bf16[256,2560]{1,0:T(8,128)(2,1)}, bf16[256,2560]{1,0:T(8,128)(2,1)}, u32[]{:S(2)}, u32[]{:S(2)}) collective-permute-start(bf16[256,2560]{1,0:T(8,128)(2,1)} %get-tuple-element.38), channel_id=1, source_target_pairs={{0,17},{17,0},{1,16},{16,1},{2,19},{19,2},{3,18},{18,3},{4,21},{21... | collective-permute-start | bytes 3932168 | tf_op jit(solution)/shard_map/ppermute | solution.py:344
  70.8 2.7 %copy-start = (bf16[32,48,512]{2,1,0:T(8,128)(2,1)}, bf16[32,48,512]{2,1,0:T(8,128)(2,1)S(1)}, u32[]{:S(2)}) copy-start(bf16[32,48,512]{2,1,0:T(8,128)(2,1)S(1)} %all-to-all-done.1) | copy-start | bytes 4718596
  70.8 5.3 %copy-start.5 = (bf16[512,1024]{1,0:T(8,128)(2,1)S(1)}, bf16[512,1024]{1,0:T(8,128)(2,1)}, u32[]{:S(2)}) copy-start(bf16[512,1024]{1,0:T(8,128)(2,1)} %k_own.3) | copy-start | bytes 3145732
  73.6 3.6 %collective-permute-start.2 = (f32[8,128]{1,0:T(8,128)S(1)}, f32[8,128]{1,0:T(8,128)S(1)}, u32[]{:S(2)}, u32[]{:S(2)}) collective-permute-start(f32[8,128]{1,0:T(8,128)S(1)} %get-tuple-element.24.rest_1_.own), channel_id=1, source_target_pairs={{0,2},{2,0},{1,3},{3,1},{4,6},{6,4},{5,7},{7,5},{8,10},{10,8},{9,1... | collective-permute-start | bytes 12296 | tf_op jit(solution)/shard_map/ppermute | solution.py:321
  82.9 27.7 %all-to-all-start.2 = ((bf16[32,48,512]{2,1,0:T(8,128)(2,1)}), bf16[32,48,512]{2,1,0:T(8,128)(2,1)S(1)}, u32[]{:S(2)}, u32[]{:S(2)}) async-start(bf16[32,48,512]{2,1,0:T(8,128)(2,1)} %bitcast.8), calls=%async_computation.2 | async-start | bytes 3145728 | tf_op jit(solution)/shard_map/all_to_all | solution.py:306
  88.8 31.4 %collective-permute-start.11 = (bf16[256,2560]{1,0:T(8,128)(2,1)}, bf16[256,2560]{1,0:T(8,128)(2,1)S(1)}, u32[]{:S(2)}, u32[]{:S(2)}) collective-permute-start(bf16[256,2560]{1,0:T(8,128)(2,1)} %get-tuple-element.31), channel_id=1, source_target_pairs={{0,17},{17,0},{1,16},{16,1},{2,19},{19,2},{3,18},{18,3},{4,21},{21... | collective-permute-start | bytes 3932168 | tf_op jit(solution)/shard_map/ppermute | solution.py:345
  112.1 27.2 %all-to-all-start.3 = ((bf16[32,48,512]{2,1,0:T(8,128)(2,1)}), bf16[32,48,512]{2,1,0:T(8,128)(2,1)S(1)}, u32[]{:S(2)}, u32[]{:S(2)}) async-start(bf16[32,48,512]{2,1,0:T(8,128)(2,1)} %shard_map.89), calls=%async_computation.3 | async-start | bytes 3145728 | tf_op jit(solution)/shard_map/all_to_all | solution.py:316
  118.6 29.4 %collective-permute-start.3 = (bf16[512,1024]{1,0:T(8,128)(2,1)}, bf16[512,1024]{1,0:T(8,128)(2,1)}, u32[]{:S(2)}, u32[]{:S(2)}) collective-permute-start(bf16[512,1024]{1,0:T(8,128)(2,1)} %own_far.1), channel_id=1, source_target_pairs={{0,2},{2,0},{1,3},{3,1},{4,6},{6,4},{5,7},{7,5},{8,10},{10,8},{9,1... | collective-permute-start | bytes 3145736 | tf_op jit(solution)/shard_map/ppermute | solution.py:321
  120.2 31.8 %collective-permute-start.12 = (bf16[256,2560]{1,0:T(8,128)(2,1)}, bf16[256,2560]{1,0:T(8,128)(2,1)}, u32[]{:S(2)}, u32[]{:S(2)}) collective-permute-start(bf16[256,2560]{1,0:T(8,128)(2,1)} %collective-permute-done.10.first_a), channel_id=1, source_target_pairs={{0,2},{2,0},{1,3},{3,1},{4,6},{6,4},{5,7},{7,5},{8,10},{10,8},{9,1... | collective-permute-start | bytes 3932168 | tf_op jit(solution)/shard_map/ppermute | solution.py:321
  121.5 33.6 %collective-permute-start.13 = (bf16[256,2560]{1,0:T(8,128)(2,1)S(1)}, bf16[256,2560]{1,0:T(8,128)(2,1)}, u32[]{:S(2)}, u32[]{:S(2)}) collective-permute-start(bf16[256,2560]{1,0:T(8,128)(2,1)S(1)} %collective-permute-done.11.first_b), channel_id=1, source_target_pairs={{0,2},{2,0},{1,3},{3,1},{4,6},{6,4},{5,7},{7,5},{8,10},{10,8},{9,1... | collective-permute-start | bytes 3932168 | tf_op jit(solution)/shard_map/ppermute | solution.py:321
  141.1 24.1 %collective-permute-start.7 = (bf16[256,1024]{1,0:T(8,128)(2,1)S(1)}, bf16[256,1024]{1,0:T(8,128)(2,1)S(1)}, u32[]{:S(2)}, u32[]{:S(2)}) collective-permute-start(bf16[256,1024]{1,0:T(8,128)(2,1)S(1)} %get-tuple-element.30.w2_own), channel_id=1, source_target_pairs={{0,17},{17,0},{1,16},{16,1},{2,19},{19,2},{3,18},{18,3},{4,21},{21... | collective-permute-start | bytes 1572872 | tf_op jit(solution)/shard_map/ppermute | solution.py:398
  142.8 15.0 %collective-permute-start.6 = (bf16[256,1024]{1,0:T(8,128)(2,1)S(1)}, bf16[256,1024]{1,0:T(8,128)(2,1)S(1)}, u32[]{:S(2)}, u32[]{:S(2)}) collective-permute-start(bf16[256,1024]{1,0:T(8,128)(2,1)S(1)} %get-tuple-element.30.w2_own), channel_id=1, source_target_pairs={{0,2},{2,0},{1,3},{3,1},{4,6},{6,4},{5,7},{7,5},{8,10},{10,8},{9,1... | collective-permute-start | bytes 1572872 | tf_op jit(solution)/shard_map/ppermute | solution.py:321
  147.9 2.8 %collective-permute-start.4 = (f32[8,128]{1,0:T(8,128)S(1)}, f32[8,128]{1,0:T(8,128)S(1)}, u32[]{:S(2)}, u32[]{:S(2)}) collective-permute-start(f32[8,128]{1,0:T(8,128)S(1)} %get-tuple-element.29.sq_own), channel_id=1, source_target_pairs={{0,2},{2,0},{1,3},{3,1},{4,6},{6,4},{5,7},{7,5},{8,10},{10,8},{9,1... | collective-permute-start | bytes 12296 | tf_op jit(solution)/shard_map/ppermute | solution.py:321
  151.1 1.7 collective-permute-start.5
  152.0 13.2 %collective-permute-start.8 = (bf16[256,512]{1,0:T(8,128)(2,1)S(1)}, bf16[256,512]{1,0:T(8,128)(2,1)S(1)}, u32[]{:S(2)}, u32[]{:S(2)}) collective-permute-start(bf16[256,512]{1,0:T(8,128)(2,1)S(1)} %shard_map.93.hq_own), channel_id=1, source_target_pairs={{0,1},{1,0},{2,3},{3,2},{4,5},{5,4},{6,7},{7,6},{8,9},{9,8},{10,11... | collective-permute-start | bytes 786440 | tf_op jit(solution)/shard_map/ppermute | solution.py:416
  152.8 14.3 %collective-permute-start.9 = (bf16[256,512]{1,0:T(8,128)(2,1)S(1)}, bf16[256,512]{1,0:T(8,128)(2,1)S(1)}, u32[]{:S(2)}, u32[]{:S(2)}) collective-permute-start(bf16[256,512]{1,0:T(8,128)(2,1)S(1)} %collective-permute-done.5.hq_got.after), channel_id=1, source_target_pairs={{0,1},{1,0},{2,3},{3,2},{4,5},{5,4},{6,7},{7,6},{8,9},{9,8},{10,11... | collective-permute-start | bytes 786440 | tf_op jit(solution)/shard_map/ppermute | solution.py:416
  167.1 2.4 %collective-permute-start.14 = (bf16[256,1024]{1,0:T(8,128)(2,1)S(1)}, bf16[256,1024]{1,0:T(8,128)(2,1)S(1)}, u32[]{:S(2)}, u32[]{:S(2)}) collective-permute-start(bf16[256,1024]{1,0:T(8,128)(2,1)S(1)} %collective-permute-done.7.rest_0_), channel_id=1, source_target_pairs={{0,2},{2,0},{1,3},{3,1},{4,6},{6,4},{5,7},{7,5},{8,10},{10,8},{9,1... | collective-permute-start | bytes 1572872 | tf_op jit(solution)/shard_map/ppermute | solution.py:321

commit v13 on v12

--- a/solution.py
+++ b/solution.py
@@ -84,18 +84,21 @@
 def prepare_kernel(core, up_far, gate_far, down_far, w13, w2, norm, up, gate, down, sems):
     copies = fetch(((up_far, up), (gate_far, gate), (down_far, down)), sems)
     half = w2.shape[0]
+    norm[3:8, :] = jnp.zeros((5, 128), F32)
     for i, w in enumerate((up, gate, down)):
         copies[i].wait()
+        for c in range(2):
+            at = slice(c * half, (c + 1) * half)
+
+            @pl.when(core[0] == c)
+            def _():
+                if i < 2:
+                    w13[i * half : (i + 1) * half, :] = w[:, at].T
+                else:
+                    w2[...] = w[at, :]
+
         full = w[...].astype(F32)
         norm[i : i + 1, :] = jnp.full((1, 128), jnp.sum(full * full), F32)
-    norm[3:8, :] = jnp.zeros((5, 128), F32)
-    for c in range(2):
-
-        @pl.when(core[0] == c)
-        def _():
-            w13[0:half, :] = up[:, c * half : (c + 1) * half].T
-            w13[half:, :] = gate[:, c * half : (c + 1) * half].T
-            w2[...] = down[c * half : (c + 1) * half, :]
 
 
 def factor(i, norm, own, oth):

time: 175 us -> 175 us (level)
  no operation moved by 1% of the time
where the time goes in v13:
time: 175 us; the launch traced here: 174 us
  waiting for transfers between devices  55.9 us (32%)
  Pallas kernels  42.2 us (24%)
  starting transfers between devices  39 us (22%)
  blocking collectives  30.2 us (17%)
  local copies, waits for them, and re-layouts  4.68 us (3%)
    all_to_all x2, waiting for transfers between devices, all_reduced(): gathered = lax.all_to_all(copies, CHIPS, 0, 0, tiled=True)  32.9 us
    pallas_call x15, Pallas kernels, with_places(): run(*(pltpu.with_memory_space_constraint(x, HELD[id(spec)]) if id(spec) i...  31.2 us
    all_to_all x1, blocking collectives, all_reduced(): arrived = lax.all_to_all(pieces, CHIPS, 0, 0, tiled=True)  30.2 us
    all_to_all x1, waiting for transfers between devices, all_reduced(): arrived = lax.all_to_all(pieces, CHIPS, 0, 0, tiled=True)  19.3 us
    all_to_all x2, starting transfers between devices, all_reduced(): gathered = lax.all_to_all(copies, CHIPS, 0, 0, tiled=True)  12.2 us
    ppermute x10, starting transfers between devices, swap(): return lax.ppermute(x, 'c', SWAP)  11.2 us
    pallas_call x1, Pallas kernels, partial_product(): pl.pallas_call(partial_kernel, out_shape=shape((tokens, n), F32), grid_sp...  6.59 us
    all_to_all x1, starting transfers between devices, all_reduced(): arrived = lax.all_to_all(pieces, CHIPS, 0, 0, tiled=True)  5.83 us
  transfers between devices with their start and end apart: 18, of which 6 were waited for; matrix products, arithmetic and copies ran while one was open for 2% of the time, Pallas kernels for 19%

profile of v13, /device:TPU:1, one launch (start us, length us, event | category | flops | bytes accessed | tf_op | source)
XLA Modules:
  0.0 174.0 jit_solution(12524082586858541287)
XLA Ops:
  0.0 1.5 multiply_convert_fusion.targets.u_own
  1.6 1.5 collective-permute-start.1
  3.1 0.1 collective-permute-start
  3.2 3.7 %shard_map.82 = (bf16[512,1024]{1,0:T(8,128)(2,1)S(1)}, bf16[256,1024]{1,0:T(8,128)(2,1)S(1)}, f32[8,128]{1,0:T(8,128)S(1)}) custom-call(s32[1]{0:T(128)} %bitcast.1.core, bf16[1024,512]{1,0:T(8,128)(2,1)} %bitcast.16, bf16[1024,512]{1,0:T(8,128)(2,1)} %bitcast.17, bf16[512,1024]{1,0:T(8,128)(2,1)} %bitcast.18), custom_call_target="tpu_custom_call" | custom-call | flops 2097152 | bytes 5242880 | tf_op jit(solution)/shard_map/pallas_call | solution.py:55
  6.8 0.0 copy-start.1
  6.9 0.0 copy-start.3
  6.9 1.0 shard_map.83.raw
  7.9 0.0 collective-permute-done.1.u_oth
  7.9 0.0 collective-permute-done.k_oth
  7.9 0.0 copy-done.1
  7.9 0.1 copy-done.3
  8.0 4.6 %shard_map.84 = bf16[2,768,512]{2,1,0:T(8,128)(2,1)S(1)} custom-call(bf16[512,1024]{1,0:T(8,128)(2,1)S(1)} %get-tuple-element.21.w13.w13_far.w_far, bf16[256,1024]{1,0:T(8,128)(2,1)S(1)} %get-tuple-element.22.w2.w2_far.w_far, f32[768,512]{1,0:T(8,128)S(1)} %shard_map.83.raw, bf16[512,1024]{1,0:T(8,128)(2,1)S(1)} %copy-done.4, ...), custom_call_target="tpu_custom_call" | custom-call | flops 2415919104 | bytes 8388608 | tf_op jit(solution)/shard_map/pallas_call | solution.py:55
  12.6 30.2 %all_to_all.20.arrived = bf16[32,48,512]{2,1,0:T(8,128)(2,1)S(1)} all-to-all(bf16[32,48,512]{2,1,0:T(8,128)(2,1)S(1)} %bitcast.15), channel_id=1, replica_groups=mesh['z'=4,'xl'=2,'y'=4,'c'=2,'h'=2] {'z','xl','y'}, dimensions={0} | all-to-all | bytes 3145728 | tf_op jit(solution)/shard_map/all_to_all | solution.py:309
  42.8 0.3 shard_map.85
  43.1 0.0 copy-start.2
  43.1 1.1 copy-done.2
  44.3 5.7 %all-to-all-start.1 = ((bf16[32,48,512]{2,1,0:T(8,128)(2,1)}), bf16[32,48,512]{2,1,0:T(8,128)(2,1)S(1)}, u32[]{:S(2)}, u32[]{:S(2)}) async-start(bf16[32,48,512]{2,1,0:T(8,128)(2,1)} %copy-done.2), calls=%async_computation.1 | async-start | bytes 3145728 | tf_op jit(solution)/shard_map/all_to_all | solution.py:319
  50.0 3.4 %fusion = (bf16[256,2560]{1,0:T(8,128)(2,1)}, bf16[256,2560]{1,0:T(8,128)(2,1)}) fusion(bf16[1024,5120]{1,0:T(8,128)(2,1)} %w_own.1, s32[]{:T(128)S(6)} %select_n.12, s32[]{:T(128)S(6)} %select_n.11, s32[]{:T(128)S(6)} %select_n.10), kind=kLoop, calls=%fused_computation.2 | loop fusion | bytes 5242892 | tf_op jit(solution)/shard_map/dynamic_slice | solution.py:343
  53.4 2.5 %collective-permute-start.10 = (bf16[256,2560]{1,0:T(8,128)(2,1)}, bf16[256,2560]{1,0:T(8,128)(2,1)}, u32[]{:S(2)}, u32[]{:S(2)}) collective-permute-start(bf16[256,2560]{1,0:T(8,128)(2,1)} %get-tuple-element.38), channel_id=1, source_target_pairs={{0,17},{17,0},{1,16},{16,1},{2,19},{19,2},{3,18},{18,3},{4,21},{21... | collective-permute-start | bytes 3932168 | tf_op jit(solution)/shard_map/ppermute | solution.py:347
  55.9 15.1 %all-to-all-done.1 = bf16[32,48,512]{2,1,0:T(8,128)(2,1)S(1)} async-done(((bf16[32,48,512]{2,1,0:T(8,128)(2,1)}), bf16[32,48,512]{2,1,0:T(8,128)(2,1)S(1)}, u32[]{:S(2)}, u32[]{:S(2)}) %all-to-all-start.1) | async-done | bytes 1572896 | tf_op jit(solution)/shard_map/all_to_all | solution.py:319
  71.0 2.7 %shard_map.86 = (bf16[512,1024]{1,0:T(8,128)(2,1)S(1)}, bf16[256,1024]{1,0:T(8,128)(2,1)S(1)}, f32[8,128]{1,0:T(8,128)S(1)}) custom-call(bf16[512,1024]{1,0:T(8,128)(2,1)} %copy-done.1, bf16[256,1024]{1,0:T(8,128)(2,1)} %copy-done.3, bf16[2,768,512]{2,1,0:T(8,128)(2,1)S(1)} %bitcast.10), custom_call_target="tpu_custom_call" | custom-call | flops 4194304 | bytes 5242880 | tf_op jit(solution)/shard_map/pallas_call | solution.py:55
  73.7 2.5 %collective-permute-start.2 = (f32[8,128]{1,0:T(8,128)S(1)}, f32[8,128]{1,0:T(8,128)S(1)}, u32[]{:S(2)}, u32[]{:S(2)}) collective-permute-start(f32[8,128]{1,0:T(8,128)S(1)} %get-tuple-element.24.rest_1_.own), channel_id=1, source_target_pairs={{0,2},{2,0},{1,3},{3,1},{4,6},{6,4},{5,7},{7,5},{8,10},{10,8},{9,1... | collective-permute-start | bytes 12296 | tf_op jit(solution)/shard_map/ppermute | solution.py:324
  76.2 0.0 copy-done.5
  76.2 1.0 shard_map.87.raw
  77.2 0.0 collective-permute-done.2.rest_2_.oth
  77.3 5.7 %shard_map.88 = bf16[2,768,512]{2,1,0:T(8,128)(2,1)} custom-call(bf16[512,1024]{1,0:T(8,128)(2,1)S(1)} %get-tuple-element.25.w13, bf16[256,1024]{1,0:T(8,128)(2,1)S(1)} %get-tuple-element.26.w2, f32[768,512]{1,0:T(8,128)S(1)} %shard_map.87.raw, bf16[512,1024]{1,0:T(8,128)(2,1)S(1)} %copy-done.5, bf16[512,1024]{1,0:T(8,128)(2,1)} %collective-permute-done.k_oth, ...), custom_call_target="tpu_custom_call" | custom-call | flops 2415919104 | bytes 8388608 | tf_op jit(solution)/shard_map/pallas_call | solution.py:55
  83.0 5.8 %all-to-all-start.2 = ((bf16[32,48,512]{2,1,0:T(8,128)(2,1)}), bf16[32,48,512]{2,1,0:T(8,128)(2,1)S(1)}, u32[]{:S(2)}, u32[]{:S(2)}) async-start(bf16[32,48,512]{2,1,0:T(8,128)(2,1)} %bitcast.8), calls=%async_computation.2 | async-start | bytes 3145728 | tf_op jit(solution)/shard_map/all_to_all | solution.py:309
  88.8 0.0 collective-permute-done.10.first_a
  88.8 2.6 %collective-permute-start.11 = (bf16[256,2560]{1,0:T(8,128)(2,1)}, bf16[256,2560]{1,0:T(8,128)(2,1)S(1)}, u32[]{:S(2)}, u32[]{:S(2)}) collective-permute-start(bf16[256,2560]{1,0:T(8,128)(2,1)} %get-tuple-element.31), channel_id=1, source_target_pairs={{0,17},{17,0},{1,16},{16,1},{2,19},{19,2},{3,18},{18,3},{4,21},{21... | collective-permute-start | bytes 3932168 | tf_op jit(solution)/shard_map/ppermute | solution.py:348
  91.4 19.3 %all-to-all-done.2.arrived = bf16[32,48,512]{2,1,0:T(8,128)(2,1)S(1)} async-done(((bf16[32,48,512]{2,1,0:T(8,128)(2,1)}), bf16[32,48,512]{2,1,0:T(8,128)(2,1)S(1)}, u32[]{:S(2)}, u32[]{:S(2)}) %all-to-all-start.2) | async-done | bytes 1572896 | tf_op jit(solution)/shard_map/all_to_all | solution.py:309
  110.7 1.5 shard_map.89
  112.2 6.5 %all-to-all-start.3 = ((bf16[32,48,512]{2,1,0:T(8,128)(2,1)}), bf16[32,48,512]{2,1,0:T(8,128)(2,1)S(1)}, u32[]{:S(2)}, u32[]{:S(2)}) async-start(bf16[32,48,512]{2,1,0:T(8,128)(2,1)} %shard_map.89), calls=%async_computation.3 | async-start | bytes 3145728 | tf_op jit(solution)/shard_map/all_to_all | solution.py:319
  118.7 1.4 collective-permute-start.3
  120.1 0.2 collective-permute-done.11.first_b
  120.3 1.3 collective-permute-start.12
  121.5 0.0 collective-permute-start.13
  121.5 17.9 %all-to-all-done.3 = bf16[32,48,512]{2,1,0:T(8,128)(2,1)S(1)} async-done(((bf16[32,48,512]{2,1,0:T(8,128)(2,1)}), bf16[32,48,512]{2,1,0:T(8,128)(2,1)S(1)}, u32[]{:S(2)}, u32[]{:S(2)}) %all-to-all-start.3) | async-done | bytes 1572896 | tf_op jit(solution)/shard_map/all_to_all | solution.py:319
  139.4 1.7 shard_map.90
  141.1 1.7 collective-permute-start.7
  142.8 2.8 %collective-permute-start.6 = (bf16[256,1024]{1,0:T(8,128)(2,1)S(1)}, bf16[256,1024]{1,0:T(8,128)(2,1)S(1)}, u32[]{:S(2)}, u32[]{:S(2)}) collective-permute-start(bf16[256,1024]{1,0:T(8,128)(2,1)S(1)} %get-tuple-element.30.w2_own), channel_id=1, source_target_pairs={{0,2},{2,0},{1,3},{3,1},{4,6},{6,4},{5,7},{7,5},{8,10},{10,8},{9,1... | collective-permute-start | bytes 1572872 | tf_op jit(solution)/shard_map/ppermute | solution.py:324
  145.6 2.3 %shard_map.91 = (bf16[512,1024]{1,0:T(8,128)(2,1)S(1)}, f32[8,128]{1,0:T(8,128)S(1)}) custom-call(bf16[512,1024]{1,0:T(8,128)(2,1)} %copy-done.1, bf16[2,768,512]{2,1,0:T(8,128)(2,1)} %bitcast.12, f32[8,128]{1,0:T(8,128)S(1)} %get-tuple-element.23.rest_0_.norm, f32[8,128]{1,0:T(8,128)S(1)} %get-tuple-element.24.rest_1_.own, ...), custom_call_target="tpu_custom_call" | custom-call | flops 1048576 | bytes 1048576 | tf_op jit(solution)/shard_map/pallas_call | solution.py:55
  147.9 0.0 collective-permute-done.3.oth_far
  147.9 0.1 collective-permute-start.4
  148.0 2.7 %shard_map.92.raw = f32[2,512,512]{2,1,0:T(8,128)S(1)} custom-call(bf16[512,1024]{1,0:T(8,128)(2,1)S(1)} %get-tuple-element.28.m13, bf16[512,1024]{1,0:T(8,128)(2,1)} %collective-permute-done.3.oth_far, bf16[512,1024]{1,0:T(8,128)(2,1)} %own_far.1), custom_call_target="tpu_custom_call" | custom-call | flops 1073741824 | bytes 5242880 | tf_op jit(solution)/shard_map/pallas_call | solution.py:55
  150.7 0.0 collective-permute-done.4.sq_oth
  150.7 0.3 shard_map.94
  151.0 0.6 collective-permute-start.5
  151.6 0.3 shard_map.93.hq_own
  151.9 0.0 collective-permute-done.12.second_a
  151.9 0.9 collective-permute-start.8
  152.8 0.0 collective-permute-done.5.hq_got.after
  152.8 2.2 %collective-permute-start.9 = (bf16[256,512]{1,0:T(8,128)(2,1)S(1)}, bf16[256,512]{1,0:T(8,128)(2,1)S(1)}, u32[]{:S(2)}, u32[]{:S(2)}) collective-permute-start(bf16[256,512]{1,0:T(8,128)(2,1)S(1)} %collective-permute-done.5.hq_got.after), channel_id=1, source_target_pairs={{0,1},{1,0},{2,3},{3,2},{4,5},{5,4},{6,7},{7,6},{8,9},{9,8},{10,11... | collective-permute-start | bytes 786440 | tf_op jit(solution)/shard_map/ppermute | solution.py:419
  155.0 0.1 pad_add_fusion.place
  155.0 0.0 collective-permute-done.13.second_b
  155.0 2.7 %shard_map.97.rest_2_ = bf16[1024,2560]{1,0:T(8,128)(2,1)S(1)} custom-call(s32[2]{0:T(128)S(1)} %pad_add_fusion.place, bf16[256,512]{1,0:T(8,128)(2,1)S(1)} %collective-permute-done.5.hq_got.after, bf16[256,2560]{1,0:T(8,128)(2,1)} %collective-permute-done.10.first_a, bf16[256,2560]{1,0:T(8,128)(2,1)S(1)} %collective-permute-done.11.first_b, ...), custom_call_target="tpu_custom_call" | custom-call | flops 65536 | bytes 65536 | tf_op jit(solution)/shard_map/pallas_call | solution.py:55
  157.7 0.0 collective-permute-done.6.w2_got
  157.7 0.7 shard_map.95.o
  158.5 6.6 %shard_map.96.part = f32[512,2560]{1,0:T(8,128)S(1)} custom-call(s32[2]{0:T(128)S(1)} %pad_add_fusion.place, bf16[512,1024]{1,0:T(8,128)(2,1)S(1)} %shard_map.95.o, bf16[1024,5120]{1,0:T(8,128)(2,1)} %w_own.1), custom_call_target="tpu_custom_call" | custom-call | flops 1048576 | bytes 65536 | tf_op jit(solution)/shard_map/pallas_call | solution.py:253
  165.1 0.0 collective-permute-done.8.hq_a
  165.1 0.0 collective-permute-done.7.rest_0_
  165.1 2.0 %collective-permute-done.9.hq_b = bf16[256,512]{1,0:T(8,128)(2,1)S(1)} collective-permute-done((bf16[256,512]{1,0:T(8,128)(2,1)S(1)}, bf16[256,512]{1,0:T(8,128)(2,1)S(1)}, u32[]{:S(2)}, u32[]{:S(2)}) %collective-permute-start.9) | collective-permute-done | bytes 262176 | tf_op jit(solution)/shard_map/ppermute | solution.py:419
  167.1 0.9 collective-permute-start.14
  168.0 1.5 collective-permute-done.14.rest_1_
  169.5 4.3 %shard_map.98 = bf16[512,2560]{1,0:T(8,128)(2,1)} custom-call(f32[512,2560]{1,0:T(8,128)S(1)} %shard_map.96.part, bf16[256,512]{1,0:T(8,128)(2,1)S(1)} %collective-permute-done.8.hq_a, bf16[256,512]{1,0:T(8,128)(2,1)S(1)} %collective-permute-done.9.hq_b, bf16[256,1024]{1,0:T(8,128)(2,1)S(1)} %collective-permute-done.7.rest_0_, ...), custom_call_target="tpu_custom_call" | custom-call | flops 3221225472 | bytes 6291456 | tf_op jit(solution)/shard_map/pallas_call | solution.py:289
  (5 shorter events, 0.0 us)
Async XLA Ops:
  0.0 3.1 %copy-start.4 = (bf16[512,1024]{1,0:T(8,128)(2,1)S(1)}, bf16[512,1024]{1,0:T(8,128)(2,1)}, u32[]{:S(2)}) copy-start(bf16[512,1024]{1,0:T(8,128)(2,1)} %k_own.3) | copy-start | bytes 3145732
  1.6 6.3 %collective-permute-start.1 = (bf16[512,1024]{1,0:T(8,128)(2,1)S(1)}, bf16[512,1024]{1,0:T(8,128)(2,1)}, u32[]{:S(2)}, u32[]{:S(2)}) collective-permute-start(bf16[512,1024]{1,0:T(8,128)(2,1)S(1)} %multiply_convert_fusion.targets.u_own), channel_id=1, source_target_pairs={{0,2},{2,0},{1,3},{3,1},{4,6},{6,4},{5,7},{7,5},{8,10},{10,8},{9,1... | collective-permute-start | bytes 3145736 | tf_op jit(solution)/shard_map/ppermute | solution.py:324
  3.1 4.8 %collective-permute-start = (bf16[512,1024]{1,0:T(8,128)(2,1)S(1)}, bf16[512,1024]{1,0:T(8,128)(2,1)}, u32[]{:S(2)}, u32[]{:S(2)}) collective-permute-start(bf16[512,1024]{1,0:T(8,128)(2,1)S(1)} %copy-done.4), channel_id=1, source_target_pairs={{0,2},{2,0},{1,3},{3,1},{4,6},{6,4},{5,7},{7,5},{8,10},{10,8},{9,1... | collective-permute-start | bytes 3145736 | tf_op jit(solution)/shard_map/ppermute | solution.py:324
  6.8 1.1 copy-start.1
  6.9 1.2 copy-start.3
  43.1 1.1 copy-start.2
  44.3 26.7 %all-to-all-start.1 = ((bf16[32,48,512]{2,1,0:T(8,128)(2,1)}), bf16[32,48,512]{2,1,0:T(8,128)(2,1)S(1)}, u32[]{:S(2)}, u32[]{:S(2)}) async-start(bf16[32,48,512]{2,1,0:T(8,128)(2,1)} %copy-done.2), calls=%async_computation.1 | async-start | bytes 3145728 | tf_op jit(solution)/shard_map/all_to_all | solution.py:319
  53.4 35.4 %collective-permute-start.10 = (bf16[256,2560]{1,0:T(8,128)(2,1)}, bf16[256,2560]{1,0:T(8,128)(2,1)}, u32[]{:S(2)}, u32[]{:S(2)}) collective-permute-start(bf16[256,2560]{1,0:T(8,128)(2,1)} %get-tuple-element.38), channel_id=1, source_target_pairs={{0,17},{17,0},{1,16},{16,1},{2,19},{19,2},{3,18},{18,3},{4,21},{21... | collective-permute-start | bytes 3932168 | tf_op jit(solution)/shard_map/ppermute | solution.py:347
  71.0 2.7 %copy-start = (bf16[32,48,512]{2,1,0:T(8,128)(2,1)}, bf16[32,48,512]{2,1,0:T(8,128)(2,1)S(1)}, u32[]{:S(2)}) copy-start(bf16[32,48,512]{2,1,0:T(8,128)(2,1)S(1)} %all-to-all-done.1) | copy-start | bytes 4718596
  71.0 5.3 %copy-start.5 = (bf16[512,1024]{1,0:T(8,128)(2,1)S(1)}, bf16[512,1024]{1,0:T(8,128)(2,1)}, u32[]{:S(2)}) copy-start(bf16[512,1024]{1,0:T(8,128)(2,1)} %k_own.3) | copy-start | bytes 3145732
  73.7 3.5 %collective-permute-start.2 = (f32[8,128]{1,0:T(8,128)S(1)}, f32[8,128]{1,0:T(8,128)S(1)}, u32[]{:S(2)}, u32[]{:S(2)}) collective-permute-start(f32[8,128]{1,0:T(8,128)S(1)} %get-tuple-element.24.rest_1_.own), channel_id=1, source_target_pairs={{0,2},{2,0},{1,3},{3,1},{4,6},{6,4},{5,7},{7,5},{8,10},{10,8},{9,1... | collective-permute-start | bytes 12296 | tf_op jit(solution)/shard_map/ppermute | solution.py:324
  83.0 27.7 %all-to-all-start.2 = ((bf16[32,48,512]{2,1,0:T(8,128)(2,1)}), bf16[32,48,512]{2,1,0:T(8,128)(2,1)S(1)}, u32[]{:S(2)}, u32[]{:S(2)}) async-start(bf16[32,48,512]{2,1,0:T(8,128)(2,1)} %bitcast.8), calls=%async_computation.2 | async-start | bytes 3145728 | tf_op jit(solution)/shard_map/all_to_all | solution.py:309
  88.8 31.4 %collective-permute-start.11 = (bf16[256,2560]{1,0:T(8,128)(2,1)}, bf16[256,2560]{1,0:T(8,128)(2,1)S(1)}, u32[]{:S(2)}, u32[]{:S(2)}) collective-permute-start(bf16[256,2560]{1,0:T(8,128)(2,1)} %get-tuple-element.31), channel_id=1, source_target_pairs={{0,17},{17,0},{1,16},{16,1},{2,19},{19,2},{3,18},{18,3},{4,21},{21... | collective-permute-start | bytes 3932168 | tf_op jit(solution)/shard_map/ppermute | solution.py:348
  112.2 27.2 %all-to-all-start.3 = ((bf16[32,48,512]{2,1,0:T(8,128)(2,1)}), bf16[32,48,512]{2,1,0:T(8,128)(2,1)S(1)}, u32[]{:S(2)}, u32[]{:S(2)}) async-start(bf16[32,48,512]{2,1,0:T(8,128)(2,1)} %shard_map.89), calls=%async_computation.3 | async-start | bytes 3145728 | tf_op jit(solution)/shard_map/all_to_all | solution.py:319
  118.7 29.2 %collective-permute-start.3 = (bf16[512,1024]{1,0:T(8,128)(2,1)}, bf16[512,1024]{1,0:T(8,128)(2,1)}, u32[]{:S(2)}, u32[]{:S(2)}) collective-permute-start(bf16[512,1024]{1,0:T(8,128)(2,1)} %own_far.1), channel_id=1, source_target_pairs={{0,2},{2,0},{1,3},{3,1},{4,6},{6,4},{5,7},{7,5},{8,10},{10,8},{9,1... | collective-permute-start | bytes 3145736 | tf_op jit(solution)/shard_map/ppermute | solution.py:324
  120.3 31.6 %collective-permute-start.12 = (bf16[256,2560]{1,0:T(8,128)(2,1)}, bf16[256,2560]{1,0:T(8,128)(2,1)}, u32[]{:S(2)}, u32[]{:S(2)}) collective-permute-start(bf16[256,2560]{1,0:T(8,128)(2,1)} %collective-permute-done.10.first_a), channel_id=1, source_target_pairs={{0,2},{2,0},{1,3},{3,1},{4,6},{6,4},{5,7},{7,5},{8,10},{10,8},{9,1... | collective-permute-start | bytes 3932168 | tf_op jit(solution)/shard_map/ppermute | solution.py:324
  121.5 33.5 %collective-permute-start.13 = (bf16[256,2560]{1,0:T(8,128)(2,1)S(1)}, bf16[256,2560]{1,0:T(8,128)(2,1)}, u32[]{:S(2)}, u32[]{:S(2)}) collective-permute-start(bf16[256,2560]{1,0:T(8,128)(2,1)S(1)} %collective-permute-done.11.first_b), channel_id=1, source_target_pairs={{0,2},{2,0},{1,3},{3,1},{4,6},{6,4},{5,7},{7,5},{8,10},{10,8},{9,1... | collective-permute-start | bytes 3932168 | tf_op jit(solution)/shard_map/ppermute | solution.py:324
  141.1 24.0 %collective-permute-start.7 = (bf16[256,1024]{1,0:T(8,128)(2,1)S(1)}, bf16[256,1024]{1,0:T(8,128)(2,1)S(1)}, u32[]{:S(2)}, u32[]{:S(2)}) collective-permute-start(bf16[256,1024]{1,0:T(8,128)(2,1)S(1)} %get-tuple-element.30.w2_own), channel_id=1, source_target_pairs={{0,17},{17,0},{1,16},{16,1},{2,19},{19,2},{3,18},{18,3},{4,21},{21... | collective-permute-start | bytes 1572872 | tf_op jit(solution)/shard_map/ppermute | solution.py:401
  142.8 14.9 %collective-permute-start.6 = (bf16[256,1024]{1,0:T(8,128)(2,1)S(1)}, bf16[256,1024]{1,0:T(8,128)(2,1)S(1)}, u32[]{:S(2)}, u32[]{:S(2)}) collective-permute-start(bf16[256,1024]{1,0:T(8,128)(2,1)S(1)} %get-tuple-element.30.w2_own), channel_id=1, source_target_pairs={{0,2},{2,0},{1,3},{3,1},{4,6},{6,4},{5,7},{7,5},{8,10},{10,8},{9,1... | collective-permute-start | bytes 1572872 | tf_op jit(solution)/shard_map/ppermute | solution.py:324
  147.9 2.8 %collective-permute-start.4 = (f32[8,128]{1,0:T(8,128)S(1)}, f32[8,128]{1,0:T(8,128)S(1)}, u32[]{:S(2)}, u32[]{:S(2)}) collective-permute-start(f32[8,128]{1,0:T(8,128)S(1)} %get-tuple-element.29.sq_own), channel_id=1, source_target_pairs={{0,2},{2,0},{1,3},{3,1},{4,6},{6,4},{5,7},{7,5},{8,10},{10,8},{9,1... | collective-permute-start | bytes 12296 | tf_op jit(solution)/shard_map/ppermute | solution.py:324
  151.0 1.7 %collective-permute-start.5 = (bf16[256,512]{1,0:T(8,128)(2,1)S(1)}, bf16[256,512]{1,0:T(8,128)(2,1)S(1)}, u32[]{:S(2)}, u32[]{:S(2)}) collective-permute-start(bf16[256,512]{1,0:T(8,128)(2,1)S(1)} %shard_map.94), channel_id=1, source_target_pairs={{0,2},{2,0},{1,3},{3,1},{4,6},{6,4},{5,7},{7,5},{8,10},{10,8},{9,1... | collective-permute-start | bytes 786440 | tf_op jit(solution)/shard_map/ppermute | solution.py:324
  151.9 13.2 %collective-permute-start.8 = (bf16[256,512]{1,0:T(8,128)(2,1)S(1)}, bf16[256,512]{1,0:T(8,128)(2,1)S(1)}, u32[]{:S(2)}, u32[]{:S(2)}) collective-permute-start(bf16[256,512]{1,0:T(8,128)(2,1)S(1)} %shard_map.93.hq_own), channel_id=1, source_target_pairs={{0,1},{1,0},{2,3},{3,2},{4,5},{5,4},{6,7},{7,6},{8,9},{9,8},{10,11... | collective-permute-start | bytes 786440 | tf_op jit(solution)/shard_map/ppermute | solution.py:419
  152.8 14.3 %collective-permute-start.9 = (bf16[256,512]{1,0:T(8,128)(2,1)S(1)}, bf16[256,512]{1,0:T(8,128)(2,1)S(1)}, u32[]{:S(2)}, u32[]{:S(2)}) collective-permute-start(bf16[256,512]{1,0:T(8,128)(2,1)S(1)} %collective-permute-done.5.hq_got.after), channel_id=1, source_target_pairs={{0,1},{1,0},{2,3},{3,2},{4,5},{5,4},{6,7},{7,6},{8,9},{9,8},{10,11... | collective-permute-start | bytes 786440 | tf_op jit(solution)/shard_map/ppermute | solution.py:419
  167.1 2.5 %collective-permute-start.14 = (bf16[256,1024]{1,0:T(8,128)(2,1)S(1)}, bf16[256,1024]{1,0:T(8,128)(2,1)S(1)}, u32[]{:S(2)}, u32[]{:S(2)}) collective-permute-start(bf16[256,1024]{1,0:T(8,128)(2,1)S(1)} %collective-permute-done.7.rest_0_), channel_id=1, source_target_pairs={{0,2},{2,0},{1,3},{3,1},{4,6},{6,4},{5,7},{7,5},{8,10},{10,8},{9,1... | collective-permute-start | bytes 1572872 | tf_op jit(solution)/shard_map/ppermute | solution.py:324
